TPU v7x, 32 devices: a whole 2x2x4 slice. The times are simulated.
32 devices in a mesh: dp: 4 (over y, core), seq: 8 (over z, x).
Axes of the slice: x: 2, y: 2, z: 4, core: 2. Of those that a mesh axis runs over, the one named last changes fastest.
Arguments:
- tokens: bfloat16 [4, 2048, 2048], P('dp', 'seq'), may hold values from -6 to 6
- cotangent: bfloat16 [4, 2048, 2048], P('dp', 'seq'), may hold values from -6 to 6
- lengths: int32 [4, 4], replicated, may hold values from 256 to 1024, as said below
- placement: int32 [4], replicated, may hold values from 0 to 3, each once
- w_query: bfloat16 [2048, 2048], P(('dp', 'seq')), may hold values from -0.125 to 0.125
- w_key: bfloat16 [2048, 2048], P(('dp', 'seq')), may hold values from -0.125 to 0.125
- w_value: bfloat16 [2048, 2048], P(('dp', 'seq')), may hold values from -0.125 to 0.125
- w_output: bfloat16 [2048, 2048], P(('dp', 'seq')), may hold values from -0.125 to 0.125
- query_gain: bfloat16 [2048], P(('dp', 'seq')), may hold values from 0.099609375 to 1.8984375
- key_gain: bfloat16 [2048], P(('dp', 'seq')), may hold values from 0.099609375 to 1.8984375
- attn_gain: bfloat16 [2048], P(('dp', 'seq')), may hold values from 0.099609375 to 1.8984375
- w_gate: bfloat16 [2048, 8192], P('dp', 'seq'), may hold values from -0.125 to 0.125
- w_up: bfloat16 [2048, 8192], P('dp', 'seq'), may hold values from -0.125 to 0.125
- w_down: bfloat16 [8192, 2048], P('seq', 'dp'), may hold values from -0.0625 to 0.0625
- mlp_gain: bfloat16 [2048], P(('dp', 'seq')), may hold values from 0.099609375 to 1.8984375
Outputs:
- layer_out: bfloat16 [4, 2048, 2048], P('dp', 'seq')
- grad_tokens: bfloat16 [4, 2048, 2048], P('dp', 'seq')
- grad_query: float32 [2048, 2048], P(('dp', 'seq'))
- grad_key: float32 [2048, 2048], P(('dp', 'seq'))
- grad_value: float32 [2048, 2048], P(('dp', 'seq'))
- grad_output: float32 [2048, 2048], P(('dp', 'seq'))
- grad_query_gain: float32 [2048], P(('dp', 'seq'))
- grad_key_gain: float32 [2048], P(('dp', 'seq'))
- grad_attn_gain: float32 [2048], P(('dp', 'seq'))
- grad_gate: float32 [2048, 8192], P('dp', 'seq')
- grad_up: float32 [2048, 8192], P('dp', 'seq')
- grad_down: float32 [8192, 2048], P('seq', 'dp')
- grad_mlp_gain: float32 [2048], P(('dp', 'seq'))
Inputs may be any that keep to these rules, and one draw needn't show every extreme that they name: In every row the 4 lengths sum to 2048; one of them is 1024 and another 2048 // 8. `placement`: each stored row is held at exactly one data position.
All inputs are finite; a program needn't handle non-finite values.
Results may differ from a plain program's by a relative error of at most 0.019.
Values may be sent and summed in bfloat16 or wider, within the bound.
No kernel may reach another device: no remote copies, remote signals or barrier semaphores. Data moves between devices by JAX's collectives and lax.ppermute only.
A program may use at most 320 MiB of HBM per device.

v0:
```python
import jax
import jax.numpy as jnp
from jax import lax
from jax.sharding import PartitionSpec as P

HEAD = 128


EPSILON = 1e-06
ROPE_BASE = 500000.0


def as_sent(shard):
    return jax.tree.map(lambda a: a.astype(jnp.bfloat16) if a.dtype == jnp.float32 else a, shard)


def times_plain(left, right):
    return jnp.dot(left, right, preferred_element_type=jnp.float32)


def times_trans(left, right):
    return lax.dot_general(
        left, right, (((1,), (1,)), ((), ())), preferred_element_type=jnp.float32
    )


def trans_times(left, right):
    return lax.dot_general(
        left, right, (((0,), (0,)), ((), ())), preferred_element_type=jnp.float32
    )


def rms_scale(vals):
    return lax.rsqrt(jnp.mean(vals * vals, axis=-1, keepdims=True) + EPSILON)


def norm_back(grad_out, pre, scale, gain):
    weighted = grad_out * gain
    inner = jnp.mean(weighted * pre, axis=-1, keepdims=True)
    grad_pre = scale * weighted - pre * (scale * scale * scale) * inner
    grad_gain = jnp.sum(grad_out * pre * scale, axis=0)
    return (grad_pre, grad_gain)


def rope_tables(positions, width):
    half = width // 2
    freq = ROPE_BASE ** (-2.0 * jnp.arange(half, dtype=jnp.float32) / width)
    angle = positions.astype(jnp.float32)[:, None] * freq[None, :]
    return (jnp.cos(angle)[:, None, :], jnp.sin(angle)[:, None, :])


def rotate(vals, cosine, sine):
    half = vals.shape[-1] // 2
    first = vals[..., :half]
    second = vals[..., half:]
    return jnp.concatenate(
        [first * cosine - second * sine, second * cosine + first * sine], axis=-1
    )


def unrotate(grads, cosine, sine):
    half = grads.shape[-1] // 2
    first = grads[..., :half]
    second = grads[..., half:]
    return jnp.concatenate(
        [first * cosine + second * sine, second * cosine - first * sine], axis=-1
    )


def layouts(lengths, placement, row_first, rows_here, row_len):
    stored = lengths.shape[0]
    doc_count = lengths.shape[1]
    picked = lax.dynamic_slice_in_dim(placement, row_first, rows_here, 0)
    match = picked[:, None] == jnp.arange(stored, dtype=jnp.int32)[None, :]
    doc_lens = jnp.sum(jnp.where(match[:, :, None], lengths[None, :, :], 0), axis=1)
    doc_ends = jnp.cumsum(doc_lens, axis=1)
    positions = jnp.arange(row_len, dtype=jnp.int32)
    doc_ids = jnp.sum((positions[None, :, None] >= doc_ends[:, None, :]).astype(jnp.int32), axis=2)
    doc_starts = doc_ends - doc_lens
    picks = doc_ids[:, :, None] == jnp.arange(doc_count, dtype=jnp.int32)[None, None, :]
    doc_first = jnp.sum(jnp.where(picks, doc_starts[:, None, :], 0), axis=2)
    return (doc_ids, positions[None, :] - doc_first)


def block_scores(query_blk, keys, docs, start, block, scale):
    row_len = keys.shape[0]
    keys_at = jnp.arange(row_len, dtype=jnp.int32)
    rows_at = start + jnp.arange(block, dtype=jnp.int32)
    scores = jnp.einsum("qhd,khd->hqk", query_blk, keys, preferred_element_type=jnp.float32) * scale
    allowed = (docs[start : start + block][:, None] == docs[None, :]) & (
        keys_at[None, :] <= rows_at[:, None]
    )
    return jnp.where(allowed[None], scores, -1e30)


def attend_forward(query_rot, key_rot, values, doc_ids):
    row_len = query_rot.shape[1]
    block = min(512, row_len)
    scale = query_rot.shape[3] ** (-0.5)

    def one_row(item):
        queries, keys, vals, docs = item
        outputs = []
        totals = []
        for start in range(0, row_len, block):
            scores = block_scores(queries[start : start + block], keys, docs, start, block, scale)
            top = jnp.max(scores, axis=-1, keepdims=True)
            expo = jnp.exp(scores - top)
            total = jnp.sum(expo, axis=-1, keepdims=True)
            probs = (expo / total).astype(jnp.bfloat16)
            outputs.append(
                jnp.einsum("hqk,khd->qhd", probs, vals, preferred_element_type=jnp.float32)
            )
            totals.append((top + jnp.log(total))[..., 0])
        return (
            jnp.concatenate(outputs, axis=0).astype(jnp.bfloat16),
            jnp.concatenate(totals, axis=1),
        )

    return lax.map(one_row, (query_rot, key_rot, values, doc_ids))


def attend_backward(query_rot, key_rot, values, doc_ids, log_sums, grad_heads):
    row_len = query_rot.shape[1]
    block = min(512, row_len)
    scale = query_rot.shape[3] ** (-0.5)

    def one_row(item):
        queries, keys, vals, docs, sums, grads = item
        grad_queries = []
        grad_keys = jnp.zeros(keys.shape, jnp.float32)
        grad_vals = jnp.zeros(vals.shape, jnp.float32)
        for start in range(0, row_len, block):
            query_blk = queries[start : start + block]
            grad_blk = grads[start : start + block]
            scores = block_scores(query_blk, keys, docs, start, block, scale)
            probs = jnp.exp(scores - sums[:, start : start + block, None])
            grad_probs = jnp.einsum(
                "qhd,khd->hqk", grad_blk, vals, preferred_element_type=jnp.float32
            )
            inner = jnp.sum(probs * grad_probs, axis=-1, keepdims=True)
            grad_scores = (probs * (grad_probs - inner)).astype(jnp.bfloat16)
            grad_queries.append(
                jnp.einsum("hqk,khd->qhd", grad_scores, keys, preferred_element_type=jnp.float32)
                * scale
            )
            grad_keys = (
                grad_keys
                + jnp.einsum(
                    "hqk,qhd->khd", grad_scores, query_blk, preferred_element_type=jnp.float32
                )
                * scale
            )
            grad_vals = grad_vals + jnp.einsum(
                "hqk,qhd->khd",
                probs.astype(jnp.bfloat16),
                grad_blk,
                preferred_element_type=jnp.float32,
            )
        grad_q = jnp.concatenate(grad_queries, axis=0).astype(jnp.bfloat16)
        return jnp.stack([grad_q, grad_keys.astype(jnp.bfloat16), grad_vals.astype(jnp.bfloat16)])

    stacked = lax.map(one_row, (query_rot, key_rot, values, doc_ids, log_sums, grad_heads))
    return jnp.moveaxis(stacked, 1, 0)


def per_device(
    tokens,
    cotangent,
    lengths,
    placement,
    w_query,
    w_key,
    w_value,
    w_output,
    query_gain,
    key_gain,
    attn_gain,
    w_gate,
    w_up,
    w_down,
    mlp_gain,
):
    rows_here, tok_here, width = tokens.shape
    seq_count = lax.axis_size("seq")
    seq_index = lax.axis_index("seq")
    row_len = tok_here * seq_count
    count = rows_here * tok_here
    head_width = HEAD
    heads_all = width // head_width
    doc_ids, positions = layouts(
        lengths, placement, lax.axis_index("dp") * rows_here, rows_here, row_len
    )
    local_pos = lax.dynamic_slice_in_dim(positions, seq_index * tok_here, tok_here, 1).reshape(
        count
    )
    cosine, sine = rope_tables(local_pos, head_width)
    full_query, full_key, full_value, full_output, gain_query, gain_key, gain_attn, gain_mlp = (
        lax.all_gather(w_query, ("dp", "seq"), axis=0, tiled=True),
        lax.all_gather(w_key, ("dp", "seq"), axis=0, tiled=True),
        lax.all_gather(w_value, ("dp", "seq"), axis=0, tiled=True),
        lax.all_gather(w_output, ("dp", "seq"), axis=0, tiled=True),
        lax.all_gather(query_gain, ("dp", "seq"), axis=0, tiled=True),
        lax.all_gather(key_gain, ("dp", "seq"), axis=0, tiled=True),
        lax.all_gather(attn_gain, ("dp", "seq"), axis=0, tiled=True),
        lax.all_gather(mlp_gain, ("dp", "seq"), axis=0, tiled=True),
    )
    gate_cols, up_cols, down_rows = (
        lax.all_gather(w_gate, "dp", axis=0, tiled=True),
        lax.all_gather(w_up, "dp", axis=0, tiled=True),
        lax.all_gather(w_down, "dp", axis=1, tiled=True),
    )
    gain_query = gain_query.astype(jnp.float32)
    gain_key = gain_key.astype(jnp.float32)
    gain_attn = gain_attn.astype(jnp.float32)
    gain_mlp = gain_mlp.astype(jnp.float32)
    inputs = tokens.reshape(count, width)
    query_pre = times_plain(inputs, full_query)
    key_pre = times_plain(inputs, full_key)
    value_low = times_plain(inputs, full_value).astype(jnp.bfloat16)
    query_scale = rms_scale(query_pre)
    key_scale = rms_scale(key_pre)
    query_norm = query_pre * query_scale * gain_query
    key_norm = key_pre * key_scale * gain_key
    query_rot = rotate(query_norm.reshape(count, heads_all, head_width), cosine, sine).astype(
        jnp.bfloat16
    )
    key_rot = rotate(key_norm.reshape(count, heads_all, head_width), cosine, sine).astype(
        jnp.bfloat16
    )
    packed = jnp.stack([query_rot, key_rot, value_low.reshape(count, heads_all, head_width)])
    packed = packed.reshape(3, rows_here, tok_here, heads_all, head_width)
    by_head = lax.all_to_all(packed, "seq", split_axis=3, concat_axis=2, tiled=True)
    attn_heads, log_sums = attend_forward(by_head[0], by_head[1], by_head[2], doc_ids)
    attn_tokens = jax.tree.map(
        lambda part, own: part.astype(own.dtype),
        lax.all_to_all(as_sent(attn_heads), "seq", split_axis=1, concat_axis=2, tiled=True),
        attn_heads,
    ).reshape(count, width)
    attn_pre = times_plain(attn_tokens, full_output)
    attn_scale = rms_scale(attn_pre)
    middle = inputs.astype(jnp.float32) + attn_pre * attn_scale * gain_attn
    middle_low = middle.astype(jnp.bfloat16)
    middle_rows = lax.all_gather(middle_low, "seq", axis=0, tiled=True)
    gate_pre = times_plain(middle_rows, gate_cols)
    up_pre = times_plain(middle_rows, up_cols)
    gate_sigmoid = jax.nn.sigmoid(gate_pre)
    swish = gate_pre * gate_sigmoid
    hidden = (swish * up_pre).astype(jnp.bfloat16)
    mlp_pre = lax.psum_scatter(
        times_plain(
            lax.slice_in_dim(hidden, 0, count * lax.axis_size("seq"), axis=0), down_rows
        ).astype(jnp.bfloat16),
        "seq",
        scatter_dimension=0,
        tiled=True,
    ).astype(jnp.float32)
    mlp_scale = rms_scale(mlp_pre)
    layer_out = (middle + mlp_pre * mlp_scale * gain_mlp).astype(jnp.bfloat16).reshape(tokens.shape)
    grad_final = cotangent.reshape(count, width).astype(jnp.float32)
    grad_mlp_pre, grad_gain_mlp = norm_back(grad_final, mlp_pre, mlp_scale, gain_mlp)
    grad_mlp_rows = lax.all_gather(grad_mlp_pre.astype(jnp.bfloat16), "seq", axis=0, tiled=True)
    grad_hidden = times_trans(grad_mlp_rows, down_rows)
    grad_gate_pre = (
        grad_hidden * up_pre * gate_sigmoid * (1.0 + gate_pre * (1.0 - gate_sigmoid))
    ).astype(jnp.bfloat16)
    grad_up_pre = (grad_hidden * swish).astype(jnp.bfloat16)
    part_down = trans_times(hidden, grad_mlp_rows)
    part_gate = trans_times(middle_rows, grad_gate_pre)
    part_up = trans_times(middle_rows, grad_up_pre)
    gate_rows = lax.slice_in_dim(grad_gate_pre, 0, count * lax.axis_size("seq"), axis=0)
    up_rows = lax.slice_in_dim(grad_up_pre, 0, count * lax.axis_size("seq"), axis=0)
    grad_middle_mlp = lax.psum_scatter(
        (times_trans(gate_rows, gate_cols) + times_trans(up_rows, up_cols)).astype(jnp.bfloat16),
        "seq",
        scatter_dimension=0,
        tiled=True,
    ).astype(jnp.float32)
    grad_gate, grad_up, grad_down = (
        lax.psum_scatter(
            part_gate.astype(jnp.bfloat16), "dp", scatter_dimension=0, tiled=True
        ).astype(jnp.float32),
        lax.psum_scatter(
            part_up.astype(jnp.bfloat16), "dp", scatter_dimension=0, tiled=True
        ).astype(jnp.float32),
        lax.psum_scatter(
            part_down.astype(jnp.bfloat16), "dp", scatter_dimension=1, tiled=True
        ).astype(jnp.float32),
    )
    grad_middle = grad_final + grad_middle_mlp
    grad_attn_pre, grad_gain_attn = norm_back(grad_middle, attn_pre, attn_scale, gain_attn)
    grad_attn_low = grad_attn_pre.astype(jnp.bfloat16)
    back_query, back_key, back_value, back_output = (
        lax.all_gather(w_query, ("dp", "seq"), axis=0, tiled=True),
        lax.all_gather(w_key, ("dp", "seq"), axis=0, tiled=True),
        lax.all_gather(w_value, ("dp", "seq"), axis=0, tiled=True),
        lax.all_gather(w_output, ("dp", "seq"), axis=0, tiled=True),
    )
    part_output = trans_times(attn_tokens, grad_attn_low)
    grad_attn_tokens = times_trans(grad_attn_low, back_output).astype(jnp.bfloat16)
    grad_attn_tokens = grad_attn_tokens.reshape(rows_here, tok_here, heads_all, head_width)
    grad_heads = lax.all_to_all(grad_attn_tokens, "seq", split_axis=2, concat_axis=1, tiled=True)
    grad_stack = attend_backward(by_head[0], by_head[1], by_head[2], doc_ids, log_sums, grad_heads)
    back_tokens = lax.all_to_all(
        as_sent(grad_stack), "seq", split_axis=2, concat_axis=3, tiled=True
    ).astype(grad_stack.dtype)
    grad_query_rot = back_tokens[0].reshape(count, heads_all, head_width).astype(jnp.float32)
    grad_key_rot = back_tokens[1].reshape(count, heads_all, head_width).astype(jnp.float32)
    grad_value_low = back_tokens[2].reshape(count, width)
    grad_query_norm = unrotate(grad_query_rot, cosine, sine).reshape(count, width)
    grad_key_norm = unrotate(grad_key_rot, cosine, sine).reshape(count, width)
    grad_query_pre, grad_gain_query = norm_back(grad_query_norm, query_pre, query_scale, gain_query)
    grad_key_pre, grad_gain_key = norm_back(grad_key_norm, key_pre, key_scale, gain_key)
    grad_query_low = grad_query_pre.astype(jnp.bfloat16)
    grad_key_low = grad_key_pre.astype(jnp.bfloat16)
    grad_input = (
        grad_middle + times_trans(grad_query_low, back_query) + times_trans(grad_key_low, back_key)
    )
    grad_input = grad_input + times_trans(grad_value_low, back_value)
    part_query = trans_times(inputs, grad_query_low)
    part_key = trans_times(inputs, grad_key_low)
    part_value = trans_times(inputs, grad_value_low)
    summed = (
        lax.psum_scatter(part_query, ("dp", "seq"), scatter_dimension=0, tiled=True),
        lax.psum_scatter(part_key, ("dp", "seq"), scatter_dimension=0, tiled=True),
        lax.psum_scatter(part_value, ("dp", "seq"), scatter_dimension=0, tiled=True),
        lax.psum_scatter(part_output, ("dp", "seq"), scatter_dimension=0, tiled=True),
        lax.psum_scatter(grad_gain_query, ("dp", "seq"), scatter_dimension=0, tiled=True),
        lax.psum_scatter(grad_gain_key, ("dp", "seq"), scatter_dimension=0, tiled=True),
        lax.psum_scatter(grad_gain_attn, ("dp", "seq"), scatter_dimension=0, tiled=True),
        lax.psum_scatter(grad_gain_mlp, ("dp", "seq"), scatter_dimension=0, tiled=True),
    )
    (
        grad_query,
        grad_key,
        grad_value,
        grad_output,
        grad_query_gain,
        grad_key_gain,
        grad_attn_gain,
        grad_mlp_gain,
    ) = summed
    grad_tokens = grad_input.astype(jnp.bfloat16).reshape(tokens.shape)
    return (
        layer_out,
        grad_tokens,
        grad_query,
        grad_key,
        grad_value,
        grad_output,
        grad_query_gain,
        grad_key_gain,
        grad_attn_gain,
        grad_gate,
        grad_up,
        grad_down,
        grad_mlp_gain,
    )


def solution(mesh):
    return jax.shard_map(
        per_device,
        mesh=mesh,
        in_specs=(
            P("dp", "seq", None),
            P("dp", "seq", None),
            P(),
            P(),
            P(("dp", "seq"), None),
            P(("dp", "seq"), None),
            P(("dp", "seq"), None),
            P(("dp", "seq"), None),
            P(("dp", "seq")),
            P(("dp", "seq")),
            P(("dp", "seq")),
            P("dp", "seq"),
            P("dp", "seq"),
            P("seq", "dp"),
            P(("dp", "seq")),
        ),
        out_specs=(
            P("dp", "seq", None),
            P("dp", "seq", None),
            P(("dp", "seq"), None),
            P(("dp", "seq"), None),
            P(("dp", "seq"), None),
            P(("dp", "seq"), None),
            P(("dp", "seq")),
            P(("dp", "seq")),
            P(("dp", "seq")),
            P("dp", "seq"),
            P("dp", "seq"),
            P("seq", "dp"),
            P(("dp", "seq")),
        ),
        check_vma=False,
    )
```

profile of v0, /device:TPU:0, one launch (start us, length us, event | category | flops | bytes accessed | tf_op | source)
XLA Modules:
  0.0 2748.8 jit_solution(18099297494707571214)
XLA Ops:
  16.2 42.5 %all-reduce.9 = (bf16[2048]{0:T(1024)(128)(2,1)S(1)}, bf16[2048]{0:T(1024)(128)(2,1)S(1)}, bf16[2048]{0:T(1024)(128)(2,1)S(1)}, bf16[2048]{0:T(1024)(128)(2,1)}) all-reduce(bf16[2048]{0:T(1024)(128)(2,1)S(1)} %dynamic-update-slice.1, bf16[2048]{0:T(1024)(128)(2,1)S(1)} %dynamic-update-slice, ...), channel_id=1, replica_groups=mesh['dp'=4,'seq'=8] {'dp','seq'}, use_global_device_ids=true, to_apply=%add.1 | all-reduce | flops 8192 | bytes 32768
  59.5 31.9 %all-gather.14.cloned.1.call-done = bf16[2048,2048]{1,0:T(8,128)(2,1)} async-done(((bf16[64,2048]{1,0:T(8,128)(2,1)}), bf16[2048,2048]{1,0:T(8,128)(2,1)}) %all-gather.14.cloned.1.call-update) | async-done | bytes 8388624 | tf_op jit(solution)/shard_map/all_gather | solution.py:201
  91.4 6.1 fusion.64
  98.9 71.5 %all-gather.12.cloned.1.call-done = bf16[2048,2048]{1,0:T(8,128)(2,1)} async-done(((bf16[64,2048]{1,0:T(8,128)(2,1)}), bf16[2048,2048]{1,0:T(8,128)(2,1)}) %all-gather.12.cloned.1.call-update) | async-done | bytes 8388624 | tf_op jit(solution)/shard_map/all_gather | solution.py:200
  170.4 5.8 multiply_reduce_fusion.9
  178.2 71.3 %all-gather.10.cloned.1.call-done = bf16[2048,2048]{1,0:T(8,128)(2,1)} async-done(((bf16[64,2048]{1,0:T(8,128)(2,1)}), bf16[2048,2048]{1,0:T(8,128)(2,1)}) %all-gather.10.cloned.1.call-update) | async-done | bytes 8388624 | tf_op jit(solution)/shard_map/all_gather | solution.py:199
  249.4 5.8 multiply_reduce_fusion.10
  274.8 93.6 %all-to-all-done = bf16[3,1,256,16,128]{4,2,0,1,3:T(8,128)(2,1)} async-done(((bf16[3,1,256,16,128]{4,2,0,1,3:T(8,128)(2,1)}), bf16[3,1,256,16,128]{4,2,0,1,3:T(8,128)(2,1)}, u32[]{:S(2)}, u32[]{:S(2)}) %all-to-all-start) | async-done | bytes 3145760 | tf_op jit(solution)/shard_map/all_to_all | solution.py:233
  406.1 26.1 all-to-all-done.1
  432.9 6.2 multiply_reduce_fusion.8
  443.4 121.8 %all-gather.18.cloned.1.call-done = bf16[2048,2048]{1,0:T(8,128)(2,1)} async-done(((bf16[256,2048]{1,0:T(8,128)(2,1)}), bf16[2048,2048]{1,0:T(8,128)(2,1)}) %all-gather.18.cloned.1.call-update) | async-done | bytes 8388624 | tf_op jit(solution)/shard_map/all_gather | solution.py:244
  565.2 14.7 fusion.108
  579.9 19.5 all-gather.22.cloned.1.call-done
  599.5 16.9 multiply_convert_fusion.6
  616.4 19.2 all-gather.24.cloned.1.call-done
  635.5 13.9 convolution_convert_fusion
  650.2 148.5 %reduce-scatter.16.cloned.1.call-done = bf16[256,2048]{1,0:T(8,128)(2,1)} async-done(((bf16[2048,2048]{1,0:T(8,128)(2,1)}), bf16[256,2048]{1,0:T(8,128)(2,1)}) %reduce-scatter.16.cloned.1.call-update) | async-done | bytes 1048592 | tf_op jit(solution)/shard_map/reduce_scatter | solution.py:250
  805.5 124.0 %all-gather.26.cloned.1.call-done = bf16[2048,2048]{1,0:T(8,128)(2,1)} async-done(((bf16[256,2048]{1,0:T(8,128)(2,1)}), bf16[2048,2048]{1,0:T(8,128)(2,1)}) %all-gather.26.cloned.1.call-update) | async-done | bytes 8388624 | tf_op jit(solution)/shard_map/all_gather | solution.py:262
  929.6 22.1 multiply_convert_fusion.4
  951.7 14.0 fusion.109
  965.7 16.6 add_convert_fusion
  982.3 14.0 convolution_convert_fusion.1
  996.5 14.3 convolution_convert_fusion.2
  1010.8 14.1 convolution_convert_fusion.3
  1025.2 104.4 %reduce-scatter.18.cloned.1.call-done = bf16[256,2048]{1,0:T(8,128)(2,1)} async-done(((bf16[2048,2048]{1,0:T(8,128)(2,1)}), bf16[256,2048]{1,0:T(8,128)(2,1)}) %reduce-scatter.18.cloned.1.call-update) | async-done | bytes 1048592 | tf_op jit(solution)/shard_map/reduce_scatter | solution.py:273
  1136.0 9.0 fusion.111
  1146.3 5.8 fusion.65
  1158.2 25.4 all-to-all-done.2
  1184.7 5.9 multiply_reduce_fusion
  1201.8 5.8 multiply_convert_fusion.3
  1217.2 9.0 multiply_convert_fusion.2
  1235.9 6.0 multiply_convert_fusion.1
  1262.2 5.8 copy.224
  1267.9 107.4 %all_to_all.60 = bf16[3,1,2048,2,128]{4,3,0,1,2:T(2,128)(2,1)S(1)} all-to-all(bf16[3,1,2048,2,128]{4,3,0,1,2:T(2,128)(2,1)} %copy.224), channel_id=1, replica_groups=mesh['dp'=4,'seq'=8] {'seq'}, dimensions={2} | all-to-all | bytes 6291456 | tf_op jit(solution)/shard_map/all_to_all | solution.py:304
  1380.2 9.5 convolution_bitcast_fusion
  1389.6 17.6 copy.255
  1415.6 8.2 convolution_bitcast_fusion.1
  1423.8 17.6 copy.253
  1448.5 8.2 convolution_bitcast_fusion.2
  1456.7 17.6 copy.251
  1483.0 50.5 %all-reduce.8 = (f32[2048]{0:T(1024)S(1)}, f32[2048]{0:T(1024)S(1)}, f32[2048]{0:T(1024)S(1)}, f32[2048]{0:T(1024)S(1)}) all-reduce(f32[2048]{0:T(1024)S(1)} %get-tuple-element.140, f32[2048]{0:T(1024)S(1)} %get-tuple-element.138, f32[2048]{0:T(1024)S(1)} %copy-done.71, ...), channel_id=8, replica_groups=mesh['dp'=4,'seq'=8] {'dp','seq'}, use_global_device_ids=true, to_apply=%region_31.32.clone | all-reduce | flops 8192 | bytes 65536
  1535.8 5.9 convolution_add_fusion.5
  1541.8 5.9 convolution_add_fusion.4
  1547.7 6.8 fusion.49
  1554.4 106.9 %reduce-scatter.20.cloned.1.call-done = f32[64,2048]{1,0:T(8,128)} async-done(((f32[2048,2048]{1,0:T(8,128)}), f32[64,2048]{1,0:T(8,128)}) %reduce-scatter.20.cloned.1.call-update) | async-done | bytes 524304 | tf_op jit(solution)/shard_map/reduce_scatter | solution.py:327
  1661.3 359.8 %reduce-scatter.32.cloned.1.call-done = f32[64,2048]{1,0:T(8,128)} async-done(((f32[2048,2048]{1,0:T(8,128)}), f32[64,2048]{1,0:T(8,128)}) %reduce-scatter.32.cloned.1.call-update) | async-done | bytes 524304
  2021.2 360.1 %reduce-scatter.30.cloned.1.call-done = f32[64,2048]{1,0:T(8,128)} async-done(((f32[2048,2048]{1,0:T(8,128)}), f32[64,2048]{1,0:T(8,128)}) %reduce-scatter.30.cloned.1.call-update) | async-done | bytes 524304
  2381.3 360.2 %reduce-scatter.28.cloned.1.call-done = f32[64,2048]{1,0:T(8,128)} async-done(((f32[2048,2048]{1,0:T(8,128)}), f32[64,2048]{1,0:T(8,128)}) %reduce-scatter.28.cloned.1.call-update) | async-done | bytes 524304
  (378 shorter events, 178.9 us)
Async XLA Ops:
  7.2 84.2 %all-gather.14.cloned.1.call-start = ((), (), s32[]{:S(2)}) async-start(), calls=%async_computation.15 | async-start | bytes 8650752 | tf_op jit(solution)/shard_map/all_gather | solution.py:201
  7.9 162.5 %all-gather.12.cloned.1.call-start = ((), (), s32[]{:S(2)}) async-start(), calls=%async_computation.14 | async-start | bytes 8650752 | tf_op jit(solution)/shard_map/all_gather | solution.py:200
  8.7 240.8 %all-gather.10.cloned.1.call-start = ((), (), s32[]{:S(2)}) async-start(), calls=%async_computation.13 | async-start | bytes 8650752 | tf_op jit(solution)/shard_map/all_gather | solution.py:199
  9.4 423.5 %all-gather.16.cloned.1.call-start = ((), (), s32[]{:S(2)}) async-start(), calls=%async_computation.16 | async-start | bytes 8650752 | tf_op jit(solution)/shard_map/all_gather | solution.py:202
  58.7 118.1 %copy-start.66 = (f32[2048]{0:T(1024)}, f32[2048]{0:T(1024)S(1)}, u32[]{:S(2)}) copy-start(f32[2048]{0:T(1024)S(1)} %convert_element_type.216) | copy-start | bytes 24580
  58.7 197.2 %copy-start.64 = (f32[2048]{0:T(1024)}, f32[2048]{0:T(1024)S(1)}, u32[]{:S(2)}) copy-start(f32[2048]{0:T(1024)S(1)} %convert_element_type.212) | copy-start | bytes 24580
  59.5 198.4 %copy-start.46 = (f32[256,64]{1,0:T(8,128)}, f32[256,64]{1,0:T(8,128)S(1)}, u32[]{:S(2)}) copy-start(f32[256,64]{1,0:T(8,128)S(1)} %get-tuple-element.193) | copy-start | bytes 196612
  59.5 198.4 %copy-start.48 = (f32[256,64]{1,0:T(8,128)}, f32[256,64]{1,0:T(8,128)S(1)}, u32[]{:S(2)}) copy-start(f32[256,64]{1,0:T(8,128)S(1)} %get-tuple-element.194) | copy-start | bytes 196612
  97.4 73.0 %copy-start.11 = (bf16[1,256,2048]{2,1,0:T(8,128)(2,1)S(1)}, bf16[1,256,2048]{2,1,0:T(8,128)(2,1)}, u32[]{:S(2)}) copy-start(bf16[1,256,2048]{2,1,0:T(8,128)(2,1)} %param.15) | copy-start | bytes 3145732
  264.7 103.7 %all-to-all-start = ((bf16[3,1,256,16,128]{4,2,0,1,3:T(8,128)(2,1)}), bf16[3,1,256,16,128]{4,2,0,1,3:T(8,128)(2,1)}, u32[]{:S(2)}, u32[]{:S(2)}) async-start(bf16[3,1,256,16,128]{4,2,0,1,3:T(8,128)(2,1)} %copy.200), calls=%async_computation | async-start | bytes 6291456 | tf_op jit(solution)/shard_map/all_to_all | solution.py:233
  269.2 174.2 %all-gather.20.cloned.1.call-start = ((), (), s32[]{:S(2)}) async-start(), calls=%async_computation.18 | async-start | bytes 5242880 | tf_op jit(solution)/shard_map/all_gather | solution.py:209
  370.8 9.3 copy-start.56
  370.8 17.8 copy-start.52
  370.8 21.1 copy-start.54
  371.1 20.9 copy-start.14
  371.1 26.6 copy-start.9
  402.2 30.0 %all-to-all-start.1 = ((bf16[1,2048,2,128]{3,2,0,1:T(2,128)(2,1)}), bf16[1,2048,2,128]{3,2,0,1:T(2,128)(2,1)S(1)}, u32[]{:S(2)}, u32[]{:S(2)}) async-start(bf16[1,2048,2,128]{3,2,0,1:T(2,128)(2,1)} %copy.203), calls=%async_computation.1 | async-start | bytes 2097152 | tf_op jit(solution)/shard_map/all_to_all | solution.py:237
  406.0 159.2 %all-gather.18.cloned.1.call-start = ((), (), s32[]{:S(2)}) async-start(), calls=%async_computation.17 | async-start | bytes 9437184 | tf_op jit(solution)/shard_map/all_gather | solution.py:244
  406.1 33.7 %copy-start.68 = (f32[2048]{0:T(1024)}, f32[2048]{0:T(1024)S(1)}, u32[]{:S(2)}) copy-start(f32[2048]{0:T(1024)S(1)} %convert_element_type.222) | copy-start | bytes 24580
  439.7 140.2 %copy-start.92 = (f32[256]{0:T(256)}, f32[256]{0:T(256)S(1)}, u32[]{:S(2)}) copy-start(f32[256]{0:T(256)S(1)} %get-tuple-element.200) | copy-start | bytes 3076
  441.8 157.6 %all-gather.22.cloned.1.call-start = ((), (), s32[]{:S(2)}) async-start(), calls=%async_computation.19 | async-start | bytes 5242880 | tf_op jit(solution)/shard_map/all_gather | solution.py:210
  442.6 193.0 %all-gather.24.cloned.1.call-start = ((), (), s32[]{:S(2)}) async-start(), calls=%async_computation.20 | async-start | bytes 5242880 | tf_op jit(solution)/shard_map/all_gather | solution.py:211
  443.3 355.4 %reduce-scatter.16.cloned.1.call-start = ((), (), s32[]{:S(2)}) async-start(), calls=%async_computation.21 | async-start | bytes 9437184 | tf_op jit(solution)/shard_map/reduce_scatter | solution.py:250
  649.5 150.7 %copy-start.23 = (bf16[1,256,2048]{2,1,0:T(8,128)(2,1)S(1)}, bf16[1,256,2048]{2,1,0:T(8,128)(2,1)}, u32[]{:S(2)}) copy-start(bf16[1,256,2048]{2,1,0:T(8,128)(2,1)} %param.16) | copy-start | bytes 3145732
  649.5 280.0 %all-gather.26.cloned.1.call-start = ((), (), s32[]{:S(2)}) async-start(), calls=%async_computation.22 | async-start | bytes 9437184 | tf_op jit(solution)/shard_map/all_gather | solution.py:262
  805.5 324.2 %reduce-scatter.18.cloned.1.call-start = ((), (), s32[]{:S(2)}) async-start(), calls=%async_computation.23 | async-start | bytes 9437184 | tf_op jit(solution)/shard_map/reduce_scatter | solution.py:273
  929.6 22.1 copy-start.98
  982.3 492.1 %reduce-scatter.26.cloned.1.call-start = ((), (), s32[]{:S(2)}) async-start(), calls=%async_computation.27 | async-start | bytes 5242880 | tf_op jit(solution)/shard_map/reduce_scatter | solution.py:286
  996.4 481.0 %reduce-scatter.24.cloned.1.call-start = ((), (), s32[]{:S(2)}) async-start(), calls=%async_computation.26 | async-start | bytes 5242880 | tf_op jit(solution)/shard_map/reduce_scatter | solution.py:283
  1010.8 469.4 %reduce-scatter.22.cloned.1.call-start = ((), (), s32[]{:S(2)}) async-start(), calls=%async_computation.25 | async-start | bytes 5242880 | tf_op jit(solution)/shard_map/reduce_scatter | solution.py:280
  1024.9 104.7 %copy-start.8 = (f32[256,2048]{1,0:T(8,128)S(1)}, f32[256,2048]{1,0:T(8,128)}, u32[]{:S(2)}) copy-start(f32[256,2048]{1,0:T(8,128)} %copy-done.7) | copy-start | bytes 6291460
  1024.9 104.7 %copy-start.69 = (f32[2048]{0:T(1024)S(1)}, f32[2048]{0:T(1024)}, u32[]{:S(2)}) copy-start(f32[2048]{0:T(1024)} %copy-done.68) | copy-start | bytes 24580
  1024.9 104.7 %copy-start.93 = (f32[256]{0:T(256)S(1)}, f32[256]{0:T(256)}, u32[]{:S(2)}) copy-start(f32[256]{0:T(256)} %copy-done.92) | copy-start | bytes 3076
  1024.9 107.8 %copy-start.12 = (bf16[1,256,2048]{2,1,0:T(8,128)(2,1)S(1)}, bf16[1,256,2048]{2,1,0:T(8,128)(2,1)}, u32[]{:S(2)}) copy-start(bf16[1,256,2048]{2,1,0:T(8,128)(2,1)} %param.15) | copy-start | bytes 3145732
  1024.9 107.8 %copy-start.97 = (f32[256]{0:T(256)S(1)}, f32[256]{0:T(256)}, u32[]{:S(2)}) copy-start(f32[256]{0:T(256)} %get-tuple-element.199) | copy-start | bytes 3076
  1024.9 636.4 %reduce-scatter.20.cloned.1.call-start = ((), (), s32[]{:S(2)}) async-start(), calls=%async_computation.24 | async-start | bytes 17301504 | tf_op jit(solution)/shard_map/reduce_scatter | solution.py:327
  1152.3 32.3 %copy-start.10 = (bf16[1,1,8,256,2,128]{5,3,2,4,1,0:T(8,128)(2,1)S(1)}, bf16[1,1,8,256,2,128]{5,3,2,4,1,0:T(8,128)(2,1)}, u32[]{:S(2)}) copy-start(bf16[1,1,8,256,2,128]{5,3,2,4,1,0:T(8,128)(2,1)} %copy-done.9) | copy-start | bytes 3145732
  1153.6 30.1 %all-to-all-start.2 = ((bf16[1,256,16,128]{3,1,0,2:T(8,128)(2,1)}), bf16[1,256,16,128]{3,1,0,2:T(8,128)(2,1)S(1)}, u32[]{:S(2)}, u32[]{:S(2)}) async-start(bf16[1,256,16,128]{3,1,0,2:T(8,128)(2,1)} %copy.206), calls=%async_computation.4 | async-start | bytes 2097152 | tf_op jit(solution)/shard_map/all_to_all | solution.py:302
  1157.6 863.6 %reduce-scatter.32.cloned.1.call-start = ((), (), s32[]{:S(2)}) async-start(), calls=%async_computation.30 | async-start | bytes 17301504
  1201.8 11.2 slice-start.6
  1201.8 11.2 slice-start.7
  1217.2 13.8 slice-start.4
  1217.2 13.8 slice-start.5
  1407.3 974.1 %reduce-scatter.30.cloned.1.call-start = ((), (), s32[]{:S(2)}) async-start(), calls=%async_computation.29 | async-start | bytes 17301504
  1441.4 1300.1 %reduce-scatter.28.cloned.1.call-start = ((), (), s32[]{:S(2)}) async-start(), calls=%async_computation.28 | async-start | bytes 17301504
  1474.3 61.5 %copy-start.25 = (bf16[1,256,2048]{2,1,0:T(8,128)(2,1)S(1)}, bf16[1,256,2048]{2,1,0:T(8,128)(2,1)}, u32[]{:S(2)}) copy-start(bf16[1,256,2048]{2,1,0:T(8,128)(2,1)} %param.16) | copy-start | bytes 3145732
  1474.3 61.5 %copy-start.31 = (bf16[256,2048]{1,0:T(8,128)(2,1)S(1)}, bf16[256,2048]{1,0:T(8,128)(2,1)}, u32[]{:S(2)}) copy-start(bf16[256,2048]{1,0:T(8,128)(2,1)} %copy-done.30) | copy-start | bytes 3145732
  1474.3 61.5 %copy-start.37 = (bf16[256,2048]{1,0:T(8,128)(2,1)S(1)}, bf16[256,2048]{1,0:T(8,128)(2,1)}, u32[]{:S(2)}) copy-start(bf16[256,2048]{1,0:T(8,128)(2,1)} %reduce-scatter.18.cloned.1.call-done) | copy-start | bytes 3145732
  (82 other events, 291.6 us)
Sparse Core Ops, SparseCore 0:
  11.0 80.3 all-gather.13
  94.4 76.0 all-gather.11
  173.4 75.9 all-gather.9
  252.3 124.2 all-gather.15
  377.9 33.7 all-gather.19
  441.9 123.2 all-gather.17
  566.8 32.6 all-gather.21
  601.0 34.4 all-gather.23
  649.6 149.0 reduce-scatter.15
  805.6 123.9 all-gather.25
  982.4 147.1 reduce-scatter.17
  1132.0 43.5 reduce-scatter.25
  1178.3 44.5 reduce-scatter.23
  1225.2 44.5 reduce-scatter.21
  1272.6 388.7 reduce-scatter.19
  1664.2 356.9 reduce-scatter.31
  2024.0 357.2 reduce-scatter.29
  2384.1 357.3 reduce-scatter.27
where the time goes:
time: 2760 us; the launch traced here: 2750 us
  waiting for transfers between devices  2050 us (74%)
  matrix products  290 us (11%)
  blocking collectives  200 us (7%)
  local copies, waits for them, and re-layouts  102 us (4%)
  other arithmetic  76.6 us (3%)
    unnamed x21, waiting for transfers between devices  1080 us
    reduce_scatter x1, waiting for transfers between devices, per_device(): lax.psum_scatter(times_plain(lax.slice_in_dim(hidden, 0, count * lax.axis...  149 us
    all_gather x1, waiting for transfers between devices, per_device(): lax.all_gather(grad_mlp_pre.astype(jnp.bfloat16), 'seq', axis=0, tiled=True)  124 us
    all_gather x1, waiting for transfers between devices, per_device(): middle_rows = lax.all_gather(middle_low, 'seq', axis=0, tiled=True)  122 us
    all_to_all x1, blocking collectives, per_device(): lax.all_to_all(as_sent(grad_stack), 'seq', split_axis=2, concat_axis=3, t...  107 us
    reduce_scatter x1, waiting for transfers between devices, per_device(): lax.psum_scatter(part_output, ('dp', 'seq'), scatter_dimension=0, tiled=T...  107 us
    reduce_scatter x1, waiting for transfers between devices, per_device(): lax.psum_scatter((times_trans(gate_rows, gate_cols) + times_trans(up_rows...  104 us
    all_to_all x1, waiting for transfers between devices, per_device(): lax.all_to_all(packed, 'seq', split_axis=3, concat_axis=2, tiled=True)  93.6 us
  transfers between devices with their start and end apart: 21, of which 16 were waited for; matrix products, arithmetic and copies ran while one was open for 14% of the time, Pallas kernels for 0%

commit v1 on v0

v1 whole, which is shorter than its diff:
```python
import jax
import jax.numpy as jnp
from jax import lax
from jax.sharding import PartitionSpec as P

HEAD = 128
RING = 4
LEVELS = 4
EPSILON = 1e-06
ROPE_BASE = 500000.0
LOW = jnp.bfloat16
FULL = jnp.float32


def dot(left, right):
    return jnp.dot(left, right, preferred_element_type=FULL)


def dot_nt(left, right):
    return lax.dot_general(left, right, (((1,), (1,)), ((), ())), preferred_element_type=FULL)


def dot_tn(left, right):
    return lax.dot_general(left, right, (((0,), (0,)), ((), ())), preferred_element_type=FULL)


def swap(val, axis, mask):
    size = lax.axis_size(axis)
    return lax.ppermute(val, axis, [(i, i ^ mask) for i in range(size)])


def swap_all(val, mask):
    size = lax.axis_size("dp") * lax.axis_size("seq")
    return lax.ppermute(val, ("dp", "seq"), [(i, i ^ mask) for i in range(size)])


def bits_of(size):
    return [1 << i for i in range(size.bit_length() - 1)]


def sum_over(val, axis, size):
    for bit in bits_of(size):
        val = val + swap(val, axis, bit)
    return val


class Ring:
    def __init__(self, cycles):
        self.size = len(cycles[0])
        self.forth = [(c[i], c[(i + 1) % self.size]) for c in cycles for i in range(self.size)]
        self.back = [(b, a) for a, b in self.forth]
        total = self.size * len(cycles)
        owners = [[0] * self.size for _ in range(total)]
        for c in cycles:
            for i, dev in enumerate(c):
                for off in range(self.size):
                    owners[dev][off] = c[(i + off) % self.size]
        self.owners = owners

    def owner(self, offset):
        table = jnp.array([row[offset % self.size] for row in self.owners], jnp.int32)
        return lax.dynamic_index_in_dim(table, lax.axis_index("seq"), 0, False)

    def right(self, val):
        return lax.ppermute(val, "seq", self.forth)

    def left(self, val):
        return lax.ppermute(val, "seq", self.back)

    def gather(self, own):
        half = self.size // 2
        chunks = {0: own}
        r = l = own
        for k in range(1, half):
            r, l = self.right(r), self.left(l)
            chunks[-k], chunks[k] = r, l
        mid = own.shape[0] // 2
        chunks[half] = jnp.concatenate([self.right(r[:mid]), self.left(l[mid:])], axis=0)
        return chunks

    def scatter(self, part):
        half = self.size // 2
        far = part(half).astype(LOW)
        mid = far.shape[0] // 2
        r, l = self.right(far[:mid]), self.left(far[mid:])
        zero = jnp.zeros((), LOW)
        r = lax.pad(r, zero, ((0, mid, 0), (0, 0, 0)))
        l = lax.pad(l, zero, ((mid, 0, 0), (0, 0, 0)))
        for k in range(half - 1, 0, -1):
            a = part(k) + r.astype(FULL)
            b = part(-k) + l.astype(FULL)
            r, l = self.right(a.astype(LOW)), self.left(b.astype(LOW))
        return part(0) + r.astype(FULL) + l.astype(FULL)


def row_cycle(size):
    if size % LEVELS or size == LEVELS:
        return list(range(size))
    cols = size // LEVELS
    walk = [(0, 0)]
    for z in range(LEVELS):
        span = list(range(1, cols))
        walk += [(z, x) for x in (span if z % 2 == 0 else span[::-1])]
    walk += [(z, 0) for z in range(LEVELS - 1, 0, -1)]
    return [z * cols + x for z, x in walk]


def block_cycles(size):
    order = [0, 1, 3, 2] if size // LEVELS == 2 else [0, 1, 2, 3]
    return [[base + i for i in order] for base in range(0, size, RING)]


def data_bits(size):
    return [b for b in bits_of(size) if b != 1] + [1]


def copies_over_data(shard, size):
    copies = [(0, shard)]
    for bit in data_bits(size):
        copies = copies + [(mask ^ bit, swap(val, "dp", bit)) for mask, val in copies]
    return copies


def gather_over_data(shard, axis):
    size = lax.axis_size("dp")
    me = lax.axis_index("dp")
    shape = list(shard.shape)
    shape[axis] *= size
    whole = jnp.zeros(shape, shard.dtype)
    for mask, val in copies_over_data(shard, size):
        start = [0] * len(shape)
        start[axis] = (me ^ mask) * shard.shape[axis]
        whole = lax.dynamic_update_slice(whole, val, start)
    return whole


def scatter_over_data(whole):
    size = lax.axis_size("dp")
    me = lax.axis_index("dp")
    rest = whole.shape[1:]
    order = data_bits(size)[::-1]
    whole = whole.reshape((2,) * len(bits_of(size)) + rest)
    left = sorted(bits_of(size), reverse=True)
    for step, bit in enumerate(order):
        dim = left.index(bit)
        left.remove(bit)
        mine = (me // bit) % 2
        kept = lax.dynamic_index_in_dim(whole, mine, dim, False)
        sent = lax.dynamic_index_in_dim(whole, 1 - mine, dim, False)
        got = swap(sent, "dp", bit)
        whole = kept.astype(FULL) + got.astype(FULL)
        if step < len(order) - 1:
            whole = whole.astype(LOW)
    return whole


def gather_gains(gains):
    total = lax.axis_size("dp") * lax.axis_size("seq")
    me = lax.axis_index("dp") * lax.axis_size("seq") + lax.axis_index("seq")
    val = gains[None]
    for bit in bits_of(total):
        got = swap_all(val, bit)
        upper = (me // bit) % 2 == 1
        val = jnp.concatenate([jnp.where(upper, got, val), jnp.where(upper, val, got)], axis=0)
    return jnp.moveaxis(val, 0, 1).reshape(gains.shape[0], -1)


def gather_output_weights(w_output, row_ring):
    data, seq = lax.axis_size("dp"), lax.axis_size("seq")
    me = lax.axis_index("dp")
    rows, width = w_output.shape
    tall = data // 2
    stack = w_output[None]
    for bit in data_bits(data)[:-1]:
        got = swap(stack, "dp", bit)
        upper = (me // bit) % 2 == 1
        stack = jnp.concatenate([jnp.where(upper, got, stack), jnp.where(upper, stack, got)], axis=0)
    chunks = row_ring.gather(stack.reshape(tall * rows, width))
    whole = jnp.zeros((tall, 2, seq, rows, width), w_output.dtype)
    for offset, chunk in chunks.items():
        owner = row_ring.owner(offset)
        other = swap(chunk, "dp", 1)
        for core, val in ((me % 2, chunk), (1 - me % 2, other)):
            val = val.reshape(tall, 1, 1, rows, width)
            whole = lax.dynamic_update_slice(whole, val, (0, core, owner, 0, 0))
    return whole.reshape(data * seq * rows, width)


def scatter_output_grad(part, row_ring):
    data, seq = lax.axis_size("dp"), lax.axis_size("seq")
    me = lax.axis_index("dp")
    tall = data // 2
    width = part.shape[1]
    rows = part.shape[0] // (data * seq)
    part = part.astype(LOW).reshape(tall, 2, seq, rows, width)
    kept = lax.dynamic_index_in_dim(part, me % 2, 1, False)
    sent = lax.dynamic_index_in_dim(part, 1 - me % 2, 1, False)
    kept = (kept.astype(FULL) + swap(sent, "dp", 1).astype(FULL)).astype(LOW)

    def block(offset):
        one = lax.dynamic_index_in_dim(kept, row_ring.owner(offset), 1, False)
        return one.reshape(tall * rows, width).astype(FULL)

    val = row_ring.scatter(block).reshape(tall, rows, width)
    for bit in data_bits(data)[:-1][::-1]:
        upper = (me // bit) % 2
        val = val.reshape(2, val.shape[0] // 2, rows, width)
        kept = lax.dynamic_index_in_dim(val, upper, 0, False)
        sent = lax.dynamic_index_in_dim(val, 1 - upper, 0, False)
        val = kept + swap(sent, "dp", bit)
    return val.reshape(rows, width)


def rms_scale(vals):
    return lax.rsqrt(jnp.mean(vals * vals, axis=-1, keepdims=True) + EPSILON)


def norm_back(grad_out, pre, scale, gain):
    weighted = grad_out * gain
    inner = jnp.mean(weighted * pre, axis=-1, keepdims=True)
    grad_pre = scale * weighted - pre * (scale * scale * scale) * inner
    grad_gain = jnp.sum(grad_out * pre * scale, axis=0)
    return (grad_pre, grad_gain)


def rope_tables(positions, width):
    half = width // 2
    freq = ROPE_BASE ** (-2.0 * jnp.arange(half, dtype=FULL) / width)
    angle = positions.astype(FULL)[:, None] * freq[None, :]
    return (jnp.cos(angle)[:, None, :], jnp.sin(angle)[:, None, :])


def rotate(vals, cosine, sine):
    half = vals.shape[-1] // 2
    first = vals[..., :half]
    second = vals[..., half:]
    return jnp.concatenate(
        [first * cosine - second * sine, second * cosine + first * sine], axis=-1
    )


def layout(lengths, placement, row_len):
    stored, docs = lengths.shape
    row = lax.dynamic_index_in_dim(placement, lax.axis_index("dp"), 0, False)
    doc_lens = jnp.sum(
        jnp.where(jnp.arange(stored, dtype=jnp.int32)[:, None] == row, lengths, 0), axis=0
    )
    upto = jnp.arange(docs, dtype=jnp.int32)
    doc_ends = jnp.sum(jnp.where(upto[None, :] <= upto[:, None], doc_lens[None, :], 0), axis=1)
    at = jnp.arange(row_len, dtype=jnp.int32)
    passed = at[:, None] >= doc_ends[None, :]
    doc_ids = jnp.sum(passed.astype(jnp.int32), axis=1)
    doc_first = jnp.max(jnp.where(passed, doc_ends[None, :], 0), axis=1)
    return doc_ids, at - doc_first


def scores_of(queries, keys, doc_ids):
    at = jnp.arange(doc_ids.shape[0], dtype=jnp.int32)
    scores = jnp.einsum("qhd,khd->hqk", queries, keys, preferred_element_type=FULL) * HEAD**-0.5
    allowed = (doc_ids[:, None] == doc_ids[None, :]) & (at[None, :] <= at[:, None])
    return jnp.where(allowed[None], scores, -1e30)


def attend_forward(queries, keys, vals, doc_ids):
    scores = scores_of(queries, keys, doc_ids)
    top = jnp.max(scores, axis=-1, keepdims=True)
    expo = jnp.exp(scores - top)
    total = jnp.sum(expo, axis=-1, keepdims=True)
    probs = (expo / total).astype(LOW)
    out = jnp.einsum("hqk,khd->qhd", probs, vals, preferred_element_type=FULL)
    return out.astype(LOW), top + jnp.log(total)


def attend_backward(queries, keys, vals, doc_ids, sums, grads):
    probs = jnp.exp(scores_of(queries, keys, doc_ids) - sums)
    grad_probs = jnp.einsum("qhd,khd->hqk", grads, vals, preferred_element_type=FULL)
    inner = jnp.sum(probs * grad_probs, axis=-1, keepdims=True)
    grad_scores = (probs * (grad_probs - inner)).astype(LOW)
    scale = HEAD**-0.5
    grad_q = jnp.einsum("hqk,khd->qhd", grad_scores, keys, preferred_element_type=FULL) * scale
    grad_k = jnp.einsum("hqk,qhd->khd", grad_scores, queries, preferred_element_type=FULL) * scale
    grad_v = jnp.einsum("hqk,qhd->khd", probs.astype(LOW), grads, preferred_element_type=FULL)
    return grad_q.astype(LOW), grad_k.astype(LOW), grad_v.astype(LOW)


def per_device(
    tokens,
    cotangent,
    lengths,
    placement,
    w_query,
    w_key,
    w_value,
    w_output,
    query_gain,
    key_gain,
    attn_gain,
    w_gate,
    w_up,
    w_down,
    mlp_gain,
):
    data, seq = lax.axis_size("dp"), lax.axis_size("seq")
    seq_at = lax.axis_index("seq")
    _, count, width = tokens.shape
    row_len = count * seq
    own = width // seq
    heads = own // HEAD
    row_ring = Ring([row_cycle(seq)])
    ring = Ring(block_cycles(seq))
    sets = seq // RING
    inputs = tokens.reshape(count, width)
    doc_ids, positions = layout(lengths, placement, row_len)
    cosine, sine = rope_tables(positions, HEAD)

    packed = jnp.stack([w_query, w_key, w_value], axis=1).reshape(-1, 3, seq, own)
    packed = jnp.moveaxis(packed, 2, 0).reshape(seq, -1, 3 * own)
    packed = lax.all_to_all(packed, "seq", split_axis=0, concat_axis=0, tiled=True)
    w_heads = gather_over_data(packed.reshape(-1, 3 * own), 0)

    row_chunks = row_ring.gather(inputs)
    pre = jnp.zeros((row_len, 3 * own), FULL)
    row_tokens = jnp.zeros((row_len, width), LOW)
    for offset, chunk in row_chunks.items():
        start = row_ring.owner(offset) * count
        pre = lax.dynamic_update_slice(pre, dot(chunk, w_heads), (start, 0))
        row_tokens = lax.dynamic_update_slice(row_tokens, chunk, (start, 0))

    gains = gather_gains(jnp.stack([query_gain, key_gain, attn_gain, mlp_gain]))
    gains = gains.astype(FULL)
    gain_attn, gain_mlp = gains[2], gains[3]
    gains_own = lax.dynamic_slice(gains, (0, seq_at * own), (2, own))

    w_in = jnp.concatenate([w_gate, w_up], axis=1)
    gate_up, downs = [], []
    for k in range(sets):
        part_in = w_in if k == 0 else swap(w_in, "seq", RING * k)
        part_down = w_down if k == 0 else swap(w_down, "seq", RING * k)
        gate_up.append(gather_over_data(part_in, 0))
        downs.append(gather_over_data(part_down, 1))
    hid = w_gate.shape[1]
    w_out = gather_output_weights(w_output, row_ring)

    query_pre, key_pre, value_pre = pre[:, :own], pre[:, own : 2 * own], pre[:, 2 * own :]
    squares = jnp.stack([jnp.sum(query_pre * query_pre, axis=1), jnp.sum(key_pre * key_pre, axis=1)])
    scales = lax.rsqrt(sum_over(squares, "seq", seq) / width + EPSILON)
    query_scale, key_scale = scales[0][:, None], scales[1][:, None]

    def split(val):
        return val.reshape(row_len, heads, HEAD)

    query_rot = rotate(split(query_pre * query_scale * gains_own[0]), cosine, sine).astype(LOW)
    key_rot = rotate(split(key_pre * key_scale * gains_own[1]), cosine, sine).astype(LOW)
    values = split(value_pre.astype(LOW))
    attn_heads, log_sums = attend_forward(query_rot, key_rot, values, doc_ids)
    attn_tokens = lax.all_to_all(
        attn_heads.reshape(seq, count, own), "seq", split_axis=0, concat_axis=0, tiled=True
    )
    attn_tokens = jnp.moveaxis(attn_tokens, 0, 1).reshape(count, width)
    attn_pre = dot(attn_tokens, w_out)
    attn_scale = rms_scale(attn_pre)
    middle = inputs.astype(FULL) + attn_pre * attn_scale * gain_attn
    middle_low = middle.astype(LOW)

    mids = ring.gather(middle_low)
    saved = {}

    def mlp_part(offset):
        offset = offset if offset in mids else -offset
        total = 0.0
        for k in range(sets):
            both = dot(mids[offset], gate_up[k])
            gate, up = both[:, :hid], both[:, hid:]
            hidden = (gate * jax.nn.sigmoid(gate) * up).astype(LOW)
            saved[offset, k] = gate, up, hidden
            total = total + dot(hidden, downs[k])
        return total

    mlp_pre = ring.scatter(mlp_part)
    mlp_scale = rms_scale(mlp_pre)
    layer_out = (middle + mlp_pre * mlp_scale * gain_mlp).astype(LOW).reshape(tokens.shape)
    grad_final = cotangent.reshape(count, width).astype(FULL)
    grad_mlp_pre, grad_gain_mlp = norm_back(grad_final, mlp_pre, mlp_scale, gain_mlp)
    grads = ring.gather(grad_mlp_pre.astype(LOW))
    grad_both = {}

    def middle_part(offset):
        offset = offset if offset in mids else -offset
        total = 0.0
        for k in range(sets):
            gate, up, hidden = saved[offset, k]
            grad_hidden = dot_nt(grads[offset], downs[k])
            sig = jax.nn.sigmoid(gate)
            grad_gate = grad_hidden * up * sig * (1.0 + gate * (1.0 - sig))
            grad_up = grad_hidden * gate * sig
            both = jnp.concatenate([grad_gate.astype(LOW), grad_up.astype(LOW)], axis=1)
            grad_both[offset, k] = both
            total = total + dot_nt(both, gate_up[k])
        return total

    grad_middle = grad_final + ring.scatter(middle_part)
    order = list(mids)
    mid_rows = jnp.concatenate([mids[o] for o in order])
    grad_rows = jnp.concatenate([grads[o] for o in order])
    grad_in, grad_down = 0.0, 0.0
    for k in reversed(range(sets)):
        hidden = jnp.concatenate([saved[o, k][2] for o in order])
        both = jnp.concatenate([grad_both[o, k] for o in order])
        part_down = dot_tn(hidden, grad_rows).astype(LOW).reshape(hid, data, width // data)
        part_down = scatter_over_data(jnp.moveaxis(part_down, 1, 0))
        part_in = dot_tn(mid_rows, both).astype(LOW).reshape(data, width // data, 2 * hid)
        part_in = scatter_over_data(part_in)
        if k:
            part_down = swap(part_down.astype(LOW), "seq", RING * k).astype(FULL)
            part_in = swap(part_in.astype(LOW), "seq", RING * k).astype(FULL)
        grad_down = grad_down + part_down
        grad_in = grad_in + part_in
    grad_gate, grad_up = grad_in[:, :hid], grad_in[:, hid:]

    grad_attn_pre, grad_gain_attn = norm_back(grad_middle, attn_pre, attn_scale, gain_attn)
    grad_attn_low = grad_attn_pre.astype(LOW)
    grad_heads = dot_nt(grad_attn_low, w_out).astype(LOW).reshape(count, seq, own)
    grad_heads = lax.all_to_all(
        jnp.moveaxis(grad_heads, 1, 0), "seq", split_axis=0, concat_axis=0, tiled=True
    )
    grad_heads = split(grad_heads)
    grad_output = scatter_output_grad(dot_tn(attn_tokens, grad_attn_low), row_ring)
    grad_q, grad_k, grad_v = attend_backward(
        query_rot, key_rot, values, doc_ids, log_sums, grad_heads
    )
    grad_q = rotate(grad_q.astype(FULL), cosine, -sine).reshape(row_len, own)
    grad_k = rotate(grad_k.astype(FULL), cosine, -sine).reshape(row_len, own)
    weighted_q, weighted_k = grad_q * gains_own[0], grad_k * gains_own[1]
    inner = jnp.stack(
        [jnp.sum(weighted_q * query_pre, axis=1), jnp.sum(weighted_k * key_pre, axis=1)]
    )
    inner = sum_over(inner, "seq", seq) / width
    grad_qp = query_scale * weighted_q - query_pre * (query_scale**3) * inner[0][:, None]
    grad_kp = key_scale * weighted_k - key_pre * (key_scale**3) * inner[1][:, None]
    grad_pre = jnp.concatenate(
        [grad_qp.astype(LOW), grad_kp.astype(LOW), grad_v.reshape(row_len, own)], axis=1
    )

    def token_part(offset):
        start = row_ring.owner(offset) * count
        return dot_nt(lax.dynamic_slice_in_dim(grad_pre, start, count, 0), w_heads)

    grad_tokens = (grad_middle + row_ring.scatter(token_part)).astype(LOW).reshape(tokens.shape)
    part = dot_tn(row_tokens, grad_pre).astype(LOW).reshape(data, width // data, 3 * own)
    part = scatter_over_data(part).astype(LOW)
    part = lax.all_to_all(
        part.reshape(seq, -1, 3 * own), "seq", split_axis=0, concat_axis=0, tiled=True
    ).astype(FULL)
    part = jnp.moveaxis(part.reshape(seq, -1, 3, own), 0, 2).reshape(-1, 3, width)

    placed = lax.dynamic_update_slice(
        jnp.zeros((2, width), FULL),
        jnp.stack(
            [
                jnp.sum(grad_q * query_pre * query_scale, axis=0),
                jnp.sum(grad_k * key_pre * key_scale, axis=0),
            ]
        ),
        (0, seq_at * own),
    )
    placed = jnp.concatenate([placed, grad_gain_attn[None], grad_gain_mlp[None]])
    for bit in bits_of(data * seq):
        placed = placed + swap_all(placed, bit)
    share = width // (data * seq)
    start = (lax.axis_index("dp") * seq + seq_at) * share
    gain_grads = lax.dynamic_slice(placed, (0, start), (4, share))

    return (
        layer_out,
        grad_tokens,
        part[:, 0],
        part[:, 1],
        part[:, 2],
        grad_output,
        gain_grads[0],
        gain_grads[1],
        gain_grads[2],
        grad_gate,
        grad_up,
        grad_down,
        gain_grads[3],
    )


def solution(mesh):
    rows = P("dp", "seq", None)
    both = P(("dp", "seq"), None)
    flat = P(("dp", "seq"))
    return jax.shard_map(
        per_device,
        mesh=mesh,
        in_specs=(rows, rows, P(), P())
        + (both,) * 4
        + (flat,) * 3
        + (P("dp", "seq"), P("dp", "seq"), P("seq", "dp"), flat),
        out_specs=(rows, rows)
        + (both,) * 4
        + (flat,) * 3
        + (P("dp", "seq"), P("dp", "seq"), P("seq", "dp"), flat),
        check_vma=False,
    )
```

time: 2760 us -> 1380 us (0.50)
  waiting for transfers between devices: 2050 us -> 467 us
  starting transfers between devices: 14.4 us -> 231 us
  blocking collectives: 200 us -> 0 us
  local copies, waits for them, and re-layouts: 102 us -> 179 us
  other arithmetic: 76.6 us -> 130 us
  matrix products: 290 us -> 338 us
    unnamed x21 -> x0, waiting for transfers between devices: 1080 us -> none
    all_gather x9 -> x0, waiting for transfers between devices: 459 us -> none  [the longest x1 124 us: per_device(): lax.all_gather(grad_mlp_pre.astype(jnp.bfloat16), 'seq', axis=0, tiled=True)]
    ppermute x0 -> x104, waiting for transfers between devices: none -> 456 us  [the longest x46 197 us: swap(): return lax.ppermute(val, axis, [(i, i ^ mask) for i in range(size)])]
    reduce_scatter x6 -> x0, waiting for transfers between devices: 360 us -> none  [the longest x1 149 us: per_device(): lax.psum_scatter(times_plain(lax.slice_in_dim(hidden, 0, count * lax.axis...]
    ppermute x0 -> x104, starting transfers between devices: none -> 210 us  [the longest x24 137 us: left(): return lax.ppermute(val, 'seq', self.back)]
    all_to_all x3 -> x4, waiting for transfers between devices: 145 us -> 11.2 us  [the longest x1 11.2 us: per_device(): lax.all_to_all(attn_heads.reshape(seq, count, own), 'seq', split_axis=0,...]
    all_to_all x1 -> x0, blocking collectives: 107 us -> none  [per_device(): lax.all_to_all(as_sent(grad_stack), 'seq', split_axis=2, concat_axis=3, t...]
    unnamed x2 -> x0, blocking collectives: 93 us -> none
  transfers between devices with their start and end apart: 21 -> 108, of which waited for: 16 -> 40; matrix products, arithmetic and copies ran while one was open for 14% -> 42% of each run, Pallas kernels for 0% -> 0%
where the time goes in v1:
time: 1380 us; the launch traced here: 1370 us
  waiting for transfers between devices  467 us (34%)
  matrix products  338 us (24%)
  starting transfers between devices  231 us (17%)
  local copies, waits for them, and re-layouts  179 us (13%)
  other arithmetic  130 us (9%)
  between operations  22 us (2%)
    ppermute x46, waiting for transfers between devices, swap(): return lax.ppermute(val, axis, [(i, i ^ mask) for i in range(size)])  197 us
    ppermute x24, waiting for transfers between devices, left(): return lax.ppermute(val, 'seq', self.back)  139 us
    ppermute x24, starting transfers between devices, left(): return lax.ppermute(val, 'seq', self.back)  137 us
    dot_general x25, matrix products, dot_nt(): lax.dot_general(left, right, (((1,), (1,)), ((), ())), preferred_element_...  116 us
    ppermute x24, waiting for transfers between devices, right(): return lax.ppermute(val, 'seq', self.forth)  101 us
    dot_general x25, matrix products, dot(): return jnp.dot(left, right, preferred_element_type=FULL)  84.2 us
    dot_general x6, matrix products, dot_tn(): lax.dot_general(left, right, (((0,), (0,)), ((), ())), preferred_element_...  47.7 us
    dynamic_update_slice x20, local copies, waits for them, and re-layouts, gather_over_data(): whole = lax.dynamic_update_slice(whole, val, start)  38.6 us
  transfers between devices with their start and end apart: 108, of which 40 were waited for; matrix products, arithmetic and copies ran while one was open for 42% of the time, Pallas kernels for 0%

profile of v1, /device:TPU:0, one launch (start us, length us, event | category | flops | bytes accessed | tf_op | source)
XLA Modules:
  0.0 1366.6 jit_solution(8028098420273791125)
XLA Ops:
  36.7 15.5 %collective-permute-done.15 = bf16[2,4,64]{2,1,0:T(4,128)(2,1)S(1)} collective-permute-done((bf16[2,4,64]{2,1,0:T(4,128)(2,1)S(1)}, bf16[2,4,64]{2,1,0:T(4,128)(2,1)S(1)}, u32[]{:S(2)}, u32[]{:S(2)}) %collective-permute-start.15) | collective-permute-done | bytes 1056 | tf_op jit(solution)/shard_map/ppermute | solution.py:34
  114.9 43.0 %collective-permute-start.27 = (bf16[128,2048]{1,0:T(8,128)(2,1)}, bf16[128,2048]{1,0:T(8,128)(2,1)}, u32[]{:S(2)}, u32[]{:S(2)}) collective-permute-start(bf16[128,2048]{1,0:T(8,128)(2,1)} %collective-permute-done.23), channel_id=1, source_target_pairs={{1,0},{3,1},{5,3},{7,5},{6,7},{4,6},{2,4},{0,2},{9,8},{11,9},{13,1... | collective-permute-start | bytes 1572872 | tf_op jit(solution)/shard_map/ppermute | solution.py:68
  177.4 7.9 collective-permute-done.31
  193.8 6.1 collective-permute-done.3
  201.0 10.4 collective-permute-done.29
  218.3 32.7 %collective-permute-done.34 = bf16[64,2048]{1,0:T(8,128)(2,1)S(1)} collective-permute-done((bf16[64,2048]{1,0:T(8,128)(2,1)S(1)}, bf16[64,2048]{1,0:T(8,128)(2,1)S(1)}, u32[]{:S(2)}, u32[]{:S(2)}) %collective-permute-start.34) | collective-permute-done | bytes 262176 | tf_op jit(solution)/shard_map/ppermute | solution.py:68
  263.2 14.2 %collective-permute-done.47 = bf16[1024,512]{1,0:T(8,128)(2,1)} collective-permute-done((bf16[1024,512]{1,0:T(8,128)(2,1)}, bf16[1024,512]{1,0:T(8,128)(2,1)}, u32[]{:S(2)}, u32[]{:S(2)}) %collective-permute-start.47) | collective-permute-done | bytes 1048608 | tf_op jit(solution)/shard_map/ppermute | solution.py:29
  279.7 46.3 %collective-permute-start.6 = (bf16[256,2048]{1,0:T(8,128)(2,1)}, bf16[256,2048]{1,0:T(8,128)(2,1)S(1)}, u32[]{:S(2)}, u32[]{:S(2)}) collective-permute-start(bf16[256,2048]{1,0:T(8,128)(2,1)} %collective-permute-done.4), channel_id=1, source_target_pairs={{1,0},{3,1},{5,3},{7,5},{6,7},{4,6},{2,4},{0,2},{9,8},{11,9},{13,1... | collective-permute-start | bytes 3145736 | tf_op jit(solution)/shard_map/ppermute | solution.py:68
  333.8 15.7 %collective-permute-done.6 = bf16[256,2048]{1,0:T(8,128)(2,1)S(1)} collective-permute-done((bf16[256,2048]{1,0:T(8,128)(2,1)}, bf16[256,2048]{1,0:T(8,128)(2,1)S(1)}, u32[]{:S(2)}, u32[]{:S(2)}) %collective-permute-start.6) | collective-permute-done | bytes 1048608 | tf_op jit(solution)/shard_map/ppermute | solution.py:68
  364.4 12.7 collective-permute-done.8
  381.9 10.1 collective-permute-done.9
  422.7 6.0 subtract_convert_fusion.4
  428.7 17.9 %fusion.199 = (f32[2,2048]{1,0:T(2,128)S(1)}, f32[2,2048,2048]{1,2,0:T(8,128)}) fusion(bf16[2048,2,64]{2,0,1:T(8,128)(2,1)} %get-tuple-element.76, bf16[2048,2,64]{2,0,1:T(8,128)(2,1)} %get-tuple-element.77, bf16[2048,2,64]{2,0,1:T(8,128)(2,1)} %get-tuple-element.36, bf16[2048,2,64]{2,0,1:T(8,128)(2,1)} %get-tuple-element.35, pred[2048,2048]{0,1:T(8,128)(4,1)} %fusion.5), kind=kOutput, calls=%fused_computation.466 | convolution fusion | flops 2176839680 | bytes 39862272 | tf_op jit(solution)/shard_map/qhd,khd->hqk/dot_general | solution.py:259
  446.6 13.1 fusion
  459.8 13.9 %fusion.77 = bf16[2,128,2048]{2,1,0:T(8,128)(2,1)S(1)} fusion(bf16[2048,2,128]{0,2,1:T(8,128)(2,1)S(1)} %bitcast.427, f32[2,2048,2048]{1,2,0:T(8,128)} %get-tuple-element.130, f32[2,2048]{1,0:T(2,128)S(1)} %fusion, f32[2,2048]{1,0:T(2,128)S(1)} %get-tuple-element.129), kind=kOutput, calls=%fused_computation.123 | convolution fusion | flops 2173173760 | bytes 35684352 | tf_op jit(solution)/shard_map/hqk,khd->qhd/dot_general | solution.py:270
  494.4 11.2 all-to-all-done.1
  505.5 6.2 multiply_reduce_fusion.6
  532.4 7.4 collective-permute-done.51
  575.2 6.2 fusion.206
  592.2 9.0 collective-permute-done.56
  614.2 12.6 collective-permute-done.57
  649.3 7.5 fusion.116
  656.8 9.9 collective-permute-done.59
  672.9 7.5 fusion.123
  684.2 7.5 fusion.137
  741.4 13.1 convolution_convert_fusion
  754.6 10.8 fusion.74
  765.7 6.9 fusion.75
  774.5 15.2 %convolution_convert_fusion.1 = bf16[2048,2048]{1,0:T(8,128)(2,1)} fusion(bf16[1024,2048]{1,0:T(8,128)(2,1)} %copy-done.77, bf16[256,1024]{1,0:T(8,128)(2,1)} %get-tuple-element.63, bf16[256,1024]{1,0:T(8,128)(2,1)S(1)} %copy-done.115, bf16[256,1024]{1,0:T(8,128)(2,1)} %get-tuple-element.59, bf16[256,1024]{1,0:T(8,128)(2,1)} %get-tuple-element.58, ...), kind=kOutput, calls=%fused_computation.20 | convolution fusion | flops 8627683328 | bytes 16777216 | tf_op jit(solution)/shard_map/dot_general | solution.py:24
  798.6 7.4 multiply_reduce_fusion.1
  839.0 11.9 collective-permute-done.100
  853.3 14.7 %fusion.68 = bf16[2,128,2048]{2,1,0:T(8,128)(2,1)} fusion(bf16[2048,2,128]{0,2,1:T(8,128)(2,1)S(1)} %reshape.491, f32[2,2048,2048]{1,2,0:T(8,128)} %get-tuple-element.130, f32[2,2048]{1,0:T(2,128)S(1)} %copy-done.64), kind=kOutput, calls=%fused_computation.114 | convolution fusion | flops 2164785152 | bytes 35667968 | tf_op jit(solution)/shard_map/hqk,qhd->khd/dot_general | solution.py:282
  868.0 21.9 %multiply_reduce_fusion = (f32[2,2048]{1,0:T(2,128)S(1)}, f32[2,2048,2048]{1,2,0:T(8,128)}) fusion(f32[2,2048,2048]{1,2,0:T(8,128)} %get-tuple-element.130, f32[2,2048]{1,0:T(2,128)S(1)} %copy-done.64, bf16[2048,2,128]{0,2,1:T(8,128)(2,1)S(1)} %reshape.491, bf16[2048,2,128]{0,2,1:T(8,128)(2,1)S(1)} %bitcast.428), kind=kOutput, calls=%fused_computation.1 | convolution fusion | flops 2172645376 | bytes 69238784 | tf_op jit(solution)/shard_map/qhd,khd->hqk/dot_general | solution.py:276
  889.9 28.6 %multiply_convert_fusion = bf16[2,2048,2048]{1,2,0:T(8,128)(2,1)} fusion(f32[2,2048,2048]{1,2,0:T(8,128)} %get-tuple-element.137, f32[2,2048,2048]{1,2,0:T(8,128)} %get-tuple-element.130, f32[2,2048]{1,0:T(2,128)S(1)} %get-tuple-element.136, f32[2,2048]{1,0:T(2,128)S(1)} %copy-done.64), kind=kLoop, calls=%fused_computation | loop fusion | flops 33554432 | bytes 83918848 | tf_op jit(solution)/shard_map/convert_element_type | solution.py:278
  918.5 9.9 fusion.67
  928.4 11.6 fusion.58
  978.6 7.1 convolution_convert_fusion.5
  994.9 8.1 collective-permute-done.73
  1023.6 28.0 %collective-permute-done.101 = bf16[1024,512]{1,0:T(8,128)(2,1)} collective-permute-done((bf16[1024,512]{1,0:T(8,128)(2,1)}, bf16[1024,512]{1,0:T(8,128)(2,1)}, u32[]{:S(2)}, u32[]{:S(2)}) %collective-permute-start.101) | collective-permute-done | bytes 1048608 | tf_op jit(solution)/shard_map/ppermute | solution.py:29
  1065.4 11.8 collective-permute-start.75
  1089.4 69.2 %collective-permute-done.78 = bf16[512,768]{1,0:T(8,128)(2,1)S(1)} collective-permute-done((bf16[512,768]{1,0:T(8,128)(2,1)S(1)}, bf16[512,768]{1,0:T(8,128)(2,1)S(1)}, u32[]{:S(2)}, u32[]{:S(2)}) %collective-permute-start.78) | collective-permute-done | bytes 786464 | tf_op jit(solution)/shard_map/ppermute | solution.py:29
  1161.2 6.5 all-to-all-start.3
  1171.0 14.7 %collective-permute-done.80 = bf16[64,2048]{1,0:T(8,128)(2,1)S(1)} collective-permute-done((bf16[64,2048]{1,0:T(8,128)(2,1)S(1)}, bf16[64,2048]{1,0:T(8,128)(2,1)S(1)}, u32[]{:S(2)}, u32[]{:S(2)}) %collective-permute-start.80) | collective-permute-done | bytes 262176 | tf_op jit(solution)/shard_map/ppermute | solution.py:65
  1185.7 7.4 collective-permute-start.85
  1210.5 27.7 %collective-permute-done.86 = bf16[128,2048]{1,0:T(8,128)(2,1)S(1)} collective-permute-done((bf16[128,2048]{1,0:T(8,128)(2,1)S(1)}, bf16[128,2048]{1,0:T(8,128)(2,1)S(1)}, u32[]{:S(2)}, u32[]{:S(2)}) %collective-permute-start.86) | collective-permute-done | bytes 524320 | tf_op jit(solution)/shard_map/ppermute | solution.py:68
  1247.1 6.0 collective-permute-done.87
  1253.1 23.2 %collective-permute-done.83 = bf16[128,2048]{1,0:T(8,128)(2,1)S(1)} collective-permute-done((bf16[128,2048]{1,0:T(8,128)(2,1)S(1)}, bf16[128,2048]{1,0:T(8,128)(2,1)S(1)}, u32[]{:S(2)}, u32[]{:S(2)}) %collective-permute-start.83) | collective-permute-done | bytes 524320 | tf_op jit(solution)/shard_map/ppermute | solution.py:65
  1292.1 68.4 %collective-permute-done.96 = bf16[512,2048]{1,0:T(8,128)(2,1)} collective-permute-done((bf16[512,2048]{1,0:T(8,128)(2,1)}, bf16[512,2048]{1,0:T(8,128)(2,1)}, u32[]{:S(2)}, u32[]{:S(2)}) %collective-permute-start.96) | collective-permute-done | bytes 2097184 | tf_op jit(solution)/shard_map/ppermute | solution.py:29
  (731 shorter events, 564.2 us)
Async XLA Ops:
  1.4 33.7 %collective-permute-start.14 = (bf16[1,4,64]{2,1,0:T(4,128)(2,1)S(1)}, bf16[1,4,64]{2,1,0:T(4,128)(2,1)S(1)}, u32[]{:S(2)}, u32[]{:S(2)}) collective-permute-start(bf16[1,4,64]{2,1,0:T(4,128)(2,1)S(1)} %maximum_bitcast_fusion.1), channel_id=1, source_target_pairs={{0,1},{1,0},{2,3},{3,2},{4,5},{5,4},{6,7},{7,6},{8,9},{9,8},{10,11... | collective-permute-start | bytes 1544 | tf_op jit(solution)/shard_map/ppermute | solution.py:34
  12.1 177.4 %all-to-all-start = ((bf16[8,64,768]{2,1,0:T(8,128)(2,1)}), bf16[8,64,768]{2,1,0:T(8,128)(2,1)}, u32[]{:S(2)}, u32[]{:S(2)}) async-start(bf16[8,64,768]{2,1,0:T(8,128)(2,1)} %reshape.465), calls=%async_computation | async-start | bytes 1572864 | tf_op jit(solution)/shard_map/all_to_all | solution.py:318
  17.0 47.2 %collective-permute-start.19 = (bf16[1,64,2048]{2,1,0:T(8,128)(2,1)S(1)}, bf16[1,64,2048]{2,1,0:T(8,128)(2,1)}, u32[]{:S(2)}, u32[]{:S(2)}) collective-permute-start(bf16[1,64,2048]{2,1,0:T(8,128)(2,1)S(1)} %bitcast.448), channel_id=1, source_target_pairs={{0,16},{8,24},{16,0},{24,8},{1,17},{9,25},{17,1},{25,9},{2,18},{10... | collective-permute-start | bytes 786440 | tf_op jit(solution)/shard_map/ppermute | solution.py:29
  18.6 139.3 %collective-permute-start.4 = (bf16[256,2048]{1,0:T(8,128)(2,1)}, bf16[256,2048]{1,0:T(8,128)(2,1)}, u32[]{:S(2)}, u32[]{:S(2)}) collective-permute-start(bf16[256,2048]{1,0:T(8,128)(2,1)} %bitcast), channel_id=1, source_target_pairs={{1,0},{3,1},{5,3},{7,5},{6,7},{4,6},{2,4},{0,2},{9,8},{11,9},{13,1... | collective-permute-start | bytes 3145736 | tf_op jit(solution)/shard_map/ppermute | solution.py:68
  20.6 139.3 %collective-permute-start.39 = (bf16[1024,512]{1,0:T(8,128)(2,1)}, bf16[1024,512]{1,0:T(8,128)(2,1)}, u32[]{:S(2)}, u32[]{:S(2)}) collective-permute-start(bf16[1024,512]{1,0:T(8,128)(2,1)} %param.60), channel_id=1, source_target_pairs={{0,16},{8,24},{16,0},{24,8},{1,17},{9,25},{17,1},{25,9},{2,18},{10... | collective-permute-start | bytes 3145736 | tf_op jit(solution)/shard_map/ppermute | solution.py:29
  62.7 34.1 %collective-permute-start.18 = (bf16[16,4,64]{2,1,0:T(4,128)(2,1)S(1)}, bf16[16,4,64]{2,1,0:T(4,128)(2,1)S(1)}, u32[]{:S(2)}, u32[]{:S(2)}) collective-permute-start(bf16[16,4,64]{2,1,0:T(4,128)(2,1)S(1)} %pad_maximum_fusion.12), channel_id=1, source_target_pairs={{0,16},{1,17},{2,18},{3,19},{4,20},{5,21},{6,22},{7,23},{8,24},{9,... | collective-permute-start | bytes 24584 | tf_op jit(solution)/shard_map/ppermute | solution.py:34
  96.8 63.6 %collective-permute-start.46 = (bf16[1024,512]{1,0:T(8,128)(2,1)}, bf16[1024,512]{1,0:T(8,128)(2,1)}, u32[]{:S(2)}, u32[]{:S(2)}) collective-permute-start(bf16[1024,512]{1,0:T(8,128)(2,1)} %param.60), channel_id=1, source_target_pairs={{0,4},{1,5},{2,6},{3,7},{4,0},{5,1},{6,2},{7,3},{8,12},{9,13},{10,... | collective-permute-start | bytes 3145736 | tf_op jit(solution)/shard_map/ppermute | solution.py:29
  100.2 67.4 %collective-permute-start.40 = (bf16[1024,512]{1,0:T(8,128)(2,1)}, bf16[1024,512]{1,0:T(8,128)(2,1)}, u32[]{:S(2)}, u32[]{:S(2)}) collective-permute-start(bf16[1024,512]{1,0:T(8,128)(2,1)} %param.60), channel_id=1, source_target_pairs={{0,8},{8,0},{16,24},{24,16},{1,9},{9,1},{17,25},{25,17},{2,10},{10... | collective-permute-start | bytes 3145736 | tf_op jit(solution)/shard_map/ppermute | solution.py:29
  114.9 55.7 %collective-permute-start.27 = (bf16[128,2048]{1,0:T(8,128)(2,1)}, bf16[128,2048]{1,0:T(8,128)(2,1)}, u32[]{:S(2)}, u32[]{:S(2)}) collective-permute-start(bf16[128,2048]{1,0:T(8,128)(2,1)} %collective-permute-done.23), channel_id=1, source_target_pairs={{1,0},{3,1},{5,3},{7,5},{6,7},{4,6},{2,4},{0,2},{9,8},{11,9},{13,1... | collective-permute-start | bytes 1572872 | tf_op jit(solution)/shard_map/ppermute | solution.py:68
  167.6 86.7 %collective-permute-start.36 = (bf16[512,2048]{1,0:T(8,128)(2,1)S(1)}, bf16[512,2048]{1,0:T(8,128)(2,1)}, u32[]{:S(2)}, u32[]{:S(2)}) collective-permute-start(bf16[512,2048]{1,0:T(8,128)(2,1)S(1)} %constant_dynamic-update-slice_fusion.4), channel_id=1, source_target_pairs={{0,16},{8,24},{16,0},{24,8},{1,17},{9,25},{17,1},{25,9},{2,18},{10... | collective-permute-start | bytes 6291464 | tf_op jit(solution)/shard_map/ppermute | solution.py:29
  170.6 87.4 %collective-permute-start.37 = (bf16[512,2048]{1,0:T(8,128)(2,1)S(1)}, bf16[512,2048]{1,0:T(8,128)(2,1)}, u32[]{:S(2)}, u32[]{:S(2)}) collective-permute-start(bf16[512,2048]{1,0:T(8,128)(2,1)S(1)} %constant_dynamic-update-slice_fusion.4), channel_id=1, source_target_pairs={{0,8},{8,0},{16,24},{24,16},{1,9},{9,1},{17,25},{25,17},{2,10},{10... | collective-permute-start | bytes 6291464 | tf_op jit(solution)/shard_map/ppermute | solution.py:29
  199.9 128.6 %collective-permute-start.42 = (bf16[512,2048]{1,0:T(8,128)(2,1)S(1)}, bf16[512,2048]{1,0:T(8,128)(2,1)}, u32[]{:S(2)}, u32[]{:S(2)}) collective-permute-start(bf16[512,2048]{1,0:T(8,128)(2,1)S(1)} %constant_dynamic-update-slice_fusion.4), channel_id=1, source_target_pairs={{0,4},{1,5},{2,6},{3,7},{4,0},{5,1},{6,2},{7,3},{8,12},{9,13},{10,... | collective-permute-start | bytes 6291464 | tf_op jit(solution)/shard_map/ppermute | solution.py:29
  211.4 39.6 %collective-permute-start.34 = (bf16[64,2048]{1,0:T(8,128)(2,1)S(1)}, bf16[64,2048]{1,0:T(8,128)(2,1)S(1)}, u32[]{:S(2)}, u32[]{:S(2)}) collective-permute-start(bf16[64,2048]{1,0:T(8,128)(2,1)S(1)} %slice.265), channel_id=1, source_target_pairs={{1,0},{3,1},{5,3},{7,5},{6,7},{4,6},{2,4},{0,2},{9,8},{11,9},{13,1... | collective-permute-start | bytes 786440 | tf_op jit(solution)/shard_map/ppermute | solution.py:68
  214.3 40.0 %collective-permute-start.33 = (bf16[64,2048]{1,0:T(8,128)(2,1)S(1)}, bf16[64,2048]{1,0:T(8,128)(2,1)S(1)}, u32[]{:S(2)}, u32[]{:S(2)}) collective-permute-start(bf16[64,2048]{1,0:T(8,128)(2,1)S(1)} %slice.264), channel_id=1, source_target_pairs={{0,1},{1,3},{3,5},{5,7},{7,6},{6,4},{4,2},{2,0},{8,9},{9,11},{11,1... | collective-permute-start | bytes 786440 | tf_op jit(solution)/shard_map/ppermute | solution.py:65
  254.3 71.7 %collective-permute-start.48 = (bf16[1024,512]{1,0:T(8,128)(2,1)}, bf16[1024,512]{1,0:T(8,128)(2,1)S(1)}, u32[]{:S(2)}, u32[]{:S(2)}) collective-permute-start(bf16[1024,512]{1,0:T(8,128)(2,1)} %collective-permute-done.46), channel_id=1, source_target_pairs={{0,8},{8,0},{16,24},{24,16},{1,9},{9,1},{17,25},{25,17},{2,10},{10... | collective-permute-start | bytes 3145736 | tf_op jit(solution)/shard_map/ppermute | solution.py:29
  258.0 69.2 %collective-permute-start = (bf16[512,768]{1,0:T(8,128)(2,1)}, bf16[512,768]{1,0:T(8,128)(2,1)S(1)}, u32[]{:S(2)}, u32[]{:S(2)}) collective-permute-start(bf16[512,768]{1,0:T(8,128)(2,1)} %bitcast.2), channel_id=1, source_target_pairs={{0,16},{8,24},{16,0},{24,8},{1,17},{9,25},{17,1},{25,9},{2,18},{10... | collective-permute-start | bytes 2359304 | tf_op jit(solution)/shard_map/ppermute | solution.py:29
  277.4 54.4 %collective-permute-start.1 = (bf16[512,768]{1,0:T(8,128)(2,1)}, bf16[512,768]{1,0:T(8,128)(2,1)S(1)}, u32[]{:S(2)}, u32[]{:S(2)}) collective-permute-start(bf16[512,768]{1,0:T(8,128)(2,1)} %bitcast.2), channel_id=1, source_target_pairs={{0,8},{8,0},{16,24},{24,16},{1,9},{9,1},{17,25},{25,17},{2,10},{10... | collective-permute-start | bytes 2359304 | tf_op jit(solution)/shard_map/ppermute | solution.py:29
  279.7 69.7 %collective-permute-start.6 = (bf16[256,2048]{1,0:T(8,128)(2,1)}, bf16[256,2048]{1,0:T(8,128)(2,1)S(1)}, u32[]{:S(2)}, u32[]{:S(2)}) collective-permute-start(bf16[256,2048]{1,0:T(8,128)(2,1)} %collective-permute-done.4), channel_id=1, source_target_pairs={{1,0},{3,1},{5,3},{7,5},{6,7},{4,6},{2,4},{0,2},{9,8},{11,9},{13,1... | collective-permute-start | bytes 3145736 | tf_op jit(solution)/shard_map/ppermute | solution.py:68
  331.8 67.5 %collective-permute-start.32 = (bf16[128,2048]{1,0:T(8,128)(2,1)}, bf16[128,2048]{1,0:T(8,128)(2,1)S(1)}, u32[]{:S(2)}, u32[]{:S(2)}) collective-permute-start(bf16[128,2048]{1,0:T(8,128)(2,1)} %collective-permute-done.31), channel_id=1, source_target_pairs={{0,8},{8,0},{16,24},{24,16},{1,9},{9,1},{17,25},{25,17},{2,10},{10... | collective-permute-start | bytes 1572872 | tf_op jit(solution)/shard_map/ppermute | solution.py:29
  332.2 147.0 %collective-permute-start.35 = (bf16[128,2048]{1,0:T(8,128)(2,1)}, bf16[128,2048]{1,0:T(8,128)(2,1)}, u32[]{:S(2)}, u32[]{:S(2)}) collective-permute-start(bf16[128,2048]{1,0:T(8,128)(2,1)} %constant_dynamic-update-slice_fusion.2), channel_id=1, source_target_pairs={{0,8},{8,0},{16,24},{24,16},{1,9},{9,1},{17,25},{25,17},{2,10},{10... | collective-permute-start | bytes 1572872 | tf_op jit(solution)/shard_map/ppermute | solution.py:29
  349.4 131.6 %collective-permute-start.49 = (bf16[1024,512]{1,0:T(8,128)(2,1)}, bf16[1024,512]{1,0:T(8,128)(2,1)}, u32[]{:S(2)}, u32[]{:S(2)}) collective-permute-start(bf16[1024,512]{1,0:T(8,128)(2,1)} %collective-permute-done.47), channel_id=1, source_target_pairs={{0,8},{8,0},{16,24},{24,16},{1,9},{9,1},{17,25},{25,17},{2,10},{10... | collective-permute-start | bytes 3145736 | tf_op jit(solution)/shard_map/ppermute | solution.py:29
  392.1 99.1 %collective-permute-start.44 = (bf16[512,2048]{1,0:T(8,128)(2,1)}, bf16[512,2048]{1,0:T(8,128)(2,1)}, u32[]{:S(2)}, u32[]{:S(2)}) collective-permute-start(bf16[512,2048]{1,0:T(8,128)(2,1)} %collective-permute-done.42), channel_id=1, source_target_pairs={{0,8},{8,0},{16,24},{24,16},{1,9},{9,1},{17,25},{25,17},{2,10},{10... | collective-permute-start | bytes 6291464 | tf_op jit(solution)/shard_map/ppermute | solution.py:29
  397.9 86.7 %collective-permute-start.43 = (bf16[512,2048]{1,0:T(8,128)(2,1)}, bf16[512,2048]{1,0:T(8,128)(2,1)}, u32[]{:S(2)}, u32[]{:S(2)}) collective-permute-start(bf16[512,2048]{1,0:T(8,128)(2,1)} %collective-permute-done.42), channel_id=1, source_target_pairs={{0,16},{8,24},{16,0},{24,8},{1,17},{9,25},{17,1},{25,9},{2,18},{10... | collective-permute-start | bytes 6291464 | tf_op jit(solution)/shard_map/ppermute | solution.py:29
  407.9 80.2 %collective-permute-start.38 = (bf16[512,2048]{1,0:T(8,128)(2,1)}, bf16[512,2048]{1,0:T(8,128)(2,1)}, u32[]{:S(2)}, u32[]{:S(2)}) collective-permute-start(bf16[512,2048]{1,0:T(8,128)(2,1)} %collective-permute-done.36), channel_id=1, source_target_pairs={{0,8},{8,0},{16,24},{24,16},{1,9},{9,1},{17,25},{25,17},{2,10},{10... | collective-permute-start | bytes 6291464 | tf_op jit(solution)/shard_map/ppermute | solution.py:29
  484.6 45.9 %collective-permute-start.45 = (bf16[512,2048]{1,0:T(8,128)(2,1)}, bf16[512,2048]{1,0:T(8,128)(2,1)}, u32[]{:S(2)}, u32[]{:S(2)}) collective-permute-start(bf16[512,2048]{1,0:T(8,128)(2,1)} %collective-permute-done.43), channel_id=1, source_target_pairs={{0,8},{8,0},{16,24},{24,16},{1,9},{9,1},{17,25},{25,17},{2,10},{10... | collective-permute-start | bytes 6291464 | tf_op jit(solution)/shard_map/ppermute | solution.py:29
  666.7 36.8 %collective-permute-start.60 = (bf16[128,2048]{1,0:T(8,128)(2,1)S(1)}, bf16[128,2048]{1,0:T(8,128)(2,1)S(1)}, u32[]{:S(2)}, u32[]{:S(2)}) collective-permute-start(bf16[128,2048]{1,0:T(8,128)(2,1)S(1)} %slice.288), channel_id=1, source_target_pairs={{0,1},{1,3},{3,2},{2,0},{4,5},{5,7},{7,6},{6,4},{8,9},{9,11},{11,1... | collective-permute-start | bytes 1572872 | tf_op jit(solution)/shard_map/ppermute | solution.py:65
  667.1 37.3 %collective-permute-start.61 = (bf16[128,2048]{1,0:T(8,128)(2,1)S(1)}, bf16[128,2048]{1,0:T(8,128)(2,1)S(1)}, u32[]{:S(2)}, u32[]{:S(2)}) collective-permute-start(bf16[128,2048]{1,0:T(8,128)(2,1)S(1)} %slice.289), channel_id=1, source_target_pairs={{1,0},{3,1},{2,3},{0,2},{5,4},{7,5},{6,7},{4,6},{9,8},{11,9},{10,1... | collective-permute-start | bytes 1572872 | tf_op jit(solution)/shard_map/ppermute | solution.py:68
  740.9 81.9 %collective-permute-start.99 = (bf16[2,1024,512]{2,1,0:T(8,128)(2,1)}, bf16[2,1024,512]{2,1,0:T(8,128)(2,1)}, u32[]{:S(2)}, u32[]{:S(2)}) collective-permute-start(bf16[2,1024,512]{2,1,0:T(8,128)(2,1)} %dynamic-slice_bitcast_fusion.4), channel_id=1, source_target_pairs={{0,8},{8,0},{16,24},{24,16},{1,9},{9,1},{17,25},{25,17},{2,10},{10... | collective-permute-start | bytes 6291464 | tf_op jit(solution)/shard_map/ppermute | solution.py:29
  740.9 93.5 %collective-permute-start.102 = (bf16[2,1024,512]{2,1,0:T(8,128)(2,1)}, bf16[2,1024,512]{2,1,0:T(8,128)(2,1)}, u32[]{:S(2)}, u32[]{:S(2)}) collective-permute-start(bf16[2,1024,512]{2,1,0:T(8,128)(2,1)} %dynamic-slice_bitcast_fusion.3), channel_id=1, source_target_pairs={{0,8},{8,0},{16,24},{24,16},{1,9},{9,1},{17,25},{25,17},{2,10},{10... | collective-permute-start | bytes 6291464 | tf_op jit(solution)/shard_map/ppermute | solution.py:29
  794.5 212.8 %collective-permute-start.94 = (bf16[2,512,2048]{2,1,0:T(8,128)(2,1)}, bf16[2,512,2048]{2,1,0:T(8,128)(2,1)}, u32[]{:S(2)}, u32[]{:S(2)}) collective-permute-start(bf16[2,512,2048]{2,1,0:T(8,128)(2,1)} %dynamic-slice_bitcast_fusion.1), channel_id=1, source_target_pairs={{0,8},{8,0},{16,24},{24,16},{1,9},{9,1},{17,25},{25,17},{2,10},{10... | collective-permute-start | bytes 12582920 | tf_op jit(solution)/shard_map/ppermute | solution.py:29
  797.0 215.9 %collective-permute-start.97 = (bf16[2,512,2048]{2,1,0:T(8,128)(2,1)}, bf16[2,512,2048]{2,1,0:T(8,128)(2,1)}, u32[]{:S(2)}, u32[]{:S(2)}) collective-permute-start(bf16[2,512,2048]{2,1,0:T(8,128)(2,1)} %dynamic-slice_bitcast_fusion), channel_id=1, source_target_pairs={{0,8},{8,0},{16,24},{24,16},{1,9},{9,1},{17,25},{25,17},{2,10},{10... | collective-permute-start | bytes 12582920 | tf_op jit(solution)/shard_map/ppermute | solution.py:29
  817.2 35.0 %all-to-all-start.2 = ((bf16[8,256,256]{1,2,0:T(8,128)(2,1)}), bf16[8,256,256]{1,2,0:T(8,128)(2,1)S(1)}, u32[]{:S(2)}, u32[]{:S(2)}) async-start(bf16[8,256,256]{1,2,0:T(8,128)(2,1)} %bitcast.66), calls=%async_computation.2 | async-start | bytes 2097152 | tf_op jit(solution)/shard_map/all_to_all | solution.py:423
  834.4 246.8 %collective-permute-start.79 = (bf16[2,8,64,2048]{3,2,1,0:T(8,128)(2,1)}, bf16[2,8,64,2048]{3,2,1,0:T(8,128)(2,1)}, u32[]{:S(2)}, u32[]{:S(2)}) collective-permute-start(bf16[2,8,64,2048]{3,2,1,0:T(8,128)(2,1)} %dynamic-slice_bitcast_fusion.2), channel_id=1, source_target_pairs={{0,8},{8,0},{16,24},{24,16},{1,9},{9,1},{17,25},{25,17},{2,10},{10... | collective-permute-start | bytes 12582920 | tf_op jit(solution)/shard_map/ppermute | solution.py:29
  1003.0 48.6 %collective-permute-start.101 = (bf16[1024,512]{1,0:T(8,128)(2,1)}, bf16[1024,512]{1,0:T(8,128)(2,1)}, u32[]{:S(2)}, u32[]{:S(2)}) collective-permute-start(bf16[1024,512]{1,0:T(8,128)(2,1)} %fusion.101), channel_id=1, source_target_pairs={{0,4},{1,5},{2,6},{3,7},{4,0},{5,1},{6,2},{7,3},{8,12},{9,13},{10,... | collective-permute-start | bytes 3145736 | tf_op jit(solution)/shard_map/ppermute | solution.py:29
  1007.3 73.0 %collective-permute-start.77 = (bf16[2,512,768]{2,1,0:T(8,128)(2,1)}, bf16[2,512,768]{2,1,0:T(8,128)(2,1)S(1)}, u32[]{:S(2)}, u32[]{:S(2)}) collective-permute-start(bf16[2,512,768]{2,1,0:T(8,128)(2,1)} %dynamic-slice_bitcast_fusion.7), channel_id=1, source_target_pairs={{0,8},{8,0},{16,24},{24,16},{1,9},{9,1},{17,25},{25,17},{2,10},{10... | collective-permute-start | bytes 4718600 | tf_op jit(solution)/shard_map/ppermute | solution.py:29
  1012.8 42.7 %collective-permute-start.74 = (bf16[256,2048]{1,0:T(8,128)(2,1)}, bf16[256,2048]{1,0:T(8,128)(2,1)}, u32[]{:S(2)}, u32[]{:S(2)}) collective-permute-start(bf16[256,2048]{1,0:T(8,128)(2,1)} %fusion.64), channel_id=1, source_target_pairs={{1,0},{3,1},{5,3},{7,5},{6,7},{4,6},{2,4},{0,2},{9,8},{11,9},{13,1... | collective-permute-start | bytes 3145736 | tf_op jit(solution)/shard_map/ppermute | solution.py:68
  1018.9 46.6 %collective-permute-start.70 = (bf16[256,2048]{1,0:T(8,128)(2,1)}, bf16[256,2048]{1,0:T(8,128)(2,1)S(1)}, u32[]{:S(2)}, u32[]{:S(2)}) collective-permute-start(bf16[256,2048]{1,0:T(8,128)(2,1)} %fusion.61), channel_id=1, source_target_pairs={{0,1},{1,3},{3,5},{5,7},{7,6},{6,4},{4,2},{2,0},{8,9},{9,11},{11,1... | collective-permute-start | bytes 3145736 | tf_op jit(solution)/shard_map/ppermute | solution.py:65
  1051.6 189.6 %collective-permute-start.95 = (bf16[512,2048]{1,0:T(8,128)(2,1)}, bf16[512,2048]{1,0:T(8,128)(2,1)}, u32[]{:S(2)}, u32[]{:S(2)}) collective-permute-start(bf16[512,2048]{1,0:T(8,128)(2,1)} %dynamic-slice_bitcast_fusion.6), channel_id=1, source_target_pairs={{0,16},{8,24},{16,0},{24,8},{1,17},{9,25},{17,1},{25,9},{2,18},{10... | collective-permute-start | bytes 6291464 | tf_op jit(solution)/shard_map/ppermute | solution.py:29
  1055.5 236.6 %collective-permute-start.98 = (bf16[512,2048]{1,0:T(8,128)(2,1)}, bf16[512,2048]{1,0:T(8,128)(2,1)}, u32[]{:S(2)}, u32[]{:S(2)}) collective-permute-start(bf16[512,2048]{1,0:T(8,128)(2,1)} %dynamic-slice_bitcast_fusion.5), channel_id=1, source_target_pairs={{0,16},{8,24},{16,0},{24,8},{1,17},{9,25},{17,1},{25,9},{2,18},{10... | collective-permute-start | bytes 6291464 | tf_op jit(solution)/shard_map/ppermute | solution.py:29
  1065.4 128.8 %collective-permute-start.75 = (bf16[256,2048]{1,0:T(8,128)(2,1)}, bf16[256,2048]{1,0:T(8,128)(2,1)}, u32[]{:S(2)}, u32[]{:S(2)}) collective-permute-start(bf16[256,2048]{1,0:T(8,128)(2,1)} %fusion.63), channel_id=1, source_target_pairs={{1,0},{3,1},{5,3},{7,5},{6,7},{4,6},{2,4},{0,2},{9,8},{11,9},{13,1... | collective-permute-start | bytes 3145736 | tf_op jit(solution)/shard_map/ppermute | solution.py:68
  1080.2 126.1 %collective-permute-start.71 = (bf16[256,2048]{1,0:T(8,128)(2,1)}, bf16[256,2048]{1,0:T(8,128)(2,1)}, u32[]{:S(2)}, u32[]{:S(2)}) collective-permute-start(bf16[256,2048]{1,0:T(8,128)(2,1)} %fusion.60), channel_id=1, source_target_pairs={{0,1},{1,3},{3,5},{5,7},{7,6},{6,4},{4,2},{2,0},{8,9},{9,11},{11,1... | collective-permute-start | bytes 3145736 | tf_op jit(solution)/shard_map/ppermute | solution.py:65
  1081.2 77.4 %collective-permute-start.78 = (bf16[512,768]{1,0:T(8,128)(2,1)S(1)}, bf16[512,768]{1,0:T(8,128)(2,1)S(1)}, u32[]{:S(2)}, u32[]{:S(2)}) collective-permute-start(bf16[512,768]{1,0:T(8,128)(2,1)S(1)} %dynamic-slice_bitcast_fusion.10), channel_id=1, source_target_pairs={{0,16},{8,24},{16,0},{24,8},{1,17},{9,25},{17,1},{25,9},{2,18},{10... | collective-permute-start | bytes 2359304 | tf_op jit(solution)/shard_map/ppermute | solution.py:29
  1161.2 121.0 %all-to-all-start.3 = ((bf16[8,64,768]{2,1,0:T(8,128)(2,1)}), bf16[8,64,768]{2,1,0:T(8,128)(2,1)}, u32[]{:S(2)}, u32[]{:S(2)}) async-start(bf16[8,64,768]{2,1,0:T(8,128)(2,1)} %bitcast.434), calls=%async_computation.3 | async-start | bytes 1572864 | tf_op jit(solution)/shard_map/all_to_all | solution.py:451
  1202.7 76.3 %collective-permute-start.76 = (bf16[256,2048]{1,0:T(8,128)(2,1)S(1)}, bf16[256,2048]{1,0:T(8,128)(2,1)S(1)}, u32[]{:S(2)}, u32[]{:S(2)}) collective-permute-start(bf16[256,2048]{1,0:T(8,128)(2,1)S(1)} %fusion.62), channel_id=1, source_target_pairs={{1,0},{3,1},{5,3},{7,5},{6,7},{4,6},{2,4},{0,2},{9,8},{11,9},{13,1... | collective-permute-start | bytes 3145736 | tf_op jit(solution)/shard_map/ppermute | solution.py:68
  1206.3 34.6 %collective-permute-start.82 = (bf16[128,2048]{1,0:T(8,128)(2,1)S(1)}, bf16[128,2048]{1,0:T(8,128)(2,1)S(1)}, u32[]{:S(2)}, u32[]{:S(2)}) collective-permute-start(bf16[128,2048]{1,0:T(8,128)(2,1)S(1)} %fusion.148), channel_id=1, source_target_pairs={{0,1},{1,3},{3,5},{5,7},{7,6},{6,4},{4,2},{2,0},{8,9},{9,11},{11,1... | collective-permute-start | bytes 1572872 | tf_op jit(solution)/shard_map/ppermute | solution.py:65
  1238.3 40.7 %collective-permute-start.72 = (bf16[256,2048]{1,0:T(8,128)(2,1)S(1)}, bf16[256,2048]{1,0:T(8,128)(2,1)S(1)}, u32[]{:S(2)}, u32[]{:S(2)}) collective-permute-start(bf16[256,2048]{1,0:T(8,128)(2,1)S(1)} %fusion.59), channel_id=1, source_target_pairs={{0,1},{1,3},{3,5},{5,7},{7,6},{6,4},{4,2},{2,0},{8,9},{9,11},{11,1... | collective-permute-start | bytes 3145736 | tf_op jit(solution)/shard_map/ppermute | solution.py:65
  1241.2 35.1 %collective-permute-start.83 = (bf16[128,2048]{1,0:T(8,128)(2,1)S(1)}, bf16[128,2048]{1,0:T(8,128)(2,1)S(1)}, u32[]{:S(2)}, u32[]{:S(2)}) collective-permute-start(bf16[128,2048]{1,0:T(8,128)(2,1)S(1)} %fusion.149), channel_id=1, source_target_pairs={{0,1},{1,3},{3,5},{5,7},{7,6},{6,4},{4,2},{2,0},{8,9},{9,11},{11,1... | collective-permute-start | bytes 1572872 | tf_op jit(solution)/shard_map/ppermute | solution.py:65
  1253.1 107.4 %collective-permute-start.96 = (bf16[512,2048]{1,0:T(8,128)(2,1)}, bf16[512,2048]{1,0:T(8,128)(2,1)}, u32[]{:S(2)}, u32[]{:S(2)}) collective-permute-start(bf16[512,2048]{1,0:T(8,128)(2,1)} %fusion.43), channel_id=1, source_target_pairs={{0,4},{1,5},{2,6},{3,7},{4,0},{5,1},{6,2},{7,3},{8,12},{9,13},{10,... | collective-permute-start | bytes 6291464 | tf_op jit(solution)/shard_map/ppermute | solution.py:29
  (198 other events, 4339.1 us)

commit v2 on v1

v2 whole, which is shorter than its diff:
```python
import math

import jax
import jax.numpy as jnp
from jax import lax
from jax.experimental import pallas as pl
from jax.experimental.pallas import tpu as pltpu
from jax.sharding import PartitionSpec as P

HEAD = 128
LEVELS = 4
EPSILON = 1e-06
ROPE_BASE = 500000.0
LOW = jnp.bfloat16
FULL = jnp.float32
NEG = -1e30
LOG2E = math.log2(math.e)
BLOCK = 512


def dot(left, right):
    return jnp.dot(left, right, preferred_element_type=FULL)


def dot_nt(left, right):
    return lax.dot_general(left, right, (((1,), (1,)), ((), ())), preferred_element_type=FULL)


def dot_tn(left, right):
    return lax.dot_general(left, right, (((0,), (0,)), ((), ())), preferred_element_type=FULL)


def swap(val, axis, mask):
    size = lax.axis_size(axis)
    return lax.ppermute(val, axis, [(i, i ^ mask) for i in range(size)])


def swap_all(val, mask):
    size = lax.axis_size("dp") * lax.axis_size("seq")
    return lax.ppermute(val, ("dp", "seq"), [(i, i ^ mask) for i in range(size)])


def after(vals, *first):
    return lax.optimization_barrier((vals, first))[0]


def bits_of(size):
    return [1 << i for i in range(size.bit_length() - 1)]


def sum_over(val, axis, size):
    for bit in bits_of(size):
        val = val + swap(val, axis, bit)
    return val


class Ring:
    def __init__(self, cycles):
        self.size = len(cycles[0])
        self.forth = [(c[i], c[(i + 1) % self.size]) for c in cycles for i in range(self.size)]
        self.back = [(b, a) for a, b in self.forth]
        total = self.size * len(cycles)
        owners = [[0] * self.size for _ in range(total)]
        for c in cycles:
            for i, dev in enumerate(c):
                for off in range(self.size):
                    owners[dev][off] = c[(i + off) % self.size]
        self.owners = owners

    def owner(self, offset):
        table = jnp.array([row[offset % self.size] for row in self.owners], jnp.int32)
        return lax.dynamic_index_in_dim(table, lax.axis_index("seq"), 0, False)

    def right(self, val):
        return lax.ppermute(val, "seq", self.forth)

    def left(self, val):
        return lax.ppermute(val, "seq", self.back)

    def gather(self, own, between=None):
        half = self.size // 2
        chunks = {0: own}
        r = l = own
        for k in range(1, half):
            beside = between(k) if between else ()
            r, l = self.right(r), self.left(l)
            chunks[-k], chunks[k] = r, l
            r, l = after((r, l), beside)
        mid = own.shape[0] // 2
        chunks[half] = jnp.concatenate([self.right(r[:mid]), self.left(l[mid:])], axis=0)
        return chunks

    def scatter(self, part):
        half = self.size // 2
        far = part(half).astype(LOW)
        mid = far.shape[0] // 2
        r, l = self.right(far[:mid]), self.left(far[mid:])
        zero = jnp.zeros((), LOW)
        r = lax.pad(r, zero, ((0, mid, 0), (0, 0, 0)))
        l = lax.pad(l, zero, ((mid, 0, 0), (0, 0, 0)))
        for k in range(half - 1, 0, -1):
            a = part(k) + r.astype(FULL)
            b = part(-k) + l.astype(FULL)
            r, l = self.right(a.astype(LOW)), self.left(b.astype(LOW))
        return part(0) + r.astype(FULL) + l.astype(FULL)


def row_cycle(size):
    if size % LEVELS or size == LEVELS:
        return list(range(size))
    cols = size // LEVELS
    walk = [(0, 0)]
    for z in range(LEVELS):
        span = list(range(1, cols))
        walk += [(z, x) for x in (span if z % 2 == 0 else span[::-1])]
    walk += [(z, 0) for z in range(LEVELS - 1, 0, -1)]
    return [z * cols + x for z, x in walk]


def data_bits(size):
    return [b for b in bits_of(size) if b != 1] + [1]


def swap_chips(shard, bits):
    copies = {0: shard}
    for bit in bits:
        copies |= {mask ^ bit: swap(val, "dp", bit) for mask, val in copies.items()}
    return copies


def swap_cores(copies):
    return copies | {mask ^ 1: swap(val, "dp", 1) for mask, val in copies.items()}


def swap_blocks(val):
    size = lax.axis_size("dp")
    me = lax.axis_index("dp")
    part = val.shape[1] // size
    blocks = [lax.dynamic_slice_in_dim(val, (me ^ m) * part, part, 1) for m in range(size)]
    return jnp.concatenate(blocks, axis=1)


def place_over_data(copies):
    me = lax.axis_index("dp")
    rows, cols = copies[0].shape
    whole = jnp.zeros((rows * len(copies), cols), copies[0].dtype)
    for mask, val in copies.items():
        whole = lax.dynamic_update_slice(whole, val, ((me ^ mask) * rows, 0))
    return whole


def pack(gates, ups):
    rows, cols = gates[0].shape
    whole = jnp.zeros((rows * len(gates), 2 * cols), LOW)
    for mask in gates:
        whole = lax.dynamic_update_slice(whole, gates[mask], (mask * rows, 0))
        whole = lax.dynamic_update_slice(whole, ups[mask], (mask * rows, cols))
    return whole


def scatter_over_data(blocks):
    order = data_bits(len(blocks))[::-1]
    blocks = dict(enumerate(blocks))
    for step, bit in enumerate(order):
        out = {}
        for m in [m for m in blocks if not m & bit]:
            total = blocks[m].astype(FULL) + swap(blocks[m ^ bit], "dp", bit).astype(FULL)
            out[m] = total if step == len(order) - 1 else total.astype(LOW)
        blocks = out
    return blocks[0]


def gain_step(val, bit):
    me = lax.axis_index("dp") * lax.axis_size("seq") + lax.axis_index("seq")
    got = swap_all(val, bit)
    upper = (me // bit) % 2 == 1
    return jnp.concatenate([jnp.where(upper, got, val), jnp.where(upper, val, got)], axis=0)


def stack_output_weights(w_output):
    me = lax.axis_index("dp")
    stack = w_output[None]
    for bit in data_bits(lax.axis_size("dp"))[:-1]:
        got = swap(stack, "dp", bit)
        upper = (me // bit) % 2 == 1
        stack = jnp.concatenate([jnp.where(upper, got, stack), jnp.where(upper, stack, got)], axis=0)
    return stack


def gather_output_weights(stack, row_ring):
    data, seq = lax.axis_size("dp"), lax.axis_size("seq")
    me = lax.axis_index("dp")
    tall, rows, width = stack.shape
    chunks = row_ring.gather(stack.reshape(tall * rows, width))
    whole = jnp.zeros((tall, 2, seq, rows, width), stack.dtype)
    for offset, chunk in chunks.items():
        owner = row_ring.owner(offset)
        other = swap(chunk, "dp", 1)
        for core, val in ((me % 2, chunk), (1 - me % 2, other)):
            val = val.reshape(tall, 1, 1, rows, width)
            whole = lax.dynamic_update_slice(whole, val, (0, core, owner, 0, 0))
    return whole.reshape(data * seq * rows, width)


def scatter_output_grad(part, row_ring):
    data, seq = lax.axis_size("dp"), lax.axis_size("seq")
    me = lax.axis_index("dp")
    tall = data // 2
    width = part.shape[1]
    rows = part.shape[0] // (data * seq)
    part = part.astype(LOW).reshape(tall, 2, seq, rows, width)
    kept = lax.dynamic_index_in_dim(part, me % 2, 1, False)
    sent = lax.dynamic_index_in_dim(part, 1 - me % 2, 1, False)
    kept = (kept.astype(FULL) + swap(sent, "dp", 1).astype(FULL)).astype(LOW)

    def block(offset):
        one = lax.dynamic_index_in_dim(kept, row_ring.owner(offset), 1, False)
        return one.reshape(tall * rows, width).astype(FULL)

    val = row_ring.scatter(block).reshape(tall, rows, width)
    for bit in data_bits(data)[:-1][::-1]:
        upper = (me // bit) % 2
        val = val.reshape(2, val.shape[0] // 2, rows, width)
        kept = lax.dynamic_index_in_dim(val, upper, 0, False)
        sent = lax.dynamic_index_in_dim(val, 1 - upper, 0, False)
        val = kept + swap(sent, "dp", bit)
    return val.reshape(rows, width)


def rms_scale(vals):
    return lax.rsqrt(jnp.mean(vals * vals, axis=-1, keepdims=True) + EPSILON)


def norm_back(grad_out, pre, scale, gain):
    weighted = grad_out * gain
    inner = jnp.mean(weighted * pre, axis=-1, keepdims=True)
    grad_pre = scale * weighted - pre * (scale * scale * scale) * inner
    grad_gain = jnp.sum(grad_out * pre * scale, axis=0)
    return (grad_pre, grad_gain)


def rope_tables(positions):
    half = HEAD // 2
    freq = ROPE_BASE ** (-2.0 * jnp.arange(half, dtype=FULL) / HEAD)
    angle = positions.astype(FULL)[:, None] * freq[None, :]
    cosine, sine = jnp.cos(angle), jnp.sin(angle)
    return jnp.concatenate([cosine, cosine], 1), jnp.concatenate([-sine, sine], 1)


def layout(lengths, placement, row_len):
    stored, docs = lengths.shape
    row = lax.dynamic_index_in_dim(placement, lax.axis_index("dp"), 0, False)
    doc_lens = jnp.sum(
        jnp.where(jnp.arange(stored, dtype=jnp.int32)[:, None] == row, lengths, 0), axis=0
    )
    upto = jnp.arange(docs, dtype=jnp.int32)
    doc_ends = jnp.sum(jnp.where(upto[None, :] <= upto[:, None], doc_lens[None, :], 0), axis=1)
    at = jnp.arange(row_len, dtype=jnp.int32)
    passed = at[:, None] >= doc_ends[None, :]
    return jnp.max(jnp.where(passed, doc_ends[None, :], 0), axis=1)


def column(row):
    return jnp.broadcast_to(row, (HEAD, row.shape[1])).T

def attend_forward_kernel(first_ref, q_ref, k_ref, v_ref, scale_ref, gain_ref, cos_ref, sin_ref, begin_ref,
                          out_ref, qr_ref, kr_ref, vl_ref, lse_ref, vt_ref):
    blocks = q_ref.shape[0] // BLOCK
    factor = HEAD ** -0.5 * LOG2E

    def prepare(i, _):
        rows = pl.ds(pl.multiple_of(i * BLOCK, BLOCK), BLOCK)
        for n, (src, dst) in enumerate(((q_ref, qr_ref), (k_ref, kr_ref))):
            x = src[rows, :] * column(scale_ref[n : n + 1, rows]) * gain_ref[n : n + 1, :]
            x = x * cos_ref[rows, :] + pltpu.roll(x, HEAD // 2, 1) * sin_ref[rows, :]
            dst[rows, :] = x.astype(LOW)
        v = v_ref[rows, :].astype(LOW)
        vl_ref[rows, :] = v
        vt_ref[:, rows] = v.T
        return 0

    lax.fori_loop(0, blocks, prepare, 0)

    def one(i, _):
        rows = pl.ds(pl.multiple_of(i * BLOCK, BLOCK), BLOCK)
        q = qr_ref[rows, :]
        begin = begin_ref[0:1, rows]
        at = lax.broadcasted_iota(jnp.int32, (BLOCK, BLOCK), 0)
        query_at = lax.broadcasted_iota(jnp.int32, (1, BLOCK), 1) + i * BLOCK

        def step(j, carry):
            top, total, acc = carry
            keys = pl.ds(pl.multiple_of(j * BLOCK, BLOCK), BLOCK)
            s = dot_nt(kr_ref[keys, :], q)
            key_at = at + j * BLOCK
            s = jnp.where((key_at >= begin) & (key_at <= query_at), s, NEG)
            new = jnp.maximum(top, jnp.max(s, axis=0, keepdims=True))
            p = jnp.exp2((s - new) * factor)
            shrink = jnp.exp2((top - new) * factor)
            total = total * shrink + jnp.sum(p, axis=0, keepdims=True)
            acc = acc * shrink + dot(vt_ref[:, keys], p.astype(LOW))
            return new, total, acc

        start = (jnp.full((1, BLOCK), NEG, FULL), jnp.zeros((1, BLOCK), FULL), jnp.zeros((HEAD, BLOCK), FULL))
        top, total, acc = lax.fori_loop(first_ref[i], i + 1, step, start)
        out_ref[rows, :] = (acc / total).T.astype(LOW)
        lse_ref[0, 0:1, rows] = top * factor + jnp.log2(total)
        return 0

    lax.fori_loop(0, blocks, one, 0)


def attend_forward(pre, scales, gains, cosine, sine, first, begin):
    rows, wide = pre.shape
    heads = wide // (3 * HEAD)
    col = lambda shift: pl.BlockSpec((rows, HEAD), lambda h, f: (0, h + shift))
    fixed = lambda shape: pl.BlockSpec(shape, lambda h, f: (0,) * len(shape))
    low = jax.ShapeDtypeStruct((rows, heads * HEAD), LOW)
    return pl.pallas_call(
        attend_forward_kernel,
        grid_spec=pltpu.PrefetchScalarGridSpec(
            num_scalar_prefetch=1,
            grid=(heads,),
            in_specs=[col(0), col(heads), col(2 * heads), fixed((2, rows)),
                      pl.BlockSpec((2, HEAD), lambda h, f: (0, h)), fixed((rows, HEAD)), fixed((rows, HEAD)), fixed((1, rows))],
            out_specs=[col(0)] * 4 + [pl.BlockSpec((1, 1, rows), lambda h, f: (h, 0, 0))],
            scratch_shapes=[pltpu.VMEM((HEAD, rows), LOW)],
        ),
        out_shape=[low] * 4 + [jax.ShapeDtypeStruct((heads, 1, rows), FULL)],
        compiler_params=pltpu.CompilerParams(vmem_limit_bytes=48 * 2**20),
        cost_estimate=pl.CostEstimate(flops=heads * rows * rows * HEAD * 2, bytes_accessed=rows * wide * 8, transcendentals=heads * rows * rows // 2),
        name="attend_forward",
    )(first, pre, pre, pre, scales, gains, cosine, sine, begin)


def attend_backward_kernel(first_ref, q_ref, k_ref, v_ref, o_ref, do_ref, lse_ref, qp_ref, kp_ref, scale_ref, gain_ref, cos_ref, sin_ref, begin_ref,
                           gq_ref, gk_ref, gv_ref, inner_ref, gain_grad_ref, kt_ref, dk_ref, dv_ref):
    blocks = q_ref.shape[0] // BLOCK
    norm = HEAD ** -0.5
    factor = norm * LOG2E

    def prepare(i, _):
        rows = pl.ds(pl.multiple_of(i * BLOCK, BLOCK), BLOCK)
        kt_ref[:, rows] = k_ref[rows, :].T
        dk_ref[rows, :] = jnp.zeros((BLOCK, HEAD), FULL)
        dv_ref[rows, :] = jnp.zeros((BLOCK, HEAD), FULL)
        return 0

    lax.fori_loop(0, blocks, prepare, 0)

    def finish(rows, n, grad, pre_ref, out):
        grad = grad.astype(LOW).astype(FULL)
        grad = grad * cos_ref[rows, :] - pltpu.roll(grad, HEAD // 2, 1) * sin_ref[rows, :]
        weighted = grad * gain_ref[n : n + 1, :]
        pre = pre_ref[rows, :]
        out[rows, :] = weighted
        inner_ref[0, n : n + 1, rows] = jnp.sum((weighted * pre).T, axis=0, keepdims=True)
        return jnp.sum(grad * pre * column(scale_ref[n : n + 1, rows]), axis=0, keepdims=True)

    def one(i, gain_grad):
        rows = pl.ds(pl.multiple_of(i * BLOCK, BLOCK), BLOCK)
        q = q_ref[rows, :]
        do = do_ref[rows, :]
        begin = begin_ref[0:1, rows]
        lse = lse_ref[0, 0:1, rows]
        delta = jnp.sum((do.astype(FULL) * o_ref[rows, :].astype(FULL)).T, axis=0, keepdims=True)
        at = lax.broadcasted_iota(jnp.int32, (BLOCK, BLOCK), 0)
        query_at = lax.broadcasted_iota(jnp.int32, (1, BLOCK), 1) + i * BLOCK

        def step(j, acc):
            keys = pl.ds(pl.multiple_of(j * BLOCK, BLOCK), BLOCK)
            s = dot_nt(k_ref[keys, :], q)
            key_at = at + j * BLOCK
            s = jnp.where((key_at >= begin) & (key_at <= query_at), s, NEG)
            p = jnp.exp2(s * factor - lse)
            dp = dot_nt(v_ref[keys, :], do)
            ds = (p * (dp - delta)).astype(LOW)
            dv_ref[keys, :] += dot(p.astype(LOW), do)
            dk_ref[keys, :] += dot(ds, q)
            return acc + dot(kt_ref[:, keys], ds)

        acc = lax.fori_loop(first_ref[i], i + 1, step, jnp.zeros((HEAD, BLOCK), FULL))
        return gain_grad + finish(rows, 0, acc.T * norm, qp_ref, gq_ref)

    gain_grad_ref[0:1, :] = lax.fori_loop(0, blocks, one, jnp.zeros((1, HEAD), FULL))

    def close(i, gain_grad):
        rows = pl.ds(pl.multiple_of(i * BLOCK, BLOCK), BLOCK)
        gv_ref[rows, :] = dv_ref[rows, :].astype(LOW)
        return gain_grad + finish(rows, 1, dk_ref[rows, :] * norm, kp_ref, gk_ref)

    gain_grad_ref[1:2, :] = lax.fori_loop(0, blocks, close, jnp.zeros((1, HEAD), FULL))


def attend_backward(q, k, v, out, grad, lse, pre, scales, gains, cosine, sine, first, begin):
    rows, wide = q.shape
    heads = wide // HEAD
    col = lambda shift: pl.BlockSpec((rows, HEAD), lambda h, f: (0, h + shift))
    fixed = lambda shape: pl.BlockSpec(shape, lambda h, f: (0,) * len(shape))
    pair = pl.BlockSpec((2, HEAD), lambda h, f: (0, h))
    full = jax.ShapeDtypeStruct((rows, wide), FULL)
    return pl.pallas_call(
        attend_backward_kernel,
        grid_spec=pltpu.PrefetchScalarGridSpec(
            num_scalar_prefetch=1,
            grid=(heads,),
            in_specs=[col(0)] * 5 + [pl.BlockSpec((1, 1, rows), lambda h, f: (h, 0, 0)), col(0), col(heads), fixed((2, rows)),
                      pair, fixed((rows, HEAD)), fixed((rows, HEAD)), fixed((1, rows))],
            out_specs=[col(0)] * 3 + [pl.BlockSpec((1, 2, rows), lambda h, f: (h, 0, 0)), pair],
            scratch_shapes=[pltpu.VMEM((HEAD, rows), LOW), pltpu.VMEM((rows, HEAD), FULL), pltpu.VMEM((rows, HEAD), FULL)],
        ),
        out_shape=[full, full, jax.ShapeDtypeStruct((rows, wide), LOW), jax.ShapeDtypeStruct((heads, 2, rows), FULL), jax.ShapeDtypeStruct((2, wide), FULL)],
        compiler_params=pltpu.CompilerParams(vmem_limit_bytes=48 * 2**20),
        cost_estimate=pl.CostEstimate(flops=heads * rows * rows * HEAD * 5, bytes_accessed=rows * wide * 40, transcendentals=heads * rows * rows // 2),
        name="attend_backward",
    )(first, q, k, v, out, grad, lse, pre, pre, scales, gains, cosine, sine, begin)


def per_device(
    tokens,
    cotangent,
    lengths,
    placement,
    w_query,
    w_key,
    w_value,
    w_output,
    query_gain,
    key_gain,
    attn_gain,
    w_gate,
    w_up,
    w_down,
    mlp_gain,
):
    data, seq = lax.axis_size("dp"), lax.axis_size("seq")
    seq_at = lax.axis_index("seq")
    _, count, width = tokens.shape
    row_len = count * seq
    own = width // seq
    row_ring = Ring([row_cycle(seq)])
    inputs = tokens.reshape(count, width)
    begin = layout(lengths, placement, row_len)
    first_block = begin[::BLOCK] // BLOCK
    cosine, sine = rope_tables(jnp.arange(row_len, dtype=jnp.int32) - begin)
    begin = begin[None]

    packed = jnp.stack([w_query, w_key, w_value], axis=1).reshape(-1, 3, seq, own)
    packed = jnp.moveaxis(packed, 2, 0).reshape(seq, -1, 3 * own)
    hid = w_gate.shape[1]
    chips = data_bits(data)[:-1]
    state = {"gains": jnp.stack([query_gain, key_gain, attn_gain, mlp_gain])[None]}
    gain_bits = bits_of(data * seq)

    def more_gains():
        if gain_bits:
            state["gains"] = gain_step(state["gains"], gain_bits.pop(0))
        return state["gains"]

    def beside(step):
        out = [more_gains()]
        if step == 1:
            state["down"] = swap_chips(w_down, chips)
            state["w_heads"] = lax.all_to_all(packed, "seq", split_axis=0, concat_axis=0, tiled=True)
            out.append(state["w_heads"])
        elif step == 2:
            state["w_heads"] = swap_chips(state["w_heads"].reshape(-1, 3 * own), chips)
            state["w_out"] = stack_output_weights(w_output)
            out += [state["w_heads"], state["w_out"], state["down"]]
        elif step == 3:
            state["w_heads"] = place_over_data(swap_cores(state["w_heads"]))
            state["gate"] = swap_chips(w_gate, chips)
            out += [state["w_heads"], state["gate"]]
        return out

    row_chunks = row_ring.gather(inputs, beside)
    w_heads = state["w_heads"]
    pre = jnp.zeros((row_len, 3 * own), FULL)
    row_tokens = jnp.zeros((row_len, width), LOW)
    last = row_ring.size // 2
    for offset, chunk in row_chunks.items():
        if offset == last:
            chunk, pre = after((chunk, pre))
        start = row_ring.owner(offset) * count
        pre = lax.dynamic_update_slice(pre, dot(chunk, w_heads), (start, 0))
        row_tokens = lax.dynamic_update_slice(row_tokens, chunk, (start, 0))
    while gain_bits:
        more_gains()
    gains = jnp.moveaxis(state["gains"], 0, 1).reshape(4, -1).astype(FULL)
    gain_attn, gain_mlp = gains[2], gains[3]
    gains_own = lax.dynamic_slice(gains, (0, seq_at * own), (2, own))
    state["up"] = swap_chips(after(w_up, row_chunks[last]), chips)

    query_pre, key_pre = pre[:, :own], pre[:, own : 2 * own]
    squares = jnp.stack([jnp.sum(query_pre * query_pre, axis=1), jnp.sum(key_pre * key_pre, axis=1)])
    scales = lax.rsqrt(sum_over(squares, "seq", seq) / width + EPSILON)
    attn_heads, query_rot, key_rot, values, log_sums = attend_forward(
        pre, scales, gains_own, cosine, sine, first_block, begin
    )
    w_out = gather_output_weights(after(state["w_out"], scales), row_ring)
    attn_tokens = lax.all_to_all(
        attn_heads.reshape(seq, count, own), "seq", split_axis=0, concat_axis=0, tiled=True
    )

    near = after([state[n] for n in ("gate", "up", "down")], attn_heads)
    near = [swap_cores(n) for n in near]
    gate_up = pack(near[0], near[1])
    down = jnp.concatenate([near[2][m] for m in range(data)], axis=1)
    attn_tokens = jnp.moveaxis(attn_tokens, 0, 1).reshape(count, width)
    attn_pre = dot(attn_tokens, w_out)
    attn_scale = rms_scale(attn_pre)
    middle = inputs.astype(FULL) + attn_pre * attn_scale * gain_attn
    middle_low = middle.astype(LOW)

    mids = row_ring.gather(swap_blocks(middle_low))
    saved = {}

    def mlp_part(offset):
        offset = offset if offset in mids else -offset
        both = dot(mids[offset], gate_up)
        gate, up = both[:, :hid], both[:, hid:]
        hidden = (gate * jax.nn.sigmoid(gate) * up).astype(LOW)
        saved[offset] = gate, up, hidden
        return dot(hidden, down)

    mlp_pre = swap_blocks(row_ring.scatter(mlp_part))
    mlp_scale = rms_scale(mlp_pre)
    layer_out = (middle + mlp_pre * mlp_scale * gain_mlp).astype(LOW).reshape(tokens.shape)
    grad_final = cotangent.reshape(count, width).astype(FULL)
    grad_mlp_pre, grad_gain_mlp = norm_back(grad_final, mlp_pre, mlp_scale, gain_mlp)
    grads = row_ring.gather(swap_blocks(grad_mlp_pre.astype(LOW)))
    grad_both = {}

    def middle_part(offset):
        offset = offset if offset in mids else -offset
        gate, up, hidden = saved[offset]
        grad_hidden = dot_nt(grads[offset], down)
        sig = jax.nn.sigmoid(gate)
        grad_gate = grad_hidden * up * sig * (1.0 + gate * (1.0 - sig))
        grad_up = grad_hidden * gate * sig
        both = jnp.concatenate([grad_gate.astype(LOW), grad_up.astype(LOW)], axis=1)
        grad_both[offset] = both
        return dot_nt(both, gate_up)

    grad_middle = grad_final + swap_blocks(row_ring.scatter(middle_part))
    order = list(mids)
    mid_rows = jnp.concatenate([mids[o] for o in order])
    grad_rows = jnp.concatenate([grads[o] for o in order])
    hidden = jnp.concatenate([saved[o][2] for o in order])
    both = jnp.concatenate([grad_both[o] for o in order])
    part_down = dot_tn(hidden, grad_rows).astype(LOW)
    grad_down = scatter_over_data(jnp.split(part_down, data, axis=1))
    grad_in = scatter_over_data(jnp.split(dot_tn(mid_rows, both).astype(LOW), data))
    grad_gate, grad_up = grad_in[:, :hid], grad_in[:, hid:]

    grad_attn_pre, grad_gain_attn = norm_back(grad_middle, attn_pre, attn_scale, gain_attn)
    grad_attn_low = grad_attn_pre.astype(LOW)
    grad_heads = dot_nt(grad_attn_low, w_out).astype(LOW).reshape(count, seq, own)
    grad_heads = lax.all_to_all(
        jnp.moveaxis(grad_heads, 1, 0), "seq", split_axis=0, concat_axis=0, tiled=True
    )
    grad_heads = grad_heads.reshape(row_len, own)
    grad_output = scatter_output_grad(dot_tn(attn_tokens, grad_attn_low), row_ring)
    weighted_q, weighted_k, grad_v, inner, gain_part = attend_backward(
        query_rot,
        key_rot,
        values,
        attn_heads,
        grad_heads,
        log_sums,
        pre,
        scales,
        gains_own,
        cosine,
        sine,
        first_block,
        begin,
    )
    inner = sum_over(jnp.sum(inner, axis=0), "seq", seq) * (scales**3) / width
    by_token = jnp.concatenate([scales, inner]).T
    grad_qp = by_token[:, 0:1] * weighted_q - by_token[:, 2:3] * query_pre
    grad_kp = by_token[:, 1:2] * weighted_k - by_token[:, 3:4] * key_pre
    grad_pre = jnp.concatenate([grad_qp.astype(LOW), grad_kp.astype(LOW), grad_v], axis=1)

    def token_part(offset):
        start = row_ring.owner(offset) * count
        return dot_nt(lax.dynamic_slice_in_dim(grad_pre, start, count, 0), w_heads)

    grad_tokens = (grad_middle + row_ring.scatter(token_part)).astype(LOW).reshape(tokens.shape)
    part = dot_tn(row_tokens, grad_pre).astype(LOW)
    part = [
        lax.dynamic_slice_in_dim(part, (lax.axis_index("dp") ^ m) * (width // data), width // data, 0)
        for m in range(data)
    ]
    part = scatter_over_data(part).astype(LOW)
    part = lax.all_to_all(
        part.reshape(seq, -1, 3 * own), "seq", split_axis=0, concat_axis=0, tiled=True
    ).astype(FULL)
    part = jnp.moveaxis(part.reshape(seq, -1, 3, own), 0, 2).reshape(-1, 3, width)

    placed = lax.dynamic_update_slice(jnp.zeros((2, width), FULL), gain_part, (0, seq_at * own))
    placed = jnp.concatenate([placed, grad_gain_attn[None], grad_gain_mlp[None]])
    for bit in bits_of(data * seq):
        placed = placed + swap_all(placed, bit)
    share = width // (data * seq)
    start = (lax.axis_index("dp") * seq + seq_at) * share
    gain_grads = lax.dynamic_slice(placed, (0, start), (4, share))

    return (
        layer_out,
        grad_tokens,
        part[:, 0],
        part[:, 1],
        part[:, 2],
        grad_output,
        gain_grads[0],
        gain_grads[1],
        gain_grads[2],
        grad_gate,
        grad_up,
        grad_down,
        gain_grads[3],
    )


def solution(mesh):
    rows = P("dp", "seq", None)
    both = P(("dp", "seq"), None)
    flat = P(("dp", "seq"))
    return jax.shard_map(
        per_device,
        mesh=mesh,
        in_specs=(rows, rows, P(), P())
        + (both,) * 4
        + (flat,) * 3
        + (P("dp", "seq"), P("dp", "seq"), P("seq", "dp"), flat),
        out_specs=(rows, rows)
        + (both,) * 4
        + (flat,) * 3
        + (P("dp", "seq"), P("dp", "seq"), P("seq", "dp"), flat),
        check_vma=False,
    )
```

time: 1380 us -> 911 us (0.66)
  matrix products: 338 us -> 160 us
  waiting for transfers between devices: 467 us -> 345 us
  starting transfers between devices: 231 us -> 135 us
  local copies, waits for them, and re-layouts: 179 us -> 119 us
  other arithmetic: 130 us -> 77 us
  Pallas kernels: 0 us -> 41.8 us
    ppermute x46 -> x38, waiting for transfers between devices: 197 us -> 36.7 us  [swap(): return lax.ppermute(val, axis, [(i, i ^ mask) for i in range(size)])]
    ppermute x24 -> x32, starting transfers between devices: 137 us -> 43 us  [left(): return lax.ppermute(val, 'seq', self.back)]
    dot_general x6 -> x0, matrix products: 89.9 us -> none  [the longest x1 21.9 us: attend_backward(): jnp.einsum('qhd,khd->hqk', grads, vals, preferred_element_type=FULL)]
    ppermute x24 -> x32, waiting for transfers between devices: 101 us -> 154 us  [right(): return lax.ppermute(val, 'seq', self.forth)]
    dot_general x25, matrix products: 116 us -> 65.5 us  [dot_nt(): lax.dot_general(left, right, (((1,), (1,)), ((), ())), preferred_element_...]
    convert_element_type x17 -> x6, other arithmetic: 51.3 us -> 9.14 us  [the longest x3 8.18 us: scatter_over_data(): out[m] = total if step == len(order) - 1 else total.astype(LOW)]
    pallas_call x0 -> x2, Pallas kernels: none -> 41.8 us  [the longest x1 24.3 us: attend_backward(): pl.pallas_call(attend_backward_kernel, grid_spec=pltpu.PrefetchScalarGrid...]
    dot_general x25, matrix products: 84.2 us -> 48 us  [dot(): return jnp.dot(left, right, preferred_element_type=FULL)]
  transfers between devices with their start and end apart: 108 -> 116, of which waited for: 40 -> 56; matrix products, arithmetic and copies ran while one was open for 42% -> 36% of each run, Pallas kernels for 0% -> 5%
where the time goes in v2:
time: 911 us; the launch traced here: 900 us
  waiting for transfers between devices  345 us (38%)
  matrix products  160 us (18%)
  starting transfers between devices  135 us (15%)
  local copies, waits for them, and re-layouts  119 us (13%)
  other arithmetic  77 us (8%)
  Pallas kernels  41.8 us (5%)
  between operations  21.7 us (2%)
    ppermute x32, waiting for transfers between devices, right(): return lax.ppermute(val, 'seq', self.forth)  154 us
    ppermute x32, waiting for transfers between devices, left(): return lax.ppermute(val, 'seq', self.back)  130 us
    dot_general x25, matrix products, dot_nt(): lax.dot_general(left, right, (((1,), (1,)), ((), ())), preferred_element_...  65.5 us
    dot_general x25, matrix products, dot(): return jnp.dot(left, right, preferred_element_type=FULL)  48 us
    dot_general x4, matrix products, dot_tn(): lax.dot_general(left, right, (((0,), (0,)), ((), ())), preferred_element_...  46.9 us
    ppermute x32, starting transfers between devices, left(): return lax.ppermute(val, 'seq', self.back)  43 us
    unnamed x296, local copies, waits for them, and re-layouts  38.6 us
    ppermute x32, starting transfers between devices, right(): return lax.ppermute(val, 'seq', self.forth)  36.9 us
  transfers between devices with their start and end apart: 116, of which 56 were waited for; matrix products, arithmetic and copies ran while one was open for 36% of the time, Pallas kernels for 5%

profile of v2, /device:TPU:0, one launch (start us, length us, event | category | flops | bytes accessed | tf_op | source)
XLA Modules:
  0.0 900.4 jit_solution(13673482347578105348)
XLA Ops:
  14.3 4.9 all-to-all-start
  22.3 5.4 fusion.69
  30.3 8.9 collective-permute-done.5
  80.2 17.5 %collective-permute-done.8 = bf16[1024,512]{1,0:T(8,128)(2,1)} collective-permute-done((bf16[1024,512]{1,0:T(8,128)(2,1)}, bf16[1024,512]{1,0:T(8,128)(2,1)}, u32[]{:S(2)}, u32[]{:S(2)}) %collective-permute-start.8) | collective-permute-done | bytes 1048608 | tf_op jit(solution)/shard_map/ppermute | solution.py:35
  112.7 6.3 collective-permute-done.14
  119.0 6.2 collective-permute-done.9
  130.1 8.1 collective-permute-done.15
  157.7 17.5 %attend_forward.1 = (bf16[2048,256]{1,0:T(8,128)(2,1)S(1)}, bf16[2048,256]{1,0:T(8,128)(2,1)S(1)}, bf16[2048,256]{1,0:T(8,128)(2,1)S(1)}, bf16[2048,256]{1,0:T(8,128)(2,1)S(1)}, f32[2,1,2048]{2,1,0:T(1,128)S(1)}) custom-call(s32[4]{0:T(128)S(1)} %and_select_fusion.first_ref, f32[2048,768]{1,0:T(8,128)} %copy-done.15, f32[2048,768]{1,0:T(8,128)} %copy-done.15, ...), custom_call_target="tpu_custom_call" | custom-call | flops 2147483648 | bytes 12582912 | tf_op jit(solution)/shard_map/attend_forward/pallas_call | solution.py:319
  182.2 4.3 broadcast_in_dim.81
  201.6 11.7 %collective-permute-done.27 = bf16[128,2048]{1,0:T(8,128)(2,1)S(1)} collective-permute-done((bf16[128,2048]{1,0:T(8,128)(2,1)}, bf16[128,2048]{1,0:T(8,128)(2,1)S(1)}, u32[]{:S(2)}, u32[]{:S(2)}) %collective-permute-start.27) | collective-permute-done | bytes 524320 | tf_op jit(solution)/shard_map/ppermute | solution.py:75
  214.5 5.6 collective-permute-start.33
  225.6 6.8 collective-permute-done.31
  256.3 6.2 multiply_reduce_fusion.3
  272.3 18.2 %collective-permute-done.46 = bf16[256,2048]{1,0:T(8,128)(2,1)S(1)} collective-permute-done((bf16[256,2048]{1,0:T(8,128)(2,1)S(1)}, bf16[256,2048]{1,0:T(8,128)(2,1)S(1)}, u32[]{:S(2)}, u32[]{:S(2)}) %collective-permute-start.46) | collective-permute-done | bytes 1048608 | tf_op jit(solution)/shard_map/ppermute | solution.py:75
  300.8 14.4 %collective-permute-done.48 = bf16[256,2048]{1,0:T(8,128)(2,1)S(1)} collective-permute-done((bf16[256,2048]{1,0:T(8,128)(2,1)S(1)}, bf16[256,2048]{1,0:T(8,128)(2,1)S(1)}, u32[]{:S(2)}, u32[]{:S(2)}) %collective-permute-start.48) | collective-permute-done | bytes 1048608 | tf_op jit(solution)/shard_map/ppermute | solution.py:75
  325.2 13.7 %collective-permute-done.50 = bf16[256,2048]{1,0:T(8,128)(2,1)S(1)} collective-permute-done((bf16[256,2048]{1,0:T(8,128)(2,1)S(1)}, bf16[256,2048]{1,0:T(8,128)(2,1)S(1)}, u32[]{:S(2)}, u32[]{:S(2)}) %collective-permute-start.50) | collective-permute-done | bytes 1048608 | tf_op jit(solution)/shard_map/ppermute | solution.py:75
  358.5 4.4 broadcast.131
  383.6 12.0 %collective-permute-done.58 = bf16[256,2048]{1,0:T(8,128)(2,1)S(1)} collective-permute-done((bf16[256,2048]{1,0:T(8,128)(2,1)S(1)}, bf16[256,2048]{1,0:T(8,128)(2,1)S(1)}, u32[]{:S(2)}, u32[]{:S(2)}) %collective-permute-start.58) | collective-permute-done | bytes 1048608 | tf_op jit(solution)/shard_map/ppermute | solution.py:78
  406.9 12.3 %collective-permute-done.59 = bf16[256,2048]{1,0:T(8,128)(2,1)S(1)} collective-permute-done((bf16[256,2048]{1,0:T(8,128)(2,1)S(1)}, bf16[256,2048]{1,0:T(8,128)(2,1)S(1)}, u32[]{:S(2)}, u32[]{:S(2)}) %collective-permute-start.59) | collective-permute-done | bytes 1048608 | tf_op jit(solution)/shard_map/ppermute | solution.py:78
  432.2 6.6 collective-permute-done.60
  438.8 5.2 collective-permute-done.56
  454.8 17.6 %collective-permute-done.62 = bf16[256,2048]{1,0:T(8,128)(2,1)S(1)} collective-permute-done((bf16[256,2048]{1,0:T(8,128)(2,1)S(1)}, bf16[256,2048]{1,0:T(8,128)(2,1)S(1)}, u32[]{:S(2)}, u32[]{:S(2)}) %collective-permute-start.62) | collective-permute-done | bytes 1048608 | tf_op jit(solution)/shard_map/ppermute | solution.py:75
  482.0 13.7 %collective-permute-done.64 = bf16[256,2048]{1,0:T(8,128)(2,1)S(1)} collective-permute-done((bf16[256,2048]{1,0:T(8,128)(2,1)S(1)}, bf16[256,2048]{1,0:T(8,128)(2,1)S(1)}, u32[]{:S(2)}, u32[]{:S(2)}) %collective-permute-start.64) | collective-permute-done | bytes 1048608 | tf_op jit(solution)/shard_map/ppermute | solution.py:75
  505.3 10.9 %collective-permute-done.66 = bf16[256,2048]{1,0:T(8,128)(2,1)S(1)} collective-permute-done((bf16[256,2048]{1,0:T(8,128)(2,1)S(1)}, bf16[256,2048]{1,0:T(8,128)(2,1)S(1)}, u32[]{:S(2)}, u32[]{:S(2)}) %collective-permute-start.66) | collective-permute-done | bytes 1048608 | tf_op jit(solution)/shard_map/ppermute | solution.py:75
  526.8 5.1 collective-permute-done.68
  542.0 9.6 %collective-permute-done.73 = bf16[128,2048]{1,0:T(8,128)(2,1)S(1)} collective-permute-done((bf16[128,2048]{1,0:T(8,128)(2,1)S(1)}, bf16[128,2048]{1,0:T(8,128)(2,1)S(1)}, u32[]{:S(2)}, u32[]{:S(2)}) %collective-permute-start.73) | collective-permute-done | bytes 524320 | tf_op jit(solution)/shard_map/ppermute | solution.py:78
  561.2 12.7 %convolution_convert_fusion.2 = bf16[1024,2048]{1,0:T(8,128)(2,1)S(1)} fusion(bf16[2048,1024]{1,0:T(8,128)(2,1)} %copy-done.116, bf16[2048,2048]{1,0:T(8,128)(2,1)} %constant_dynamic-update-slice_fusion.25), kind=kOutput, calls=%fused_computation.8 | convolution fusion | flops 8592031744 | bytes 16777216 | tf_op jit(solution)/shard_map/dot_general | solution.py:30
  573.9 5.1 collective-permute-done.74
  578.9 4.6 fusion.9
  592.2 6.5 collective-permute-done.75
  604.5 4.6 fusion.5
  609.3 22.4 %convolution_convert_fusion = bf16[2048,2048]{1,0:T(8,128)(2,1)S(1)} fusion(bf16[2048,2048]{1,0:T(8,128)(2,1)} %constant_dynamic-update-slice_fusion.8, bf16[2048,2048]{1,0:T(8,128)(2,1)} %fusion.55), kind=kOutput, calls=%fused_computation.2 | convolution fusion | flops 17184063488 | bytes 25165824 | tf_op jit(solution)/shard_map/dot_general | solution.py:30
  648.8 5.7 convolution_convert_fusion.6
  655.6 4.7 all-to-all-start.2
  660.3 4.6 add_convert_fusion
  678.5 8.7 all-to-all-done.2
  688.4 24.3 %attend_backward.1 = (f32[2048,256]{1,0:T(8,128)}, f32[2048,256]{1,0:T(8,128)}, bf16[2048,256]{1,0:T(8,128)(2,1)S(1)}, f32[2,2,2048]{2,1,0:T(2,128)S(1)}, f32[2,256]{1,0:T(2,128)S(1)}) custom-call(s32[4]{0:T(128)S(1)} %copy-done.14, bf16[2048,256]{1,0:T(8,128)(2,1)S(1)} %get-tuple-element.92.q_ref, bf16[2048,256]{1,0:T(8,128)(2,1)S(1)} %copy-done.2, ...), custom_call_target="tpu_custom_call" | custom-call | flops 5368709120 | bytes 20971520 | tf_op jit(solution)/shard_map/attend_backward/pallas_call | solution.py:402
  717.7 4.2 convert_add_fusion.1
  738.4 9.4 %convolution_convert_fusion.3 = bf16[2048,768]{1,0:T(8,128)(2,1)S(1)} fusion(bf16[2048,2048]{1,0:T(8,128)(2,1)} %constant_dynamic-update-slice_fusion.34, bf16[2048,256]{1,0:T(8,128)(2,1)S(1)} %copy-done.6, bf16[2048,256]{1,0:T(8,128)(2,1)S(1)} %get-tuple-element.128, bf16[2048,256]{1,0:T(8,128)(2,1)S(1)} %get-tuple-element.127), kind=kOutput, calls=%fused_computation.9 | convolution fusion | flops 6453460992 | bytes 14680064 | tf_op jit(solution)/shard_map/dot_general | solution.py:30
  747.8 4.5 collective-permute-done.103
  764.4 16.7 %collective-permute-done.85 = bf16[256,2048]{1,0:T(8,128)(2,1)S(1)} collective-permute-done((bf16[256,2048]{1,0:T(8,128)(2,1)S(1)}, bf16[256,2048]{1,0:T(8,128)(2,1)S(1)}, u32[]{:S(2)}, u32[]{:S(2)}) %collective-permute-start.85) | collective-permute-done | bytes 1048608 | tf_op jit(solution)/shard_map/ppermute | solution.py:78
  793.3 19.7 %collective-permute-done.96 = bf16[64,2048]{1,0:T(8,128)(2,1)S(1)} collective-permute-done((bf16[64,2048]{1,0:T(8,128)(2,1)S(1)}, bf16[64,2048]{1,0:T(8,128)(2,1)S(1)}, u32[]{:S(2)}, u32[]{:S(2)}) %collective-permute-start.96) | collective-permute-done | bytes 262176 | tf_op jit(solution)/shard_map/ppermute | solution.py:78
  814.5 4.8 collective-permute-done.92
  824.9 4.2 all-to-all-start.3
  829.1 5.3 collective-permute-done.97
  845.7 8.8 collective-permute-done.98
  855.5 4.5 collective-permute-start.99
  874.5 11.6 %collective-permute-done.99 = bf16[128,2048]{1,0:T(8,128)(2,1)} collective-permute-done((bf16[128,2048]{1,0:T(8,128)(2,1)}, bf16[128,2048]{1,0:T(8,128)(2,1)}, u32[]{:S(2)}, u32[]{:S(2)}) %collective-permute-start.99) | collective-permute-done | bytes 524320 | tf_op jit(solution)/shard_map/ppermute | solution.py:78
  (719 shorter events, 428.0 us)
Async XLA Ops:
  0.6 71.8 %collective-permute-start = (bf16[256,2048]{1,0:T(8,128)(2,1)}, bf16[256,2048]{1,0:T(8,128)(2,1)}, u32[]{:S(2)}, u32[]{:S(2)}) collective-permute-start(bf16[256,2048]{1,0:T(8,128)(2,1)} %bitcast.279), channel_id=1, source_target_pairs={{0,1},{1,3},{3,5},{5,7},{7,6},{6,4},{4,2},{2,0},{8,9},{9,11},{11,1... | collective-permute-start | bytes 3145736 | tf_op jit(solution)/shard_map/ppermute | solution.py:75
  3.6 68.8 %collective-permute-start.1 = (bf16[256,2048]{1,0:T(8,128)(2,1)}, bf16[256,2048]{1,0:T(8,128)(2,1)}, u32[]{:S(2)}, u32[]{:S(2)}) collective-permute-start(bf16[256,2048]{1,0:T(8,128)(2,1)} %bitcast.280), channel_id=1, source_target_pairs={{1,0},{3,1},{5,3},{7,5},{6,7},{4,6},{2,4},{0,2},{9,8},{11,9},{13,1... | collective-permute-start | bytes 3145736 | tf_op jit(solution)/shard_map/ppermute | solution.py:78
  4.5 25.6 %collective-permute-start.2 = (bf16[1,4,64]{2,1,0:T(4,128)(2,1)S(1)}, bf16[1,4,64]{2,1,0:T(4,128)(2,1)S(1)}, u32[]{:S(2)}, u32[]{:S(2)}) collective-permute-start(bf16[1,4,64]{2,1,0:T(4,128)(2,1)S(1)} %maximum_bitcast_fusion.2), channel_id=1, source_target_pairs={{0,1},{1,0},{2,3},{3,2},{4,5},{5,4},{6,7},{7,6},{8,9},{9,8},{10,11... | collective-permute-start | bytes 1544 | tf_op jit(solution)/shard_map/ppermute | solution.py:40
  14.3 31.8 %all-to-all-start = ((bf16[8,64,768]{2,1,0:T(8,128)(2,1)}), bf16[8,64,768]{2,1,0:T(8,128)(2,1)}, u32[]{:S(2)}, u32[]{:S(2)}) async-start(bf16[8,64,768]{2,1,0:T(8,128)(2,1)} %reshape.261), calls=%async_computation | async-start | bytes 1572864 | tf_op jit(solution)/shard_map/all_to_all | solution.py:464
  19.2 56.2 %collective-permute-start.7 = (bf16[1,64,2048]{2,1,0:T(8,128)(2,1)S(1)}, bf16[1,64,2048]{2,1,0:T(8,128)(2,1)}, u32[]{:S(2)}, u32[]{:S(2)}) collective-permute-start(bf16[1,64,2048]{2,1,0:T(8,128)(2,1)S(1)} %bitcast.306), channel_id=1, source_target_pairs={{0,16},{8,24},{16,0},{24,8},{1,17},{9,25},{17,1},{25,9},{2,18},{10... | collective-permute-start | bytes 786440 | tf_op jit(solution)/shard_map/ppermute | solution.py:35
  46.0 29.3 %collective-permute-start.6 = (bf16[512,768]{1,0:T(8,128)(2,1)}, bf16[512,768]{1,0:T(8,128)(2,1)S(1)}, u32[]{:S(2)}, u32[]{:S(2)}) collective-permute-start(bf16[512,768]{1,0:T(8,128)(2,1)} %bitcast.8), channel_id=1, source_target_pairs={{0,16},{8,24},{16,0},{24,8},{1,17},{9,25},{17,1},{25,9},{2,18},{10... | collective-permute-start | bytes 2359304 | tf_op jit(solution)/shard_map/ppermute | solution.py:35
  71.3 26.4 %collective-permute-start.8 = (bf16[1024,512]{1,0:T(8,128)(2,1)}, bf16[1024,512]{1,0:T(8,128)(2,1)}, u32[]{:S(2)}, u32[]{:S(2)}) collective-permute-start(bf16[1024,512]{1,0:T(8,128)(2,1)} %param.60), channel_id=1, source_target_pairs={{0,16},{8,24},{16,0},{24,8},{1,17},{9,25},{17,1},{25,9},{2,18},{10... | collective-permute-start | bytes 3145736 | tf_op jit(solution)/shard_map/ppermute | solution.py:35
  72.5 26.2 %collective-permute-start.3 = (bf16[256,2048]{1,0:T(8,128)(2,1)}, bf16[256,2048]{1,0:T(8,128)(2,1)S(1)}, u32[]{:S(2)}, u32[]{:S(2)}) collective-permute-start(bf16[256,2048]{1,0:T(8,128)(2,1)} %collective-permute-done), channel_id=1, source_target_pairs={{0,1},{1,3},{3,5},{5,7},{7,6},{6,4},{4,2},{2,0},{8,9},{9,11},{11,1... | collective-permute-start | bytes 3145736 | tf_op jit(solution)/shard_map/ppermute | solution.py:75
  75.3 25.4 %collective-permute-start.4 = (bf16[256,2048]{1,0:T(8,128)(2,1)}, bf16[256,2048]{1,0:T(8,128)(2,1)S(1)}, u32[]{:S(2)}, u32[]{:S(2)}) collective-permute-start(bf16[256,2048]{1,0:T(8,128)(2,1)} %collective-permute-done.1), channel_id=1, source_target_pairs={{1,0},{3,1},{5,3},{7,5},{6,7},{4,6},{2,4},{0,2},{9,8},{11,9},{13,1... | collective-permute-start | bytes 3145736 | tf_op jit(solution)/shard_map/ppermute | solution.py:78
  75.3 27.7 %collective-permute-start.13 = (bf16[512,768]{1,0:T(8,128)(2,1)S(1)}, bf16[512,768]{1,0:T(8,128)(2,1)S(1)}, u32[]{:S(2)}, u32[]{:S(2)}) collective-permute-start(bf16[512,768]{1,0:T(8,128)(2,1)S(1)} %collective-permute-done.6), channel_id=1, source_target_pairs={{0,8},{8,0},{16,24},{24,16},{1,9},{9,1},{17,25},{25,17},{2,10},{10... | collective-permute-start | bytes 2359304 | tf_op jit(solution)/shard_map/ppermute | solution.py:35
  79.0 40.0 %collective-permute-start.14 = (bf16[512,1024]{1,0:T(8,128)(2,1)S(1)}, bf16[512,1024]{1,0:T(8,128)(2,1)S(1)}, u32[]{:S(2)}, u32[]{:S(2)}) collective-permute-start(bf16[512,1024]{1,0:T(8,128)(2,1)S(1)} %copy-done.72), channel_id=1, source_target_pairs={{0,16},{8,24},{16,0},{24,8},{1,17},{9,25},{17,1},{25,9},{2,18},{10... | collective-permute-start | bytes 3145736 | tf_op jit(solution)/shard_map/ppermute | solution.py:35
  100.8 24.4 %collective-permute-start.9 = (bf16[256,2048]{1,0:T(8,128)(2,1)S(1)}, bf16[256,2048]{1,0:T(8,128)(2,1)S(1)}, u32[]{:S(2)}, u32[]{:S(2)}) collective-permute-start(bf16[256,2048]{1,0:T(8,128)(2,1)S(1)} %collective-permute-done.3), channel_id=1, source_target_pairs={{0,1},{1,3},{3,5},{5,7},{7,6},{6,4},{4,2},{2,0},{8,9},{9,11},{11,1... | collective-permute-start | bytes 3145736 | tf_op jit(solution)/shard_map/ppermute | solution.py:75
  101.1 24.7 %collective-permute-start.10 = (bf16[256,2048]{1,0:T(8,128)(2,1)S(1)}, bf16[256,2048]{1,0:T(8,128)(2,1)S(1)}, u32[]{:S(2)}, u32[]{:S(2)}) collective-permute-start(bf16[256,2048]{1,0:T(8,128)(2,1)S(1)} %collective-permute-done.4), channel_id=1, source_target_pairs={{1,0},{3,1},{5,3},{7,5},{6,7},{4,6},{2,4},{0,2},{9,8},{11,9},{13,1... | collective-permute-start | bytes 3145736 | tf_op jit(solution)/shard_map/ppermute | solution.py:78
  152.7 44.5 %collective-permute-start.38 = (bf16[512,1024]{1,0:T(8,128)(2,1)}, bf16[512,1024]{1,0:T(8,128)(2,1)}, u32[]{:S(2)}, u32[]{:S(2)}) collective-permute-start(bf16[512,1024]{1,0:T(8,128)(2,1)} %param.59), channel_id=1, source_target_pairs={{0,16},{8,24},{16,0},{24,8},{1,17},{9,25},{17,1},{25,9},{2,18},{10... | collective-permute-start | bytes 3145736 | tf_op jit(solution)/shard_map/ppermute | solution.py:35
  155.6 37.7 %collective-permute-start.22 = (bf16[128,2048]{1,0:T(8,128)(2,1)}, bf16[128,2048]{1,0:T(8,128)(2,1)}, u32[]{:S(2)}, u32[]{:S(2)}) collective-permute-start(bf16[128,2048]{1,0:T(8,128)(2,1)} %bitcast.28), channel_id=1, source_target_pairs={{0,8},{8,0},{16,24},{24,16},{1,9},{9,1},{17,25},{25,17},{2,10},{10... | collective-permute-start | bytes 1572872 | tf_op jit(solution)/shard_map/ppermute | solution.py:35
  155.6 32.8 %collective-permute-start.23 = (bf16[128,2048]{1,0:T(8,128)(2,1)}, bf16[128,2048]{1,0:T(8,128)(2,1)}, u32[]{:S(2)}, u32[]{:S(2)}) collective-permute-start(bf16[128,2048]{1,0:T(8,128)(2,1)} %bitcast.28), channel_id=1, source_target_pairs={{0,1},{1,3},{3,5},{5,7},{7,6},{6,4},{4,2},{2,0},{8,9},{9,11},{11,1... | collective-permute-start | bytes 1572872 | tf_op jit(solution)/shard_map/ppermute | solution.py:75
  156.7 31.7 %collective-permute-start.25 = (bf16[128,2048]{1,0:T(8,128)(2,1)}, bf16[128,2048]{1,0:T(8,128)(2,1)}, u32[]{:S(2)}, u32[]{:S(2)}) collective-permute-start(bf16[128,2048]{1,0:T(8,128)(2,1)} %bitcast.28), channel_id=1, source_target_pairs={{1,0},{3,1},{5,3},{7,5},{6,7},{4,6},{2,4},{0,2},{9,8},{11,9},{13,1... | collective-permute-start | bytes 1572872 | tf_op jit(solution)/shard_map/ppermute | solution.py:78
  178.6 77.7 %all-to-all-start.1 = ((bf16[8,256,256]{1,2,0:T(8,128)(2,1)}), bf16[8,256,256]{1,2,0:T(8,128)(2,1)S(1)}, u32[]{:S(2)}, u32[]{:S(2)}) async-start(bf16[8,256,256]{1,2,0:T(8,128)(2,1)} %copy.98), calls=%async_computation.1 | async-start | bytes 2097152 | tf_op jit(solution)/shard_map/all_to_all | solution.py:501
  188.4 25.0 %collective-permute-start.27 = (bf16[128,2048]{1,0:T(8,128)(2,1)}, bf16[128,2048]{1,0:T(8,128)(2,1)S(1)}, u32[]{:S(2)}, u32[]{:S(2)}) collective-permute-start(bf16[128,2048]{1,0:T(8,128)(2,1)} %collective-permute-done.23), channel_id=1, source_target_pairs={{0,1},{1,3},{3,5},{5,7},{7,6},{6,4},{4,2},{2,0},{8,9},{9,11},{11,1... | collective-permute-start | bytes 1572872 | tf_op jit(solution)/shard_map/ppermute | solution.py:75
  191.0 29.1 %collective-permute-start.24 = (bf16[128,2048]{1,0:T(8,128)(2,1)}, bf16[128,2048]{1,0:T(8,128)(2,1)S(1)}, u32[]{:S(2)}, u32[]{:S(2)}) collective-permute-start(bf16[128,2048]{1,0:T(8,128)(2,1)} %collective-permute-done.23), channel_id=1, source_target_pairs={{0,8},{8,0},{16,24},{24,16},{1,9},{9,1},{17,25},{25,17},{2,10},{10... | collective-permute-start | bytes 1572872 | tf_op jit(solution)/shard_map/ppermute | solution.py:35
  193.3 30.6 %collective-permute-start.26 = (bf16[128,2048]{1,0:T(8,128)(2,1)}, bf16[128,2048]{1,0:T(8,128)(2,1)S(1)}, u32[]{:S(2)}, u32[]{:S(2)}) collective-permute-start(bf16[128,2048]{1,0:T(8,128)(2,1)} %collective-permute-done.25), channel_id=1, source_target_pairs={{0,8},{8,0},{16,24},{24,16},{1,9},{9,1},{17,25},{25,17},{2,10},{10... | collective-permute-start | bytes 1572872 | tf_op jit(solution)/shard_map/ppermute | solution.py:35
  198.3 50.1 %collective-permute-start.39 = (bf16[512,1024]{1,0:T(8,128)(2,1)S(1)}, bf16[512,1024]{1,0:T(8,128)(2,1)S(1)}, u32[]{:S(2)}, u32[]{:S(2)}) collective-permute-start(bf16[512,1024]{1,0:T(8,128)(2,1)S(1)} %copy-done.73), channel_id=1, source_target_pairs={{0,8},{8,0},{16,24},{24,16},{1,9},{9,1},{17,25},{25,17},{2,10},{10... | collective-permute-start | bytes 3145736 | tf_op jit(solution)/shard_map/ppermute | solution.py:35
  265.2 25.3 %collective-permute-start.46 = (bf16[256,2048]{1,0:T(8,128)(2,1)S(1)}, bf16[256,2048]{1,0:T(8,128)(2,1)S(1)}, u32[]{:S(2)}, u32[]{:S(2)}) collective-permute-start(bf16[256,2048]{1,0:T(8,128)(2,1)S(1)} %get-tuple-element.176), channel_id=1, source_target_pairs={{0,1},{1,3},{3,5},{5,7},{7,6},{6,4},{4,2},{2,0},{8,9},{9,11},{11,1... | collective-permute-start | bytes 3145736 | tf_op jit(solution)/shard_map/ppermute | solution.py:75
  266.1 25.0 %collective-permute-start.45 = (bf16[256,2048]{1,0:T(8,128)(2,1)S(1)}, bf16[256,2048]{1,0:T(8,128)(2,1)S(1)}, u32[]{:S(2)}, u32[]{:S(2)}) collective-permute-start(bf16[256,2048]{1,0:T(8,128)(2,1)S(1)} %get-tuple-element.176), channel_id=1, source_target_pairs={{1,0},{3,1},{5,3},{7,5},{6,7},{4,6},{2,4},{0,2},{9,8},{11,9},{13,1... | collective-permute-start | bytes 3145736 | tf_op jit(solution)/shard_map/ppermute | solution.py:78
  291.1 24.1 %collective-permute-start.48 = (bf16[256,2048]{1,0:T(8,128)(2,1)S(1)}, bf16[256,2048]{1,0:T(8,128)(2,1)S(1)}, u32[]{:S(2)}, u32[]{:S(2)}) collective-permute-start(bf16[256,2048]{1,0:T(8,128)(2,1)S(1)} %collective-permute-done.46), channel_id=1, source_target_pairs={{0,1},{1,3},{3,5},{5,7},{7,6},{6,4},{4,2},{2,0},{8,9},{9,11},{11,1... | collective-permute-start | bytes 3145736 | tf_op jit(solution)/shard_map/ppermute | solution.py:75
  291.4 24.3 %collective-permute-start.47 = (bf16[256,2048]{1,0:T(8,128)(2,1)S(1)}, bf16[256,2048]{1,0:T(8,128)(2,1)S(1)}, u32[]{:S(2)}, u32[]{:S(2)}) collective-permute-start(bf16[256,2048]{1,0:T(8,128)(2,1)S(1)} %collective-permute-done.45), channel_id=1, source_target_pairs={{1,0},{3,1},{5,3},{7,5},{6,7},{4,6},{2,4},{0,2},{9,8},{11,9},{13,1... | collective-permute-start | bytes 3145736 | tf_op jit(solution)/shard_map/ppermute | solution.py:78
  561.0 25.0 %collective-permute-start.70 = (bf16[256,2048]{1,0:T(8,128)(2,1)}, bf16[256,2048]{1,0:T(8,128)(2,1)S(1)}, u32[]{:S(2)}, u32[]{:S(2)}) collective-permute-start(bf16[256,2048]{1,0:T(8,128)(2,1)} %fusion.7), channel_id=1, source_target_pairs={{0,1},{1,3},{3,5},{5,7},{7,6},{6,4},{4,2},{2,0},{8,9},{9,11},{11,1... | collective-permute-start | bytes 3145736 | tf_op jit(solution)/shard_map/ppermute | solution.py:75
  591.1 45.8 %collective-permute-start.110 = (bf16[1024,512]{1,0:T(8,128)(2,1)}, bf16[1024,512]{1,0:T(8,128)(2,1)S(1)}, u32[]{:S(2)}, u32[]{:S(2)}) collective-permute-start(bf16[1024,512]{1,0:T(8,128)(2,1)} %get-tuple-element.130), channel_id=1, source_target_pairs={{0,8},{8,0},{16,24},{24,16},{1,9},{9,1},{17,25},{25,17},{2,10},{10... | collective-permute-start | bytes 3145736 | tf_op jit(solution)/shard_map/ppermute | solution.py:35
  602.1 37.3 %collective-permute-start.76 = (bf16[256,2048]{1,0:T(8,128)(2,1)}, bf16[256,2048]{1,0:T(8,128)(2,1)}, u32[]{:S(2)}, u32[]{:S(2)}) collective-permute-start(bf16[256,2048]{1,0:T(8,128)(2,1)} %fusion.8), channel_id=1, source_target_pairs={{1,0},{3,1},{5,3},{7,5},{6,7},{4,6},{2,4},{0,2},{9,8},{11,9},{13,1... | collective-permute-start | bytes 3145736 | tf_op jit(solution)/shard_map/ppermute | solution.py:78
  609.1 30.2 %collective-permute-start.72 = (bf16[256,2048]{1,0:T(8,128)(2,1)}, bf16[256,2048]{1,0:T(8,128)(2,1)}, u32[]{:S(2)}, u32[]{:S(2)}) collective-permute-start(bf16[256,2048]{1,0:T(8,128)(2,1)} %fusion.5), channel_id=1, source_target_pairs={{0,1},{1,3},{3,5},{5,7},{7,6},{6,4},{4,2},{2,0},{8,9},{9,11},{11,1... | collective-permute-start | bytes 3145736 | tf_op jit(solution)/shard_map/ppermute | solution.py:75
  636.3 24.0 %collective-permute-start.107 = (bf16[512,2048]{1,0:T(8,128)(2,1)}, bf16[512,2048]{1,0:T(8,128)(2,1)}, u32[]{:S(2)}, u32[]{:S(2)}) collective-permute-start(bf16[512,2048]{1,0:T(8,128)(2,1)} %get-tuple-element.126), channel_id=1, source_target_pairs={{0,8},{8,0},{16,24},{24,16},{1,9},{9,1},{17,25},{25,17},{2,10},{10... | collective-permute-start | bytes 6291464 | tf_op jit(solution)/shard_map/ppermute | solution.py:35
  636.3 81.3 %collective-permute-start.106 = (bf16[512,2048]{1,0:T(8,128)(2,1)}, bf16[512,2048]{1,0:T(8,128)(2,1)}, u32[]{:S(2)}, u32[]{:S(2)}) collective-permute-start(bf16[512,2048]{1,0:T(8,128)(2,1)} %get-tuple-element.125), channel_id=1, source_target_pairs={{0,8},{8,0},{16,24},{24,16},{1,9},{9,1},{17,25},{25,17},{2,10},{10... | collective-permute-start | bytes 6291464 | tf_op jit(solution)/shard_map/ppermute | solution.py:35
  636.8 31.1 %collective-permute-start.109 = (bf16[1024,512]{1,0:T(8,128)(2,1)}, bf16[1024,512]{1,0:T(8,128)(2,1)}, u32[]{:S(2)}, u32[]{:S(2)}) collective-permute-start(bf16[1024,512]{1,0:T(8,128)(2,1)} %get-tuple-element.129), channel_id=1, source_target_pairs={{0,8},{8,0},{16,24},{24,16},{1,9},{9,1},{17,25},{25,17},{2,10},{10... | collective-permute-start | bytes 3145736 | tf_op jit(solution)/shard_map/ppermute | solution.py:35
  639.4 28.6 %collective-permute-start.111 = (bf16[1024,512]{1,0:T(8,128)(2,1)}, bf16[1024,512]{1,0:T(8,128)(2,1)}, u32[]{:S(2)}, u32[]{:S(2)}) collective-permute-start(bf16[1024,512]{1,0:T(8,128)(2,1)} %add_convert_fusion.2), channel_id=1, source_target_pairs={{0,16},{8,24},{16,0},{24,8},{1,17},{9,25},{17,1},{25,9},{2,18},{10... | collective-permute-start | bytes 3145736 | tf_op jit(solution)/shard_map/ppermute | solution.py:35
  655.6 31.6 %all-to-all-start.2 = ((bf16[8,256,256]{2,1,0:T(8,128)(2,1)}), bf16[8,256,256]{2,1,0:T(8,128)(2,1)}, u32[]{:S(2)}, u32[]{:S(2)}) async-start(bf16[8,256,256]{2,1,0:T(8,128)(2,1)} %bitcast.269), calls=%async_computation.2 | async-start | bytes 2097152 | tf_op jit(solution)/shard_map/all_to_all | solution.py:559
  664.9 52.8 %collective-permute-start.108 = (bf16[512,2048]{1,0:T(8,128)(2,1)}, bf16[512,2048]{1,0:T(8,128)(2,1)}, u32[]{:S(2)}, u32[]{:S(2)}) collective-permute-start(bf16[512,2048]{1,0:T(8,128)(2,1)} %add_convert_fusion), channel_id=1, source_target_pairs={{0,16},{8,24},{16,0},{24,8},{1,17},{9,25},{17,1},{25,9},{2,18},{10... | collective-permute-start | bytes 6291464 | tf_op jit(solution)/shard_map/ppermute | solution.py:35
  678.5 108.7 %collective-permute-start.91 = (bf16[2,8,64,2048]{3,2,1,0:T(8,128)(2,1)}, bf16[2,8,64,2048]{3,2,1,0:T(8,128)(2,1)}, u32[]{:S(2)}, u32[]{:S(2)}) collective-permute-start(bf16[2,8,64,2048]{3,2,1,0:T(8,128)(2,1)} %dynamic-slice_bitcast_fusion), channel_id=1, source_target_pairs={{0,8},{8,0},{16,24},{24,16},{1,9},{9,1},{17,25},{25,17},{2,10},{10... | collective-permute-start | bytes 12582920 | tf_op jit(solution)/shard_map/ppermute | solution.py:35
  756.2 24.9 %collective-permute-start.85 = (bf16[256,2048]{1,0:T(8,128)(2,1)S(1)}, bf16[256,2048]{1,0:T(8,128)(2,1)S(1)}, u32[]{:S(2)}, u32[]{:S(2)}) collective-permute-start(bf16[256,2048]{1,0:T(8,128)(2,1)S(1)} %fusion.16), channel_id=1, source_target_pairs={{1,0},{3,1},{5,3},{7,5},{6,7},{4,6},{2,4},{0,2},{9,8},{11,9},{13,1... | collective-permute-start | bytes 3145736 | tf_op jit(solution)/shard_map/ppermute | solution.py:78
  757.5 25.9 %collective-permute-start.81 = (bf16[256,2048]{1,0:T(8,128)(2,1)S(1)}, bf16[256,2048]{1,0:T(8,128)(2,1)S(1)}, u32[]{:S(2)}, u32[]{:S(2)}) collective-permute-start(bf16[256,2048]{1,0:T(8,128)(2,1)S(1)} %fusion.13), channel_id=1, source_target_pairs={{0,1},{1,3},{3,5},{5,7},{7,6},{6,4},{4,2},{2,0},{8,9},{9,11},{11,1... | collective-permute-start | bytes 3145736 | tf_op jit(solution)/shard_map/ppermute | solution.py:75
  761.8 58.8 %collective-permute-start.88 = (bf16[512,768]{1,0:T(8,128)(2,1)}, bf16[512,768]{1,0:T(8,128)(2,1)}, u32[]{:S(2)}, u32[]{:S(2)}) collective-permute-start(bf16[512,768]{1,0:T(8,128)(2,1)} %get-tuple-element.142), channel_id=1, source_target_pairs={{0,8},{8,0},{16,24},{24,16},{1,9},{9,1},{17,25},{25,17},{2,10},{10... | collective-permute-start | bytes 2359304 | tf_op jit(solution)/shard_map/ppermute | solution.py:35
  763.5 58.8 %collective-permute-start.90 = (bf16[512,768]{1,0:T(8,128)(2,1)}, bf16[512,768]{1,0:T(8,128)(2,1)}, u32[]{:S(2)}, u32[]{:S(2)}) collective-permute-start(bf16[512,768]{1,0:T(8,128)(2,1)} %add_convert_fusion.6), channel_id=1, source_target_pairs={{0,16},{8,24},{16,0},{24,8},{1,17},{9,25},{17,1},{25,9},{2,18},{10... | collective-permute-start | bytes 2359304 | tf_op jit(solution)/shard_map/ppermute | solution.py:35
  783.1 57.4 %collective-permute-start.86 = (bf16[256,2048]{1,0:T(8,128)(2,1)}, bf16[256,2048]{1,0:T(8,128)(2,1)}, u32[]{:S(2)}, u32[]{:S(2)}) collective-permute-start(bf16[256,2048]{1,0:T(8,128)(2,1)} %fusion.15), channel_id=1, source_target_pairs={{1,0},{3,1},{5,3},{7,5},{6,7},{4,6},{2,4},{0,2},{9,8},{11,9},{13,1... | collective-permute-start | bytes 3145736 | tf_op jit(solution)/shard_map/ppermute | solution.py:78
  785.5 75.5 %collective-permute-start.82 = (bf16[256,2048]{1,0:T(8,128)(2,1)}, bf16[256,2048]{1,0:T(8,128)(2,1)}, u32[]{:S(2)}, u32[]{:S(2)}) collective-permute-start(bf16[256,2048]{1,0:T(8,128)(2,1)} %fusion.12), channel_id=1, source_target_pairs={{0,1},{1,3},{3,5},{5,7},{7,6},{6,4},{4,2},{2,0},{8,9},{9,11},{11,1... | collective-permute-start | bytes 3145736 | tf_op jit(solution)/shard_map/ppermute | solution.py:75
  824.9 42.1 %all-to-all-start.3 = ((bf16[8,64,768]{2,1,0:T(8,128)(2,1)}), bf16[8,64,768]{2,1,0:T(8,128)(2,1)}, u32[]{:S(2)}, u32[]{:S(2)}) async-start(bf16[8,64,768]{2,1,0:T(8,128)(2,1)} %bitcast.286), calls=%async_computation.3 | async-start | bytes 1572864 | tf_op jit(solution)/shard_map/all_to_all | solution.py:596
  843.7 45.8 %collective-permute-start.87 = (bf16[256,2048]{1,0:T(8,128)(2,1)}, bf16[256,2048]{1,0:T(8,128)(2,1)}, u32[]{:S(2)}, u32[]{:S(2)}) collective-permute-start(bf16[256,2048]{1,0:T(8,128)(2,1)} %fusion.14), channel_id=1, source_target_pairs={{1,0},{3,1},{5,3},{7,5},{6,7},{4,6},{2,4},{0,2},{9,8},{11,9},{13,1... | collective-permute-start | bytes 3145736 | tf_op jit(solution)/shard_map/ppermute | solution.py:78
  855.5 30.6 %collective-permute-start.99 = (bf16[128,2048]{1,0:T(8,128)(2,1)}, bf16[128,2048]{1,0:T(8,128)(2,1)}, u32[]{:S(2)}, u32[]{:S(2)}) collective-permute-start(bf16[128,2048]{1,0:T(8,128)(2,1)} %fusion.47), channel_id=1, source_target_pairs={{1,0},{3,1},{5,3},{7,5},{6,7},{4,6},{2,4},{0,2},{9,8},{11,9},{13,1... | collective-permute-start | bytes 1572872 | tf_op jit(solution)/shard_map/ppermute | solution.py:78
  861.0 25.0 %collective-permute-start.95 = (bf16[128,2048]{1,0:T(8,128)(2,1)}, bf16[128,2048]{1,0:T(8,128)(2,1)}, u32[]{:S(2)}, u32[]{:S(2)}) collective-permute-start(bf16[128,2048]{1,0:T(8,128)(2,1)} %fusion.50), channel_id=1, source_target_pairs={{0,1},{1,3},{3,5},{5,7},{7,6},{6,4},{4,2},{2,0},{8,9},{9,11},{11,1... | collective-permute-start | bytes 1572872 | tf_op jit(solution)/shard_map/ppermute | solution.py:75
  864.3 29.5 %collective-permute-start.83 = (bf16[256,2048]{1,0:T(8,128)(2,1)}, bf16[256,2048]{1,0:T(8,128)(2,1)S(1)}, u32[]{:S(2)}, u32[]{:S(2)}) collective-permute-start(bf16[256,2048]{1,0:T(8,128)(2,1)} %fusion.11), channel_id=1, source_target_pairs={{0,1},{1,3},{3,5},{5,7},{7,6},{6,4},{4,2},{2,0},{8,9},{9,11},{11,1... | collective-permute-start | bytes 3145736 | tf_op jit(solution)/shard_map/ppermute | solution.py:75
  (205 other events, 2902.4 us)

commit v3 on v2

v3 whole, which is shorter than its diff:
```python
import math

import jax
import jax.numpy as jnp
from jax import lax
from jax.experimental import pallas as pl
from jax.experimental.pallas import tpu as pltpu
from jax.sharding import PartitionSpec as P

HEAD = 128
LEVELS = 4
EPSILON = 1e-06
ROPE_BASE = 500000.0
LOW = jnp.bfloat16
FULL = jnp.float32
NEG = -1e30
LOG2E = math.log2(math.e)
LIGHT = pl.CostEstimate(flops=1, bytes_accessed=1, transcendentals=0)
BLOCK = 512


def dot(left, right):
    return jnp.dot(left, right, preferred_element_type=FULL)


def dot_nt(left, right):
    return lax.dot_general(left, right, (((1,), (1,)), ((), ())), preferred_element_type=FULL)


def dot_tn(left, right):
    return lax.dot_general(left, right, (((0,), (0,)), ((), ())), preferred_element_type=FULL)


def swap(val, axis, mask):
    size = lax.axis_size(axis)
    return lax.ppermute(val, axis, [(i, i ^ mask) for i in range(size)])


def swap_all(val, mask):
    size = lax.axis_size("dp") * lax.axis_size("seq")
    return lax.ppermute(val, ("dp", "seq"), [(i, i ^ mask) for i in range(size)])


def tie(*vals):
    return lax.optimization_barrier(vals)


def bits_of(size):
    return [1 << i for i in range(size.bit_length() - 1)]


def sum_over(val, axis, size):
    for bit in bits_of(size):
        val = val + swap(val, axis, bit)
    return val


class Ring:
    def __init__(self, cycles):
        self.size = len(cycles[0])
        self.forth = [(c[i], c[(i + 1) % self.size]) for c in cycles for i in range(self.size)]
        self.back = [(b, a) for a, b in self.forth]
        total = self.size * len(cycles)
        owners = [[0] * self.size for _ in range(total)]
        for c in cycles:
            for i, dev in enumerate(c):
                for off in range(self.size):
                    owners[dev][off] = c[(i + off) % self.size]
        self.owners = owners

    def owner(self, offset):
        at = lax.axis_index("seq")
        found = jnp.int32(self.owners[0][offset % self.size])
        for dev, row in enumerate(self.owners[1:], 1):
            found = lax.select(at == dev, jnp.int32(row[offset % self.size]), found)
        return found

    def right(self, val):
        return lax.ppermute(val, "seq", self.forth)

    def left(self, val):
        return lax.ppermute(val, "seq", self.back)

    def gather(self, own, state=None, between=None):
        half = self.size // 2
        chunks = {0: own}
        r = l = own
        for k in range(1, half):
            names = between(k) if between else ()
            r, l = self.right(r), self.left(l)
            if names:
                r, l, *beside = tie(r, l, *(state[n] for n in names))
                state |= dict(zip(names, beside))
            chunks[-k], chunks[k] = r, l
        mid = own.shape[0] // 2
        chunks[half] = jnp.concatenate([self.right(r[:mid]), self.left(l[mid:])], axis=0)
        return chunks

    def scatter_steps(self, part, hold=lax.optimization_barrier):
        half = self.size // 2
        far = part(half).astype(LOW)
        mid = far.shape[0] // 2
        r, l = yield far[:mid], far[mid:]
        r, l = self.right(r), self.left(l)
        zero = jnp.zeros((), LOW)
        r = lax.pad(r, zero, ((0, mid, 0), (0, 0, 0)))
        l = lax.pad(l, zero, ((mid, 0, 0), (0, 0, 0)))
        for k in range(half - 1, 0, -1):
            a = hold(part(k)) + r.astype(FULL)
            b = hold(part(-k)) + l.astype(FULL)
            r, l = yield a.astype(LOW), b.astype(LOW)
            r, l = self.right(r), self.left(l)
        return hold(part(0)) + r.astype(FULL) + l.astype(FULL)

    def scatter(self, part, hook=None):
        return finish(self.scatter_steps(part), hook)


def finish(steps, hook=None, sent=None, step=0):
    try:
        sent = next(steps) if sent is None else sent
        while True:
            sent = steps.send(hook(step, sent) if hook else sent)
            step += 1
    except StopIteration as end:
        return end.value


def row_cycle(size):
    if size % LEVELS or size == LEVELS:
        return list(range(size))
    cols = size // LEVELS
    walk = [(0, 0)]
    for z in range(LEVELS):
        span = list(range(1, cols))
        walk += [(z, x) for x in (span if z % 2 == 0 else span[::-1])]
    walk += [(z, 0) for z in range(LEVELS - 1, 0, -1)]
    return [z * cols + x for z, x in walk]


def data_bits(size):
    return [b for b in bits_of(size) if b != 1] + [1]


def swap_chips(shard, bits):
    copies = {0: shard}
    for bit in bits:
        copies |= {mask ^ bit: swap(val, "dp", bit) for mask, val in copies.items()}
    return copies


def swap_cores(copies):
    return copies | {mask ^ 1: swap(val, "dp", 1) for mask, val in copies.items()}


def assemble_kernel(plan, at_ref, *refs):
    out_ref, sems = refs[-2], refs[-1]
    copies = []
    for i, (source, row, rows) in enumerate(plan):
        cols = refs[source].shape[1]
        place = (
            pl.ds(pl.multiple_of(at_ref[2 * i], 16), rows),
            pl.ds(pl.multiple_of(at_ref[2 * i + 1], 128), cols),
        )
        copies.append(
            pltpu.make_async_copy(refs[source].at[pl.ds(row, rows), :], out_ref.at[place], sems.at[i])
        )
    for copy in copies:
        copy.start()
    for copy in copies:
        copy.wait()


def assemble(shape, pieces):
    arrays, plan, at = [], [], []
    for val, row, rows, to_row, to_col in pieces:
        known = [i for i, a in enumerate(arrays) if a is val]
        if not known:
            arrays.append(val)
        plan.append((known[0] if known else len(arrays) - 1, row, rows))
        at += [to_row, to_col]
    at = jnp.stack([jnp.asarray(a, jnp.int32) for a in at])
    return pl.pallas_call(
        lambda at_ref, *refs: assemble_kernel(plan, at_ref, *refs),
        grid_spec=pltpu.PrefetchScalarGridSpec(
            num_scalar_prefetch=1,
            grid=(1,),
            in_specs=[pl.BlockSpec(memory_space=pl.ANY)] * len(arrays),
            out_specs=pl.BlockSpec(shape, lambda i, at: (0, 0)),
            scratch_shapes=[pltpu.SemaphoreType.DMA((len(plan),))],
        ),
        out_shape=jax.ShapeDtypeStruct(shape, LOW),
        compiler_params=pltpu.CompilerParams(vmem_limit_bytes=40 * 2**20),
        cost_estimate=pl.CostEstimate(flops=0, bytes_accessed=4 * shape[0] * shape[1], transcendentals=0),
        name="assemble",
    )(at, *arrays)


def place_over_data(copies, axis=0, shift=0):
    me = lax.axis_index("dp")
    pieces = []
    for mask, val in copies.items():
        at = [shift, shift]
        at[axis] = (me ^ mask) * val.shape[axis]
        pieces.append((val, 0, val.shape[0], at[0], at[1]))
    return pieces


def blocks_over_data(val, axis):
    size = lax.axis_size("dp")
    part = val.shape[axis] // size
    return [
        lax.dynamic_slice_in_dim(val, (lax.axis_index("dp") ^ m) * part, part, axis) for m in range(size)
    ]


def scatter_over_data(blocks):
    order = data_bits(len(blocks))[::-1]
    blocks = dict(enumerate(blocks))
    for bit in order[:-1]:
        out = {}
        for m in [m for m in blocks if not m & bit]:
            out[m] = (blocks[m].astype(FULL) + swap(blocks[m ^ bit], "dp", bit).astype(FULL)).astype(LOW)
        blocks = out
    return blocks[0], blocks[order[-1]]


def last_over_data(sent):
    return swap(sent, "dp", data_bits(lax.axis_size("dp"))[0])


def gain_step(val, bit):
    me = lax.axis_index("dp") * lax.axis_size("seq") + lax.axis_index("seq")
    got = swap_all(val, bit)
    upper = (me // bit) % 2 == 1
    return jnp.concatenate([jnp.where(upper, got, val), jnp.where(upper, val, got)], axis=0)


def gather_output_weights(row_ring, state, between, chips):
    seq = lax.axis_size("seq")
    me = lax.axis_index("dp")
    rows, width = state["w_out"].shape
    chunks = row_ring.gather(state["w_out"], state, between)
    half = row_ring.size // 2
    groups = [[0, 1, -1]] + [[k, -k] for k in range(2, half)] + [[half]]
    pieces = []
    for group in groups:
        val = jnp.concatenate([chunks[o] for o in group])
        for mask, block in swap_cores(swap_chips(val, chips)).items():
            for i, o in enumerate(group):
                to = ((me ^ mask) * seq + row_ring.owner(o)) * rows
                pieces.append((block, i * rows, rows, to, 0))
    return assemble((width, width), pieces)


def output_grad_steps(part, row_ring):
    data, seq = lax.axis_size("dp"), lax.axis_size("seq")
    me = lax.axis_index("dp")
    tall = data // 2
    width = part.shape[1]
    rows = part.shape[0] // (data * seq)
    part = part.reshape(tall, 2, seq, rows, width)
    kept = lax.dynamic_index_in_dim(part, me % 2, 1, False)
    sent = lax.dynamic_index_in_dim(part, 1 - me % 2, 1, False)
    kept = (kept.astype(FULL) + swap(sent, "dp", 1).astype(FULL)).astype(LOW)

    def block(offset):
        one = lax.dynamic_index_in_dim(kept, row_ring.owner(offset), 1, False)
        return one.reshape(tall * rows, width).astype(FULL)

    return row_ring.scatter_steps(block, lambda val: val)


def finish_output_grad(val):
    data = lax.axis_size("dp")
    me = lax.axis_index("dp")
    val = val.reshape(data // 2, -1, val.shape[1])
    _, rows, width = val.shape
    for bit in data_bits(data)[:-1][::-1]:
        upper = (me // bit) % 2
        val = val.reshape(2, val.shape[0] // 2, rows, width)
        kept = lax.dynamic_index_in_dim(val, upper, 0, False)
        sent = lax.dynamic_index_in_dim(val, 1 - upper, 0, False)
        val = kept + swap(sent, "dp", bit)
    return val.reshape(rows, width)


def rms_scale(vals):
    return lax.rsqrt(jnp.mean(vals * vals, axis=-1, keepdims=True) + EPSILON)


def norm_back(grad_out, pre, scale, gain):
    weighted = grad_out * gain
    inner = jnp.mean(weighted * pre, axis=-1, keepdims=True)
    grad_pre = scale * weighted - pre * (scale * scale * scale) * inner
    grad_gain = jnp.sum(grad_out * pre * scale, axis=0)
    return (grad_pre, grad_gain)


def rope_tables(positions):
    half = HEAD // 2
    freq = ROPE_BASE ** (-2.0 * jnp.arange(half, dtype=FULL) / HEAD)
    angle = positions.astype(FULL)[:, None] * freq[None, :]
    cosine, sine = jnp.cos(angle), jnp.sin(angle)
    return jnp.concatenate([cosine, cosine], 1), jnp.concatenate([-sine, sine], 1)


def layout(lengths, placement, row_len):
    stored, docs = lengths.shape
    rows = jnp.arange(placement.shape[0], dtype=jnp.int32)
    row = jnp.sum(jnp.where(rows == lax.axis_index("dp"), placement, 0))
    doc_lens = jnp.sum(
        jnp.where(jnp.arange(stored, dtype=jnp.int32)[:, None] == row, lengths, 0), axis=0
    )
    upto = jnp.arange(docs, dtype=jnp.int32)
    doc_ends = jnp.sum(jnp.where(upto[None, :] <= upto[:, None], doc_lens[None, :], 0), axis=1)
    at = jnp.arange(row_len, dtype=jnp.int32)
    passed = at[:, None] >= doc_ends[None, :]
    return jnp.max(jnp.where(passed, doc_ends[None, :], 0), axis=1)


def column(row):
    return jnp.broadcast_to(row, (HEAD, row.shape[1])).T

def attend_forward_kernel(first_ref, q_ref, k_ref, v_ref, scale_ref, gain_ref, cos_ref, sin_ref, begin_ref,
                          out_ref, qr_ref, kr_ref, vl_ref, lse_ref, vt_ref):
    blocks = q_ref.shape[0] // BLOCK
    factor = HEAD ** -0.5 * LOG2E

    def prepare(i, _):
        rows = pl.ds(pl.multiple_of(i * BLOCK, BLOCK), BLOCK)
        for n, (src, dst) in enumerate(((q_ref, qr_ref), (k_ref, kr_ref))):
            x = src[rows, :] * column(scale_ref[n : n + 1, rows]) * gain_ref[n : n + 1, :]
            x = x * cos_ref[rows, :] + pltpu.roll(x, HEAD // 2, 1) * sin_ref[rows, :]
            dst[rows, :] = x.astype(LOW)
        v = v_ref[rows, :].astype(LOW)
        vl_ref[rows, :] = v
        vt_ref[:, rows] = v.T
        return 0

    lax.fori_loop(0, blocks, prepare, 0)

    def one(i, _):
        rows = pl.ds(pl.multiple_of(i * BLOCK, BLOCK), BLOCK)
        q = qr_ref[rows, :]
        begin = begin_ref[0:1, rows]
        at = lax.broadcasted_iota(jnp.int32, (BLOCK, BLOCK), 0)
        query_at = lax.broadcasted_iota(jnp.int32, (1, BLOCK), 1) + i * BLOCK

        def step(j, carry):
            top, total, acc = carry
            keys = pl.ds(pl.multiple_of(j * BLOCK, BLOCK), BLOCK)
            s = dot_nt(kr_ref[keys, :], q)
            key_at = at + j * BLOCK
            s = jnp.where((key_at >= begin) & (key_at <= query_at), s, NEG)
            new = jnp.maximum(top, jnp.max(s, axis=0, keepdims=True))
            p = jnp.exp2((s - new) * factor)
            shrink = jnp.exp2((top - new) * factor)
            total = total * shrink + jnp.sum(p, axis=0, keepdims=True)
            acc = acc * shrink + dot(vt_ref[:, keys], p.astype(LOW))
            return new, total, acc

        start = (jnp.full((1, BLOCK), NEG, FULL), jnp.zeros((1, BLOCK), FULL), jnp.zeros((HEAD, BLOCK), FULL))
        top, total, acc = lax.fori_loop(first_ref[i], i + 1, step, start)
        out_ref[rows, :] = (acc / total).T.astype(LOW)
        lse_ref[0, 0:1, rows] = top * factor + jnp.log2(total)
        return 0

    lax.fori_loop(0, blocks, one, 0)


def attend_forward(pre, scales, gains, cosine, sine, first, begin):
    rows, wide = pre.shape
    heads = wide // (3 * HEAD)

    def col(shift):
        return pl.BlockSpec((rows, HEAD), lambda h, f: (0, h + shift))

    def fixed(*shape):
        return pl.BlockSpec(shape, lambda h, f: (0,) * len(shape))

    return pl.pallas_call(
        attend_forward_kernel,
        grid_spec=pltpu.PrefetchScalarGridSpec(
            num_scalar_prefetch=1,
            grid=(heads,),
            in_specs=[
                col(0),
                col(heads),
                col(2 * heads),
                fixed(2, rows),
                pl.BlockSpec((2, HEAD), lambda h, f: (0, h)),
                fixed(rows, HEAD),
                fixed(rows, HEAD),
                fixed(1, rows),
            ],
            out_specs=[col(0)] * 4 + [pl.BlockSpec((1, 1, rows), lambda h, f: (h, 0, 0))],
            scratch_shapes=[pltpu.VMEM((HEAD, rows), LOW)],
        ),
        out_shape=[jax.ShapeDtypeStruct((rows, heads * HEAD), LOW)] * 4
        + [jax.ShapeDtypeStruct((heads, 1, rows), FULL)],
        compiler_params=pltpu.CompilerParams(vmem_limit_bytes=48 * 2**20),
        cost_estimate=LIGHT,
        name="attend_forward",
    )(first, pre, pre, pre, scales, gains, cosine, sine, begin)


def attend_backward_kernel(first_ref, q_ref, k_ref, v_ref, o_ref, do_ref, lse_ref, qp_ref, kp_ref, scale_ref, gain_ref, cos_ref, sin_ref, begin_ref,
                           gq_ref, gk_ref, gv_ref, inner_ref, gain_grad_ref, kt_ref, dk_ref, dv_ref):
    blocks = q_ref.shape[0] // BLOCK
    norm = HEAD ** -0.5
    factor = norm * LOG2E

    def prepare(i, _):
        rows = pl.ds(pl.multiple_of(i * BLOCK, BLOCK), BLOCK)
        kt_ref[:, rows] = k_ref[rows, :].T
        dk_ref[rows, :] = jnp.zeros((BLOCK, HEAD), FULL)
        dv_ref[rows, :] = jnp.zeros((BLOCK, HEAD), FULL)
        return 0

    lax.fori_loop(0, blocks, prepare, 0)

    def finish(rows, n, grad, pre_ref, out):
        grad = grad.astype(LOW).astype(FULL)
        grad = grad * cos_ref[rows, :] - pltpu.roll(grad, HEAD // 2, 1) * sin_ref[rows, :]
        weighted = grad * gain_ref[n : n + 1, :]
        pre = pre_ref[rows, :]
        out[rows, :] = weighted
        inner_ref[0, n : n + 1, rows] = jnp.sum((weighted * pre).T, axis=0, keepdims=True)
        return jnp.sum(grad * pre * column(scale_ref[n : n + 1, rows]), axis=0, keepdims=True)

    def one(i, gain_grad):
        rows = pl.ds(pl.multiple_of(i * BLOCK, BLOCK), BLOCK)
        q = q_ref[rows, :]
        do = do_ref[rows, :]
        begin = begin_ref[0:1, rows]
        lse = lse_ref[0, 0:1, rows]
        delta = jnp.sum((do.astype(FULL) * o_ref[rows, :].astype(FULL)).T, axis=0, keepdims=True)
        at = lax.broadcasted_iota(jnp.int32, (BLOCK, BLOCK), 0)
        query_at = lax.broadcasted_iota(jnp.int32, (1, BLOCK), 1) + i * BLOCK

        def step(j, acc):
            keys = pl.ds(pl.multiple_of(j * BLOCK, BLOCK), BLOCK)
            s = dot_nt(k_ref[keys, :], q)
            key_at = at + j * BLOCK
            s = jnp.where((key_at >= begin) & (key_at <= query_at), s, NEG)
            p = jnp.exp2(s * factor - lse)
            dp = dot_nt(v_ref[keys, :], do)
            ds = (p * (dp - delta)).astype(LOW)
            dv_ref[keys, :] += dot(p.astype(LOW), do)
            dk_ref[keys, :] += dot(ds, q)
            return acc + dot(kt_ref[:, keys], ds)

        acc = lax.fori_loop(first_ref[i], i + 1, step, jnp.zeros((HEAD, BLOCK), FULL))
        return gain_grad + finish(rows, 0, acc.T * norm, qp_ref, gq_ref)

    gain_grad_ref[0:1, :] = lax.fori_loop(0, blocks, one, jnp.zeros((1, HEAD), FULL))

    def close(i, gain_grad):
        rows = pl.ds(pl.multiple_of(i * BLOCK, BLOCK), BLOCK)
        gv_ref[rows, :] = dv_ref[rows, :].astype(LOW)
        return gain_grad + finish(rows, 1, dk_ref[rows, :] * norm, kp_ref, gk_ref)

    gain_grad_ref[1:2, :] = lax.fori_loop(0, blocks, close, jnp.zeros((1, HEAD), FULL))


def attend_backward(head, q, k, v, out, grad, lse, pre, scales, gains, cosine, sine, first, begin):
    rows = q.shape[0]
    heads = pre.shape[1] // (3 * HEAD)

    def col(shift):
        return pl.BlockSpec((rows, HEAD), lambda i, f: (0, shift))

    def fixed(*shape):
        return pl.BlockSpec(shape, lambda i, f: (0,) * len(shape))

    full = jax.ShapeDtypeStruct((rows, HEAD), FULL)
    return pl.pallas_call(
        attend_backward_kernel,
        grid_spec=pltpu.PrefetchScalarGridSpec(
            num_scalar_prefetch=1,
            grid=(1,),
            in_specs=[col(head)] * 5
            + [
                pl.BlockSpec((1, 1, rows), lambda i, f: (head, 0, 0)),
                col(head),
                col(heads + head),
                fixed(2, rows),
                pl.BlockSpec((2, HEAD), lambda i, f: (0, head)),
                fixed(rows, HEAD),
                fixed(rows, HEAD),
                fixed(1, rows),
            ],
            out_specs=[fixed(rows, HEAD)] * 3 + [fixed(1, 2, rows), fixed(2, HEAD)],
            scratch_shapes=[
                pltpu.VMEM((HEAD, rows), LOW),
                pltpu.VMEM((rows, HEAD), FULL),
                pltpu.VMEM((rows, HEAD), FULL),
            ],
        ),
        out_shape=[
            full,
            full,
            jax.ShapeDtypeStruct((rows, HEAD), LOW),
            jax.ShapeDtypeStruct((1, 2, rows), FULL),
            jax.ShapeDtypeStruct((2, HEAD), FULL),
        ],
        compiler_params=pltpu.CompilerParams(vmem_limit_bytes=48 * 2**20),
        cost_estimate=LIGHT,
        name="attend_backward",
    )(first, q, k, v, out, grad, lse, pre, pre, scales, gains, cosine, sine, begin)


def per_device(
    tokens,
    cotangent,
    lengths,
    placement,
    w_query,
    w_key,
    w_value,
    w_output,
    query_gain,
    key_gain,
    attn_gain,
    w_gate,
    w_up,
    w_down,
    mlp_gain,
):
    data, seq = lax.axis_size("dp"), lax.axis_size("seq")
    seq_at = lax.axis_index("seq")
    _, count, width = tokens.shape
    row_len = count * seq
    own = width // seq
    row_ring = Ring([row_cycle(seq)])
    inputs = tokens.reshape(count, width)
    begin = layout(lengths, placement, row_len)

    packed = jnp.stack([w_query, w_key, w_value], axis=1).reshape(-1, 3, seq, own)
    packed = jnp.moveaxis(packed, 2, 0).reshape(seq, -1, 3 * own)
    hid = w_gate.shape[1]
    chips = data_bits(data)[:-1]
    state = {"gains": jnp.stack([query_gain, key_gain, attn_gain, mlp_gain])[None]}
    gain_bits = bits_of(data * seq)

    def more_gains():
        if gain_bits:
            state["gains"] = gain_step(state["gains"], gain_bits.pop(0))

    def beside(step):
        more_gains()
        if step == 1:
            state["down"] = swap_chips(w_down, chips)
            state["w_heads"] = lax.all_to_all(packed, "seq", split_axis=0, concat_axis=0, tiled=True)
            return ["gains"]
        if step == 2:
            state["gate"] = swap_chips(w_gate, chips)
            return ["gains", "w_heads", "down", "gate", "begin"]
        if step == 3:
            state["w_heads"] = swap_chips(state["w_heads"].reshape(-1, 3 * own), chips)
            state["w_out"], state["up"] = w_output, w_up
            return ["gains", "w_heads", "w_out", "up"]
        return ["gains"]

    state["begin"] = begin
    row_chunks = row_ring.gather(inputs, state, beside)
    begin = state["begin"]
    first_block = begin[::BLOCK] // BLOCK
    cosine, sine = rope_tables(jnp.arange(row_len, dtype=jnp.int32) - begin)
    begin = begin[None]
    state["up"] = swap_chips(state["up"], chips)
    w_heads = assemble((width, 3 * own), place_over_data(swap_cores(state["w_heads"])))
    row_tokens = jnp.zeros((row_len, width), LOW)
    for offset, chunk in row_chunks.items():
        row_tokens = lax.dynamic_update_slice(row_tokens, chunk, (row_ring.owner(offset) * count, 0))
    pre = dot(row_tokens, w_heads)
    while gain_bits:
        more_gains()
    gains = jnp.moveaxis(state["gains"], 0, 1).reshape(4, -1).astype(FULL)
    gain_attn, gain_mlp = gains[2], gains[3]
    gains_own = lax.dynamic_slice(gains, (0, seq_at * own), (2, own))
    query_pre, key_pre = pre[:, :own], pre[:, own : 2 * own]
    squares = jnp.stack([jnp.sum(query_pre * query_pre, axis=1), jnp.sum(key_pre * key_pre, axis=1)])
    scales = lax.rsqrt(sum_over(squares, "seq", seq) / width + EPSILON)
    state["scales"] = scales

    def beside_output(step):
        if step == 3:
            state["attn"] = attend_forward(
                pre, state["scales"], gains_own, cosine, sine, first_block, begin
            )
            return ["attn"]
        return ["scales", "up"] if step == 2 else []

    w_out = gather_output_weights(row_ring, state, beside_output, chips)
    scales = state["scales"]
    attn_heads, query_rot, key_rot, values, log_sums = state["attn"]
    attn_tokens = lax.all_to_all(
        attn_heads.reshape(seq, count, own), "seq", split_axis=0, concat_axis=0, tiled=True
    )
    attn_tokens = jnp.moveaxis(attn_tokens, 0, 1).reshape(count, width)

    near, attn_rows = tie([state[n] for n in ("gate", "up", "down")], attn_tokens)
    near = [swap_cores(n) for n in near]
    gate_up = assemble((width, 2 * hid), place_over_data(near[0]) + place_over_data(near[1], 0, hid))
    down = assemble((hid, width), place_over_data(near[2], 1))
    attn_pre = dot(attn_tokens, w_out)
    attn_scale = rms_scale(attn_pre)
    middle = inputs.astype(FULL) + attn_pre * attn_scale * gain_attn
    middle_low = middle.astype(LOW)

    mids = row_ring.gather(middle_low)
    saved = {}

    def mlp_part(offset):
        offset = offset if offset in mids else -offset
        both = dot(mids[offset], gate_up)
        gate, up = both[:, :hid], both[:, hid:]
        hidden = (gate * jax.nn.sigmoid(gate) * up).astype(LOW)
        saved[offset] = gate, up, hidden
        return dot(hidden, down)

    mlp_pre = row_ring.scatter(mlp_part)
    mlp_scale = rms_scale(mlp_pre)
    layer_out = (middle + mlp_pre * mlp_scale * gain_mlp).astype(LOW).reshape(tokens.shape)
    grad_final = cotangent.reshape(count, width).astype(FULL)
    grad_mlp_pre, grad_gain_mlp = norm_back(grad_final, mlp_pre, mlp_scale, gain_mlp)
    grads = row_ring.gather(grad_mlp_pre.astype(LOW))
    grad_both = {}

    def middle_part(offset):
        gate, up, hidden = saved[offset]
        grad_hidden = dot_nt(grads[offset], down)
        sig = jax.nn.sigmoid(gate)
        grad_gate = grad_hidden * up * sig * (1.0 + gate * (1.0 - sig))
        grad_up = grad_hidden * gate * sig
        grad_both[offset] = grad_gate.astype(LOW), grad_up.astype(LOW)
        return dot_nt(jnp.concatenate(grad_both[offset], axis=1), gate_up)

    order = list(mids)
    ffn = {"mids": jnp.concatenate([mids[o] for o in order])}
    ffn["grads"] = jnp.concatenate([grads[o] for o in order])
    ffn["hidden"] = jnp.concatenate([saved[o][2] for o in order])

    half = row_ring.size // 2

    def beside_middle(step, sent):
        if step == half - 2:
            ffn["down"] = dot_tn(ffn["hidden"], ffn["grads"]).astype(LOW)
            sent, ffn["down"] = tie(sent, ffn["down"])
        if step == half - 1:
            rows = jnp.concatenate([grad_both[o][0] for o in order])
            ffn["gate"] = dot_tn(ffn["mids"], rows).astype(LOW)
            sent, ffn["gate"], ffn["down"] = tie(sent, ffn["gate"], ffn["down"])
        return sent

    middle_parts = {o: middle_part(o) for o in order}
    grad_middle = row_ring.scatter(lambda o: middle_parts[o], beside_middle)
    rows = jnp.concatenate([grad_both[o][1] for o in order])
    ffn["up"] = dot_tn(ffn["mids"], rows).astype(LOW)
    sums = {n: scatter_over_data(blocks_over_data(ffn[n], a)) for n, a in (("down", 1), ("gate", 0))}
    grad_middle, sums, ffn["up"] = tie(grad_middle, sums, ffn["up"])
    grad_middle = grad_final + grad_middle

    grad_attn_pre, grad_gain_attn = norm_back(grad_middle, attn_pre, attn_scale, gain_attn)
    grad_attn_low = grad_attn_pre.astype(LOW)
    grad_heads = dot_nt(grad_attn_low, w_out).astype(LOW)
    grad_heads, grad_attn_low = tie(grad_heads, grad_attn_low)
    grad_heads = jnp.moveaxis(grad_heads.reshape(count, seq, own), 1, 0)
    grad_heads = lax.all_to_all(grad_heads, "seq", split_axis=0, concat_axis=0, tiled=True)
    grad_heads = grad_heads.reshape(row_len, own)
    steps = output_grad_steps(dot_tn(attn_rows, grad_attn_low).astype(LOW), row_ring)
    sent = next(steps)
    sums["up"] = scatter_over_data(blocks_over_data(ffn["up"], 0))
    got = {n: last_over_data(sums[n][1]) for n in ("down", "gate")}
    grad_heads, sent, sums["up"] = tie(grad_heads, sent, sums["up"])
    got["up"] = last_over_data(sums["up"][1])
    sums = {n: val[0] for n, val in sums.items()}
    heads = []
    for head in range(own // HEAD):
        if head:
            sent = steps.send(sent)
            grad_heads, sent, *early = tie(grad_heads, sent, got["down"], got["gate"])
            got["down"], got["gate"] = early
        done = attend_backward(
            head,
            query_rot,
            key_rot,
            values,
            attn_heads,
            grad_heads,
            log_sums,
            pre,
            scales,
            gains_own,
            cosine,
            sine,
            first_block,
            begin,
        )
        heads.append(list(done))
    sent = steps.send(sent)
    weighted_q, weighted_k, grad_v = (
        jnp.concatenate([h[i] for h in heads], axis=1) for i in range(3)
    )
    inner = sum(h[3][0] for h in heads)
    inner, sent, got["up"] = tie(inner, sent, got["up"])
    gain_part = jnp.concatenate([h[4] for h in heads], axis=1)
    gain_part = lax.dynamic_update_slice(jnp.zeros((2, width), FULL), gain_part, (0, seq_at * own))
    inner = jnp.concatenate([inner, jnp.zeros((2, width - row_len), FULL)], axis=1)
    small = jnp.concatenate([inner, gain_part, grad_gain_attn[None], grad_gain_mlp[None]])
    small = sum_over(small, "seq", seq)
    inner, gain_sums = small[:2, :row_len], small[2:]
    last_sent = steps.send(sent)
    inner = inner * (scales**3) / width
    by_token = jnp.concatenate([scales, inner]).T
    grad_qp = by_token[:, 0:1] * weighted_q - by_token[:, 2:3] * query_pre
    grad_kp = by_token[:, 1:2] * weighted_k - by_token[:, 3:4] * key_pre
    grad_pre = jnp.concatenate([grad_qp.astype(LOW), grad_kp.astype(LOW), grad_v], axis=1)

    rest = {"pre": grad_pre, "output": last_sent, "sums": sums, "got": got}

    token_parts = dot_nt(grad_pre, w_heads).astype(LOW)

    def token_part(offset):
        start = row_ring.owner(offset) * count
        return lax.dynamic_slice_in_dim(token_parts, start, count, 0).astype(FULL)

    def beside_tokens(step, sent):
        names = ["pre"]
        if step == 1:
            names += ["sums", "got", "output"]
        if step == 2:
            rest["part"] = dot_tn(row_tokens, rest["pre"]).astype(LOW)
            names += ["part"]
        if step == 3:
            rest["part"] = scatter_over_data(blocks_over_data(rest["part"], 0))
            rest["part"] = rest["part"][0], last_over_data(rest["part"][1])
            names += ["part"]
        sent, *tied = tie(sent, *(rest[n] for n in names))
        rest.update(zip(names, tied))
        return sent

    grad_tokens = grad_middle + finish(
        row_ring.scatter_steps(token_part, lambda val: val), beside_tokens
    )
    grad_tokens = grad_tokens.astype(LOW).reshape(tokens.shape)
    gain_sums = sum_over(gain_sums, "dp", data)
    share = width // (data * seq)
    start = (lax.axis_index("dp") * seq + seq_at) * share
    gain_grads = lax.dynamic_slice(gain_sums, (0, start), (4, share))
    part = (rest["part"][0].astype(FULL) + rest["part"][1].astype(FULL)).astype(LOW)
    part = lax.all_to_all(
        part.reshape(seq, -1, 3 * own), "seq", split_axis=0, concat_axis=0, tiled=True
    ).astype(FULL)
    part = jnp.moveaxis(part.reshape(seq, -1, 3, own), 0, 2).reshape(-1, 3, width)
    sums, got = rest["sums"], rest["got"]
    grad_output = finish_output_grad(finish(steps, sent=rest["output"]))
    grad_down, grad_gate, grad_up = (
        sums[n].astype(FULL) + got[n].astype(FULL) for n in ("down", "gate", "up")
    )

    return (
        layer_out,
        grad_tokens,
        part[:, 0],
        part[:, 1],
        part[:, 2],
        grad_output,
        gain_grads[0],
        gain_grads[1],
        gain_grads[2],
        grad_gate,
        grad_up,
        grad_down,
        gain_grads[3],
    )


def solution(mesh):
    rows = P("dp", "seq", None)
    both = P(("dp", "seq"), None)
    flat = P(("dp", "seq"))
    return jax.shard_map(
        per_device,
        mesh=mesh,
        in_specs=(rows, rows, P(), P())
        + (both,) * 4
        + (flat,) * 3
        + (P("dp", "seq"), P("dp", "seq"), P("seq", "dp"), flat),
        out_specs=(rows, rows)
        + (both,) * 4
        + (flat,) * 3
        + (P("dp", "seq"), P("dp", "seq"), P("seq", "dp"), flat),
        check_vma=False,
    )
```

time: 911 us -> 875 us (0.960)
  local copies, waits for them, and re-layouts: 119 us -> 94.2 us
  between operations: 21.7 us -> 3.26 us
  Pallas kernels: 41.8 us -> 59.9 us
  waiting for transfers between devices: 345 us -> 333 us
    ppermute x32, waiting for transfers between devices: 130 us -> 38.8 us  [left(): return lax.ppermute(val, 'seq', self.back)]
    ppermute x32, waiting for transfers between devices: 154 us -> 205 us  [right(): return lax.ppermute(val, 'seq', self.forth)]
    dynamic_update_slice x37 -> x7, local copies, waits for them, and re-layouts: 35.5 us -> 13 us  [per_device(): lax.dynamic_update_slice(row_tokens, chunk, (row_ring.owner(offset) * cou...]
    pallas_call x0 -> x4, Pallas kernels: none -> 16.8 us  [assemble(): pl.pallas_call(lambda at_ref, *refs: assemble_kernel(plan, at_ref, *refs)...]
    all_to_all x1, waiting for transfers between devices: 0.01 us -> 11.1 us  [per_device(): lax.all_to_all(part.reshape(seq, -1, 3 * own), 'seq', split_axis=0, conca...]
    unnamed x296 -> x250, local copies, waits for them, and re-layouts: 38.6 us -> 48.3 us
    ppermute x32, starting transfers between devices: 43 us -> 33.7 us  [left(): return lax.ppermute(val, 'seq', self.back)]
    ppermute x10 -> x5, waiting for transfers between devices: 15.7 us -> 24.8 us  [swap_all(): lax.ppermute(val, ('dp', 'seq'), [(i, i ^ mask) for i in range(size)])]
  transfers between devices with their start and end apart: 116 -> 119, of which waited for: 56 -> 58; matrix products, arithmetic and copies ran while one was open for 36% -> 31% of each run, Pallas kernels for 5% -> 7%
where the time goes in v3:
time: 875 us; the launch traced here: 866 us
  waiting for transfers between devices  333 us (38%)
  matrix products  159 us (18%)
  starting transfers between devices  135 us (15%)
  local copies, waits for them, and re-layouts  94.2 us (11%)
  other arithmetic  82.1 us (9%)
  Pallas kernels  59.9 us (7%)
    ppermute x32, waiting for transfers between devices, right(): return lax.ppermute(val, 'seq', self.forth)  205 us
    dot_general x18, matrix products, dot_nt(): lax.dot_general(left, right, (((1,), (1,)), ((), ())), preferred_element_...  57 us
    dot_general x18, matrix products, dot(): return jnp.dot(left, right, preferred_element_type=FULL)  54.7 us
    unnamed x250, local copies, waits for them, and re-layouts  48.3 us
    dot_general x5, matrix products, dot_tn(): lax.dot_general(left, right, (((0,), (0,)), ((), ())), preferred_element_...  47.5 us
    ppermute x32, starting transfers between devices, right(): return lax.ppermute(val, 'seq', self.forth)  43.9 us
    ppermute x46, waiting for transfers between devices, swap(): return lax.ppermute(val, axis, [(i, i ^ mask) for i in range(size)])  43.1 us
    ppermute x32, waiting for transfers between devices, left(): return lax.ppermute(val, 'seq', self.back)  38.8 us
  transfers between devices with their start and end apart: 119, of which 58 were waited for; matrix products, arithmetic and copies ran while one was open for 31% of the time, Pallas kernels for 7%

profile of v3, /device:TPU:0, one launch (start us, length us, event | category | flops | bytes accessed | tf_op | source)
XLA Modules:
  0.0 866.0 jit_solution(13926281822950487321)
XLA Ops:
  17.1 4.9 all-to-all-start
  25.6 4.3 broadcast_in_dim.73
  40.0 22.3 %collective-permute-done.5 = bf16[2,4,64]{2,1,0:T(4,128)(2,1)S(1)} collective-permute-done((bf16[2,4,64]{2,1,0:T(4,128)(2,1)S(1)}, bf16[2,4,64]{2,1,0:T(4,128)(2,1)S(1)}, u32[]{:S(2)}, u32[]{:S(2)}) %collective-permute-start.5) | collective-permute-done | bytes 1056 | tf_op jit(solution)/shard_map/ppermute | solution.py:41
  62.4 6.0 collective-permute-done.6.refs_1_
  87.8 7.1 collective-permute-done.8
  105.6 5.4 collective-permute-done.17
  114.8 11.8 %fusion.84.q_ref.k_ref.v_ref.qp_ref.kp_ref = f32[2048,768]{1,0:T(8,128)} fusion(bf16[2048,2048]{1,0:T(8,128)(2,1)} %maximum_dynamic-update-slice_fusion, bf16[2048,768]{1,0:T(8,128)(2,1)S(1)} %assemble.4), kind=kOutput, calls=%fused_computation.321 | convolution fusion | flops 6442450944 | bytes 17825792 | tf_op jit(solution)/shard_map/dot_general | solution.py:23
  149.2 17.3 %attend_forward.1 = (bf16[2048,256]{1,0:T(8,128)(2,1)S(1)}, bf16[2048,256]{1,0:T(8,128)(2,1)S(1)}, bf16[2048,256]{1,0:T(8,128)(2,1)S(1)}, bf16[2048,256]{1,0:T(8,128)(2,1)S(1)}, f32[2,1,2048]{2,1,0:T(1,128)S(1)}) custom-call(s32[4]{0:T(128)S(1)} %and_select_fusion.first_ref, f32[2048,768]{1,0:T(8,128)} %fusion.84.q_ref.k_ref.v_ref.qp_ref.kp_ref, ...), custom_call_target="tpu_custom_call" | custom-call | flops 1 | bytes 1 | tf_op jit(solution)/shard_map/attend_forward/pallas_call | solution.py:382
  183.2 10.3 %collective-permute-done.37 = bf16[32,2048]{1,0:T(8,128)(2,1)S(1)} collective-permute-done((bf16[32,2048]{1,0:T(8,128)(2,1)S(1)}, bf16[32,2048]{1,0:T(8,128)(2,1)S(1)}, u32[]{:S(2)}, u32[]{:S(2)}) %collective-permute-start.37) | collective-permute-done | bytes 131104 | tf_op jit(solution)/shard_map/ppermute | solution.py:79
  200.5 7.9 collective-permute-done.34.refs_9_
  216.3 7.0 assemble.5
  224.4 6.1 multiply_reduce_fusion.3
  238.2 7.8 collective-permute-start.48
  246.5 7.1 assemble.6
  253.6 6.2 fusion.85
  259.8 9.2 %collective-permute-done.51 = bf16[256,2048]{1,0:T(8,128)(2,1)} collective-permute-done((bf16[256,2048]{1,0:T(8,128)(2,1)}, bf16[256,2048]{1,0:T(8,128)(2,1)}, u32[]{:S(2)}, u32[]{:S(2)}) %collective-permute-start.51) | collective-permute-done | bytes 1048608 | tf_op jit(solution)/shard_map/ppermute | solution.py:79
  285.4 8.7 collective-permute-done.52
  307.0 11.0 %collective-permute-done.53 = bf16[256,2048]{1,0:T(8,128)(2,1)S(1)} collective-permute-done((bf16[256,2048]{1,0:T(8,128)(2,1)}, bf16[256,2048]{1,0:T(8,128)(2,1)S(1)}, u32[]{:S(2)}, u32[]{:S(2)}) %collective-permute-start.53) | collective-permute-done | bytes 1048608 | tf_op jit(solution)/shard_map/ppermute | solution.py:79
  318.7 4.4 collective-permute-done.50
  344.3 7.0 collective-permute-done.56
  358.9 15.8 %collective-permute-done.57 = bf16[256,2048]{1,0:T(8,128)(2,1)S(1)} collective-permute-done((bf16[256,2048]{1,0:T(8,128)(2,1)S(1)}, bf16[256,2048]{1,0:T(8,128)(2,1)S(1)}, u32[]{:S(2)}, u32[]{:S(2)}) %collective-permute-start.57) | collective-permute-done | bytes 1048608 | tf_op jit(solution)/shard_map/ppermute | solution.py:79
  383.3 14.7 %collective-permute-done.58 = bf16[256,2048]{1,0:T(8,128)(2,1)S(1)} collective-permute-done((bf16[256,2048]{1,0:T(8,128)(2,1)S(1)}, bf16[256,2048]{1,0:T(8,128)(2,1)S(1)}, u32[]{:S(2)}, u32[]{:S(2)}) %collective-permute-start.58) | collective-permute-done | bytes 1048608 | tf_op jit(solution)/shard_map/ppermute | solution.py:79
  411.0 6.8 collective-permute-done.59
  431.4 11.3 %collective-permute-done.67 = bf16[256,2048]{1,0:T(8,128)(2,1)S(1)} collective-permute-done((bf16[256,2048]{1,0:T(8,128)(2,1)S(1)}, bf16[256,2048]{1,0:T(8,128)(2,1)S(1)}, u32[]{:S(2)}, u32[]{:S(2)}) %collective-permute-start.67) | collective-permute-done | bytes 1048608 | tf_op jit(solution)/shard_map/ppermute | solution.py:79
  462.8 8.1 collective-permute-done.68
  491.0 13.2 %collective-permute-done.69 = bf16[256,2048]{1,0:T(8,128)(2,1)S(1)} collective-permute-done((bf16[256,2048]{1,0:T(8,128)(2,1)S(1)}, bf16[256,2048]{1,0:T(8,128)(2,1)S(1)}, u32[]{:S(2)}, u32[]{:S(2)}) %collective-permute-start.69) | collective-permute-done | bytes 1048608 | tf_op jit(solution)/shard_map/ppermute | solution.py:79
  527.8 10.1 %collective-permute-done.72 = bf16[128,2048]{1,0:T(8,128)(2,1)S(1)} collective-permute-done((bf16[128,2048]{1,0:T(8,128)(2,1)S(1)}, bf16[128,2048]{1,0:T(8,128)(2,1)S(1)}, u32[]{:S(2)}, u32[]{:S(2)}) %collective-permute-start.72) | collective-permute-done | bytes 524320 | tf_op jit(solution)/shard_map/ppermute | solution.py:79
  541.7 11.9 %convolution_convert_fusion.2 = bf16[1024,2048]{1,0:T(8,128)(2,1)S(1)} fusion(bf16[2048,1024]{1,0:T(8,128)(2,1)S(1)} %copy-done.95, bf16[2048,2048]{1,0:T(8,128)(2,1)} %constant_dynamic-update-slice_fusion.17), kind=kOutput, calls=%fused_computation.5 | convolution fusion | flops 8592031744 | bytes 16777216 | tf_op jit(solution)/shard_map/dot_general | solution.py:31
  553.6 8.5 collective-permute-done.73
  562.5 4.8 collective-permute-done.75
  569.7 10.9 %convolution_convert_fusion.4 = bf16[2048,1024]{1,0:T(8,128)(2,1)} fusion(bf16[2048,2048]{1,0:T(8,128)(2,1)S(1)} %bitcast.287, bf16[2048,1024]{1,0:T(8,128)(2,1)S(1)} %copy-done.106), kind=kOutput, calls=%fused_computation.7 | convolution fusion | flops 8592031744 | bytes 16777216 | tf_op jit(solution)/shard_map/dot_general | solution.py:31
  585.4 6.2 fusion.19
  594.6 11.7 %convolution_convert_fusion.3 = bf16[2048,1024]{1,0:T(8,128)(2,1)S(1)} fusion(bf16[2048,2048]{1,0:T(8,128)(2,1)} %constant_dynamic-update-slice_fusion.26, bf16[2048,1024]{1,0:T(8,128)(2,1)S(1)} %copy-done.108), kind=kOutput, calls=%fused_computation.6 | convolution fusion | flops 8592031744 | bytes 16777216 | tf_op jit(solution)/shard_map/dot_general | solution.py:31
  635.3 4.5 all-to-all-start.2
  643.4 4.5 add_convert_fusion.7
  647.9 5.4 fusion
  656.1 10.3 %all-to-all-done.2 = bf16[8,256,256]{2,1,0:T(8,128)(2,1)} async-done(((bf16[8,256,256]{2,1,0:T(8,128)(2,1)}), bf16[8,256,256]{2,1,0:T(8,128)(2,1)}, u32[]{:S(2)}, u32[]{:S(2)}) %all-to-all-start.2) | async-done | bytes 1048608 | tf_op jit(solution)/shard_map/all_to_all | solution.py:671
  672.2 12.9 %attend_backward.2 = (f32[2048,128]{1,0:T(8,128)S(1)}, f32[2048,128]{1,0:T(8,128)S(1)}, bf16[2048,128]{1,0:T(8,128)(2,1)S(1)}, f32[1,2,2048]{2,1,0:T(2,128)S(1)}, f32[2,128]{1,0:T(2,128)S(1)}) custom-call(s32[4]{0:T(128)S(1)} %copy-done.35, bf16[2048,256]{1,0:T(8,128)(2,1)S(1)} %get-tuple-element.162.q_ref, bf16[2048,256]{1,0:T(8,128)(2,1)S(1)} %copy-done.3, ...), custom_call_target="tpu_custom_call" | custom-call | flops 1 | bytes 1 | tf_op jit(solution)/shard_map/attend_backward/pallas_call | solution.py:478
  690.6 12.9 %attend_backward.3 = (f32[2048,128]{1,0:T(8,128)S(1)}, f32[2048,128]{1,0:T(8,128)S(1)}, bf16[2048,128]{1,0:T(8,128)(2,1)S(1)}, f32[1,2,2048]{2,1,0:T(2,128)S(1)}, f32[2,128]{1,0:T(2,128)S(1)}) custom-call(s32[4]{0:T(128)S(1)} %copy-done.35, bf16[2048,256]{1,0:T(8,128)(2,1)S(1)} %get-tuple-element.162.q_ref, bf16[2048,256]{1,0:T(8,128)(2,1)S(1)} %copy-done.3, ...), custom_call_target="tpu_custom_call" | custom-call | flops 1 | bytes 1 | tf_op jit(solution)/shard_map/attend_backward/pallas_call | solution.py:478
  730.3 7.2 convolution_convert_fusion
  743.8 11.0 %collective-permute-done.97 = bf16[128,2048]{1,0:T(8,128)(2,1)S(1)} collective-permute-done((bf16[128,2048]{1,0:T(8,128)(2,1)S(1)}, bf16[128,2048]{1,0:T(8,128)(2,1)S(1)}, u32[]{:S(2)}, u32[]{:S(2)}) %collective-permute-start.97) | collective-permute-done | bytes 524320 | tf_op jit(solution)/shard_map/ppermute | solution.py:79
  758.6 9.4 %convolution_convert_fusion.5 = bf16[2048,768]{1,0:T(8,128)(2,1)S(1)} fusion(bf16[2048,2048]{1,0:T(8,128)(2,1)} %maximum_dynamic-update-slice_fusion, bf16[2048,768]{1,0:T(8,128)(2,1)S(1)} %pad_maximum_fusion), kind=kOutput, calls=%fused_computation.8 | convolution fusion | flops 6444023808 | bytes 14680064 | tf_op jit(solution)/shard_map/dot_general | solution.py:31
  773.0 9.7 %collective-permute-done.101 = bf16[256,2048]{1,0:T(8,128)(2,1)S(1)} collective-permute-done((bf16[256,2048]{1,0:T(8,128)(2,1)S(1)}, bf16[256,2048]{1,0:T(8,128)(2,1)S(1)}, u32[]{:S(2)}, u32[]{:S(2)}) %collective-permute-start.101) | collective-permute-done | bytes 1048608 | tf_op jit(solution)/shard_map/ppermute | solution.py:79
  788.0 5.7 collective-permute-done.110
  797.4 17.0 %collective-permute-done.103 = bf16[256,2048]{1,0:T(8,128)(2,1)S(1)} collective-permute-done((bf16[256,2048]{1,0:T(8,128)(2,1)S(1)}, bf16[256,2048]{1,0:T(8,128)(2,1)S(1)}, u32[]{:S(2)}, u32[]{:S(2)}) %collective-permute-start.103) | collective-permute-done | bytes 1048608 | tf_op jit(solution)/shard_map/ppermute | solution.py:79
  820.3 4.8 all-to-all-start.3
  830.3 13.1 %collective-permute-done.108 = bf16[256,2048]{1,0:T(8,128)(2,1)} collective-permute-done((bf16[256,2048]{1,0:T(8,128)(2,1)}, bf16[256,2048]{1,0:T(8,128)(2,1)}, u32[]{:S(2)}, u32[]{:S(2)}) %collective-permute-start.108) | collective-permute-done | bytes 1048608 | tf_op jit(solution)/shard_map/ppermute | solution.py:79
  847.1 11.1 %all-to-all-done.3 = bf16[8,64,768]{2,1,0:T(8,128)(2,1)} async-done(((bf16[8,64,768]{2,1,0:T(8,128)(2,1)}), bf16[8,64,768]{2,1,0:T(8,128)(2,1)}, u32[]{:S(2)}, u32[]{:S(2)}) %all-to-all-start.3) | async-done | bytes 786464 | tf_op jit(solution)/shard_map/all_to_all | solution.py:754
  (640 shorter events, 417.4 us)
Async XLA Ops:
  0.6 30.5 %collective-permute-start = (bf16[256,2048]{1,0:T(8,128)(2,1)}, bf16[256,2048]{1,0:T(8,128)(2,1)}, u32[]{:S(2)}, u32[]{:S(2)}) collective-permute-start(bf16[256,2048]{1,0:T(8,128)(2,1)} %bitcast.267), channel_id=1, source_target_pairs={{0,1},{1,3},{3,5},{5,7},{7,6},{6,4},{4,2},{2,0},{8,9},{9,11},{11,1... | collective-permute-start | bytes 3145736 | tf_op jit(solution)/shard_map/ppermute | solution.py:79
  3.6 27.5 %collective-permute-start.1 = (bf16[256,2048]{1,0:T(8,128)(2,1)}, bf16[256,2048]{1,0:T(8,128)(2,1)}, u32[]{:S(2)}, u32[]{:S(2)}) collective-permute-start(bf16[256,2048]{1,0:T(8,128)(2,1)} %bitcast.268), channel_id=1, source_target_pairs={{1,0},{3,1},{5,3},{7,5},{6,7},{4,6},{2,4},{0,2},{9,8},{11,9},{13,1... | collective-permute-start | bytes 3145736 | tf_op jit(solution)/shard_map/ppermute | solution.py:82
  4.5 26.5 %collective-permute-start.2 = (bf16[1,4,64]{2,1,0:T(4,128)(2,1)S(1)}, bf16[1,4,64]{2,1,0:T(4,128)(2,1)S(1)}, u32[]{:S(2)}, u32[]{:S(2)}) collective-permute-start(bf16[1,4,64]{2,1,0:T(4,128)(2,1)S(1)} %maximum_bitcast_fusion.2), channel_id=1, source_target_pairs={{0,1},{1,0},{2,3},{3,2},{4,5},{5,4},{6,7},{7,6},{8,9},{9,8},{10,11... | collective-permute-start | bytes 1544 | tf_op jit(solution)/shard_map/ppermute | solution.py:41
  17.1 51.3 %all-to-all-start = ((bf16[8,64,768]{2,1,0:T(8,128)(2,1)}), bf16[8,64,768]{2,1,0:T(8,128)(2,1)S(1)}, u32[]{:S(2)}, u32[]{:S(2)}) async-start(bf16[8,64,768]{2,1,0:T(8,128)(2,1)} %reshape.173), calls=%async_computation | async-start | bytes 1572864 | tf_op jit(solution)/shard_map/all_to_all | solution.py:555
  22.0 40.4 %collective-permute-start.7 = (bf16[512,1024]{1,0:T(8,128)(2,1)S(1)}, bf16[512,1024]{1,0:T(8,128)(2,1)}, u32[]{:S(2)}, u32[]{:S(2)}) collective-permute-start(bf16[512,1024]{1,0:T(8,128)(2,1)S(1)} %copy-done.9), channel_id=1, source_target_pairs={{0,16},{8,24},{16,0},{24,8},{1,17},{9,25},{17,1},{25,9},{2,18},{10... | collective-permute-start | bytes 3145736 | tf_op jit(solution)/shard_map/ppermute | solution.py:36
  23.6 44.8 %collective-permute-start.6 = (bf16[1024,512]{1,0:T(8,128)(2,1)S(1)}, bf16[1024,512]{1,0:T(8,128)(2,1)}, u32[]{:S(2)}, u32[]{:S(2)}) collective-permute-start(bf16[1024,512]{1,0:T(8,128)(2,1)S(1)} %copy-done.11), channel_id=1, source_target_pairs={{0,16},{8,24},{16,0},{24,8},{1,17},{9,25},{17,1},{25,9},{2,18},{10... | collective-permute-start | bytes 3145736 | tf_op jit(solution)/shard_map/ppermute | solution.py:36
  31.1 37.3 %collective-permute-start.3 = (bf16[256,2048]{1,0:T(8,128)(2,1)}, bf16[256,2048]{1,0:T(8,128)(2,1)}, u32[]{:S(2)}, u32[]{:S(2)}) collective-permute-start(bf16[256,2048]{1,0:T(8,128)(2,1)} %collective-permute-done), channel_id=1, source_target_pairs={{0,1},{1,3},{3,5},{5,7},{7,6},{6,4},{4,2},{2,0},{8,9},{9,11},{11,1... | collective-permute-start | bytes 3145736 | tf_op jit(solution)/shard_map/ppermute | solution.py:79
  33.1 35.3 %collective-permute-start.4 = (bf16[256,2048]{1,0:T(8,128)(2,1)}, bf16[256,2048]{1,0:T(8,128)(2,1)}, u32[]{:S(2)}, u32[]{:S(2)}) collective-permute-start(bf16[256,2048]{1,0:T(8,128)(2,1)} %collective-permute-done.1), channel_id=1, source_target_pairs={{1,0},{3,1},{5,3},{7,5},{6,7},{4,6},{2,4},{0,2},{9,8},{11,9},{13,1... | collective-permute-start | bytes 3145736 | tf_op jit(solution)/shard_map/ppermute | solution.py:82
  33.4 28.9 %collective-permute-start.5 = (bf16[2,4,64]{2,1,0:T(4,128)(2,1)S(1)}, bf16[2,4,64]{2,1,0:T(4,128)(2,1)S(1)}, u32[]{:S(2)}, u32[]{:S(2)}) collective-permute-start(bf16[2,4,64]{2,1,0:T(4,128)(2,1)S(1)} %pad_maximum_fusion.8), channel_id=1, source_target_pairs={{0,2},{1,3},{2,0},{3,1},{4,6},{5,7},{6,4},{7,5},{8,10},{9,11},{10,... | collective-permute-start | bytes 3080 | tf_op jit(solution)/shard_map/ppermute | solution.py:41
  105.0 28.9 %collective-permute-start.14 = (bf16[64,2048]{1,0:T(8,128)(2,1)S(1)}, bf16[64,2048]{1,0:T(8,128)(2,1)}, u32[]{:S(2)}, u32[]{:S(2)}) collective-permute-start(bf16[64,2048]{1,0:T(8,128)(2,1)S(1)} %copy-done.89), channel_id=1, source_target_pairs={{1,0},{3,1},{5,3},{7,5},{6,7},{4,6},{2,4},{0,2},{9,8},{11,9},{13,1... | collective-permute-start | bytes 786440 | tf_op jit(solution)/shard_map/ppermute | solution.py:82
  110.9 24.5 %collective-permute-start.12 = (bf16[64,2048]{1,0:T(8,128)(2,1)S(1)}, bf16[64,2048]{1,0:T(8,128)(2,1)}, u32[]{:S(2)}, u32[]{:S(2)}) collective-permute-start(bf16[64,2048]{1,0:T(8,128)(2,1)S(1)} %copy-done.89), channel_id=1, source_target_pairs={{0,1},{1,3},{3,5},{5,7},{7,6},{6,4},{4,2},{2,0},{8,9},{9,11},{11,1... | collective-permute-start | bytes 786440 | tf_op jit(solution)/shard_map/ppermute | solution.py:79
  112.4 30.8 %collective-permute-start.23 = (bf16[512,1024]{1,0:T(8,128)(2,1)}, bf16[512,1024]{1,0:T(8,128)(2,1)}, u32[]{:S(2)}, u32[]{:S(2)}) collective-permute-start(bf16[512,1024]{1,0:T(8,128)(2,1)} %refs_4_), channel_id=1, source_target_pairs={{0,16},{8,24},{16,0},{24,8},{1,17},{9,25},{17,1},{25,9},{2,18},{10... | collective-permute-start | bytes 3145736 | tf_op jit(solution)/shard_map/ppermute | solution.py:36
  143.2 25.3 %collective-permute-start.24 = (bf16[64,2048]{1,0:T(8,128)(2,1)S(1)}, bf16[64,2048]{1,0:T(8,128)(2,1)S(1)}, u32[]{:S(2)}, u32[]{:S(2)}) collective-permute-start(bf16[64,2048]{1,0:T(8,128)(2,1)S(1)} %collective-permute-done.13), channel_id=1, source_target_pairs={{0,1},{1,3},{3,5},{5,7},{7,6},{6,4},{4,2},{2,0},{8,9},{9,11},{11,1... | collective-permute-start | bytes 786440 | tf_op jit(solution)/shard_map/ppermute | solution.py:79
  143.2 26.0 %collective-permute-start.25 = (bf16[64,2048]{1,0:T(8,128)(2,1)S(1)}, bf16[64,2048]{1,0:T(8,128)(2,1)S(1)}, u32[]{:S(2)}, u32[]{:S(2)}) collective-permute-start(bf16[64,2048]{1,0:T(8,128)(2,1)S(1)} %collective-permute-done.15), channel_id=1, source_target_pairs={{1,0},{3,1},{5,3},{7,5},{6,7},{4,6},{2,4},{0,2},{9,8},{11,9},{13,1... | collective-permute-start | bytes 786440 | tf_op jit(solution)/shard_map/ppermute | solution.py:82
  146.9 50.1 %collective-permute-start.29 = (bf16[192,2048]{1,0:T(8,128)(2,1)}, bf16[192,2048]{1,0:T(8,128)(2,1)}, u32[]{:S(2)}, u32[]{:S(2)}) collective-permute-start(bf16[192,2048]{1,0:T(8,128)(2,1)} %constant_dynamic-update-slice_fusion.refs_0_), channel_id=1, source_target_pairs={{0,8},{8,0},{16,24},{24,16},{1,9},{9,1},{17,25},{25,17},{2,10},{10... | collective-permute-start | bytes 2359304 | tf_op jit(solution)/shard_map/ppermute | solution.py:36
  146.9 36.1 %collective-permute-start.28 = (bf16[192,2048]{1,0:T(8,128)(2,1)}, bf16[192,2048]{1,0:T(8,128)(2,1)}, u32[]{:S(2)}, u32[]{:S(2)}) collective-permute-start(bf16[192,2048]{1,0:T(8,128)(2,1)} %constant_dynamic-update-slice_fusion.refs_0_), channel_id=1, source_target_pairs={{0,16},{8,24},{16,0},{24,8},{1,17},{9,25},{17,1},{25,9},{2,18},{10... | collective-permute-start | bytes 2359304 | tf_op jit(solution)/shard_map/ppermute | solution.py:36
  171.2 52.1 %all-to-all-start.1 = ((bf16[8,256,256]{1,2,0:T(8,128)(2,1)}), bf16[8,256,256]{1,2,0:T(8,128)(2,1)}, u32[]{:S(2)}, u32[]{:S(2)}) async-start(bf16[8,256,256]{1,2,0:T(8,128)(2,1)} %copy.87), calls=%async_computation.1 | async-start | bytes 2097152 | tf_op jit(solution)/shard_map/all_to_all | solution.py:599
  175.8 22.7 %collective-permute-start.31 = (bf16[128,2048]{1,0:T(8,128)(2,1)S(1)}, bf16[128,2048]{1,0:T(8,128)(2,1)}, u32[]{:S(2)}, u32[]{:S(2)}) collective-permute-start(bf16[128,2048]{1,0:T(8,128)(2,1)S(1)} %constant_dynamic-update-slice_fusion.3.refs_4_), channel_id=1, source_target_pairs={{0,16},{8,24},{16,0},{24,8},{1,17},{9,25},{17,1},{25,9},{2,18},{10... | collective-permute-start | bytes 1572872 | tf_op jit(solution)/shard_map/ppermute | solution.py:36
  233.6 35.4 %collective-permute-start.51 = (bf16[256,2048]{1,0:T(8,128)(2,1)}, bf16[256,2048]{1,0:T(8,128)(2,1)}, u32[]{:S(2)}, u32[]{:S(2)}) collective-permute-start(bf16[256,2048]{1,0:T(8,128)(2,1)} %get-tuple-element.260), channel_id=1, source_target_pairs={{0,1},{1,3},{3,5},{5,7},{7,6},{6,4},{4,2},{2,0},{8,9},{9,11},{11,1... | collective-permute-start | bytes 3145736 | tf_op jit(solution)/shard_map/ppermute | solution.py:79
  238.2 35.9 %collective-permute-start.48 = (bf16[256,2048]{1,0:T(8,128)(2,1)}, bf16[256,2048]{1,0:T(8,128)(2,1)S(1)}, u32[]{:S(2)}, u32[]{:S(2)}) collective-permute-start(bf16[256,2048]{1,0:T(8,128)(2,1)} %get-tuple-element.260), channel_id=1, source_target_pairs={{1,0},{3,1},{5,3},{7,5},{6,7},{4,6},{2,4},{0,2},{9,8},{11,9},{13,1... | collective-permute-start | bytes 3145736 | tf_op jit(solution)/shard_map/ppermute | solution.py:82
  245.9 33.8 %collective-permute-start.46 = (bf16[1024,512]{1,0:T(8,128)(2,1)S(1)}, bf16[1024,512]{1,0:T(8,128)(2,1)S(1)}, u32[]{:S(2)}, u32[]{:S(2)}) collective-permute-start(bf16[1024,512]{1,0:T(8,128)(2,1)S(1)} %copy-done.12), channel_id=1, source_target_pairs={{0,8},{8,0},{16,24},{24,16},{1,9},{9,1},{17,25},{25,17},{2,10},{10... | collective-permute-start | bytes 3145736 | tf_op jit(solution)/shard_map/ppermute | solution.py:36
  245.9 33.8 %collective-permute-start.47 = (bf16[1024,512]{1,0:T(8,128)(2,1)}, bf16[1024,512]{1,0:T(8,128)(2,1)S(1)}, u32[]{:S(2)}, u32[]{:S(2)}) collective-permute-start(bf16[1024,512]{1,0:T(8,128)(2,1)} %collective-permute-done.6.refs_1_), channel_id=1, source_target_pairs={{0,8},{8,0},{16,24},{24,16},{1,9},{9,1},{17,25},{25,17},{2,10},{10... | collective-permute-start | bytes 3145736 | tf_op jit(solution)/shard_map/ppermute | solution.py:36
  269.0 25.0 %collective-permute-start.52 = (bf16[256,2048]{1,0:T(8,128)(2,1)}, bf16[256,2048]{1,0:T(8,128)(2,1)}, u32[]{:S(2)}, u32[]{:S(2)}) collective-permute-start(bf16[256,2048]{1,0:T(8,128)(2,1)} %collective-permute-done.51), channel_id=1, source_target_pairs={{0,1},{1,3},{3,5},{5,7},{7,6},{6,4},{4,2},{2,0},{8,9},{9,11},{11,1... | collective-permute-start | bytes 3145736 | tf_op jit(solution)/shard_map/ppermute | solution.py:79
  274.1 24.9 %collective-permute-start.49 = (bf16[256,2048]{1,0:T(8,128)(2,1)S(1)}, bf16[256,2048]{1,0:T(8,128)(2,1)}, u32[]{:S(2)}, u32[]{:S(2)}) collective-permute-start(bf16[256,2048]{1,0:T(8,128)(2,1)S(1)} %collective-permute-done.48), channel_id=1, source_target_pairs={{1,0},{3,1},{5,3},{7,5},{6,7},{4,6},{2,4},{0,2},{9,8},{11,9},{13,1... | collective-permute-start | bytes 3145736 | tf_op jit(solution)/shard_map/ppermute | solution.py:82
  294.0 24.0 %collective-permute-start.53 = (bf16[256,2048]{1,0:T(8,128)(2,1)}, bf16[256,2048]{1,0:T(8,128)(2,1)S(1)}, u32[]{:S(2)}, u32[]{:S(2)}) collective-permute-start(bf16[256,2048]{1,0:T(8,128)(2,1)} %collective-permute-done.52), channel_id=1, source_target_pairs={{0,1},{1,3},{3,5},{5,7},{7,6},{6,4},{4,2},{2,0},{8,9},{9,11},{11,1... | collective-permute-start | bytes 3145736 | tf_op jit(solution)/shard_map/ppermute | solution.py:79
  298.9 24.2 %collective-permute-start.50 = (bf16[256,2048]{1,0:T(8,128)(2,1)}, bf16[256,2048]{1,0:T(8,128)(2,1)S(1)}, u32[]{:S(2)}, u32[]{:S(2)}) collective-permute-start(bf16[256,2048]{1,0:T(8,128)(2,1)} %collective-permute-done.49), channel_id=1, source_target_pairs={{1,0},{3,1},{5,3},{7,5},{6,7},{4,6},{2,4},{0,2},{9,8},{11,9},{13,1... | collective-permute-start | bytes 3145736 | tf_op jit(solution)/shard_map/ppermute | solution.py:82
  351.5 23.2 %collective-permute-start.57 = (bf16[256,2048]{1,0:T(8,128)(2,1)S(1)}, bf16[256,2048]{1,0:T(8,128)(2,1)S(1)}, u32[]{:S(2)}, u32[]{:S(2)}) collective-permute-start(bf16[256,2048]{1,0:T(8,128)(2,1)S(1)} %add_convert_fusion.25), channel_id=1, source_target_pairs={{0,1},{1,3},{3,5},{5,7},{7,6},{6,4},{4,2},{2,0},{8,9},{9,11},{11,1... | collective-permute-start | bytes 3145736 | tf_op jit(solution)/shard_map/ppermute | solution.py:79
  355.8 23.0 %collective-permute-start.61 = (bf16[256,2048]{1,0:T(8,128)(2,1)S(1)}, bf16[256,2048]{1,0:T(8,128)(2,1)S(1)}, u32[]{:S(2)}, u32[]{:S(2)}) collective-permute-start(bf16[256,2048]{1,0:T(8,128)(2,1)S(1)} %add_convert_fusion.22), channel_id=1, source_target_pairs={{1,0},{3,1},{5,3},{7,5},{6,7},{4,6},{2,4},{0,2},{9,8},{11,9},{13,1... | collective-permute-start | bytes 3145736 | tf_op jit(solution)/shard_map/ppermute | solution.py:82
  375.1 23.0 %collective-permute-start.58 = (bf16[256,2048]{1,0:T(8,128)(2,1)S(1)}, bf16[256,2048]{1,0:T(8,128)(2,1)S(1)}, u32[]{:S(2)}, u32[]{:S(2)}) collective-permute-start(bf16[256,2048]{1,0:T(8,128)(2,1)S(1)} %add_convert_fusion.24), channel_id=1, source_target_pairs={{0,1},{1,3},{3,5},{5,7},{7,6},{6,4},{4,2},{2,0},{8,9},{9,11},{11,1... | collective-permute-start | bytes 3145736 | tf_op jit(solution)/shard_map/ppermute | solution.py:79
  379.1 23.0 %collective-permute-start.62 = (bf16[256,2048]{1,0:T(8,128)(2,1)S(1)}, bf16[256,2048]{1,0:T(8,128)(2,1)S(1)}, u32[]{:S(2)}, u32[]{:S(2)}) collective-permute-start(bf16[256,2048]{1,0:T(8,128)(2,1)S(1)} %add_convert_fusion.21), channel_id=1, source_target_pairs={{1,0},{3,1},{5,3},{7,5},{6,7},{4,6},{2,4},{0,2},{9,8},{11,9},{13,1... | collective-permute-start | bytes 3145736 | tf_op jit(solution)/shard_map/ppermute | solution.py:82
  538.1 24.1 %collective-permute-start.73 = (bf16[256,2048]{1,0:T(8,128)(2,1)S(1)}, bf16[256,2048]{1,0:T(8,128)(2,1)S(1)}, u32[]{:S(2)}, u32[]{:S(2)}) collective-permute-start(bf16[256,2048]{1,0:T(8,128)(2,1)S(1)} %add_convert_fusion.18), channel_id=1, source_target_pairs={{0,1},{1,3},{3,5},{5,7},{7,6},{6,4},{4,2},{2,0},{8,9},{9,11},{11,1... | collective-permute-start | bytes 3145736 | tf_op jit(solution)/shard_map/ppermute | solution.py:79
  541.1 26.1 %collective-permute-start.75 = (bf16[256,2048]{1,0:T(8,128)(2,1)S(1)}, bf16[256,2048]{1,0:T(8,128)(2,1)S(1)}, u32[]{:S(2)}, u32[]{:S(2)}) collective-permute-start(bf16[256,2048]{1,0:T(8,128)(2,1)S(1)} %add_convert_fusion.16), channel_id=1, source_target_pairs={{1,0},{3,1},{5,3},{7,5},{6,7},{4,6},{2,4},{0,2},{9,8},{11,9},{13,1... | collective-permute-start | bytes 3145736 | tf_op jit(solution)/shard_map/ppermute | solution.py:82
  591.6 25.6 %collective-permute-start.78 = (bf16[256,2048]{1,0:T(8,128)(2,1)S(1)}, bf16[256,2048]{1,0:T(8,128)(2,1)S(1)}, u32[]{:S(2)}, u32[]{:S(2)}) collective-permute-start(bf16[256,2048]{1,0:T(8,128)(2,1)S(1)} %copy-done.82), channel_id=1, source_target_pairs={{0,1},{1,3},{3,5},{5,7},{7,6},{6,4},{4,2},{2,0},{8,9},{9,11},{11,1... | collective-permute-start | bytes 3145736 | tf_op jit(solution)/shard_map/ppermute | solution.py:79
  592.1 25.2 %collective-permute-start.79 = (bf16[256,2048]{1,0:T(8,128)(2,1)S(1)}, bf16[256,2048]{1,0:T(8,128)(2,1)S(1)}, u32[]{:S(2)}, u32[]{:S(2)}) collective-permute-start(bf16[256,2048]{1,0:T(8,128)(2,1)S(1)} %copy-done.83), channel_id=1, source_target_pairs={{1,0},{3,1},{5,3},{7,5},{6,7},{4,6},{2,4},{0,2},{9,8},{11,9},{13,1... | collective-permute-start | bytes 3145736 | tf_op jit(solution)/shard_map/ppermute | solution.py:82
  635.3 31.1 %all-to-all-start.2 = ((bf16[8,256,256]{2,1,0:T(8,128)(2,1)}), bf16[8,256,256]{2,1,0:T(8,128)(2,1)}, u32[]{:S(2)}, u32[]{:S(2)}) async-start(bf16[8,256,256]{2,1,0:T(8,128)(2,1)} %bitcast.243), calls=%async_computation.2 | async-start | bytes 2097152 | tf_op jit(solution)/shard_map/all_to_all | solution.py:671
  639.8 47.5 %collective-permute-start.89 = (bf16[1024,512]{1,0:T(8,128)(2,1)}, bf16[1024,512]{1,0:T(8,128)(2,1)}, u32[]{:S(2)}, u32[]{:S(2)}) collective-permute-start(bf16[1024,512]{1,0:T(8,128)(2,1)} %get-tuple-element.174), channel_id=1, source_target_pairs={{0,16},{8,24},{16,0},{24,8},{1,17},{9,25},{17,1},{25,9},{2,18},{10... | collective-permute-start | bytes 3145736 | tf_op jit(solution)/shard_map/ppermute | solution.py:36
  640.2 48.4 %collective-permute-start.90 = (bf16[512,1024]{1,0:T(8,128)(2,1)}, bf16[512,1024]{1,0:T(8,128)(2,1)}, u32[]{:S(2)}, u32[]{:S(2)}) collective-permute-start(bf16[512,1024]{1,0:T(8,128)(2,1)} %get-tuple-element.175), channel_id=1, source_target_pairs={{0,16},{8,24},{16,0},{24,8},{1,17},{9,25},{17,1},{25,9},{2,18},{10... | collective-permute-start | bytes 3145736 | tf_op jit(solution)/shard_map/ppermute | solution.py:36
  671.8 38.8 %collective-permute-start.93 = (bf16[512,1024]{1,0:T(8,128)(2,1)S(1)}, bf16[512,1024]{1,0:T(8,128)(2,1)}, u32[]{:S(2)}, u32[]{:S(2)}) collective-permute-start(bf16[512,1024]{1,0:T(8,128)(2,1)S(1)} %copy-done.81), channel_id=1, source_target_pairs={{0,16},{8,24},{16,0},{24,8},{1,17},{9,25},{17,1},{25,9},{2,18},{10... | collective-permute-start | bytes 3145736 | tf_op jit(solution)/shard_map/ppermute | solution.py:36
  756.5 26.1 %collective-permute-start.101 = (bf16[256,2048]{1,0:T(8,128)(2,1)S(1)}, bf16[256,2048]{1,0:T(8,128)(2,1)S(1)}, u32[]{:S(2)}, u32[]{:S(2)}) collective-permute-start(bf16[256,2048]{1,0:T(8,128)(2,1)S(1)} %get-tuple-element.201), channel_id=1, source_target_pairs={{0,1},{1,3},{3,5},{5,7},{7,6},{6,4},{4,2},{2,0},{8,9},{9,11},{11,1... | collective-permute-start | bytes 3145736 | tf_op jit(solution)/shard_map/ppermute | solution.py:79
  756.9 26.1 %collective-permute-start.102 = (bf16[256,2048]{1,0:T(8,128)(2,1)S(1)}, bf16[256,2048]{1,0:T(8,128)(2,1)S(1)}, u32[]{:S(2)}, u32[]{:S(2)}) collective-permute-start(bf16[256,2048]{1,0:T(8,128)(2,1)S(1)} %get-tuple-element.202), channel_id=1, source_target_pairs={{1,0},{3,1},{5,3},{7,5},{6,7},{4,6},{2,4},{0,2},{9,8},{11,9},{13,1... | collective-permute-start | bytes 3145736 | tf_op jit(solution)/shard_map/ppermute | solution.py:82
  768.0 25.7 %collective-permute-start.110 = (bf16[128,2048]{1,0:T(8,128)(2,1)S(1)}, bf16[128,2048]{1,0:T(8,128)(2,1)S(1)}, u32[]{:S(2)}, u32[]{:S(2)}) collective-permute-start(bf16[128,2048]{1,0:T(8,128)(2,1)S(1)} %fusion.56), channel_id=1, source_target_pairs={{0,1},{1,3},{3,5},{5,7},{7,6},{6,4},{4,2},{2,0},{8,9},{9,11},{11,1... | collective-permute-start | bytes 1572872 | tf_op jit(solution)/shard_map/ppermute | solution.py:79
  768.4 25.3 %collective-permute-start.111 = (bf16[128,2048]{1,0:T(8,128)(2,1)S(1)}, bf16[128,2048]{1,0:T(8,128)(2,1)S(1)}, u32[]{:S(2)}, u32[]{:S(2)}) collective-permute-start(bf16[128,2048]{1,0:T(8,128)(2,1)S(1)} %fusion.55), channel_id=1, source_target_pairs={{1,0},{3,1},{5,3},{7,5},{6,7},{4,6},{2,4},{0,2},{9,8},{11,9},{13,1... | collective-permute-start | bytes 1572872 | tf_op jit(solution)/shard_map/ppermute | solution.py:82
  787.4 27.0 %collective-permute-start.103 = (bf16[256,2048]{1,0:T(8,128)(2,1)S(1)}, bf16[256,2048]{1,0:T(8,128)(2,1)S(1)}, u32[]{:S(2)}, u32[]{:S(2)}) collective-permute-start(bf16[256,2048]{1,0:T(8,128)(2,1)S(1)} %get-tuple-element.204), channel_id=1, source_target_pairs={{0,1},{1,3},{3,5},{5,7},{7,6},{6,4},{4,2},{2,0},{8,9},{9,11},{11,1... | collective-permute-start | bytes 3145736 | tf_op jit(solution)/shard_map/ppermute | solution.py:79
  794.5 22.8 %collective-permute-start.107 = (bf16[512,768]{1,0:T(8,128)(2,1)S(1)}, bf16[512,768]{1,0:T(8,128)(2,1)S(1)}, u32[]{:S(2)}, u32[]{:S(2)}) collective-permute-start(bf16[512,768]{1,0:T(8,128)(2,1)S(1)} %get-tuple-element.312), channel_id=1, source_target_pairs={{0,16},{8,24},{16,0},{24,8},{1,17},{9,25},{17,1},{25,9},{2,18},{10... | collective-permute-start | bytes 2359304 | tf_op jit(solution)/shard_map/ppermute | solution.py:36
  795.9 32.5 %collective-permute-start.112 = (f32[1,64,2048]{2,1,0:T(8,128)}, f32[1,64,2048]{2,1,0:T(8,128)}, u32[]{:S(2)}, u32[]{:S(2)}) collective-permute-start(f32[1,64,2048]{2,1,0:T(8,128)} %dynamic-slice_bitcast_fusion.1), channel_id=1, source_target_pairs={{0,16},{8,24},{16,0},{24,8},{1,17},{9,25},{17,1},{25,9},{2,18},{10... | collective-permute-start | bytes 1572872 | tf_op jit(solution)/shard_map/ppermute | solution.py:36
  817.2 26.2 %collective-permute-start.108 = (bf16[256,2048]{1,0:T(8,128)(2,1)}, bf16[256,2048]{1,0:T(8,128)(2,1)}, u32[]{:S(2)}, u32[]{:S(2)}) collective-permute-start(bf16[256,2048]{1,0:T(8,128)(2,1)} %get-tuple-element.207), channel_id=1, source_target_pairs={{0,1},{1,3},{3,5},{5,7},{7,6},{6,4},{4,2},{2,0},{8,9},{9,11},{11,1... | collective-permute-start | bytes 3145736 | tf_op jit(solution)/shard_map/ppermute | solution.py:79
  818.2 25.2 %collective-permute-start.109 = (bf16[256,2048]{1,0:T(8,128)(2,1)}, bf16[256,2048]{1,0:T(8,128)(2,1)}, u32[]{:S(2)}, u32[]{:S(2)}) collective-permute-start(bf16[256,2048]{1,0:T(8,128)(2,1)} %get-tuple-element.208), channel_id=1, source_target_pairs={{1,0},{3,1},{5,3},{7,5},{6,7},{4,6},{2,4},{0,2},{9,8},{11,9},{13,1... | collective-permute-start | bytes 3145736 | tf_op jit(solution)/shard_map/ppermute | solution.py:82
  820.3 37.9 %all-to-all-start.3 = ((bf16[8,64,768]{2,1,0:T(8,128)(2,1)}), bf16[8,64,768]{2,1,0:T(8,128)(2,1)}, u32[]{:S(2)}, u32[]{:S(2)}) async-start(bf16[8,64,768]{2,1,0:T(8,128)(2,1)} %bitcast.272), calls=%async_computation.3 | async-start | bytes 1572864 | tf_op jit(solution)/shard_map/all_to_all | solution.py:754
  (185 other events, 2439.0 us)

commit v4 on v3

--- a/solution.py
+++ b/solution.py
@@ -86,12 +86,12 @@
         chunks = {0: own}
         r = l = own
         for k in range(1, half):
-            names = between(k) if between else ()
             r, l = self.right(r), self.left(l)
+            chunks[-k], chunks[k] = r, l
+            names = between(k, chunks) if between else ()
             if names:
                 r, l, *beside = tie(r, l, *(state[n] for n in names))
                 state |= dict(zip(names, beside))
-            chunks[-k], chunks[k] = r, l
         mid = own.shape[0] // 2
         chunks[half] = jnp.concatenate([self.right(r[:mid]), self.left(l[mid:])], axis=0)
         return chunks
@@ -234,23 +234,6 @@
     got = swap_all(val, bit)
     upper = (me // bit) % 2 == 1
     return jnp.concatenate([jnp.where(upper, got, val), jnp.where(upper, val, got)], axis=0)
-
-
-def gather_output_weights(row_ring, state, between, chips):
-    seq = lax.axis_size("seq")
-    me = lax.axis_index("dp")
-    rows, width = state["w_out"].shape
-    chunks = row_ring.gather(state["w_out"], state, between)
-    half = row_ring.size // 2
-    groups = [[0, 1, -1]] + [[k, -k] for k in range(2, half)] + [[half]]
-    pieces = []
-    for group in groups:
-        val = jnp.concatenate([chunks[o] for o in group])
-        for mask, block in swap_cores(swap_chips(val, chips)).items():
-            for i, o in enumerate(group):
-                to = ((me ^ mask) * seq + row_ring.owner(o)) * rows
-                pieces.append((block, i * rows, rows, to, 0))
-    return assemble((width, width), pieces)
 
 
 def output_grad_steps(part, row_ring):
@@ -542,13 +525,14 @@
     hid = w_gate.shape[1]
     chips = data_bits(data)[:-1]
     state = {"gains": jnp.stack([query_gain, key_gain, attn_gain, mlp_gain])[None]}
-    gain_bits = bits_of(data * seq)
+    gain_bits = [b * seq for b in data_bits(data)] + bits_of(seq)
+    gain_order = list(gain_bits)
 
     def more_gains():
         if gain_bits:
             state["gains"] = gain_step(state["gains"], gain_bits.pop(0))
 
-    def beside(step):
+    def beside(step, chunks):
         more_gains()
         if step == 1:
             state["down"] = swap_chips(w_down, chips)
@@ -559,8 +543,8 @@
             return ["gains", "w_heads", "down", "gate", "begin"]
         if step == 3:
             state["w_heads"] = swap_chips(state["w_heads"].reshape(-1, 3 * own), chips)
-            state["w_out"], state["up"] = w_output, w_up
-            return ["gains", "w_heads", "w_out", "up"]
+            state["up"] = w_up
+            return ["gains", "w_heads", "up"]
         return ["gains"]
 
     state["begin"] = begin
@@ -570,47 +554,47 @@
     cosine, sine = rope_tables(jnp.arange(row_len, dtype=jnp.int32) - begin)
     begin = begin[None]
     state["up"] = swap_chips(state["up"], chips)
-    w_heads = assemble((width, 3 * own), place_over_data(swap_cores(state["w_heads"])))
+    last = row_ring.size // 2
     row_tokens = jnp.zeros((row_len, width), LOW)
     for offset, chunk in row_chunks.items():
+        if offset == last:
+            chunk, w_out, row_tokens, cosine, sine = tie(
+                chunk, w_output, row_tokens, cosine, sine
+            )
         row_tokens = lax.dynamic_update_slice(row_tokens, chunk, (row_ring.owner(offset) * count, 0))
+    w_out = lax.all_gather(w_out, ("dp", "seq"), axis=0, tiled=True)
+    w_heads = assemble((width, 3 * own), place_over_data(swap_cores(state["w_heads"])))
     pre = dot(row_tokens, w_heads)
     while gain_bits:
         more_gains()
-    gains = jnp.moveaxis(state["gains"], 0, 1).reshape(4, -1).astype(FULL)
+    placed = [gain_order[::-1].index(bit) for bit in sorted(gain_order, reverse=True)]
+    gains = state["gains"].reshape((2,) * len(placed) + state["gains"].shape[1:])
+    gains = jnp.transpose(gains, [len(placed)] + placed + [len(placed) + 1])
+    gains = gains.reshape(4, -1).astype(FULL)
     gain_attn, gain_mlp = gains[2], gains[3]
     gains_own = lax.dynamic_slice(gains, (0, seq_at * own), (2, own))
     query_pre, key_pre = pre[:, :own], pre[:, own : 2 * own]
     squares = jnp.stack([jnp.sum(query_pre * query_pre, axis=1), jnp.sum(key_pre * key_pre, axis=1)])
     scales = lax.rsqrt(sum_over(squares, "seq", seq) / width + EPSILON)
-    state["scales"] = scales
-
-    def beside_output(step):
-        if step == 3:
-            state["attn"] = attend_forward(
-                pre, state["scales"], gains_own, cosine, sine, first_block, begin
-            )
-            return ["attn"]
-        return ["scales", "up"] if step == 2 else []
-
-    w_out = gather_output_weights(row_ring, state, beside_output, chips)
-    scales = state["scales"]
-    attn_heads, query_rot, key_rot, values, log_sums = state["attn"]
+    scales, state["up"] = tie(scales, state["up"])
+    attn_heads, query_rot, key_rot, values, log_sums = attend_forward(
+        pre, scales, gains_own, cosine, sine, first_block, begin
+    )
     attn_tokens = lax.all_to_all(
         attn_heads.reshape(seq, count, own), "seq", split_axis=0, concat_axis=0, tiled=True
     )
     attn_tokens = jnp.moveaxis(attn_tokens, 0, 1).reshape(count, width)
 
-    near, attn_rows = tie([state[n] for n in ("gate", "up", "down")], attn_tokens)
-    near = [swap_cores(n) for n in near]
-    gate_up = assemble((width, 2 * hid), place_over_data(near[0]) + place_over_data(near[1], 0, hid))
-    down = assemble((hid, width), place_over_data(near[2], 1))
     attn_pre = dot(attn_tokens, w_out)
     attn_scale = rms_scale(attn_pre)
     middle = inputs.astype(FULL) + attn_pre * attn_scale * gain_attn
     middle_low = middle.astype(LOW)
 
     mids = row_ring.gather(middle_low)
+    near, mids[0] = tie([state[n] for n in ("gate", "up", "down")], mids[0])
+    near = [swap_cores(n) for n in near]
+    gate_up = assemble((width, 2 * hid), place_over_data(near[0]) + place_over_data(near[1], 0, hid))
+    down = assemble((hid, width), place_over_data(near[2], 1))
     saved = {}
 
     def mlp_part(offset):
@@ -670,7 +654,7 @@
     grad_heads = jnp.moveaxis(grad_heads.reshape(count, seq, own), 1, 0)
     grad_heads = lax.all_to_all(grad_heads, "seq", split_axis=0, concat_axis=0, tiled=True)
     grad_heads = grad_heads.reshape(row_len, own)
-    steps = output_grad_steps(dot_tn(attn_rows, grad_attn_low).astype(LOW), row_ring)
+    steps = output_grad_steps(dot_tn(attn_tokens, grad_attn_low).astype(LOW), row_ring)
     sent = next(steps)
     sums["up"] = scatter_over_data(blocks_over_data(ffn["up"], 0))
     got = {n: last_over_data(sums[n][1]) for n in ("down", "gate")}
@@ -753,8 +737,11 @@
     part = (rest["part"][0].astype(FULL) + rest["part"][1].astype(FULL)).astype(LOW)
     part = lax.all_to_all(
         part.reshape(seq, -1, 3 * own), "seq", split_axis=0, concat_axis=0, tiled=True
-    ).astype(FULL)
-    part = jnp.moveaxis(part.reshape(seq, -1, 3, own), 0, 2).reshape(-1, 3, width)
+    )
+    grad_query, grad_key, grad_value = (
+        jnp.concatenate([part[d, :, n * own : (n + 1) * own] for d in range(seq)], axis=1).astype(FULL)
+        for n in range(3)
+    )
     sums, got = rest["sums"], rest["got"]
     grad_output = finish_output_grad(finish(steps, sent=rest["output"]))
     grad_down, grad_gate, grad_up = (
@@ -764,9 +751,9 @@
     return (
         layer_out,
         grad_tokens,
-        part[:, 0],
-        part[:, 1],
-        part[:, 2],
+        grad_query,
+        grad_key,
+        grad_value,
         grad_output,
         gain_grads[0],
         gain_grads[1],

time: 875 us -> 862 us (0.985)
  starting transfers between devices: 135 us -> 112 us
  between operations: 3.26 us -> 16.4 us
  matrix products: 159 us -> 168 us
    all_to_all x1, waiting for transfers between devices: 0.01 us -> 35.6 us  [per_device(): lax.all_to_all(attn_heads.reshape(seq, count, own), 'seq', split_axis=0,...]
    ppermute x5, waiting for transfers between devices: 24.8 us -> 0.01 us  [swap_all(): lax.ppermute(val, ('dp', 'seq'), [(i, i ^ mask) for i in range(size)])]
    ppermute x32 -> x28, waiting for transfers between devices: 205 us -> 181 us  [right(): return lax.ppermute(val, 'seq', self.forth)]
    ppermute x46 -> x34, waiting for transfers between devices: 43.1 us -> 59.6 us  [swap(): return lax.ppermute(val, axis, [(i, i ^ mask) for i in range(size)])]
    ppermute x32 -> x28, waiting for transfers between devices: 38.8 us -> 30.4 us  [left(): return lax.ppermute(val, 'seq', self.back)]
    ppermute x32 -> x28, starting transfers between devices: 33.7 us -> 25.4 us  [left(): return lax.ppermute(val, 'seq', self.back)]
    ppermute x32 -> x28, starting transfers between devices: 43.9 us -> 35.7 us  [right(): return lax.ppermute(val, 'seq', self.forth)]
    ppermute x46 -> x34, starting transfers between devices: 31.5 us -> 23.9 us  [swap(): return lax.ppermute(val, axis, [(i, i ^ mask) for i in range(size)])]
  transfers between devices with their start and end apart: 119 -> 100, of which waited for: 58 -> 54; matrix products, arithmetic and copies ran while one was open for 31% -> 31% of each run, Pallas kernels for 7% -> 6%
where the time goes in v4:
time: 862 us; the launch traced here: 852 us
  waiting for transfers between devices  326 us (38%)
  matrix products  168 us (19%)
  starting transfers between devices  112 us (13%)
  local copies, waits for them, and re-layouts  92.7 us (11%)
  other arithmetic  83.9 us (10%)
  Pallas kernels  53 us (6%)
  between operations  16.4 us (2%)
    ppermute x28, waiting for transfers between devices, right(): return lax.ppermute(val, 'seq', self.forth)  181 us
    dot_general x18, matrix products, dot_nt(): lax.dot_general(left, right, (((1,), (1,)), ((), ())), preferred_element_...  63 us
    ppermute x34, waiting for transfers between devices, swap(): return lax.ppermute(val, axis, [(i, i ^ mask) for i in range(size)])  59.6 us
    dot_general x18, matrix products, dot(): return jnp.dot(left, right, preferred_element_type=FULL)  55.9 us
    unnamed x225, local copies, waits for them, and re-layouts  51.4 us
    dot_general x5, matrix products, dot_tn(): lax.dot_general(left, right, (((0,), (0,)), ((), ())), preferred_element_...  49.2 us
    ppermute x28, starting transfers between devices, right(): return lax.ppermute(val, 'seq', self.forth)  35.7 us
    all_to_all x1, waiting for transfers between devices, per_device(): lax.all_to_all(attn_heads.reshape(seq, count, own), 'seq', split_axis=0,...  35.6 us
  transfers between devices with their start and end apart: 100, of which 54 were waited for; matrix products, arithmetic and copies ran while one was open for 31% of the time, Pallas kernels for 6%

profile of v4, /device:TPU:0, one launch (start us, length us, event | category | flops | bytes accessed | tf_op | source)
XLA Modules:
  0.0 852.2 jit_solution(13825027097974303368)
XLA Ops:
  23.6 5.8 all-to-all-start
  33.2 4.3 broadcast_in_dim.73
  45.6 10.2 %collective-permute-done.7.refs_1_ = bf16[512,1024]{1,0:T(8,128)(2,1)} collective-permute-done((bf16[512,1024]{1,0:T(8,128)(2,1)S(1)}, bf16[512,1024]{1,0:T(8,128)(2,1)}, u32[]{:S(2)}, u32[]{:S(2)}) %collective-permute-start.7) | collective-permute-done | bytes 1048608 | tf_op jit(solution)/shard_map/ppermute | solution.py:36
  55.8 20.1 %collective-permute-done.6.refs_1_ = bf16[1024,512]{1,0:T(8,128)(2,1)} collective-permute-done((bf16[1024,512]{1,0:T(8,128)(2,1)S(1)}, bf16[1024,512]{1,0:T(8,128)(2,1)}, u32[]{:S(2)}, u32[]{:S(2)}) %collective-permute-start.6) | collective-permute-done | bytes 1048608 | tf_op jit(solution)/shard_map/ppermute | solution.py:36
  88.3 6.1 collective-permute-done.11.refs_1_
  94.4 6.3 collective-permute-done.8
  123.8 11.8 %fusion.84.q_ref.k_ref.v_ref.qp_ref.kp_ref = f32[2048,768]{1,0:T(8,128)} fusion(bf16[2048,2048]{1,0:T(8,128)(2,1)} %constant_dynamic-update-slice_fusion.67, bf16[2048,768]{1,0:T(8,128)(2,1)S(1)} %assemble.3), kind=kOutput, calls=%fused_computation.358 | convolution fusion | flops 6442450944 | bytes 17825792 | tf_op jit(solution)/shard_map/dot_general | solution.py:23
  147.1 4.6 collective-permute-done.18
  151.8 17.4 %attend_forward.1 = (bf16[2048,256]{1,0:T(8,128)(2,1)S(1)}, bf16[2048,256]{1,0:T(8,128)(2,1)S(1)}, bf16[2048,256]{1,0:T(8,128)(2,1)S(1)}, bf16[2048,256]{1,0:T(8,128)(2,1)S(1)}, f32[2,1,2048]{2,1,0:T(1,128)S(1)}) custom-call(s32[4]{0:T(128)S(1)} %and_select_fusion.first_ref, f32[2048,768]{1,0:T(8,128)} %fusion.84.q_ref.k_ref.v_ref.qp_ref.kp_ref, ...), custom_call_target="tpu_custom_call" | custom-call | flops 1 | bytes 1 | tf_op jit(solution)/shard_map/attend_forward/pallas_call | solution.py:365
  176.1 35.6 %all-to-all-done.1 = bf16[8,256,256]{1,2,0:T(8,128)(2,1)S(1)} async-done(((bf16[8,256,256]{1,2,0:T(8,128)(2,1)}), bf16[8,256,256]{1,2,0:T(8,128)(2,1)S(1)}, u32[]{:S(2)}, u32[]{:S(2)}) %all-to-all-start.1) | async-done | bytes 1048608 | tf_op jit(solution)/shard_map/all_to_all | solution.py:583
  212.7 5.9 multiply_reduce_fusion.3
  228.9 7.1 assemble.4
  236.0 6.2 fusion.85
  242.2 5.6 collective-permute-done.31
  265.7 7.0 collective-permute-done.32
  285.6 10.5 %collective-permute-done.33 = bf16[256,2048]{1,0:T(8,128)(2,1)S(1)} collective-permute-done((bf16[256,2048]{1,0:T(8,128)(2,1)}, bf16[256,2048]{1,0:T(8,128)(2,1)S(1)}, u32[]{:S(2)}, u32[]{:S(2)}) %collective-permute-start.33) | collective-permute-done | bytes 1048608 | tf_op jit(solution)/shard_map/ppermute | solution.py:79
  297.7 4.4 collective-permute-done.30
  323.0 7.2 collective-permute-done.36
  337.6 15.5 %collective-permute-done.37 = bf16[256,2048]{1,0:T(8,128)(2,1)S(1)} collective-permute-done((bf16[256,2048]{1,0:T(8,128)(2,1)S(1)}, bf16[256,2048]{1,0:T(8,128)(2,1)S(1)}, u32[]{:S(2)}, u32[]{:S(2)}) %collective-permute-start.37) | collective-permute-done | bytes 1048608 | tf_op jit(solution)/shard_map/ppermute | solution.py:79
  362.0 14.7 %collective-permute-done.38 = bf16[256,2048]{1,0:T(8,128)(2,1)S(1)} collective-permute-done((bf16[256,2048]{1,0:T(8,128)(2,1)S(1)}, bf16[256,2048]{1,0:T(8,128)(2,1)S(1)}, u32[]{:S(2)}, u32[]{:S(2)}) %collective-permute-start.38) | collective-permute-done | bytes 1048608 | tf_op jit(solution)/shard_map/ppermute | solution.py:79
  390.9 4.8 collective-permute-done.39
  409.4 11.3 %collective-permute-done.47 = bf16[256,2048]{1,0:T(8,128)(2,1)S(1)} collective-permute-done((bf16[256,2048]{1,0:T(8,128)(2,1)S(1)}, bf16[256,2048]{1,0:T(8,128)(2,1)S(1)}, u32[]{:S(2)}, u32[]{:S(2)}) %collective-permute-start.47) | collective-permute-done | bytes 1048608 | tf_op jit(solution)/shard_map/ppermute | solution.py:79
  439.5 9.0 %collective-permute-done.48 = bf16[256,2048]{1,0:T(8,128)(2,1)} collective-permute-done((bf16[256,2048]{1,0:T(8,128)(2,1)S(1)}, bf16[256,2048]{1,0:T(8,128)(2,1)}, u32[]{:S(2)}, u32[]{:S(2)}) %collective-permute-start.48) | collective-permute-done | bytes 1048608 | tf_op jit(solution)/shard_map/ppermute | solution.py:79
  448.5 4.0 constant_dynamic-update-slice_fusion.30
  470.7 11.2 %collective-permute-done.49 = bf16[256,2048]{1,0:T(8,128)(2,1)S(1)} collective-permute-done((bf16[256,2048]{1,0:T(8,128)(2,1)}, bf16[256,2048]{1,0:T(8,128)(2,1)S(1)}, u32[]{:S(2)}, u32[]{:S(2)}) %collective-permute-start.49) | collective-permute-done | bytes 1048608 | tf_op jit(solution)/shard_map/ppermute | solution.py:79
  508.6 8.6 %collective-permute-done.52 = bf16[128,2048]{1,0:T(8,128)(2,1)S(1)} collective-permute-done((bf16[128,2048]{1,0:T(8,128)(2,1)S(1)}, bf16[128,2048]{1,0:T(8,128)(2,1)S(1)}, u32[]{:S(2)}, u32[]{:S(2)}) %collective-permute-start.52) | collective-permute-done | bytes 524320 | tf_op jit(solution)/shard_map/ppermute | solution.py:79
  521.3 12.8 %convolution_convert_fusion.2 = bf16[1024,2048]{1,0:T(8,128)(2,1)S(1)} fusion(bf16[2048,1024]{1,0:T(8,128)(2,1)} %get-tuple-element.249, bf16[2048,2048]{1,0:T(8,128)(2,1)} %constant_dynamic-update-slice_fusion.8), kind=kOutput, calls=%fused_computation.5 | convolution fusion | flops 8592031744 | bytes 16777216 | tf_op jit(solution)/shard_map/dot_general | solution.py:31
  534.2 9.1 %collective-permute-done.53 = bf16[256,2048]{1,0:T(8,128)(2,1)S(1)} collective-permute-done((bf16[256,2048]{1,0:T(8,128)(2,1)S(1)}, bf16[256,2048]{1,0:T(8,128)(2,1)S(1)}, u32[]{:S(2)}, u32[]{:S(2)}) %collective-permute-start.53) | collective-permute-done | bytes 1048608 | tf_op jit(solution)/shard_map/ppermute | solution.py:79
  546.6 13.0 %convolution_convert_fusion.4 = bf16[2048,1024]{1,0:T(8,128)(2,1)} fusion(bf16[2048,2048]{1,0:T(8,128)(2,1)} %constant_dynamic-update-slice_fusion.17, bf16[2048,1024]{1,0:T(8,128)(2,1)S(1)} %copy-done.94), kind=kOutput, calls=%fused_computation.7 | convolution fusion | flops 8592031744 | bytes 16777216 | tf_op jit(solution)/shard_map/dot_general | solution.py:31
  564.4 6.2 fusion.19
  573.6 11.7 %convolution_convert_fusion.3 = bf16[2048,1024]{1,0:T(8,128)(2,1)S(1)} fusion(bf16[2048,2048]{1,0:T(8,128)(2,1)} %constant_dynamic-update-slice_fusion.17, bf16[2048,1024]{1,0:T(8,128)(2,1)S(1)} %copy-done.95), kind=kOutput, calls=%fused_computation.6 | convolution fusion | flops 8592031744 | bytes 16777216 | tf_op jit(solution)/shard_map/dot_general | solution.py:31
  585.4 4.3 add_convert_fusion.11
  592.0 4.3 collective-permute-done.58
  614.1 4.5 all-to-all-start.2
  622.1 4.5 add_convert_fusion.7
  626.6 5.4 fusion
  634.7 10.4 %all-to-all-done.2 = bf16[8,256,256]{2,1,0:T(8,128)(2,1)} async-done(((bf16[8,256,256]{2,1,0:T(8,128)(2,1)}), bf16[8,256,256]{2,1,0:T(8,128)(2,1)}, u32[]{:S(2)}, u32[]{:S(2)}) %all-to-all-start.2) | async-done | bytes 1048608 | tf_op jit(solution)/shard_map/all_to_all | solution.py:655
  651.8 12.9 %attend_backward.2 = (f32[2048,128]{1,0:T(8,128)S(1)}, f32[2048,128]{1,0:T(8,128)S(1)}, bf16[2048,128]{1,0:T(8,128)(2,1)S(1)}, f32[1,2,2048]{2,1,0:T(2,128)S(1)}, f32[2,128]{1,0:T(2,128)S(1)}) custom-call(s32[4]{0:T(128)S(1)} %copy-done.30, bf16[2048,256]{1,0:T(8,128)(2,1)S(1)} %get-tuple-element.153.q_ref, bf16[2048,256]{1,0:T(8,128)(2,1)S(1)} %copy-done.3, ...), custom_call_target="tpu_custom_call" | custom-call | flops 1 | bytes 1 | tf_op jit(solution)/shard_map/attend_backward/pallas_call | solution.py:461
  669.5 12.9 %attend_backward.3 = (f32[2048,128]{1,0:T(8,128)S(1)}, f32[2048,128]{1,0:T(8,128)S(1)}, bf16[2048,128]{1,0:T(8,128)(2,1)S(1)}, f32[1,2,2048]{2,1,0:T(2,128)S(1)}, f32[2,128]{1,0:T(2,128)S(1)}) custom-call(s32[4]{0:T(128)S(1)} %copy-done.30, bf16[2048,256]{1,0:T(8,128)(2,1)S(1)} %get-tuple-element.153.q_ref, bf16[2048,256]{1,0:T(8,128)(2,1)S(1)} %copy-done.3, ...), custom_call_target="tpu_custom_call" | custom-call | flops 1 | bytes 1 | tf_op jit(solution)/shard_map/attend_backward/pallas_call | solution.py:461
  704.9 4.3 fusion.9
  709.2 7.2 convolution_convert_fusion
  721.7 10.9 %collective-permute-done.77 = bf16[128,2048]{1,0:T(8,128)(2,1)S(1)} collective-permute-done((bf16[128,2048]{1,0:T(8,128)(2,1)S(1)}, bf16[128,2048]{1,0:T(8,128)(2,1)S(1)}, u32[]{:S(2)}, u32[]{:S(2)}) %collective-permute-start.77) | collective-permute-done | bytes 524320 | tf_op jit(solution)/shard_map/ppermute | solution.py:79
  736.4 9.4 %convolution_convert_fusion.5 = bf16[2048,768]{1,0:T(8,128)(2,1)S(1)} fusion(bf16[2048,2048]{1,0:T(8,128)(2,1)} %constant_dynamic-update-slice_fusion.67, bf16[2048,768]{1,0:T(8,128)(2,1)S(1)} %pad_maximum_fusion), kind=kOutput, calls=%fused_computation.8 | convolution fusion | flops 6444023808 | bytes 14680064 | tf_op jit(solution)/shard_map/dot_general | solution.py:31
  750.8 9.7 %collective-permute-done.81 = bf16[256,2048]{1,0:T(8,128)(2,1)S(1)} collective-permute-done((bf16[256,2048]{1,0:T(8,128)(2,1)S(1)}, bf16[256,2048]{1,0:T(8,128)(2,1)S(1)}, u32[]{:S(2)}, u32[]{:S(2)}) %collective-permute-start.81) | collective-permute-done | bytes 1048608 | tf_op jit(solution)/shard_map/ppermute | solution.py:79
  775.0 17.2 %collective-permute-done.83 = bf16[256,2048]{1,0:T(8,128)(2,1)S(1)} collective-permute-done((bf16[256,2048]{1,0:T(8,128)(2,1)S(1)}, bf16[256,2048]{1,0:T(8,128)(2,1)S(1)}, u32[]{:S(2)}, u32[]{:S(2)}) %collective-permute-start.83) | collective-permute-done | bytes 1048608 | tf_op jit(solution)/shard_map/ppermute | solution.py:79
  798.6 4.8 all-to-all-start.3
  808.6 14.3 %collective-permute-done.88 = bf16[256,2048]{1,0:T(8,128)(2,1)} collective-permute-done((bf16[256,2048]{1,0:T(8,128)(2,1)}, bf16[256,2048]{1,0:T(8,128)(2,1)}, u32[]{:S(2)}, u32[]{:S(2)}) %collective-permute-start.88) | collective-permute-done | bytes 1048608 | tf_op jit(solution)/shard_map/ppermute | solution.py:79
  826.6 9.4 %all-to-all-done.3 = bf16[8,64,768]{2,1,0:T(8,128)(2,1)} async-done(((bf16[8,64,768]{2,1,0:T(8,128)(2,1)}), bf16[8,64,768]{2,1,0:T(8,128)(2,1)}, u32[]{:S(2)}, u32[]{:S(2)}) %all-to-all-start.3) | async-done | bytes 786464 | tf_op jit(solution)/shard_map/all_to_all | solution.py:738
  (570 shorter events, 381.4 us)
Async XLA Ops:
  7.2 31.4 %collective-permute-start = (bf16[256,2048]{1,0:T(8,128)(2,1)}, bf16[256,2048]{1,0:T(8,128)(2,1)}, u32[]{:S(2)}, u32[]{:S(2)}) collective-permute-start(bf16[256,2048]{1,0:T(8,128)(2,1)} %bitcast.324), channel_id=1, source_target_pairs={{0,1},{1,3},{3,5},{5,7},{7,6},{6,4},{4,2},{2,0},{8,9},{9,11},{11,1... | collective-permute-start | bytes 3145736 | tf_op jit(solution)/shard_map/ppermute | solution.py:79
  10.2 28.4 %collective-permute-start.1 = (bf16[256,2048]{1,0:T(8,128)(2,1)}, bf16[256,2048]{1,0:T(8,128)(2,1)}, u32[]{:S(2)}, u32[]{:S(2)}) collective-permute-start(bf16[256,2048]{1,0:T(8,128)(2,1)} %bitcast.325), channel_id=1, source_target_pairs={{1,0},{3,1},{5,3},{7,5},{6,7},{4,6},{2,4},{0,2},{9,8},{11,9},{13,1... | collective-permute-start | bytes 3145736 | tf_op jit(solution)/shard_map/ppermute | solution.py:82
  11.0 27.5 %collective-permute-start.2 = (bf16[1,4,64]{2,1,0:T(4,128)(2,1)S(1)}, bf16[1,4,64]{2,1,0:T(4,128)(2,1)S(1)}, u32[]{:S(2)}, u32[]{:S(2)}) collective-permute-start(bf16[1,4,64]{2,1,0:T(4,128)(2,1)S(1)} %maximum_bitcast_fusion.2), channel_id=1, source_target_pairs={{0,16},{1,17},{2,18},{3,19},{4,20},{5,21},{6,22},{7,23},{8,24},{9,... | collective-permute-start | bytes 1544 | tf_op jit(solution)/shard_map/ppermute | solution.py:41
  23.6 52.3 %all-to-all-start = ((bf16[8,64,768]{2,1,0:T(8,128)(2,1)}), bf16[8,64,768]{2,1,0:T(8,128)(2,1)S(1)}, u32[]{:S(2)}, u32[]{:S(2)}) async-start(bf16[8,64,768]{2,1,0:T(8,128)(2,1)} %reshape.166), calls=%async_computation | async-start | bytes 1572864 | tf_op jit(solution)/shard_map/all_to_all | solution.py:539
  29.5 182.3 %all-gather.2.cloned.1.call-start = ((), (), s32[]{:S(2)}) async-start(), calls=%async_computation.4 | async-start | bytes 8650752 | tf_op jit(solution)/shard_map/all_gather | solution.py:565
  29.5 26.3 %collective-permute-start.7 = (bf16[512,1024]{1,0:T(8,128)(2,1)S(1)}, bf16[512,1024]{1,0:T(8,128)(2,1)}, u32[]{:S(2)}, u32[]{:S(2)}) collective-permute-start(bf16[512,1024]{1,0:T(8,128)(2,1)S(1)} %copy-done.8), channel_id=1, source_target_pairs={{0,16},{8,24},{16,0},{24,8},{1,17},{9,25},{17,1},{25,9},{2,18},{10... | collective-permute-start | bytes 3145736 | tf_op jit(solution)/shard_map/ppermute | solution.py:36
  30.1 45.8 %collective-permute-start.6 = (bf16[1024,512]{1,0:T(8,128)(2,1)S(1)}, bf16[1024,512]{1,0:T(8,128)(2,1)}, u32[]{:S(2)}, u32[]{:S(2)}) collective-permute-start(bf16[1024,512]{1,0:T(8,128)(2,1)S(1)} %copy-done.10), channel_id=1, source_target_pairs={{0,16},{8,24},{16,0},{24,8},{1,17},{9,25},{17,1},{25,9},{2,18},{10... | collective-permute-start | bytes 3145736 | tf_op jit(solution)/shard_map/ppermute | solution.py:36
  38.6 37.3 %collective-permute-start.3 = (bf16[256,2048]{1,0:T(8,128)(2,1)}, bf16[256,2048]{1,0:T(8,128)(2,1)}, u32[]{:S(2)}, u32[]{:S(2)}) collective-permute-start(bf16[256,2048]{1,0:T(8,128)(2,1)} %collective-permute-done), channel_id=1, source_target_pairs={{0,1},{1,3},{3,5},{5,7},{7,6},{6,4},{4,2},{2,0},{8,9},{9,11},{11,1... | collective-permute-start | bytes 3145736 | tf_op jit(solution)/shard_map/ppermute | solution.py:79
  40.6 35.3 %collective-permute-start.4 = (bf16[256,2048]{1,0:T(8,128)(2,1)}, bf16[256,2048]{1,0:T(8,128)(2,1)}, u32[]{:S(2)}, u32[]{:S(2)}) collective-permute-start(bf16[256,2048]{1,0:T(8,128)(2,1)} %collective-permute-done.1), channel_id=1, source_target_pairs={{1,0},{3,1},{5,3},{7,5},{6,7},{4,6},{2,4},{0,2},{9,8},{11,9},{13,1... | collective-permute-start | bytes 3145736 | tf_op jit(solution)/shard_map/ppermute | solution.py:82
  78.2 22.5 %collective-permute-start.8 = (bf16[256,2048]{1,0:T(8,128)(2,1)}, bf16[256,2048]{1,0:T(8,128)(2,1)S(1)}, u32[]{:S(2)}, u32[]{:S(2)}) collective-permute-start(bf16[256,2048]{1,0:T(8,128)(2,1)} %collective-permute-done.3), channel_id=1, source_target_pairs={{0,1},{1,3},{3,5},{5,7},{7,6},{6,4},{4,2},{2,0},{8,9},{9,11},{11,1... | collective-permute-start | bytes 3145736 | tf_op jit(solution)/shard_map/ppermute | solution.py:79
  78.6 23.3 %collective-permute-start.9 = (bf16[256,2048]{1,0:T(8,128)(2,1)}, bf16[256,2048]{1,0:T(8,128)(2,1)S(1)}, u32[]{:S(2)}, u32[]{:S(2)}) collective-permute-start(bf16[256,2048]{1,0:T(8,128)(2,1)} %collective-permute-done.4), channel_id=1, source_target_pairs={{1,0},{3,1},{5,3},{7,5},{6,7},{4,6},{2,4},{0,2},{9,8},{11,9},{13,1... | collective-permute-start | bytes 3145736 | tf_op jit(solution)/shard_map/ppermute | solution.py:82
  116.5 35.2 %collective-permute-start.19 = (bf16[512,1024]{1,0:T(8,128)(2,1)}, bf16[512,1024]{1,0:T(8,128)(2,1)}, u32[]{:S(2)}, u32[]{:S(2)}) collective-permute-start(bf16[512,1024]{1,0:T(8,128)(2,1)} %refs_4_), channel_id=1, source_target_pairs={{0,16},{8,24},{16,0},{24,8},{1,17},{9,25},{17,1},{25,9},{2,18},{10... | collective-permute-start | bytes 3145736 | tf_op jit(solution)/shard_map/ppermute | solution.py:36
  118.1 21.0 %collective-permute-start.21 = (bf16[16,4,64]{2,1,0:T(4,128)(2,1)S(1)}, bf16[16,4,64]{2,1,0:T(4,128)(2,1)S(1)}, u32[]{:S(2)}, u32[]{:S(2)}) collective-permute-start(bf16[16,4,64]{2,1,0:T(4,128)(2,1)S(1)} %pad_maximum_fusion.7), channel_id=1, source_target_pairs={{0,4},{1,5},{2,6},{3,7},{4,0},{5,1},{6,2},{7,3},{8,12},{9,13},{10,... | collective-permute-start | bytes 24584 | tf_op jit(solution)/shard_map/ppermute | solution.py:41
  172.5 39.3 %all-to-all-start.1 = ((bf16[8,256,256]{1,2,0:T(8,128)(2,1)}), bf16[8,256,256]{1,2,0:T(8,128)(2,1)S(1)}, u32[]{:S(2)}, u32[]{:S(2)}) async-start(bf16[8,256,256]{1,2,0:T(8,128)(2,1)} %copy.68), calls=%async_computation.1 | async-start | bytes 2097152 | tf_op jit(solution)/shard_map/all_to_all | solution.py:583
  222.4 25.4 %collective-permute-start.31 = (bf16[256,2048]{1,0:T(8,128)(2,1)}, bf16[256,2048]{1,0:T(8,128)(2,1)}, u32[]{:S(2)}, u32[]{:S(2)}) collective-permute-start(bf16[256,2048]{1,0:T(8,128)(2,1)} %fusion.12), channel_id=1, source_target_pairs={{0,1},{1,3},{3,5},{5,7},{7,6},{6,4},{4,2},{2,0},{8,9},{9,11},{11,1... | collective-permute-start | bytes 3145736 | tf_op jit(solution)/shard_map/ppermute | solution.py:79
  226.5 28.1 %collective-permute-start.28 = (bf16[256,2048]{1,0:T(8,128)(2,1)}, bf16[256,2048]{1,0:T(8,128)(2,1)}, u32[]{:S(2)}, u32[]{:S(2)}) collective-permute-start(bf16[256,2048]{1,0:T(8,128)(2,1)} %fusion.12), channel_id=1, source_target_pairs={{1,0},{3,1},{5,3},{7,5},{6,7},{4,6},{2,4},{0,2},{9,8},{11,9},{13,1... | collective-permute-start | bytes 3145736 | tf_op jit(solution)/shard_map/ppermute | solution.py:82
  227.0 33.0 %collective-permute-start.26 = (bf16[1024,512]{1,0:T(8,128)(2,1)S(1)}, bf16[1024,512]{1,0:T(8,128)(2,1)S(1)}, u32[]{:S(2)}, u32[]{:S(2)}) collective-permute-start(bf16[1024,512]{1,0:T(8,128)(2,1)S(1)} %copy-done.11), channel_id=1, source_target_pairs={{0,8},{8,0},{16,24},{24,16},{1,9},{9,1},{17,25},{25,17},{2,10},{10... | collective-permute-start | bytes 3145736 | tf_op jit(solution)/shard_map/ppermute | solution.py:36
  227.4 32.7 %collective-permute-start.27 = (bf16[1024,512]{1,0:T(8,128)(2,1)}, bf16[1024,512]{1,0:T(8,128)(2,1)S(1)}, u32[]{:S(2)}, u32[]{:S(2)}) collective-permute-start(bf16[1024,512]{1,0:T(8,128)(2,1)} %collective-permute-done.6.refs_1_), channel_id=1, source_target_pairs={{0,8},{8,0},{16,24},{24,16},{1,9},{9,1},{17,25},{25,17},{2,10},{10... | collective-permute-start | bytes 3145736 | tf_op jit(solution)/shard_map/ppermute | solution.py:36
  247.8 24.9 %collective-permute-start.32 = (bf16[256,2048]{1,0:T(8,128)(2,1)}, bf16[256,2048]{1,0:T(8,128)(2,1)}, u32[]{:S(2)}, u32[]{:S(2)}) collective-permute-start(bf16[256,2048]{1,0:T(8,128)(2,1)} %collective-permute-done.31), channel_id=1, source_target_pairs={{0,1},{1,3},{3,5},{5,7},{7,6},{6,4},{4,2},{2,0},{8,9},{9,11},{11,1... | collective-permute-start | bytes 3145736 | tf_op jit(solution)/shard_map/ppermute | solution.py:79
  254.6 24.3 %collective-permute-start.29 = (bf16[256,2048]{1,0:T(8,128)(2,1)}, bf16[256,2048]{1,0:T(8,128)(2,1)}, u32[]{:S(2)}, u32[]{:S(2)}) collective-permute-start(bf16[256,2048]{1,0:T(8,128)(2,1)} %collective-permute-done.28), channel_id=1, source_target_pairs={{1,0},{3,1},{5,3},{7,5},{6,7},{4,6},{2,4},{0,2},{9,8},{11,9},{13,1... | collective-permute-start | bytes 3145736 | tf_op jit(solution)/shard_map/ppermute | solution.py:82
  272.7 23.5 %collective-permute-start.33 = (bf16[256,2048]{1,0:T(8,128)(2,1)}, bf16[256,2048]{1,0:T(8,128)(2,1)S(1)}, u32[]{:S(2)}, u32[]{:S(2)}) collective-permute-start(bf16[256,2048]{1,0:T(8,128)(2,1)} %collective-permute-done.32), channel_id=1, source_target_pairs={{0,1},{1,3},{3,5},{5,7},{7,6},{6,4},{4,2},{2,0},{8,9},{9,11},{11,1... | collective-permute-start | bytes 3145736 | tf_op jit(solution)/shard_map/ppermute | solution.py:79
  278.9 23.3 %collective-permute-start.30 = (bf16[256,2048]{1,0:T(8,128)(2,1)}, bf16[256,2048]{1,0:T(8,128)(2,1)S(1)}, u32[]{:S(2)}, u32[]{:S(2)}) collective-permute-start(bf16[256,2048]{1,0:T(8,128)(2,1)} %collective-permute-done.29), channel_id=1, source_target_pairs={{1,0},{3,1},{5,3},{7,5},{6,7},{4,6},{2,4},{0,2},{9,8},{11,9},{13,1... | collective-permute-start | bytes 3145736 | tf_op jit(solution)/shard_map/ppermute | solution.py:82
  330.4 22.8 %collective-permute-start.37 = (bf16[256,2048]{1,0:T(8,128)(2,1)S(1)}, bf16[256,2048]{1,0:T(8,128)(2,1)S(1)}, u32[]{:S(2)}, u32[]{:S(2)}) collective-permute-start(bf16[256,2048]{1,0:T(8,128)(2,1)S(1)} %add_convert_fusion.25), channel_id=1, source_target_pairs={{0,1},{1,3},{3,5},{5,7},{7,6},{6,4},{4,2},{2,0},{8,9},{9,11},{11,1... | collective-permute-start | bytes 3145736 | tf_op jit(solution)/shard_map/ppermute | solution.py:79
  334.1 23.0 %collective-permute-start.41 = (bf16[256,2048]{1,0:T(8,128)(2,1)S(1)}, bf16[256,2048]{1,0:T(8,128)(2,1)S(1)}, u32[]{:S(2)}, u32[]{:S(2)}) collective-permute-start(bf16[256,2048]{1,0:T(8,128)(2,1)S(1)} %add_convert_fusion.22), channel_id=1, source_target_pairs={{1,0},{3,1},{5,3},{7,5},{6,7},{4,6},{2,4},{0,2},{9,8},{11,9},{13,1... | collective-permute-start | bytes 3145736 | tf_op jit(solution)/shard_map/ppermute | solution.py:82
  353.5 23.2 %collective-permute-start.38 = (bf16[256,2048]{1,0:T(8,128)(2,1)S(1)}, bf16[256,2048]{1,0:T(8,128)(2,1)S(1)}, u32[]{:S(2)}, u32[]{:S(2)}) collective-permute-start(bf16[256,2048]{1,0:T(8,128)(2,1)S(1)} %add_convert_fusion.24), channel_id=1, source_target_pairs={{0,1},{1,3},{3,5},{5,7},{7,6},{6,4},{4,2},{2,0},{8,9},{9,11},{11,1... | collective-permute-start | bytes 3145736 | tf_op jit(solution)/shard_map/ppermute | solution.py:79
  357.4 23.0 %collective-permute-start.42 = (bf16[256,2048]{1,0:T(8,128)(2,1)S(1)}, bf16[256,2048]{1,0:T(8,128)(2,1)S(1)}, u32[]{:S(2)}, u32[]{:S(2)}) collective-permute-start(bf16[256,2048]{1,0:T(8,128)(2,1)S(1)} %add_convert_fusion.21), channel_id=1, source_target_pairs={{1,0},{3,1},{5,3},{7,5},{6,7},{4,6},{2,4},{0,2},{9,8},{11,9},{13,1... | collective-permute-start | bytes 3145736 | tf_op jit(solution)/shard_map/ppermute | solution.py:82
  460.1 21.7 %collective-permute-start.49 = (bf16[256,2048]{1,0:T(8,128)(2,1)}, bf16[256,2048]{1,0:T(8,128)(2,1)S(1)}, u32[]{:S(2)}, u32[]{:S(2)}) collective-permute-start(bf16[256,2048]{1,0:T(8,128)(2,1)} %collective-permute-done.48), channel_id=1, source_target_pairs={{0,1},{1,3},{3,5},{5,7},{7,6},{6,4},{4,2},{2,0},{8,9},{9,11},{11,1... | collective-permute-start | bytes 3145736 | tf_op jit(solution)/shard_map/ppermute | solution.py:79
  460.7 22.6 %collective-permute-start.46 = (bf16[256,2048]{1,0:T(8,128)(2,1)}, bf16[256,2048]{1,0:T(8,128)(2,1)S(1)}, u32[]{:S(2)}, u32[]{:S(2)}) collective-permute-start(bf16[256,2048]{1,0:T(8,128)(2,1)} %collective-permute-done.45), channel_id=1, source_target_pairs={{1,0},{3,1},{5,3},{7,5},{6,7},{4,6},{2,4},{0,2},{9,8},{11,9},{13,1... | collective-permute-start | bytes 3145736 | tf_op jit(solution)/shard_map/ppermute | solution.py:82
  517.4 25.9 %collective-permute-start.53 = (bf16[256,2048]{1,0:T(8,128)(2,1)S(1)}, bf16[256,2048]{1,0:T(8,128)(2,1)S(1)}, u32[]{:S(2)}, u32[]{:S(2)}) collective-permute-start(bf16[256,2048]{1,0:T(8,128)(2,1)S(1)} %add_convert_fusion.18), channel_id=1, source_target_pairs={{0,1},{1,3},{3,5},{5,7},{7,6},{6,4},{4,2},{2,0},{8,9},{9,11},{11,1... | collective-permute-start | bytes 3145736 | tf_op jit(solution)/shard_map/ppermute | solution.py:79
  519.5 24.8 %collective-permute-start.55 = (bf16[256,2048]{1,0:T(8,128)(2,1)S(1)}, bf16[256,2048]{1,0:T(8,128)(2,1)S(1)}, u32[]{:S(2)}, u32[]{:S(2)}) collective-permute-start(bf16[256,2048]{1,0:T(8,128)(2,1)S(1)} %add_convert_fusion.16), channel_id=1, source_target_pairs={{1,0},{3,1},{5,3},{7,5},{6,7},{4,6},{2,4},{0,2},{9,8},{11,9},{13,1... | collective-permute-start | bytes 3145736 | tf_op jit(solution)/shard_map/ppermute | solution.py:82
  570.7 25.6 %collective-permute-start.58 = (bf16[256,2048]{1,0:T(8,128)(2,1)S(1)}, bf16[256,2048]{1,0:T(8,128)(2,1)S(1)}, u32[]{:S(2)}, u32[]{:S(2)}) collective-permute-start(bf16[256,2048]{1,0:T(8,128)(2,1)S(1)} %copy-done.76), channel_id=1, source_target_pairs={{0,1},{1,3},{3,5},{5,7},{7,6},{6,4},{4,2},{2,0},{8,9},{9,11},{11,1... | collective-permute-start | bytes 3145736 | tf_op jit(solution)/shard_map/ppermute | solution.py:79
  571.8 25.3 %collective-permute-start.59 = (bf16[256,2048]{1,0:T(8,128)(2,1)S(1)}, bf16[256,2048]{1,0:T(8,128)(2,1)S(1)}, u32[]{:S(2)}, u32[]{:S(2)}) collective-permute-start(bf16[256,2048]{1,0:T(8,128)(2,1)S(1)} %copy-done.77), channel_id=1, source_target_pairs={{1,0},{3,1},{5,3},{7,5},{6,7},{4,6},{2,4},{0,2},{9,8},{11,9},{13,1... | collective-permute-start | bytes 3145736 | tf_op jit(solution)/shard_map/ppermute | solution.py:82
  614.1 31.1 %all-to-all-start.2 = ((bf16[8,256,256]{2,1,0:T(8,128)(2,1)}), bf16[8,256,256]{2,1,0:T(8,128)(2,1)}, u32[]{:S(2)}, u32[]{:S(2)}) async-start(bf16[8,256,256]{2,1,0:T(8,128)(2,1)} %bitcast.297), calls=%async_computation.2 | async-start | bytes 2097152 | tf_op jit(solution)/shard_map/all_to_all | solution.py:655
  618.6 48.3 %collective-permute-start.69 = (bf16[1024,512]{1,0:T(8,128)(2,1)}, bf16[1024,512]{1,0:T(8,128)(2,1)}, u32[]{:S(2)}, u32[]{:S(2)}) collective-permute-start(bf16[1024,512]{1,0:T(8,128)(2,1)} %get-tuple-element.164), channel_id=1, source_target_pairs={{0,16},{8,24},{16,0},{24,8},{1,17},{9,25},{17,1},{25,9},{2,18},{10... | collective-permute-start | bytes 3145736 | tf_op jit(solution)/shard_map/ppermute | solution.py:36
  620.1 47.3 %collective-permute-start.70 = (bf16[512,1024]{1,0:T(8,128)(2,1)}, bf16[512,1024]{1,0:T(8,128)(2,1)}, u32[]{:S(2)}, u32[]{:S(2)}) collective-permute-start(bf16[512,1024]{1,0:T(8,128)(2,1)} %get-tuple-element.165), channel_id=1, source_target_pairs={{0,16},{8,24},{16,0},{24,8},{1,17},{9,25},{17,1},{25,9},{2,18},{10... | collective-permute-start | bytes 3145736 | tf_op jit(solution)/shard_map/ppermute | solution.py:36
  645.2 21.5 %collective-permute-start.67 = (bf16[64,2048]{1,0:T(8,128)(2,1)}, bf16[64,2048]{1,0:T(8,128)(2,1)S(1)}, u32[]{:S(2)}, u32[]{:S(2)}) collective-permute-start(bf16[64,2048]{1,0:T(8,128)(2,1)} %get-tuple-element.162), channel_id=1, source_target_pairs={{0,1},{1,3},{3,5},{5,7},{7,6},{6,4},{4,2},{2,0},{8,9},{9,11},{11,1... | collective-permute-start | bytes 786440 | tf_op jit(solution)/shard_map/ppermute | solution.py:79
  650.5 38.9 %collective-permute-start.73 = (bf16[512,1024]{1,0:T(8,128)(2,1)S(1)}, bf16[512,1024]{1,0:T(8,128)(2,1)}, u32[]{:S(2)}, u32[]{:S(2)}) collective-permute-start(bf16[512,1024]{1,0:T(8,128)(2,1)S(1)} %copy-done.75), channel_id=1, source_target_pairs={{0,16},{8,24},{16,0},{24,8},{1,17},{9,25},{17,1},{25,9},{2,18},{10... | collective-permute-start | bytes 3145736 | tf_op jit(solution)/shard_map/ppermute | solution.py:36
  734.3 26.1 %collective-permute-start.81 = (bf16[256,2048]{1,0:T(8,128)(2,1)S(1)}, bf16[256,2048]{1,0:T(8,128)(2,1)S(1)}, u32[]{:S(2)}, u32[]{:S(2)}) collective-permute-start(bf16[256,2048]{1,0:T(8,128)(2,1)S(1)} %get-tuple-element.191), channel_id=1, source_target_pairs={{0,1},{1,3},{3,5},{5,7},{7,6},{6,4},{4,2},{2,0},{8,9},{9,11},{11,1... | collective-permute-start | bytes 3145736 | tf_op jit(solution)/shard_map/ppermute | solution.py:79
  735.6 26.1 %collective-permute-start.82 = (bf16[256,2048]{1,0:T(8,128)(2,1)S(1)}, bf16[256,2048]{1,0:T(8,128)(2,1)S(1)}, u32[]{:S(2)}, u32[]{:S(2)}) collective-permute-start(bf16[256,2048]{1,0:T(8,128)(2,1)S(1)} %get-tuple-element.192), channel_id=1, source_target_pairs={{1,0},{3,1},{5,3},{7,5},{6,7},{4,6},{2,4},{0,2},{9,8},{11,9},{13,1... | collective-permute-start | bytes 3145736 | tf_op jit(solution)/shard_map/ppermute | solution.py:82
  745.8 24.8 %collective-permute-start.90 = (bf16[128,2048]{1,0:T(8,128)(2,1)S(1)}, bf16[128,2048]{1,0:T(8,128)(2,1)S(1)}, u32[]{:S(2)}, u32[]{:S(2)}) collective-permute-start(bf16[128,2048]{1,0:T(8,128)(2,1)S(1)} %fusion.56), channel_id=1, source_target_pairs={{0,1},{1,3},{3,5},{5,7},{7,6},{6,4},{4,2},{2,0},{8,9},{9,11},{11,1... | collective-permute-start | bytes 1572872 | tf_op jit(solution)/shard_map/ppermute | solution.py:79
  747.0 24.3 %collective-permute-start.91 = (bf16[128,2048]{1,0:T(8,128)(2,1)S(1)}, bf16[128,2048]{1,0:T(8,128)(2,1)S(1)}, u32[]{:S(2)}, u32[]{:S(2)}) collective-permute-start(bf16[128,2048]{1,0:T(8,128)(2,1)S(1)} %fusion.55), channel_id=1, source_target_pairs={{1,0},{3,1},{5,3},{7,5},{6,7},{4,6},{2,4},{0,2},{9,8},{11,9},{13,1... | collective-permute-start | bytes 1572872 | tf_op jit(solution)/shard_map/ppermute | solution.py:82
  766.1 26.1 %collective-permute-start.83 = (bf16[256,2048]{1,0:T(8,128)(2,1)S(1)}, bf16[256,2048]{1,0:T(8,128)(2,1)S(1)}, u32[]{:S(2)}, u32[]{:S(2)}) collective-permute-start(bf16[256,2048]{1,0:T(8,128)(2,1)S(1)} %get-tuple-element.194), channel_id=1, source_target_pairs={{0,1},{1,3},{3,5},{5,7},{7,6},{6,4},{4,2},{2,0},{8,9},{9,11},{11,1... | collective-permute-start | bytes 3145736 | tf_op jit(solution)/shard_map/ppermute | solution.py:79
  770.6 22.8 %collective-permute-start.84 = (bf16[256,2048]{1,0:T(8,128)(2,1)S(1)}, bf16[256,2048]{1,0:T(8,128)(2,1)S(1)}, u32[]{:S(2)}, u32[]{:S(2)}) collective-permute-start(bf16[256,2048]{1,0:T(8,128)(2,1)S(1)} %get-tuple-element.195), channel_id=1, source_target_pairs={{1,0},{3,1},{5,3},{7,5},{6,7},{4,6},{2,4},{0,2},{9,8},{11,9},{13,1... | collective-permute-start | bytes 3145736 | tf_op jit(solution)/shard_map/ppermute | solution.py:82
  772.1 23.5 %collective-permute-start.87 = (bf16[512,768]{1,0:T(8,128)(2,1)S(1)}, bf16[512,768]{1,0:T(8,128)(2,1)S(1)}, u32[]{:S(2)}, u32[]{:S(2)}) collective-permute-start(bf16[512,768]{1,0:T(8,128)(2,1)S(1)} %get-tuple-element.298), channel_id=1, source_target_pairs={{0,16},{8,24},{16,0},{24,8},{1,17},{9,25},{17,1},{25,9},{2,18},{10... | collective-permute-start | bytes 2359304 | tf_op jit(solution)/shard_map/ppermute | solution.py:36
  773.4 33.4 %collective-permute-start.92 = (f32[1,64,2048]{2,1,0:T(8,128)}, f32[1,64,2048]{2,1,0:T(8,128)}, u32[]{:S(2)}, u32[]{:S(2)}) collective-permute-start(f32[1,64,2048]{2,1,0:T(8,128)} %dynamic-slice_bitcast_fusion.1), channel_id=1, source_target_pairs={{0,16},{8,24},{16,0},{24,8},{1,17},{9,25},{17,1},{25,9},{2,18},{10... | collective-permute-start | bytes 1572872 | tf_op jit(solution)/shard_map/ppermute | solution.py:36
  795.5 27.5 %collective-permute-start.88 = (bf16[256,2048]{1,0:T(8,128)(2,1)}, bf16[256,2048]{1,0:T(8,128)(2,1)}, u32[]{:S(2)}, u32[]{:S(2)}) collective-permute-start(bf16[256,2048]{1,0:T(8,128)(2,1)} %get-tuple-element.197), channel_id=1, source_target_pairs={{0,1},{1,3},{3,5},{5,7},{7,6},{6,4},{4,2},{2,0},{8,9},{9,11},{11,1... | collective-permute-start | bytes 3145736 | tf_op jit(solution)/shard_map/ppermute | solution.py:79
  796.9 26.0 %collective-permute-start.89 = (bf16[256,2048]{1,0:T(8,128)(2,1)}, bf16[256,2048]{1,0:T(8,128)(2,1)}, u32[]{:S(2)}, u32[]{:S(2)}) collective-permute-start(bf16[256,2048]{1,0:T(8,128)(2,1)} %get-tuple-element.198), channel_id=1, source_target_pairs={{1,0},{3,1},{5,3},{7,5},{6,7},{4,6},{2,4},{0,2},{9,8},{11,9},{13,1... | collective-permute-start | bytes 3145736 | tf_op jit(solution)/shard_map/ppermute | solution.py:82
  798.6 37.4 %all-to-all-start.3 = ((bf16[8,64,768]{2,1,0:T(8,128)(2,1)}), bf16[8,64,768]{2,1,0:T(8,128)(2,1)}, u32[]{:S(2)}, u32[]{:S(2)}) async-start(bf16[8,64,768]{2,1,0:T(8,128)(2,1)} %bitcast.328), calls=%async_computation.3 | async-start | bytes 1572864 | tf_op jit(solution)/shard_map/all_to_all | solution.py:738
  (152 other events, 1831.8 us)
Sparse Core Ops, SparseCore 0:
  114.2 96.4 all-gather.1

commit v5 on v4

--- a/solution.py
+++ b/solution.py
@@ -305,83 +305,93 @@
 def column(row):
     return jnp.broadcast_to(row, (HEAD, row.shape[1])).T
 
-def attend_forward_kernel(first_ref, q_ref, k_ref, v_ref, scale_ref, gain_ref, cos_ref, sin_ref, begin_ref,
-                          out_ref, qr_ref, kr_ref, vl_ref, lse_ref, vt_ref):
-    blocks = q_ref.shape[0] // BLOCK
-    factor = HEAD ** -0.5 * LOG2E
-
-    def prepare(i, _):
-        rows = pl.ds(pl.multiple_of(i * BLOCK, BLOCK), BLOCK)
-        for n, (src, dst) in enumerate(((q_ref, qr_ref), (k_ref, kr_ref))):
-            x = src[rows, :] * column(scale_ref[n : n + 1, rows]) * gain_ref[n : n + 1, :]
-            x = x * cos_ref[rows, :] + pltpu.roll(x, HEAD // 2, 1) * sin_ref[rows, :]
-            dst[rows, :] = x.astype(LOW)
-        v = v_ref[rows, :].astype(LOW)
-        vl_ref[rows, :] = v
-        vt_ref[:, rows] = v.T
-        return 0
-
-    lax.fori_loop(0, blocks, prepare, 0)
-
-    def one(i, _):
-        rows = pl.ds(pl.multiple_of(i * BLOCK, BLOCK), BLOCK)
-        q = qr_ref[rows, :]
-        begin = begin_ref[0:1, rows]
-        at = lax.broadcasted_iota(jnp.int32, (BLOCK, BLOCK), 0)
-        query_at = lax.broadcasted_iota(jnp.int32, (1, BLOCK), 1) + i * BLOCK
-
-        def step(j, carry):
-            top, total, acc = carry
-            keys = pl.ds(pl.multiple_of(j * BLOCK, BLOCK), BLOCK)
-            s = dot_nt(kr_ref[keys, :], q)
-            key_at = at + j * BLOCK
-            s = jnp.where((key_at >= begin) & (key_at <= query_at), s, NEG)
+def attend_forward_kernel(
+    first_ref,
+    q_ref,
+    k_ref,
+    v_ref,
+    scale_ref,
+    gain_ref,
+    cos_ref,
+    sin_ref,
+    begin_ref,
+    out_ref,
+    qr_ref,
+    kr_ref,
+    vl_ref,
+    lse_ref,
+    keys_ref,
+    vt_ref,
+):
+    i = pl.program_id(0)
+    rows = pl.ds(pl.multiple_of(i * BLOCK, BLOCK), BLOCK)
+    heads = [slice(at, at + HEAD) for at in range(0, q_ref.shape[1], HEAD)]
+    factor = HEAD**-0.5 * LOG2E
+    for n, (src, dst) in enumerate(((q_ref, qr_ref), (k_ref, kr_ref))):
+        scale = column(scale_ref[n : n + 1, :])
+        for head in heads:
+            x = src[:, head] * scale * gain_ref[n : n + 1, head]
+            x = x * cos_ref[...] + pltpu.roll(x, HEAD // 2, 1) * sin_ref[...]
+            dst[:, head] = x.astype(LOW)
+    keys_ref[rows, :] = kr_ref[...]
+    for head in heads:
+        v = v_ref[:, head].astype(LOW)
+        vl_ref[:, head] = v
+        vt_ref[head, rows] = v.T
+    begin = begin_ref[0:1, :]
+    at = lax.broadcasted_iota(jnp.int32, (BLOCK, BLOCK), 0)
+    query_at = lax.broadcasted_iota(jnp.int32, (1, BLOCK), 1) + i * BLOCK
+
+    def step(j, carry):
+        keys = pl.ds(pl.multiple_of(j * BLOCK, BLOCK), BLOCK)
+        key_at = at + j * BLOCK
+        keep = (key_at >= begin) & (key_at <= query_at)
+        scores = [
+            jnp.where(keep, dot_nt(keys_ref[keys, head], qr_ref[:, head]), NEG) for head in heads
+        ]
+        out = []
+        for head, s, (top, total, acc) in zip(heads, scores, carry):
             new = jnp.maximum(top, jnp.max(s, axis=0, keepdims=True))
             p = jnp.exp2((s - new) * factor)
             shrink = jnp.exp2((top - new) * factor)
             total = total * shrink + jnp.sum(p, axis=0, keepdims=True)
-            acc = acc * shrink + dot(vt_ref[:, keys], p.astype(LOW))
-            return new, total, acc
-
-        start = (jnp.full((1, BLOCK), NEG, FULL), jnp.zeros((1, BLOCK), FULL), jnp.zeros((HEAD, BLOCK), FULL))
-        top, total, acc = lax.fori_loop(first_ref[i], i + 1, step, start)
-        out_ref[rows, :] = (acc / total).T.astype(LOW)
-        lse_ref[0, 0:1, rows] = top * factor + jnp.log2(total)
-        return 0
-
-    lax.fori_loop(0, blocks, one, 0)
+            acc = acc * shrink + dot(vt_ref[head, keys], p.astype(LOW))
+            out.append((new, total, acc))
+        return tuple(out)
+
+    start = (
+        jnp.full((1, BLOCK), NEG, FULL),
+        jnp.zeros((1, BLOCK), FULL),
+        jnp.zeros((HEAD, BLOCK), FULL),
+    )
+    done = lax.fori_loop(first_ref[i], i + 1, step, (start,) * len(heads))
+    for h, (top, total, acc) in enumerate(done):
+        out_ref[:, heads[h]] = (acc / total).T.astype(LOW)
+        lse_ref[h, 0:1, :] = top * factor + jnp.log2(total)
 
 
 def attend_forward(pre, scales, gains, cosine, sine, first, begin):
     rows, wide = pre.shape
-    heads = wide // (3 * HEAD)
-
-    def col(shift):
-        return pl.BlockSpec((rows, HEAD), lambda h, f: (0, h + shift))
-
-    def fixed(*shape):
-        return pl.BlockSpec(shape, lambda h, f: (0,) * len(shape))
+    own = wide // 3
+
+    def part(cols, at=0):
+        return pl.BlockSpec((BLOCK, cols), lambda i, f: (i, at))
+
+    def along(*lead):
+        return pl.BlockSpec((*lead, BLOCK), lambda i, f: (0,) * len(lead) + (i,))
 
     return pl.pallas_call(
         attend_forward_kernel,
         grid_spec=pltpu.PrefetchScalarGridSpec(
             num_scalar_prefetch=1,
-            grid=(heads,),
-            in_specs=[
-                col(0),
-                col(heads),
-                col(2 * heads),
-                fixed(2, rows),
-                pl.BlockSpec((2, HEAD), lambda h, f: (0, h)),
-                fixed(rows, HEAD),
-                fixed(rows, HEAD),
-                fixed(1, rows),
-            ],
-            out_specs=[col(0)] * 4 + [pl.BlockSpec((1, 1, rows), lambda h, f: (h, 0, 0))],
-            scratch_shapes=[pltpu.VMEM((HEAD, rows), LOW)],
+            grid=(rows // BLOCK,),
+            in_specs=[part(own), part(own, 1), part(own, 2), along(2)]
+            + [pl.BlockSpec((2, own), lambda i, f: (0, 0)), part(HEAD), part(HEAD), along(1)],
+            out_specs=[part(own)] * 4 + [along(own // HEAD, 1)],
+            scratch_shapes=[pltpu.VMEM((rows, own), LOW), pltpu.VMEM((own, rows), LOW)],
         ),
-        out_shape=[jax.ShapeDtypeStruct((rows, heads * HEAD), LOW)] * 4
-        + [jax.ShapeDtypeStruct((heads, 1, rows), FULL)],
+        out_shape=[jax.ShapeDtypeStruct((rows, own), LOW)] * 4
+        + [jax.ShapeDtypeStruct((own // HEAD, 1, rows), FULL)],
         compiler_params=pltpu.CompilerParams(vmem_limit_bytes=48 * 2**20),
         cost_estimate=LIGHT,
         name="attend_forward",
@@ -539,12 +549,11 @@
             state["w_heads"] = lax.all_to_all(packed, "seq", split_axis=0, concat_axis=0, tiled=True)
             return ["gains"]
         if step == 2:
-            state["gate"] = swap_chips(w_gate, chips)
-            return ["gains", "w_heads", "down", "gate", "begin"]
+            return ["gains", "w_heads", "down", "begin"]
         if step == 3:
             state["w_heads"] = swap_chips(state["w_heads"].reshape(-1, 3 * own), chips)
-            state["up"] = w_up
-            return ["gains", "w_heads", "up"]
+            state["gate"], state["up"] = w_gate, w_up
+            return ["gains", "w_heads", "gate", "up"]
         return ["gains"]
 
     state["begin"] = begin
@@ -553,7 +562,7 @@
     first_block = begin[::BLOCK] // BLOCK
     cosine, sine = rope_tables(jnp.arange(row_len, dtype=jnp.int32) - begin)
     begin = begin[None]
-    state["up"] = swap_chips(state["up"], chips)
+    state["gate"] = swap_chips(state["gate"], chips)
     last = row_ring.size // 2
     row_tokens = jnp.zeros((row_len, width), LOW)
     for offset, chunk in row_chunks.items():
@@ -576,7 +585,8 @@
     query_pre, key_pre = pre[:, :own], pre[:, own : 2 * own]
     squares = jnp.stack([jnp.sum(query_pre * query_pre, axis=1), jnp.sum(key_pre * key_pre, axis=1)])
     scales = lax.rsqrt(sum_over(squares, "seq", seq) / width + EPSILON)
-    scales, state["up"] = tie(scales, state["up"])
+    scales, state["gate"], state["up"] = tie(scales, state["gate"], state["up"])
+    state["up"] = swap_chips(state["up"], chips)
     attn_heads, query_rot, key_rot, values, log_sums = attend_forward(
         pre, scales, gains_own, cosine, sine, first_block, begin
     )

time: 862 us -> 860 us (level)
    ppermute x34, waiting for transfers between devices: 59.6 us -> 33.4 us  [swap(): return lax.ppermute(val, axis, [(i, i ^ mask) for i in range(size)])]
    ppermute x28, waiting for transfers between devices: 181 us -> 200 us  [right(): return lax.ppermute(val, 'seq', self.forth)]
    ppermute x28, starting transfers between devices: 25.4 us -> 34 us  [left(): return lax.ppermute(val, 'seq', self.back)]
    unnamed x225 -> x235, local copies, waits for them, and re-layouts: 51.4 us -> 52.9 us
  transfers between devices with their start and end apart: 100 -> 100, of which waited for: 54 -> 56; matrix products, arithmetic and copies ran while one was open for 31% -> 32% of each run, Pallas kernels for 6% -> 6%
where the time goes in v5:
time: 860 us; the launch traced here: 850 us
  waiting for transfers between devices  323 us (38%)
  matrix products  169 us (20%)
  starting transfers between devices  112 us (13%)
  local copies, waits for them, and re-layouts  94.1 us (11%)
  other arithmetic  80.8 us (9%)
  Pallas kernels  54.4 us (6%)
  between operations  16.4 us (2%)
    ppermute x28, waiting for transfers between devices, right(): return lax.ppermute(val, 'seq', self.forth)  200 us
    dot_general x18, matrix products, dot_nt(): lax.dot_general(left, right, (((1,), (1,)), ((), ())), preferred_element_...  69.4 us
    dot_general x18, matrix products, dot(): return jnp.dot(left, right, preferred_element_type=FULL)  53.6 us
    unnamed x235, local copies, waits for them, and re-layouts  52.9 us
    dot_general x5, matrix products, dot_tn(): lax.dot_general(left, right, (((0,), (0,)), ((), ())), preferred_element_...  46.1 us
    all_to_all x1, waiting for transfers between devices, per_device(): lax.all_to_all(attn_heads.reshape(seq, count, own), 'seq', split_axis=0,...  35.2 us
    ppermute x28, starting transfers between devices, left(): return lax.ppermute(val, 'seq', self.back)  34 us
    ppermute x34, waiting for transfers between devices, swap(): return lax.ppermute(val, axis, [(i, i ^ mask) for i in range(size)])  33.4 us
  transfers between devices with their start and end apart: 100, of which 56 were waited for; matrix products, arithmetic and copies ran while one was open for 32% of the time, Pallas kernels for 6%

profile of v5, /device:TPU:0, one launch (start us, length us, event | category | flops | bytes accessed | tf_op | source)
XLA Modules:
  0.0 849.6 jit_solution(953013234455785763)
XLA Ops:
  20.8 5.8 all-to-all-start
  28.8 4.3 broadcast_in_dim.73
  44.0 6.5 collective-permute-done.6.refs_1_
  52.8 16.0 %collective-permute-done.3 = bf16[256,2048]{1,0:T(8,128)(2,1)} collective-permute-done((bf16[256,2048]{1,0:T(8,128)(2,1)}, bf16[256,2048]{1,0:T(8,128)(2,1)}, u32[]{:S(2)}, u32[]{:S(2)}) %collective-permute-start.3) | collective-permute-done | bytes 1048608 | tf_op jit(solution)/shard_map/ppermute | solution.py:79
  73.4 5.7 collective-permute-start.8
  89.6 11.1 %collective-permute-done.7 = bf16[256,2048]{1,0:T(8,128)(2,1)S(1)} collective-permute-done((bf16[256,2048]{1,0:T(8,128)(2,1)}, bf16[256,2048]{1,0:T(8,128)(2,1)S(1)}, u32[]{:S(2)}, u32[]{:S(2)}) %collective-permute-start.7) | collective-permute-done | bytes 1048608 | tf_op jit(solution)/shard_map/ppermute | solution.py:79
  107.6 4.6 collective-permute-done.12
  124.8 10.2 %fusion.84.q_ref.k_ref.v_ref.qp_ref.kp_ref = f32[2048,768]{1,0:T(8,128)S(1)} fusion(bf16[2048,2048]{1,0:T(8,128)(2,1)} %constant_dynamic-update-slice_fusion.67, bf16[2048,768]{1,0:T(8,128)(2,1)S(1)} %assemble.3), kind=kOutput, calls=%fused_computation.358 | convolution fusion | flops 6442450944 | bytes 17825792 | tf_op jit(solution)/shard_map/dot_general | solution.py:23
  150.8 15.5 %attend_forward.1 = (bf16[2048,256]{1,0:T(8,128)(2,1)S(1)}, bf16[2048,256]{1,0:T(8,128)(2,1)S(1)}, bf16[2048,256]{1,0:T(8,128)(2,1)S(1)}, bf16[2048,256]{1,0:T(8,128)(2,1)S(1)}, f32[2,1,2048]{2,1,0:T(1,128)S(1)}) custom-call(s32[4]{0:T(128)S(1)} %and_select_fusion.first_ref, f32[2048,768]{1,0:T(8,128)} %copy-done.35, f32[2048,768]{1,0:T(8,128)} %copy-done.35, ...), custom_call_target="tpu_custom_call" | custom-call | flops 1 | bytes 1 | tf_op jit(solution)/shard_map/attend_forward/pallas_call | solution.py:383
  174.5 35.2 %all-to-all-done.1 = bf16[8,256,256]{1,2,0:T(8,128)(2,1)S(1)} async-done(((bf16[8,256,256]{1,2,0:T(8,128)(2,1)}), bf16[8,256,256]{1,2,0:T(8,128)(2,1)S(1)}, u32[]{:S(2)}, u32[]{:S(2)}) %all-to-all-start.1) | async-done | bytes 1048608 | tf_op jit(solution)/shard_map/all_to_all | solution.py:593
  210.7 5.9 multiply_reduce_fusion.3
  226.1 7.1 assemble.4
  233.3 6.2 fusion.85
  239.5 5.7 collective-permute-done.31
  262.0 7.7 collective-permute-done.32
  282.6 10.7 %collective-permute-done.33 = bf16[256,2048]{1,0:T(8,128)(2,1)S(1)} collective-permute-done((bf16[256,2048]{1,0:T(8,128)(2,1)}, bf16[256,2048]{1,0:T(8,128)(2,1)S(1)}, u32[]{:S(2)}, u32[]{:S(2)}) %collective-permute-start.33) | collective-permute-done | bytes 1048608 | tf_op jit(solution)/shard_map/ppermute | solution.py:79
  294.9 4.6 collective-permute-done.30
  320.1 7.0 collective-permute-done.36
  334.7 15.8 %collective-permute-done.37 = bf16[256,2048]{1,0:T(8,128)(2,1)S(1)} collective-permute-done((bf16[256,2048]{1,0:T(8,128)(2,1)S(1)}, bf16[256,2048]{1,0:T(8,128)(2,1)S(1)}, u32[]{:S(2)}, u32[]{:S(2)}) %collective-permute-start.37) | collective-permute-done | bytes 1048608 | tf_op jit(solution)/shard_map/ppermute | solution.py:79
  359.1 14.8 %collective-permute-done.38 = bf16[256,2048]{1,0:T(8,128)(2,1)S(1)} collective-permute-done((bf16[256,2048]{1,0:T(8,128)(2,1)S(1)}, bf16[256,2048]{1,0:T(8,128)(2,1)S(1)}, u32[]{:S(2)}, u32[]{:S(2)}) %collective-permute-start.38) | collective-permute-done | bytes 1048608 | tf_op jit(solution)/shard_map/ppermute | solution.py:79
  388.0 5.0 collective-permute-done.39
  406.7 11.1 %collective-permute-done.47 = bf16[256,2048]{1,0:T(8,128)(2,1)S(1)} collective-permute-done((bf16[256,2048]{1,0:T(8,128)(2,1)S(1)}, bf16[256,2048]{1,0:T(8,128)(2,1)S(1)}, u32[]{:S(2)}, u32[]{:S(2)}) %collective-permute-start.47) | collective-permute-done | bytes 1048608 | tf_op jit(solution)/shard_map/ppermute | solution.py:79
  426.1 4.9 fusion.23
  440.6 7.5 collective-permute-done.48
  461.2 4.7 fusion.42
  470.6 10.4 %collective-permute-done.49 = bf16[256,2048]{1,0:T(8,128)(2,1)S(1)} collective-permute-done((bf16[256,2048]{1,0:T(8,128)(2,1)}, bf16[256,2048]{1,0:T(8,128)(2,1)S(1)}, u32[]{:S(2)}, u32[]{:S(2)}) %collective-permute-start.49) | collective-permute-done | bytes 1048608 | tf_op jit(solution)/shard_map/ppermute | solution.py:79
  512.7 5.5 collective-permute-done.52
  522.1 11.9 %convolution_convert_fusion.2 = bf16[1024,2048]{1,0:T(8,128)(2,1)S(1)} fusion(bf16[2048,1024]{1,0:T(8,128)(2,1)S(1)} %copy-done.87, bf16[2048,2048]{1,0:T(8,128)(2,1)} %constant_dynamic-update-slice_fusion.8), kind=kOutput, calls=%fused_computation.5 | convolution fusion | flops 8592031744 | bytes 16777216 | tf_op jit(solution)/shard_map/dot_general | solution.py:31
  534.0 8.2 collective-permute-done.53
  545.0 10.9 %convolution_convert_fusion.4 = bf16[2048,1024]{1,0:T(8,128)(2,1)} fusion(bf16[2048,2048]{1,0:T(8,128)(2,1)S(1)} %bitcast.346, bf16[2048,1024]{1,0:T(8,128)(2,1)S(1)} %copy-done.98), kind=kOutput, calls=%fused_computation.7 | convolution fusion | flops 8592031744 | bytes 16777216 | tf_op jit(solution)/shard_map/dot_general | solution.py:31
  561.8 6.2 fusion.19
  571.0 11.7 %convolution_convert_fusion.3 = bf16[2048,1024]{1,0:T(8,128)(2,1)S(1)} fusion(bf16[2048,2048]{1,0:T(8,128)(2,1)} %constant_dynamic-update-slice_fusion.17, bf16[2048,1024]{1,0:T(8,128)(2,1)S(1)} %copy-done.99), kind=kOutput, calls=%fused_computation.6 | convolution fusion | flops 8592031744 | bytes 16777216 | tf_op jit(solution)/shard_map/dot_general | solution.py:31
  589.3 4.3 collective-permute-done.58
  610.1 5.4 all-to-all-start.2
  618.2 4.5 add_convert_fusion.7
  622.7 5.4 fusion
  630.8 11.1 %all-to-all-done.2 = bf16[8,256,256]{2,1,0:T(8,128)(2,1)} async-done(((bf16[8,256,256]{2,1,0:T(8,128)(2,1)}), bf16[8,256,256]{2,1,0:T(8,128)(2,1)}, u32[]{:S(2)}, u32[]{:S(2)}) %all-to-all-start.2) | async-done | bytes 1048608 | tf_op jit(solution)/shard_map/all_to_all | solution.py:665
  648.8 14.8 %attend_backward.2 = (f32[2048,128]{1,0:T(8,128)S(1)}, f32[2048,128]{1,0:T(8,128)S(1)}, bf16[2048,128]{1,0:T(8,128)(2,1)S(1)}, f32[1,2,2048]{2,1,0:T(2,128)S(1)}, f32[2,128]{1,0:T(2,128)S(1)}) custom-call(s32[4]{0:T(128)S(1)} %copy-done.34, bf16[2048,256]{1,0:T(8,128)(2,1)S(1)} %get-tuple-element.153.q_ref, bf16[2048,256]{1,0:T(8,128)(2,1)S(1)} %copy-done.3, ...), custom_call_target="tpu_custom_call" | custom-call | flops 1 | bytes 1 | tf_op jit(solution)/shard_map/attend_backward/pallas_call | solution.py:471
  667.9 14.8 %attend_backward.3 = (f32[2048,128]{1,0:T(8,128)S(1)}, f32[2048,128]{1,0:T(8,128)S(1)}, bf16[2048,128]{1,0:T(8,128)(2,1)S(1)}, f32[1,2,2048]{2,1,0:T(2,128)S(1)}, f32[2,128]{1,0:T(2,128)S(1)}) custom-call(s32[4]{0:T(128)S(1)} %copy-done.34, bf16[2048,256]{1,0:T(8,128)(2,1)S(1)} %get-tuple-element.153.q_ref, bf16[2048,256]{1,0:T(8,128)(2,1)S(1)} %copy-done.3, ...), custom_call_target="tpu_custom_call" | custom-call | flops 1 | bytes 1 | tf_op jit(solution)/shard_map/attend_backward/pallas_call | solution.py:471
  692.5 4.6 collective-permute-done.75
  708.0 7.2 convolution_convert_fusion
  720.5 9.6 %collective-permute-done.77 = bf16[128,2048]{1,0:T(8,128)(2,1)S(1)} collective-permute-done((bf16[128,2048]{1,0:T(8,128)(2,1)S(1)}, bf16[128,2048]{1,0:T(8,128)(2,1)S(1)}, u32[]{:S(2)}, u32[]{:S(2)}) %collective-permute-start.77) | collective-permute-done | bytes 524320 | tf_op jit(solution)/shard_map/ppermute | solution.py:79
  733.8 9.3 %convolution_convert_fusion.5 = bf16[2048,768]{1,0:T(8,128)(2,1)S(1)} fusion(bf16[2048,2048]{1,0:T(8,128)(2,1)} %constant_dynamic-update-slice_fusion.67, bf16[2048,768]{1,0:T(8,128)(2,1)S(1)} %pad_maximum_fusion), kind=kOutput, calls=%fused_computation.8 | convolution fusion | flops 6444023808 | bytes 14680064 | tf_op jit(solution)/shard_map/dot_general | solution.py:31
  748.1 9.8 %collective-permute-done.81 = bf16[256,2048]{1,0:T(8,128)(2,1)S(1)} collective-permute-done((bf16[256,2048]{1,0:T(8,128)(2,1)S(1)}, bf16[256,2048]{1,0:T(8,128)(2,1)S(1)}, u32[]{:S(2)}, u32[]{:S(2)}) %collective-permute-start.81) | collective-permute-done | bytes 1048608 | tf_op jit(solution)/shard_map/ppermute | solution.py:79
  772.6 17.3 %collective-permute-done.83 = bf16[256,2048]{1,0:T(8,128)(2,1)S(1)} collective-permute-done((bf16[256,2048]{1,0:T(8,128)(2,1)S(1)}, bf16[256,2048]{1,0:T(8,128)(2,1)S(1)}, u32[]{:S(2)}, u32[]{:S(2)}) %collective-permute-start.83) | collective-permute-done | bytes 1048608 | tf_op jit(solution)/shard_map/ppermute | solution.py:79
  796.2 4.8 all-to-all-start.3
  806.2 13.5 %collective-permute-done.88 = bf16[256,2048]{1,0:T(8,128)(2,1)} collective-permute-done((bf16[256,2048]{1,0:T(8,128)(2,1)}, bf16[256,2048]{1,0:T(8,128)(2,1)}, u32[]{:S(2)}, u32[]{:S(2)}) %collective-permute-start.88) | collective-permute-done | bytes 1048608 | tf_op jit(solution)/shard_map/ppermute | solution.py:79
  823.8 9.6 %all-to-all-done.3 = bf16[8,64,768]{2,1,0:T(8,128)(2,1)} async-done(((bf16[8,64,768]{2,1,0:T(8,128)(2,1)}), bf16[8,64,768]{2,1,0:T(8,128)(2,1)}, u32[]{:S(2)}, u32[]{:S(2)}) %all-to-all-start.3) | async-done | bytes 786464 | tf_op jit(solution)/shard_map/all_to_all | solution.py:748
  (581 shorter events, 388.8 us)
Async XLA Ops:
  7.2 28.8 %collective-permute-start = (bf16[256,2048]{1,0:T(8,128)(2,1)}, bf16[256,2048]{1,0:T(8,128)(2,1)}, u32[]{:S(2)}, u32[]{:S(2)}) collective-permute-start(bf16[256,2048]{1,0:T(8,128)(2,1)} %bitcast.324), channel_id=1, source_target_pairs={{0,1},{1,3},{3,5},{5,7},{7,6},{6,4},{4,2},{2,0},{8,9},{9,11},{11,1... | collective-permute-start | bytes 3145736 | tf_op jit(solution)/shard_map/ppermute | solution.py:79
  10.2 26.5 %collective-permute-start.1 = (bf16[256,2048]{1,0:T(8,128)(2,1)}, bf16[256,2048]{1,0:T(8,128)(2,1)}, u32[]{:S(2)}, u32[]{:S(2)}) collective-permute-start(bf16[256,2048]{1,0:T(8,128)(2,1)} %bitcast.325), channel_id=1, source_target_pairs={{1,0},{3,1},{5,3},{7,5},{6,7},{4,6},{2,4},{0,2},{9,8},{11,9},{13,1... | collective-permute-start | bytes 3145736 | tf_op jit(solution)/shard_map/ppermute | solution.py:82
  11.0 23.1 %collective-permute-start.2 = (bf16[1,4,64]{2,1,0:T(4,128)(2,1)S(1)}, bf16[1,4,64]{2,1,0:T(4,128)(2,1)S(1)}, u32[]{:S(2)}, u32[]{:S(2)}) collective-permute-start(bf16[1,4,64]{2,1,0:T(4,128)(2,1)S(1)} %maximum_bitcast_fusion.2), channel_id=1, source_target_pairs={{0,16},{1,17},{2,18},{3,19},{4,20},{5,21},{6,22},{7,23},{8,24},{9,... | collective-permute-start | bytes 1544 | tf_op jit(solution)/shard_map/ppermute | solution.py:41
  20.8 32.0 %all-to-all-start = ((bf16[8,64,768]{2,1,0:T(8,128)(2,1)}), bf16[8,64,768]{2,1,0:T(8,128)(2,1)S(1)}, u32[]{:S(2)}, u32[]{:S(2)}) async-start(bf16[8,64,768]{2,1,0:T(8,128)(2,1)} %reshape.166), calls=%async_computation | async-start | bytes 1572864 | tf_op jit(solution)/shard_map/all_to_all | solution.py:549
  26.6 183.1 %all-gather.2.cloned.1.call-start = ((), (), s32[]{:S(2)}) async-start(), calls=%async_computation.4 | async-start | bytes 8650752 | tf_op jit(solution)/shard_map/all_gather | solution.py:574
  26.6 23.8 %collective-permute-start.6 = (bf16[1024,512]{1,0:T(8,128)(2,1)S(1)}, bf16[1024,512]{1,0:T(8,128)(2,1)S(1)}, u32[]{:S(2)}, u32[]{:S(2)}) collective-permute-start(bf16[1024,512]{1,0:T(8,128)(2,1)S(1)} %copy-done.10), channel_id=1, source_target_pairs={{0,16},{8,24},{16,0},{24,8},{1,17},{9,25},{17,1},{25,9},{2,18},{10... | collective-permute-start | bytes 3145736 | tf_op jit(solution)/shard_map/ppermute | solution.py:36
  36.6 32.2 %collective-permute-start.3 = (bf16[256,2048]{1,0:T(8,128)(2,1)}, bf16[256,2048]{1,0:T(8,128)(2,1)}, u32[]{:S(2)}, u32[]{:S(2)}) collective-permute-start(bf16[256,2048]{1,0:T(8,128)(2,1)} %collective-permute-done), channel_id=1, source_target_pairs={{0,1},{1,3},{3,5},{5,7},{7,6},{6,4},{4,2},{2,0},{8,9},{9,11},{11,1... | collective-permute-start | bytes 3145736 | tf_op jit(solution)/shard_map/ppermute | solution.py:79
  39.1 29.7 %collective-permute-start.4 = (bf16[256,2048]{1,0:T(8,128)(2,1)}, bf16[256,2048]{1,0:T(8,128)(2,1)}, u32[]{:S(2)}, u32[]{:S(2)}) collective-permute-start(bf16[256,2048]{1,0:T(8,128)(2,1)} %collective-permute-done.1), channel_id=1, source_target_pairs={{1,0},{3,1},{5,3},{7,5},{6,7},{4,6},{2,4},{0,2},{9,8},{11,9},{13,1... | collective-permute-start | bytes 3145736 | tf_op jit(solution)/shard_map/ppermute | solution.py:82
  73.3 27.4 %collective-permute-start.7 = (bf16[256,2048]{1,0:T(8,128)(2,1)}, bf16[256,2048]{1,0:T(8,128)(2,1)S(1)}, u32[]{:S(2)}, u32[]{:S(2)}) collective-permute-start(bf16[256,2048]{1,0:T(8,128)(2,1)} %collective-permute-done.3), channel_id=1, source_target_pairs={{0,1},{1,3},{3,5},{5,7},{7,6},{6,4},{4,2},{2,0},{8,9},{9,11},{11,1... | collective-permute-start | bytes 3145736 | tf_op jit(solution)/shard_map/ppermute | solution.py:79
  73.4 27.4 %collective-permute-start.8 = (bf16[256,2048]{1,0:T(8,128)(2,1)}, bf16[256,2048]{1,0:T(8,128)(2,1)S(1)}, u32[]{:S(2)}, u32[]{:S(2)}) collective-permute-start(bf16[256,2048]{1,0:T(8,128)(2,1)} %collective-permute-done.4), channel_id=1, source_target_pairs={{1,0},{3,1},{5,3},{7,5},{6,7},{4,6},{2,4},{0,2},{9,8},{11,9},{13,1... | collective-permute-start | bytes 3145736 | tf_op jit(solution)/shard_map/ppermute | solution.py:82
  116.9 33.9 %collective-permute-start.18 = (bf16[512,1024]{1,0:T(8,128)(2,1)S(1)}, bf16[512,1024]{1,0:T(8,128)(2,1)}, u32[]{:S(2)}, u32[]{:S(2)}) collective-permute-start(bf16[512,1024]{1,0:T(8,128)(2,1)S(1)} %copy-done.8), channel_id=1, source_target_pairs={{0,16},{8,24},{16,0},{24,8},{1,17},{9,25},{17,1},{25,9},{2,18},{10... | collective-permute-start | bytes 3145736 | tf_op jit(solution)/shard_map/ppermute | solution.py:36
  169.7 40.0 %all-to-all-start.1 = ((bf16[8,256,256]{1,2,0:T(8,128)(2,1)}), bf16[8,256,256]{1,2,0:T(8,128)(2,1)S(1)}, u32[]{:S(2)}, u32[]{:S(2)}) async-start(bf16[8,256,256]{1,2,0:T(8,128)(2,1)} %copy.68), calls=%async_computation.1 | async-start | bytes 2097152 | tf_op jit(solution)/shard_map/all_to_all | solution.py:593
  173.4 45.1 %collective-permute-start.21 = (bf16[512,1024]{1,0:T(8,128)(2,1)}, bf16[512,1024]{1,0:T(8,128)(2,1)}, u32[]{:S(2)}, u32[]{:S(2)}) collective-permute-start(bf16[512,1024]{1,0:T(8,128)(2,1)} %refs_4_), channel_id=1, source_target_pairs={{0,16},{8,24},{16,0},{24,8},{1,17},{9,25},{17,1},{25,9},{2,18},{10... | collective-permute-start | bytes 3145736 | tf_op jit(solution)/shard_map/ppermute | solution.py:36
  219.7 25.5 %collective-permute-start.31 = (bf16[256,2048]{1,0:T(8,128)(2,1)}, bf16[256,2048]{1,0:T(8,128)(2,1)}, u32[]{:S(2)}, u32[]{:S(2)}) collective-permute-start(bf16[256,2048]{1,0:T(8,128)(2,1)} %fusion.12), channel_id=1, source_target_pairs={{0,1},{1,3},{3,5},{5,7},{7,6},{6,4},{4,2},{2,0},{8,9},{9,11},{11,1... | collective-permute-start | bytes 3145736 | tf_op jit(solution)/shard_map/ppermute | solution.py:79
  223.7 27.7 %collective-permute-start.28 = (bf16[256,2048]{1,0:T(8,128)(2,1)}, bf16[256,2048]{1,0:T(8,128)(2,1)}, u32[]{:S(2)}, u32[]{:S(2)}) collective-permute-start(bf16[256,2048]{1,0:T(8,128)(2,1)} %fusion.12), channel_id=1, source_target_pairs={{1,0},{3,1},{5,3},{7,5},{6,7},{4,6},{2,4},{0,2},{9,8},{11,9},{13,1... | collective-permute-start | bytes 3145736 | tf_op jit(solution)/shard_map/ppermute | solution.py:82
  224.7 32.3 %collective-permute-start.26 = (bf16[1024,512]{1,0:T(8,128)(2,1)S(1)}, bf16[1024,512]{1,0:T(8,128)(2,1)S(1)}, u32[]{:S(2)}, u32[]{:S(2)}) collective-permute-start(bf16[1024,512]{1,0:T(8,128)(2,1)S(1)} %copy-done.11), channel_id=1, source_target_pairs={{0,8},{8,0},{16,24},{24,16},{1,9},{9,1},{17,25},{25,17},{2,10},{10... | collective-permute-start | bytes 3145736 | tf_op jit(solution)/shard_map/ppermute | solution.py:36
  224.7 32.3 %collective-permute-start.27 = (bf16[1024,512]{1,0:T(8,128)(2,1)}, bf16[1024,512]{1,0:T(8,128)(2,1)S(1)}, u32[]{:S(2)}, u32[]{:S(2)}) collective-permute-start(bf16[1024,512]{1,0:T(8,128)(2,1)} %copy-done.12), channel_id=1, source_target_pairs={{0,8},{8,0},{16,24},{24,16},{1,9},{9,1},{17,25},{25,17},{2,10},{10... | collective-permute-start | bytes 3145736 | tf_op jit(solution)/shard_map/ppermute | solution.py:36
  245.1 24.6 %collective-permute-start.32 = (bf16[256,2048]{1,0:T(8,128)(2,1)}, bf16[256,2048]{1,0:T(8,128)(2,1)}, u32[]{:S(2)}, u32[]{:S(2)}) collective-permute-start(bf16[256,2048]{1,0:T(8,128)(2,1)} %collective-permute-done.31), channel_id=1, source_target_pairs={{0,1},{1,3},{3,5},{5,7},{7,6},{6,4},{4,2},{2,0},{8,9},{9,11},{11,1... | collective-permute-start | bytes 3145736 | tf_op jit(solution)/shard_map/ppermute | solution.py:79
  251.5 24.4 %collective-permute-start.29 = (bf16[256,2048]{1,0:T(8,128)(2,1)}, bf16[256,2048]{1,0:T(8,128)(2,1)}, u32[]{:S(2)}, u32[]{:S(2)}) collective-permute-start(bf16[256,2048]{1,0:T(8,128)(2,1)} %collective-permute-done.28), channel_id=1, source_target_pairs={{1,0},{3,1},{5,3},{7,5},{6,7},{4,6},{2,4},{0,2},{9,8},{11,9},{13,1... | collective-permute-start | bytes 3145736 | tf_op jit(solution)/shard_map/ppermute | solution.py:82
  269.7 23.6 %collective-permute-start.33 = (bf16[256,2048]{1,0:T(8,128)(2,1)}, bf16[256,2048]{1,0:T(8,128)(2,1)S(1)}, u32[]{:S(2)}, u32[]{:S(2)}) collective-permute-start(bf16[256,2048]{1,0:T(8,128)(2,1)} %collective-permute-done.32), channel_id=1, source_target_pairs={{0,1},{1,3},{3,5},{5,7},{7,6},{6,4},{4,2},{2,0},{8,9},{9,11},{11,1... | collective-permute-start | bytes 3145736 | tf_op jit(solution)/shard_map/ppermute | solution.py:79
  275.9 23.6 %collective-permute-start.30 = (bf16[256,2048]{1,0:T(8,128)(2,1)}, bf16[256,2048]{1,0:T(8,128)(2,1)S(1)}, u32[]{:S(2)}, u32[]{:S(2)}) collective-permute-start(bf16[256,2048]{1,0:T(8,128)(2,1)} %collective-permute-done.29), channel_id=1, source_target_pairs={{1,0},{3,1},{5,3},{7,5},{6,7},{4,6},{2,4},{0,2},{9,8},{11,9},{13,1... | collective-permute-start | bytes 3145736 | tf_op jit(solution)/shard_map/ppermute | solution.py:82
  327.3 23.2 %collective-permute-start.37 = (bf16[256,2048]{1,0:T(8,128)(2,1)S(1)}, bf16[256,2048]{1,0:T(8,128)(2,1)S(1)}, u32[]{:S(2)}, u32[]{:S(2)}) collective-permute-start(bf16[256,2048]{1,0:T(8,128)(2,1)S(1)} %add_convert_fusion.25), channel_id=1, source_target_pairs={{0,1},{1,3},{3,5},{5,7},{7,6},{6,4},{4,2},{2,0},{8,9},{9,11},{11,1... | collective-permute-start | bytes 3145736 | tf_op jit(solution)/shard_map/ppermute | solution.py:79
  331.1 23.0 %collective-permute-start.41 = (bf16[256,2048]{1,0:T(8,128)(2,1)S(1)}, bf16[256,2048]{1,0:T(8,128)(2,1)S(1)}, u32[]{:S(2)}, u32[]{:S(2)}) collective-permute-start(bf16[256,2048]{1,0:T(8,128)(2,1)S(1)} %add_convert_fusion.22), channel_id=1, source_target_pairs={{1,0},{3,1},{5,3},{7,5},{6,7},{4,6},{2,4},{0,2},{9,8},{11,9},{13,1... | collective-permute-start | bytes 3145736 | tf_op jit(solution)/shard_map/ppermute | solution.py:82
  350.8 23.0 %collective-permute-start.38 = (bf16[256,2048]{1,0:T(8,128)(2,1)S(1)}, bf16[256,2048]{1,0:T(8,128)(2,1)S(1)}, u32[]{:S(2)}, u32[]{:S(2)}) collective-permute-start(bf16[256,2048]{1,0:T(8,128)(2,1)S(1)} %add_convert_fusion.24), channel_id=1, source_target_pairs={{0,1},{1,3},{3,5},{5,7},{7,6},{6,4},{4,2},{2,0},{8,9},{9,11},{11,1... | collective-permute-start | bytes 3145736 | tf_op jit(solution)/shard_map/ppermute | solution.py:79
  354.4 23.0 %collective-permute-start.42 = (bf16[256,2048]{1,0:T(8,128)(2,1)S(1)}, bf16[256,2048]{1,0:T(8,128)(2,1)S(1)}, u32[]{:S(2)}, u32[]{:S(2)}) collective-permute-start(bf16[256,2048]{1,0:T(8,128)(2,1)S(1)} %add_convert_fusion.21), channel_id=1, source_target_pairs={{1,0},{3,1},{5,3},{7,5},{6,7},{4,6},{2,4},{0,2},{9,8},{11,9},{13,1... | collective-permute-start | bytes 3145736 | tf_op jit(solution)/shard_map/ppermute | solution.py:82
  459.1 21.8 %collective-permute-start.49 = (bf16[256,2048]{1,0:T(8,128)(2,1)}, bf16[256,2048]{1,0:T(8,128)(2,1)S(1)}, u32[]{:S(2)}, u32[]{:S(2)}) collective-permute-start(bf16[256,2048]{1,0:T(8,128)(2,1)} %collective-permute-done.48), channel_id=1, source_target_pairs={{0,1},{1,3},{3,5},{5,7},{7,6},{6,4},{4,2},{2,0},{8,9},{9,11},{11,1... | collective-permute-start | bytes 3145736 | tf_op jit(solution)/shard_map/ppermute | solution.py:79
  459.5 22.7 %collective-permute-start.46 = (bf16[256,2048]{1,0:T(8,128)(2,1)}, bf16[256,2048]{1,0:T(8,128)(2,1)S(1)}, u32[]{:S(2)}, u32[]{:S(2)}) collective-permute-start(bf16[256,2048]{1,0:T(8,128)(2,1)} %copy-done.77), channel_id=1, source_target_pairs={{1,0},{3,1},{5,3},{7,5},{6,7},{4,6},{2,4},{0,2},{9,8},{11,9},{13,1... | collective-permute-start | bytes 3145736 | tf_op jit(solution)/shard_map/ppermute | solution.py:82
  518.5 23.8 %collective-permute-start.53 = (bf16[256,2048]{1,0:T(8,128)(2,1)S(1)}, bf16[256,2048]{1,0:T(8,128)(2,1)S(1)}, u32[]{:S(2)}, u32[]{:S(2)}) collective-permute-start(bf16[256,2048]{1,0:T(8,128)(2,1)S(1)} %add_convert_fusion.18), channel_id=1, source_target_pairs={{0,1},{1,3},{3,5},{5,7},{7,6},{6,4},{4,2},{2,0},{8,9},{9,11},{11,1... | collective-permute-start | bytes 3145736 | tf_op jit(solution)/shard_map/ppermute | solution.py:79
  520.1 22.5 %collective-permute-start.55 = (bf16[256,2048]{1,0:T(8,128)(2,1)S(1)}, bf16[256,2048]{1,0:T(8,128)(2,1)S(1)}, u32[]{:S(2)}, u32[]{:S(2)}) collective-permute-start(bf16[256,2048]{1,0:T(8,128)(2,1)S(1)} %add_convert_fusion.16), channel_id=1, source_target_pairs={{1,0},{3,1},{5,3},{7,5},{6,7},{4,6},{2,4},{0,2},{9,8},{11,9},{13,1... | collective-permute-start | bytes 3145736 | tf_op jit(solution)/shard_map/ppermute | solution.py:82
  568.1 25.6 %collective-permute-start.58 = (bf16[256,2048]{1,0:T(8,128)(2,1)S(1)}, bf16[256,2048]{1,0:T(8,128)(2,1)S(1)}, u32[]{:S(2)}, u32[]{:S(2)}) collective-permute-start(bf16[256,2048]{1,0:T(8,128)(2,1)S(1)} %copy-done.79), channel_id=1, source_target_pairs={{0,1},{1,3},{3,5},{5,7},{7,6},{6,4},{4,2},{2,0},{8,9},{9,11},{11,1... | collective-permute-start | bytes 3145736 | tf_op jit(solution)/shard_map/ppermute | solution.py:79
  568.8 25.3 %collective-permute-start.59 = (bf16[256,2048]{1,0:T(8,128)(2,1)S(1)}, bf16[256,2048]{1,0:T(8,128)(2,1)S(1)}, u32[]{:S(2)}, u32[]{:S(2)}) collective-permute-start(bf16[256,2048]{1,0:T(8,128)(2,1)S(1)} %copy-done.80), channel_id=1, source_target_pairs={{1,0},{3,1},{5,3},{7,5},{6,7},{4,6},{2,4},{0,2},{9,8},{11,9},{13,1... | collective-permute-start | bytes 3145736 | tf_op jit(solution)/shard_map/ppermute | solution.py:82
  610.1 31.8 %all-to-all-start.2 = ((bf16[8,256,256]{2,1,0:T(8,128)(2,1)}), bf16[8,256,256]{2,1,0:T(8,128)(2,1)}, u32[]{:S(2)}, u32[]{:S(2)}) async-start(bf16[8,256,256]{2,1,0:T(8,128)(2,1)} %bitcast.297), calls=%async_computation.2 | async-start | bytes 2097152 | tf_op jit(solution)/shard_map/all_to_all | solution.py:665
  615.5 50.3 %collective-permute-start.69 = (bf16[1024,512]{1,0:T(8,128)(2,1)}, bf16[1024,512]{1,0:T(8,128)(2,1)}, u32[]{:S(2)}, u32[]{:S(2)}) collective-permute-start(bf16[1024,512]{1,0:T(8,128)(2,1)} %get-tuple-element.164), channel_id=1, source_target_pairs={{0,16},{8,24},{16,0},{24,8},{1,17},{9,25},{17,1},{25,9},{2,18},{10... | collective-permute-start | bytes 3145736 | tf_op jit(solution)/shard_map/ppermute | solution.py:36
  617.1 48.7 %collective-permute-start.70 = (bf16[512,1024]{1,0:T(8,128)(2,1)}, bf16[512,1024]{1,0:T(8,128)(2,1)}, u32[]{:S(2)}, u32[]{:S(2)}) collective-permute-start(bf16[512,1024]{1,0:T(8,128)(2,1)} %get-tuple-element.165), channel_id=1, source_target_pairs={{0,16},{8,24},{16,0},{24,8},{1,17},{9,25},{17,1},{25,9},{2,18},{10... | collective-permute-start | bytes 3145736 | tf_op jit(solution)/shard_map/ppermute | solution.py:36
  641.9 23.7 %collective-permute-start.67 = (bf16[64,2048]{1,0:T(8,128)(2,1)}, bf16[64,2048]{1,0:T(8,128)(2,1)S(1)}, u32[]{:S(2)}, u32[]{:S(2)}) collective-permute-start(bf16[64,2048]{1,0:T(8,128)(2,1)} %get-tuple-element.162), channel_id=1, source_target_pairs={{0,1},{1,3},{3,5},{5,7},{7,6},{6,4},{4,2},{2,0},{8,9},{9,11},{11,1... | collective-permute-start | bytes 786440 | tf_op jit(solution)/shard_map/ppermute | solution.py:79
  647.2 40.3 %collective-permute-start.73 = (bf16[512,1024]{1,0:T(8,128)(2,1)S(1)}, bf16[512,1024]{1,0:T(8,128)(2,1)}, u32[]{:S(2)}, u32[]{:S(2)}) collective-permute-start(bf16[512,1024]{1,0:T(8,128)(2,1)S(1)} %copy-done.78), channel_id=1, source_target_pairs={{0,16},{8,24},{16,0},{24,8},{1,17},{9,25},{17,1},{25,9},{2,18},{10... | collective-permute-start | bytes 3145736 | tf_op jit(solution)/shard_map/ppermute | solution.py:36
  698.5 21.7 %collective-permute-start.79 = (bf16[128,2048]{1,0:T(8,128)(2,1)}, bf16[128,2048]{1,0:T(8,128)(2,1)S(1)}, u32[]{:S(2)}, u32[]{:S(2)}) collective-permute-start(bf16[128,2048]{1,0:T(8,128)(2,1)} %fusion.58), channel_id=1, source_target_pairs={{0,1},{1,3},{3,5},{5,7},{7,6},{6,4},{4,2},{2,0},{8,9},{9,11},{11,1... | collective-permute-start | bytes 1572872 | tf_op jit(solution)/shard_map/ppermute | solution.py:79
  731.7 26.1 %collective-permute-start.81 = (bf16[256,2048]{1,0:T(8,128)(2,1)S(1)}, bf16[256,2048]{1,0:T(8,128)(2,1)S(1)}, u32[]{:S(2)}, u32[]{:S(2)}) collective-permute-start(bf16[256,2048]{1,0:T(8,128)(2,1)S(1)} %get-tuple-element.191), channel_id=1, source_target_pairs={{0,1},{1,3},{3,5},{5,7},{7,6},{6,4},{4,2},{2,0},{8,9},{9,11},{11,1... | collective-permute-start | bytes 3145736 | tf_op jit(solution)/shard_map/ppermute | solution.py:79
  732.7 26.1 %collective-permute-start.82 = (bf16[256,2048]{1,0:T(8,128)(2,1)S(1)}, bf16[256,2048]{1,0:T(8,128)(2,1)S(1)}, u32[]{:S(2)}, u32[]{:S(2)}) collective-permute-start(bf16[256,2048]{1,0:T(8,128)(2,1)S(1)} %get-tuple-element.192), channel_id=1, source_target_pairs={{1,0},{3,1},{5,3},{7,5},{6,7},{4,6},{2,4},{0,2},{9,8},{11,9},{13,1... | collective-permute-start | bytes 3145736 | tf_op jit(solution)/shard_map/ppermute | solution.py:82
  743.1 25.8 %collective-permute-start.90 = (bf16[128,2048]{1,0:T(8,128)(2,1)S(1)}, bf16[128,2048]{1,0:T(8,128)(2,1)S(1)}, u32[]{:S(2)}, u32[]{:S(2)}) collective-permute-start(bf16[128,2048]{1,0:T(8,128)(2,1)S(1)} %fusion.56), channel_id=1, source_target_pairs={{0,1},{1,3},{3,5},{5,7},{7,6},{6,4},{4,2},{2,0},{8,9},{9,11},{11,1... | collective-permute-start | bytes 1572872 | tf_op jit(solution)/shard_map/ppermute | solution.py:79
  744.1 24.8 %collective-permute-start.91 = (bf16[128,2048]{1,0:T(8,128)(2,1)S(1)}, bf16[128,2048]{1,0:T(8,128)(2,1)S(1)}, u32[]{:S(2)}, u32[]{:S(2)}) collective-permute-start(bf16[128,2048]{1,0:T(8,128)(2,1)S(1)} %fusion.55), channel_id=1, source_target_pairs={{1,0},{3,1},{5,3},{7,5},{6,7},{4,6},{2,4},{0,2},{9,8},{11,9},{13,1... | collective-permute-start | bytes 1572872 | tf_op jit(solution)/shard_map/ppermute | solution.py:82
  763.2 26.7 %collective-permute-start.83 = (bf16[256,2048]{1,0:T(8,128)(2,1)S(1)}, bf16[256,2048]{1,0:T(8,128)(2,1)S(1)}, u32[]{:S(2)}, u32[]{:S(2)}) collective-permute-start(bf16[256,2048]{1,0:T(8,128)(2,1)S(1)} %get-tuple-element.194), channel_id=1, source_target_pairs={{0,1},{1,3},{3,5},{5,7},{7,6},{6,4},{4,2},{2,0},{8,9},{9,11},{11,1... | collective-permute-start | bytes 3145736 | tf_op jit(solution)/shard_map/ppermute | solution.py:79
  768.9 22.0 %collective-permute-start.84 = (bf16[256,2048]{1,0:T(8,128)(2,1)S(1)}, bf16[256,2048]{1,0:T(8,128)(2,1)S(1)}, u32[]{:S(2)}, u32[]{:S(2)}) collective-permute-start(bf16[256,2048]{1,0:T(8,128)(2,1)S(1)} %get-tuple-element.195), channel_id=1, source_target_pairs={{1,0},{3,1},{5,3},{7,5},{6,7},{4,6},{2,4},{0,2},{9,8},{11,9},{13,1... | collective-permute-start | bytes 3145736 | tf_op jit(solution)/shard_map/ppermute | solution.py:82
  769.7 23.4 %collective-permute-start.87 = (bf16[512,768]{1,0:T(8,128)(2,1)S(1)}, bf16[512,768]{1,0:T(8,128)(2,1)S(1)}, u32[]{:S(2)}, u32[]{:S(2)}) collective-permute-start(bf16[512,768]{1,0:T(8,128)(2,1)S(1)} %get-tuple-element.298), channel_id=1, source_target_pairs={{0,16},{8,24},{16,0},{24,8},{1,17},{9,25},{17,1},{25,9},{2,18},{10... | collective-permute-start | bytes 2359304 | tf_op jit(solution)/shard_map/ppermute | solution.py:36
  772.3 32.0 %collective-permute-start.92 = (f32[1,64,2048]{2,1,0:T(8,128)}, f32[1,64,2048]{2,1,0:T(8,128)}, u32[]{:S(2)}, u32[]{:S(2)}) collective-permute-start(f32[1,64,2048]{2,1,0:T(8,128)} %dynamic-slice_bitcast_fusion.1), channel_id=1, source_target_pairs={{0,16},{8,24},{16,0},{24,8},{1,17},{9,25},{17,1},{25,9},{2,18},{10... | collective-permute-start | bytes 1572872 | tf_op jit(solution)/shard_map/ppermute | solution.py:36
  793.1 26.6 %collective-permute-start.88 = (bf16[256,2048]{1,0:T(8,128)(2,1)}, bf16[256,2048]{1,0:T(8,128)(2,1)}, u32[]{:S(2)}, u32[]{:S(2)}) collective-permute-start(bf16[256,2048]{1,0:T(8,128)(2,1)} %get-tuple-element.197), channel_id=1, source_target_pairs={{0,1},{1,3},{3,5},{5,7},{7,6},{6,4},{4,2},{2,0},{8,9},{9,11},{11,1... | collective-permute-start | bytes 3145736 | tf_op jit(solution)/shard_map/ppermute | solution.py:79
  794.7 25.5 %collective-permute-start.89 = (bf16[256,2048]{1,0:T(8,128)(2,1)}, bf16[256,2048]{1,0:T(8,128)(2,1)}, u32[]{:S(2)}, u32[]{:S(2)}) collective-permute-start(bf16[256,2048]{1,0:T(8,128)(2,1)} %get-tuple-element.198), channel_id=1, source_target_pairs={{1,0},{3,1},{5,3},{7,5},{6,7},{4,6},{2,4},{0,2},{9,8},{11,9},{13,1... | collective-permute-start | bytes 3145736 | tf_op jit(solution)/shard_map/ppermute | solution.py:82
  796.2 37.2 %all-to-all-start.3 = ((bf16[8,64,768]{2,1,0:T(8,128)(2,1)}), bf16[8,64,768]{2,1,0:T(8,128)(2,1)}, u32[]{:S(2)}, u32[]{:S(2)}) async-start(bf16[8,64,768]{2,1,0:T(8,128)(2,1)} %bitcast.328), calls=%async_computation.3 | async-start | bytes 1572864 | tf_op jit(solution)/shard_map/all_to_all | solution.py:748
  (157 other events, 1925.0 us)
Sparse Core Ops, SparseCore 0:
  114.8 94.7 all-gather.1

commit v6 on v5

--- a/solution.py
+++ b/solution.py
@@ -549,11 +549,12 @@
             state["w_heads"] = lax.all_to_all(packed, "seq", split_axis=0, concat_axis=0, tiled=True)
             return ["gains"]
         if step == 2:
-            return ["gains", "w_heads", "down", "begin"]
+            state["gate"] = swap_chips(w_gate, chips)
+            return ["gains", "w_heads", "down", "gate", "begin"]
         if step == 3:
             state["w_heads"] = swap_chips(state["w_heads"].reshape(-1, 3 * own), chips)
-            state["gate"], state["up"] = w_gate, w_up
-            return ["gains", "w_heads", "gate", "up"]
+            state["up"] = w_up
+            return ["gains", "w_heads", "up"]
         return ["gains"]
 
     state["begin"] = begin
@@ -562,7 +563,7 @@
     first_block = begin[::BLOCK] // BLOCK
     cosine, sine = rope_tables(jnp.arange(row_len, dtype=jnp.int32) - begin)
     begin = begin[None]
-    state["gate"] = swap_chips(state["gate"], chips)
+    state["up"] = swap_chips(state["up"], chips)
     last = row_ring.size // 2
     row_tokens = jnp.zeros((row_len, width), LOW)
     for offset, chunk in row_chunks.items():
@@ -585,8 +586,7 @@
     query_pre, key_pre = pre[:, :own], pre[:, own : 2 * own]
     squares = jnp.stack([jnp.sum(query_pre * query_pre, axis=1), jnp.sum(key_pre * key_pre, axis=1)])
     scales = lax.rsqrt(sum_over(squares, "seq", seq) / width + EPSILON)
-    scales, state["gate"], state["up"] = tie(scales, state["gate"], state["up"])
-    state["up"] = swap_chips(state["up"], chips)
+    scales, state["up"] = tie(scales, state["up"])
     attn_heads, query_rot, key_rot, values, log_sums = attend_forward(
         pre, scales, gains_own, cosine, sine, first_block, begin
     )

time: 860 us -> 862 us (level)
    ppermute x34, waiting for transfers between devices: 33.4 us -> 57.8 us  [swap(): return lax.ppermute(val, axis, [(i, i ^ mask) for i in range(size)])]
    ppermute x28, waiting for transfers between devices: 200 us -> 179 us  [right(): return lax.ppermute(val, 'seq', self.forth)]
    unnamed x235 -> x225, local copies, waits for them, and re-layouts: 52.9 us -> 51.7 us
  transfers between devices with their start and end apart: 100 -> 100, of which waited for: 56 -> 53; matrix products, arithmetic and copies ran while one was open for 32% -> 31% of each run, Pallas kernels for 6% -> 6%
where the time goes in v6:
time: 862 us; the launch traced here: 852 us
  waiting for transfers between devices  328 us (38%)
  matrix products  168 us (19%)
  starting transfers between devices  114 us (13%)
  local copies, waits for them, and re-layouts  93 us (11%)
  other arithmetic  83.9 us (10%)
  Pallas kernels  48.7 us (6%)
  between operations  16.5 us (2%)
    ppermute x28, waiting for transfers between devices, right(): return lax.ppermute(val, 'seq', self.forth)  179 us
    dot_general x18, matrix products, dot_nt(): lax.dot_general(left, right, (((1,), (1,)), ((), ())), preferred_element_...  62.9 us
    ppermute x34, waiting for transfers between devices, swap(): return lax.ppermute(val, axis, [(i, i ^ mask) for i in range(size)])  57.8 us
    dot_general x18, matrix products, dot(): return jnp.dot(left, right, preferred_element_type=FULL)  55.9 us
    unnamed x225, local copies, waits for them, and re-layouts  51.7 us
    dot_general x5, matrix products, dot_tn(): lax.dot_general(left, right, (((0,), (0,)), ((), ())), preferred_element_...  49.2 us
    all_to_all x1, waiting for transfers between devices, per_device(): lax.all_to_all(attn_heads.reshape(seq, count, own), 'seq', split_axis=0,...  39.9 us
    ppermute x28, starting transfers between devices, right(): return lax.ppermute(val, 'seq', self.forth)  34 us
  transfers between devices with their start and end apart: 100, of which 53 were waited for; matrix products, arithmetic and copies ran while one was open for 31% of the time, Pallas kernels for 6%

profile of v6, /device:TPU:0, one launch (start us, length us, event | category | flops | bytes accessed | tf_op | source)
XLA Modules:
  0.0 852.0 jit_solution(3053938492910349144)
XLA Ops:
  23.6 5.8 all-to-all-start
  33.2 4.3 broadcast_in_dim.73
  45.6 10.2 %collective-permute-done.7.refs_1_ = bf16[512,1024]{1,0:T(8,128)(2,1)} collective-permute-done((bf16[512,1024]{1,0:T(8,128)(2,1)S(1)}, bf16[512,1024]{1,0:T(8,128)(2,1)}, u32[]{:S(2)}, u32[]{:S(2)}) %collective-permute-start.7) | collective-permute-done | bytes 1048608 | tf_op jit(solution)/shard_map/ppermute | solution.py:36
  55.8 20.1 %collective-permute-done.6.refs_1_ = bf16[1024,512]{1,0:T(8,128)(2,1)} collective-permute-done((bf16[1024,512]{1,0:T(8,128)(2,1)S(1)}, bf16[1024,512]{1,0:T(8,128)(2,1)}, u32[]{:S(2)}, u32[]{:S(2)}) %collective-permute-start.6) | collective-permute-done | bytes 1048608 | tf_op jit(solution)/shard_map/ppermute | solution.py:36
  88.3 6.1 collective-permute-done.11.refs_1_
  94.4 6.3 collective-permute-done.8
  123.8 11.8 %fusion.84.q_ref.k_ref.v_ref.qp_ref.kp_ref = f32[2048,768]{1,0:T(8,128)} fusion(bf16[2048,2048]{1,0:T(8,128)(2,1)} %constant_dynamic-update-slice_fusion.67, bf16[2048,768]{1,0:T(8,128)(2,1)S(1)} %assemble.3), kind=kOutput, calls=%fused_computation.358 | convolution fusion | flops 6442450944 | bytes 17825792 | tf_op jit(solution)/shard_map/dot_general | solution.py:23
  147.1 4.6 collective-permute-done.18
  151.8 13.0 %attend_forward.1 = (bf16[2048,256]{1,0:T(8,128)(2,1)S(1)}, bf16[2048,256]{1,0:T(8,128)(2,1)S(1)}, bf16[2048,256]{1,0:T(8,128)(2,1)S(1)}, bf16[2048,256]{1,0:T(8,128)(2,1)S(1)}, f32[2,1,2048]{2,1,0:T(1,128)S(1)}) custom-call(s32[4]{0:T(128)S(1)} %and_select_fusion.first_ref, f32[2048,768]{1,0:T(8,128)} %fusion.84.q_ref.k_ref.v_ref.qp_ref.kp_ref, ...), custom_call_target="tpu_custom_call" | custom-call | flops 1 | bytes 1 | tf_op jit(solution)/shard_map/attend_forward/pallas_call | solution.py:383
  171.8 39.9 %all-to-all-done.1 = bf16[8,256,256]{1,2,0:T(8,128)(2,1)S(1)} async-done(((bf16[8,256,256]{1,2,0:T(8,128)(2,1)}), bf16[8,256,256]{1,2,0:T(8,128)(2,1)S(1)}, u32[]{:S(2)}, u32[]{:S(2)}) %all-to-all-start.1) | async-done | bytes 1048608 | tf_op jit(solution)/shard_map/all_to_all | solution.py:593
  212.7 5.9 multiply_reduce_fusion.3
  228.8 7.1 assemble.4
  236.0 6.2 fusion.85
  242.2 5.6 collective-permute-done.31
  265.3 7.0 collective-permute-done.32
  285.4 10.4 %collective-permute-done.33 = bf16[256,2048]{1,0:T(8,128)(2,1)S(1)} collective-permute-done((bf16[256,2048]{1,0:T(8,128)(2,1)}, bf16[256,2048]{1,0:T(8,128)(2,1)S(1)}, u32[]{:S(2)}, u32[]{:S(2)}) %collective-permute-start.33) | collective-permute-done | bytes 1048608 | tf_op jit(solution)/shard_map/ppermute | solution.py:79
  297.3 4.8 collective-permute-done.30
  322.7 7.0 collective-permute-done.36
  337.4 15.7 %collective-permute-done.37 = bf16[256,2048]{1,0:T(8,128)(2,1)S(1)} collective-permute-done((bf16[256,2048]{1,0:T(8,128)(2,1)S(1)}, bf16[256,2048]{1,0:T(8,128)(2,1)S(1)}, u32[]{:S(2)}, u32[]{:S(2)}) %collective-permute-start.37) | collective-permute-done | bytes 1048608 | tf_op jit(solution)/shard_map/ppermute | solution.py:79
  361.8 14.7 %collective-permute-done.38 = bf16[256,2048]{1,0:T(8,128)(2,1)S(1)} collective-permute-done((bf16[256,2048]{1,0:T(8,128)(2,1)S(1)}, bf16[256,2048]{1,0:T(8,128)(2,1)S(1)}, u32[]{:S(2)}, u32[]{:S(2)}) %collective-permute-start.38) | collective-permute-done | bytes 1048608 | tf_op jit(solution)/shard_map/ppermute | solution.py:79
  390.7 4.8 collective-permute-done.39
  409.2 11.0 %collective-permute-done.47 = bf16[256,2048]{1,0:T(8,128)(2,1)S(1)} collective-permute-done((bf16[256,2048]{1,0:T(8,128)(2,1)S(1)}, bf16[256,2048]{1,0:T(8,128)(2,1)S(1)}, u32[]{:S(2)}, u32[]{:S(2)}) %collective-permute-start.47) | collective-permute-done | bytes 1048608 | tf_op jit(solution)/shard_map/ppermute | solution.py:79
  439.1 8.6 %collective-permute-done.48 = bf16[256,2048]{1,0:T(8,128)(2,1)} collective-permute-done((bf16[256,2048]{1,0:T(8,128)(2,1)S(1)}, bf16[256,2048]{1,0:T(8,128)(2,1)}, u32[]{:S(2)}, u32[]{:S(2)}) %collective-permute-start.48) | collective-permute-done | bytes 1048608 | tf_op jit(solution)/shard_map/ppermute | solution.py:79
  447.7 4.0 constant_dynamic-update-slice_fusion.30
  470.2 10.9 %collective-permute-done.49 = bf16[256,2048]{1,0:T(8,128)(2,1)S(1)} collective-permute-done((bf16[256,2048]{1,0:T(8,128)(2,1)}, bf16[256,2048]{1,0:T(8,128)(2,1)S(1)}, u32[]{:S(2)}, u32[]{:S(2)}) %collective-permute-start.49) | collective-permute-done | bytes 1048608 | tf_op jit(solution)/shard_map/ppermute | solution.py:79
  507.9 8.6 %collective-permute-done.52 = bf16[128,2048]{1,0:T(8,128)(2,1)S(1)} collective-permute-done((bf16[128,2048]{1,0:T(8,128)(2,1)S(1)}, bf16[128,2048]{1,0:T(8,128)(2,1)S(1)}, u32[]{:S(2)}, u32[]{:S(2)}) %collective-permute-start.52) | collective-permute-done | bytes 524320 | tf_op jit(solution)/shard_map/ppermute | solution.py:79
  520.7 12.8 %convolution_convert_fusion.2 = bf16[1024,2048]{1,0:T(8,128)(2,1)S(1)} fusion(bf16[2048,1024]{1,0:T(8,128)(2,1)} %get-tuple-element.249, bf16[2048,2048]{1,0:T(8,128)(2,1)} %constant_dynamic-update-slice_fusion.8), kind=kOutput, calls=%fused_computation.5 | convolution fusion | flops 8592031744 | bytes 16777216 | tf_op jit(solution)/shard_map/dot_general | solution.py:31
  533.5 9.2 %collective-permute-done.53 = bf16[256,2048]{1,0:T(8,128)(2,1)S(1)} collective-permute-done((bf16[256,2048]{1,0:T(8,128)(2,1)S(1)}, bf16[256,2048]{1,0:T(8,128)(2,1)S(1)}, u32[]{:S(2)}, u32[]{:S(2)}) %collective-permute-start.53) | collective-permute-done | bytes 1048608 | tf_op jit(solution)/shard_map/ppermute | solution.py:79
  545.4 13.0 %convolution_convert_fusion.4 = bf16[2048,1024]{1,0:T(8,128)(2,1)} fusion(bf16[2048,2048]{1,0:T(8,128)(2,1)} %constant_dynamic-update-slice_fusion.17, bf16[2048,1024]{1,0:T(8,128)(2,1)S(1)} %copy-done.94), kind=kOutput, calls=%fused_computation.7 | convolution fusion | flops 8592031744 | bytes 16777216 | tf_op jit(solution)/shard_map/dot_general | solution.py:31
  563.2 6.2 fusion.19
  572.4 11.7 %convolution_convert_fusion.3 = bf16[2048,1024]{1,0:T(8,128)(2,1)S(1)} fusion(bf16[2048,2048]{1,0:T(8,128)(2,1)} %constant_dynamic-update-slice_fusion.17, bf16[2048,1024]{1,0:T(8,128)(2,1)S(1)} %copy-done.95), kind=kOutput, calls=%fused_computation.6 | convolution fusion | flops 8592031744 | bytes 16777216 | tf_op jit(solution)/shard_map/dot_general | solution.py:31
  584.2 4.3 add_convert_fusion.11
  590.8 4.3 collective-permute-done.58
  612.9 5.3 all-to-all-start.2
  621.0 4.5 add_convert_fusion.7
  625.5 5.4 fusion
  633.6 11.0 %all-to-all-done.2 = bf16[8,256,256]{2,1,0:T(8,128)(2,1)} async-done(((bf16[8,256,256]{2,1,0:T(8,128)(2,1)}), bf16[8,256,256]{2,1,0:T(8,128)(2,1)}, u32[]{:S(2)}, u32[]{:S(2)}) %all-to-all-start.2) | async-done | bytes 1048608 | tf_op jit(solution)/shard_map/all_to_all | solution.py:665
  651.4 12.9 %attend_backward.2 = (f32[2048,128]{1,0:T(8,128)S(1)}, f32[2048,128]{1,0:T(8,128)S(1)}, bf16[2048,128]{1,0:T(8,128)(2,1)S(1)}, f32[1,2,2048]{2,1,0:T(2,128)S(1)}, f32[2,128]{1,0:T(2,128)S(1)}) custom-call(s32[4]{0:T(128)S(1)} %copy-done.30, bf16[2048,256]{1,0:T(8,128)(2,1)S(1)} %get-tuple-element.153.q_ref, bf16[2048,256]{1,0:T(8,128)(2,1)S(1)} %copy-done.3, ...), custom_call_target="tpu_custom_call" | custom-call | flops 1 | bytes 1 | tf_op jit(solution)/shard_map/attend_backward/pallas_call | solution.py:471
  669.2 12.9 %attend_backward.3 = (f32[2048,128]{1,0:T(8,128)S(1)}, f32[2048,128]{1,0:T(8,128)S(1)}, bf16[2048,128]{1,0:T(8,128)(2,1)S(1)}, f32[1,2,2048]{2,1,0:T(2,128)S(1)}, f32[2,128]{1,0:T(2,128)S(1)}) custom-call(s32[4]{0:T(128)S(1)} %copy-done.30, bf16[2048,256]{1,0:T(8,128)(2,1)S(1)} %get-tuple-element.153.q_ref, bf16[2048,256]{1,0:T(8,128)(2,1)S(1)} %copy-done.3, ...), custom_call_target="tpu_custom_call" | custom-call | flops 1 | bytes 1 | tf_op jit(solution)/shard_map/attend_backward/pallas_call | solution.py:471
  704.7 4.3 fusion.9
  709.0 7.2 convolution_convert_fusion
  721.7 11.0 %collective-permute-done.77 = bf16[128,2048]{1,0:T(8,128)(2,1)S(1)} collective-permute-done((bf16[128,2048]{1,0:T(8,128)(2,1)S(1)}, bf16[128,2048]{1,0:T(8,128)(2,1)S(1)}, u32[]{:S(2)}, u32[]{:S(2)}) %collective-permute-start.77) | collective-permute-done | bytes 524320 | tf_op jit(solution)/shard_map/ppermute | solution.py:79
  736.2 9.4 %convolution_convert_fusion.5 = bf16[2048,768]{1,0:T(8,128)(2,1)S(1)} fusion(bf16[2048,2048]{1,0:T(8,128)(2,1)} %constant_dynamic-update-slice_fusion.67, bf16[2048,768]{1,0:T(8,128)(2,1)S(1)} %pad_maximum_fusion), kind=kOutput, calls=%fused_computation.8 | convolution fusion | flops 6444023808 | bytes 14680064 | tf_op jit(solution)/shard_map/dot_general | solution.py:31
  750.6 9.7 %collective-permute-done.81 = bf16[256,2048]{1,0:T(8,128)(2,1)S(1)} collective-permute-done((bf16[256,2048]{1,0:T(8,128)(2,1)S(1)}, bf16[256,2048]{1,0:T(8,128)(2,1)S(1)}, u32[]{:S(2)}, u32[]{:S(2)}) %collective-permute-start.81) | collective-permute-done | bytes 1048608 | tf_op jit(solution)/shard_map/ppermute | solution.py:79
  775.4 16.6 %collective-permute-done.83 = bf16[256,2048]{1,0:T(8,128)(2,1)S(1)} collective-permute-done((bf16[256,2048]{1,0:T(8,128)(2,1)S(1)}, bf16[256,2048]{1,0:T(8,128)(2,1)S(1)}, u32[]{:S(2)}, u32[]{:S(2)}) %collective-permute-start.83) | collective-permute-done | bytes 1048608 | tf_op jit(solution)/shard_map/ppermute | solution.py:79
  798.8 4.9 all-to-all-start.3
  808.8 13.8 %collective-permute-done.88 = bf16[256,2048]{1,0:T(8,128)(2,1)} collective-permute-done((bf16[256,2048]{1,0:T(8,128)(2,1)}, bf16[256,2048]{1,0:T(8,128)(2,1)}, u32[]{:S(2)}, u32[]{:S(2)}) %collective-permute-start.88) | collective-permute-done | bytes 1048608 | tf_op jit(solution)/shard_map/ppermute | solution.py:79
  826.5 9.3 %all-to-all-done.3 = bf16[8,64,768]{2,1,0:T(8,128)(2,1)} async-done(((bf16[8,64,768]{2,1,0:T(8,128)(2,1)}), bf16[8,64,768]{2,1,0:T(8,128)(2,1)}, u32[]{:S(2)}, u32[]{:S(2)}) %all-to-all-start.3) | async-done | bytes 786464 | tf_op jit(solution)/shard_map/all_to_all | solution.py:748
  (570 shorter events, 381.4 us)
Async XLA Ops:
  7.2 31.4 %collective-permute-start = (bf16[256,2048]{1,0:T(8,128)(2,1)}, bf16[256,2048]{1,0:T(8,128)(2,1)}, u32[]{:S(2)}, u32[]{:S(2)}) collective-permute-start(bf16[256,2048]{1,0:T(8,128)(2,1)} %bitcast.324), channel_id=1, source_target_pairs={{0,1},{1,3},{3,5},{5,7},{7,6},{6,4},{4,2},{2,0},{8,9},{9,11},{11,1... | collective-permute-start | bytes 3145736 | tf_op jit(solution)/shard_map/ppermute | solution.py:79
  10.2 28.4 %collective-permute-start.1 = (bf16[256,2048]{1,0:T(8,128)(2,1)}, bf16[256,2048]{1,0:T(8,128)(2,1)}, u32[]{:S(2)}, u32[]{:S(2)}) collective-permute-start(bf16[256,2048]{1,0:T(8,128)(2,1)} %bitcast.325), channel_id=1, source_target_pairs={{1,0},{3,1},{5,3},{7,5},{6,7},{4,6},{2,4},{0,2},{9,8},{11,9},{13,1... | collective-permute-start | bytes 3145736 | tf_op jit(solution)/shard_map/ppermute | solution.py:82
  11.0 27.5 %collective-permute-start.2 = (bf16[1,4,64]{2,1,0:T(4,128)(2,1)S(1)}, bf16[1,4,64]{2,1,0:T(4,128)(2,1)S(1)}, u32[]{:S(2)}, u32[]{:S(2)}) collective-permute-start(bf16[1,4,64]{2,1,0:T(4,128)(2,1)S(1)} %maximum_bitcast_fusion.2), channel_id=1, source_target_pairs={{0,16},{1,17},{2,18},{3,19},{4,20},{5,21},{6,22},{7,23},{8,24},{9,... | collective-permute-start | bytes 1544 | tf_op jit(solution)/shard_map/ppermute | solution.py:41
  23.6 52.3 %all-to-all-start = ((bf16[8,64,768]{2,1,0:T(8,128)(2,1)}), bf16[8,64,768]{2,1,0:T(8,128)(2,1)S(1)}, u32[]{:S(2)}, u32[]{:S(2)}) async-start(bf16[8,64,768]{2,1,0:T(8,128)(2,1)} %reshape.166), calls=%async_computation | async-start | bytes 1572864 | tf_op jit(solution)/shard_map/all_to_all | solution.py:549
  29.5 182.3 %all-gather.2.cloned.1.call-start = ((), (), s32[]{:S(2)}) async-start(), calls=%async_computation.4 | async-start | bytes 8650752 | tf_op jit(solution)/shard_map/all_gather | solution.py:575
  29.5 26.3 %collective-permute-start.7 = (bf16[512,1024]{1,0:T(8,128)(2,1)S(1)}, bf16[512,1024]{1,0:T(8,128)(2,1)}, u32[]{:S(2)}, u32[]{:S(2)}) collective-permute-start(bf16[512,1024]{1,0:T(8,128)(2,1)S(1)} %copy-done.8), channel_id=1, source_target_pairs={{0,16},{8,24},{16,0},{24,8},{1,17},{9,25},{17,1},{25,9},{2,18},{10... | collective-permute-start | bytes 3145736 | tf_op jit(solution)/shard_map/ppermute | solution.py:36
  30.1 45.8 %collective-permute-start.6 = (bf16[1024,512]{1,0:T(8,128)(2,1)S(1)}, bf16[1024,512]{1,0:T(8,128)(2,1)}, u32[]{:S(2)}, u32[]{:S(2)}) collective-permute-start(bf16[1024,512]{1,0:T(8,128)(2,1)S(1)} %copy-done.10), channel_id=1, source_target_pairs={{0,16},{8,24},{16,0},{24,8},{1,17},{9,25},{17,1},{25,9},{2,18},{10... | collective-permute-start | bytes 3145736 | tf_op jit(solution)/shard_map/ppermute | solution.py:36
  38.6 37.3 %collective-permute-start.3 = (bf16[256,2048]{1,0:T(8,128)(2,1)}, bf16[256,2048]{1,0:T(8,128)(2,1)}, u32[]{:S(2)}, u32[]{:S(2)}) collective-permute-start(bf16[256,2048]{1,0:T(8,128)(2,1)} %collective-permute-done), channel_id=1, source_target_pairs={{0,1},{1,3},{3,5},{5,7},{7,6},{6,4},{4,2},{2,0},{8,9},{9,11},{11,1... | collective-permute-start | bytes 3145736 | tf_op jit(solution)/shard_map/ppermute | solution.py:79
  40.6 35.3 %collective-permute-start.4 = (bf16[256,2048]{1,0:T(8,128)(2,1)}, bf16[256,2048]{1,0:T(8,128)(2,1)}, u32[]{:S(2)}, u32[]{:S(2)}) collective-permute-start(bf16[256,2048]{1,0:T(8,128)(2,1)} %collective-permute-done.1), channel_id=1, source_target_pairs={{1,0},{3,1},{5,3},{7,5},{6,7},{4,6},{2,4},{0,2},{9,8},{11,9},{13,1... | collective-permute-start | bytes 3145736 | tf_op jit(solution)/shard_map/ppermute | solution.py:82
  78.2 22.5 %collective-permute-start.8 = (bf16[256,2048]{1,0:T(8,128)(2,1)}, bf16[256,2048]{1,0:T(8,128)(2,1)S(1)}, u32[]{:S(2)}, u32[]{:S(2)}) collective-permute-start(bf16[256,2048]{1,0:T(8,128)(2,1)} %collective-permute-done.3), channel_id=1, source_target_pairs={{0,1},{1,3},{3,5},{5,7},{7,6},{6,4},{4,2},{2,0},{8,9},{9,11},{11,1... | collective-permute-start | bytes 3145736 | tf_op jit(solution)/shard_map/ppermute | solution.py:79
  78.6 23.3 %collective-permute-start.9 = (bf16[256,2048]{1,0:T(8,128)(2,1)}, bf16[256,2048]{1,0:T(8,128)(2,1)S(1)}, u32[]{:S(2)}, u32[]{:S(2)}) collective-permute-start(bf16[256,2048]{1,0:T(8,128)(2,1)} %collective-permute-done.4), channel_id=1, source_target_pairs={{1,0},{3,1},{5,3},{7,5},{6,7},{4,6},{2,4},{0,2},{9,8},{11,9},{13,1... | collective-permute-start | bytes 3145736 | tf_op jit(solution)/shard_map/ppermute | solution.py:82
  116.5 35.2 %collective-permute-start.19 = (bf16[512,1024]{1,0:T(8,128)(2,1)}, bf16[512,1024]{1,0:T(8,128)(2,1)}, u32[]{:S(2)}, u32[]{:S(2)}) collective-permute-start(bf16[512,1024]{1,0:T(8,128)(2,1)} %refs_4_), channel_id=1, source_target_pairs={{0,16},{8,24},{16,0},{24,8},{1,17},{9,25},{17,1},{25,9},{2,18},{10... | collective-permute-start | bytes 3145736 | tf_op jit(solution)/shard_map/ppermute | solution.py:36
  118.1 21.0 %collective-permute-start.21 = (bf16[16,4,64]{2,1,0:T(4,128)(2,1)S(1)}, bf16[16,4,64]{2,1,0:T(4,128)(2,1)S(1)}, u32[]{:S(2)}, u32[]{:S(2)}) collective-permute-start(bf16[16,4,64]{2,1,0:T(4,128)(2,1)S(1)} %pad_maximum_fusion.7), channel_id=1, source_target_pairs={{0,4},{1,5},{2,6},{3,7},{4,0},{5,1},{6,2},{7,3},{8,12},{9,13},{10,... | collective-permute-start | bytes 24584 | tf_op jit(solution)/shard_map/ppermute | solution.py:41
  168.2 43.6 %all-to-all-start.1 = ((bf16[8,256,256]{1,2,0:T(8,128)(2,1)}), bf16[8,256,256]{1,2,0:T(8,128)(2,1)S(1)}, u32[]{:S(2)}, u32[]{:S(2)}) async-start(bf16[8,256,256]{1,2,0:T(8,128)(2,1)} %copy.68), calls=%async_computation.1 | async-start | bytes 2097152 | tf_op jit(solution)/shard_map/all_to_all | solution.py:593
  222.3 25.4 %collective-permute-start.31 = (bf16[256,2048]{1,0:T(8,128)(2,1)}, bf16[256,2048]{1,0:T(8,128)(2,1)}, u32[]{:S(2)}, u32[]{:S(2)}) collective-permute-start(bf16[256,2048]{1,0:T(8,128)(2,1)} %fusion.12), channel_id=1, source_target_pairs={{0,1},{1,3},{3,5},{5,7},{7,6},{6,4},{4,2},{2,0},{8,9},{9,11},{11,1... | collective-permute-start | bytes 3145736 | tf_op jit(solution)/shard_map/ppermute | solution.py:79
  226.4 27.8 %collective-permute-start.28 = (bf16[256,2048]{1,0:T(8,128)(2,1)}, bf16[256,2048]{1,0:T(8,128)(2,1)}, u32[]{:S(2)}, u32[]{:S(2)}) collective-permute-start(bf16[256,2048]{1,0:T(8,128)(2,1)} %fusion.12), channel_id=1, source_target_pairs={{1,0},{3,1},{5,3},{7,5},{6,7},{4,6},{2,4},{0,2},{9,8},{11,9},{13,1... | collective-permute-start | bytes 3145736 | tf_op jit(solution)/shard_map/ppermute | solution.py:82
  227.4 32.3 %collective-permute-start.26 = (bf16[1024,512]{1,0:T(8,128)(2,1)S(1)}, bf16[1024,512]{1,0:T(8,128)(2,1)S(1)}, u32[]{:S(2)}, u32[]{:S(2)}) collective-permute-start(bf16[1024,512]{1,0:T(8,128)(2,1)S(1)} %copy-done.11), channel_id=1, source_target_pairs={{0,8},{8,0},{16,24},{24,16},{1,9},{9,1},{17,25},{25,17},{2,10},{10... | collective-permute-start | bytes 3145736 | tf_op jit(solution)/shard_map/ppermute | solution.py:36
  227.4 32.3 %collective-permute-start.27 = (bf16[1024,512]{1,0:T(8,128)(2,1)}, bf16[1024,512]{1,0:T(8,128)(2,1)S(1)}, u32[]{:S(2)}, u32[]{:S(2)}) collective-permute-start(bf16[1024,512]{1,0:T(8,128)(2,1)} %collective-permute-done.6.refs_1_), channel_id=1, source_target_pairs={{0,8},{8,0},{16,24},{24,16},{1,9},{9,1},{17,25},{25,17},{2,10},{10... | collective-permute-start | bytes 3145736 | tf_op jit(solution)/shard_map/ppermute | solution.py:36
  247.7 24.5 %collective-permute-start.32 = (bf16[256,2048]{1,0:T(8,128)(2,1)}, bf16[256,2048]{1,0:T(8,128)(2,1)}, u32[]{:S(2)}, u32[]{:S(2)}) collective-permute-start(bf16[256,2048]{1,0:T(8,128)(2,1)} %collective-permute-done.31), channel_id=1, source_target_pairs={{0,1},{1,3},{3,5},{5,7},{7,6},{6,4},{4,2},{2,0},{8,9},{9,11},{11,1... | collective-permute-start | bytes 3145736 | tf_op jit(solution)/shard_map/ppermute | solution.py:79
  254.2 24.3 %collective-permute-start.29 = (bf16[256,2048]{1,0:T(8,128)(2,1)}, bf16[256,2048]{1,0:T(8,128)(2,1)}, u32[]{:S(2)}, u32[]{:S(2)}) collective-permute-start(bf16[256,2048]{1,0:T(8,128)(2,1)} %collective-permute-done.28), channel_id=1, source_target_pairs={{1,0},{3,1},{5,3},{7,5},{6,7},{4,6},{2,4},{0,2},{9,8},{11,9},{13,1... | collective-permute-start | bytes 3145736 | tf_op jit(solution)/shard_map/ppermute | solution.py:82
  272.3 23.5 %collective-permute-start.33 = (bf16[256,2048]{1,0:T(8,128)(2,1)}, bf16[256,2048]{1,0:T(8,128)(2,1)S(1)}, u32[]{:S(2)}, u32[]{:S(2)}) collective-permute-start(bf16[256,2048]{1,0:T(8,128)(2,1)} %collective-permute-done.32), channel_id=1, source_target_pairs={{0,1},{1,3},{3,5},{5,7},{7,6},{6,4},{4,2},{2,0},{8,9},{9,11},{11,1... | collective-permute-start | bytes 3145736 | tf_op jit(solution)/shard_map/ppermute | solution.py:79
  278.5 23.6 %collective-permute-start.30 = (bf16[256,2048]{1,0:T(8,128)(2,1)}, bf16[256,2048]{1,0:T(8,128)(2,1)S(1)}, u32[]{:S(2)}, u32[]{:S(2)}) collective-permute-start(bf16[256,2048]{1,0:T(8,128)(2,1)} %collective-permute-done.29), channel_id=1, source_target_pairs={{1,0},{3,1},{5,3},{7,5},{6,7},{4,6},{2,4},{0,2},{9,8},{11,9},{13,1... | collective-permute-start | bytes 3145736 | tf_op jit(solution)/shard_map/ppermute | solution.py:82
  329.9 23.2 %collective-permute-start.37 = (bf16[256,2048]{1,0:T(8,128)(2,1)S(1)}, bf16[256,2048]{1,0:T(8,128)(2,1)S(1)}, u32[]{:S(2)}, u32[]{:S(2)}) collective-permute-start(bf16[256,2048]{1,0:T(8,128)(2,1)S(1)} %add_convert_fusion.25), channel_id=1, source_target_pairs={{0,1},{1,3},{3,5},{5,7},{7,6},{6,4},{4,2},{2,0},{8,9},{9,11},{11,1... | collective-permute-start | bytes 3145736 | tf_op jit(solution)/shard_map/ppermute | solution.py:79
  333.7 23.0 %collective-permute-start.41 = (bf16[256,2048]{1,0:T(8,128)(2,1)S(1)}, bf16[256,2048]{1,0:T(8,128)(2,1)S(1)}, u32[]{:S(2)}, u32[]{:S(2)}) collective-permute-start(bf16[256,2048]{1,0:T(8,128)(2,1)S(1)} %add_convert_fusion.22), channel_id=1, source_target_pairs={{1,0},{3,1},{5,3},{7,5},{6,7},{4,6},{2,4},{0,2},{9,8},{11,9},{13,1... | collective-permute-start | bytes 3145736 | tf_op jit(solution)/shard_map/ppermute | solution.py:82
  353.4 23.0 %collective-permute-start.38 = (bf16[256,2048]{1,0:T(8,128)(2,1)S(1)}, bf16[256,2048]{1,0:T(8,128)(2,1)S(1)}, u32[]{:S(2)}, u32[]{:S(2)}) collective-permute-start(bf16[256,2048]{1,0:T(8,128)(2,1)S(1)} %add_convert_fusion.24), channel_id=1, source_target_pairs={{0,1},{1,3},{3,5},{5,7},{7,6},{6,4},{4,2},{2,0},{8,9},{9,11},{11,1... | collective-permute-start | bytes 3145736 | tf_op jit(solution)/shard_map/ppermute | solution.py:79
  357.0 23.0 %collective-permute-start.42 = (bf16[256,2048]{1,0:T(8,128)(2,1)S(1)}, bf16[256,2048]{1,0:T(8,128)(2,1)S(1)}, u32[]{:S(2)}, u32[]{:S(2)}) collective-permute-start(bf16[256,2048]{1,0:T(8,128)(2,1)S(1)} %add_convert_fusion.21), channel_id=1, source_target_pairs={{1,0},{3,1},{5,3},{7,5},{6,7},{4,6},{2,4},{0,2},{9,8},{11,9},{13,1... | collective-permute-start | bytes 3145736 | tf_op jit(solution)/shard_map/ppermute | solution.py:82
  459.7 21.5 %collective-permute-start.49 = (bf16[256,2048]{1,0:T(8,128)(2,1)}, bf16[256,2048]{1,0:T(8,128)(2,1)S(1)}, u32[]{:S(2)}, u32[]{:S(2)}) collective-permute-start(bf16[256,2048]{1,0:T(8,128)(2,1)} %collective-permute-done.48), channel_id=1, source_target_pairs={{0,1},{1,3},{3,5},{5,7},{7,6},{6,4},{4,2},{2,0},{8,9},{9,11},{11,1... | collective-permute-start | bytes 3145736 | tf_op jit(solution)/shard_map/ppermute | solution.py:79
  459.9 22.5 %collective-permute-start.46 = (bf16[256,2048]{1,0:T(8,128)(2,1)}, bf16[256,2048]{1,0:T(8,128)(2,1)S(1)}, u32[]{:S(2)}, u32[]{:S(2)}) collective-permute-start(bf16[256,2048]{1,0:T(8,128)(2,1)} %collective-permute-done.45), channel_id=1, source_target_pairs={{1,0},{3,1},{5,3},{7,5},{6,7},{4,6},{2,4},{0,2},{9,8},{11,9},{13,1... | collective-permute-start | bytes 3145736 | tf_op jit(solution)/shard_map/ppermute | solution.py:82
  516.7 26.0 %collective-permute-start.53 = (bf16[256,2048]{1,0:T(8,128)(2,1)S(1)}, bf16[256,2048]{1,0:T(8,128)(2,1)S(1)}, u32[]{:S(2)}, u32[]{:S(2)}) collective-permute-start(bf16[256,2048]{1,0:T(8,128)(2,1)S(1)} %add_convert_fusion.18), channel_id=1, source_target_pairs={{0,1},{1,3},{3,5},{5,7},{7,6},{6,4},{4,2},{2,0},{8,9},{9,11},{11,1... | collective-permute-start | bytes 3145736 | tf_op jit(solution)/shard_map/ppermute | solution.py:79
  518.6 24.4 %collective-permute-start.55 = (bf16[256,2048]{1,0:T(8,128)(2,1)S(1)}, bf16[256,2048]{1,0:T(8,128)(2,1)S(1)}, u32[]{:S(2)}, u32[]{:S(2)}) collective-permute-start(bf16[256,2048]{1,0:T(8,128)(2,1)S(1)} %add_convert_fusion.16), channel_id=1, source_target_pairs={{1,0},{3,1},{5,3},{7,5},{6,7},{4,6},{2,4},{0,2},{9,8},{11,9},{13,1... | collective-permute-start | bytes 3145736 | tf_op jit(solution)/shard_map/ppermute | solution.py:82
  569.5 25.6 %collective-permute-start.58 = (bf16[256,2048]{1,0:T(8,128)(2,1)S(1)}, bf16[256,2048]{1,0:T(8,128)(2,1)S(1)}, u32[]{:S(2)}, u32[]{:S(2)}) collective-permute-start(bf16[256,2048]{1,0:T(8,128)(2,1)S(1)} %copy-done.76), channel_id=1, source_target_pairs={{0,1},{1,3},{3,5},{5,7},{7,6},{6,4},{4,2},{2,0},{8,9},{9,11},{11,1... | collective-permute-start | bytes 3145736 | tf_op jit(solution)/shard_map/ppermute | solution.py:79
  570.6 25.3 %collective-permute-start.59 = (bf16[256,2048]{1,0:T(8,128)(2,1)S(1)}, bf16[256,2048]{1,0:T(8,128)(2,1)S(1)}, u32[]{:S(2)}, u32[]{:S(2)}) collective-permute-start(bf16[256,2048]{1,0:T(8,128)(2,1)S(1)} %copy-done.77), channel_id=1, source_target_pairs={{1,0},{3,1},{5,3},{7,5},{6,7},{4,6},{2,4},{0,2},{9,8},{11,9},{13,1... | collective-permute-start | bytes 3145736 | tf_op jit(solution)/shard_map/ppermute | solution.py:82
  612.9 31.7 %all-to-all-start.2 = ((bf16[8,256,256]{2,1,0:T(8,128)(2,1)}), bf16[8,256,256]{2,1,0:T(8,128)(2,1)}, u32[]{:S(2)}, u32[]{:S(2)}) async-start(bf16[8,256,256]{2,1,0:T(8,128)(2,1)} %bitcast.297), calls=%async_computation.2 | async-start | bytes 2097152 | tf_op jit(solution)/shard_map/all_to_all | solution.py:665
  618.2 48.3 %collective-permute-start.69 = (bf16[1024,512]{1,0:T(8,128)(2,1)}, bf16[1024,512]{1,0:T(8,128)(2,1)}, u32[]{:S(2)}, u32[]{:S(2)}) collective-permute-start(bf16[1024,512]{1,0:T(8,128)(2,1)} %get-tuple-element.164), channel_id=1, source_target_pairs={{0,16},{8,24},{16,0},{24,8},{1,17},{9,25},{17,1},{25,9},{2,18},{10... | collective-permute-start | bytes 3145736 | tf_op jit(solution)/shard_map/ppermute | solution.py:36
  619.8 47.3 %collective-permute-start.70 = (bf16[512,1024]{1,0:T(8,128)(2,1)}, bf16[512,1024]{1,0:T(8,128)(2,1)}, u32[]{:S(2)}, u32[]{:S(2)}) collective-permute-start(bf16[512,1024]{1,0:T(8,128)(2,1)} %get-tuple-element.165), channel_id=1, source_target_pairs={{0,16},{8,24},{16,0},{24,8},{1,17},{9,25},{17,1},{25,9},{2,18},{10... | collective-permute-start | bytes 3145736 | tf_op jit(solution)/shard_map/ppermute | solution.py:36
  644.6 21.6 %collective-permute-start.67 = (bf16[64,2048]{1,0:T(8,128)(2,1)}, bf16[64,2048]{1,0:T(8,128)(2,1)S(1)}, u32[]{:S(2)}, u32[]{:S(2)}) collective-permute-start(bf16[64,2048]{1,0:T(8,128)(2,1)} %get-tuple-element.162), channel_id=1, source_target_pairs={{0,1},{1,3},{3,5},{5,7},{7,6},{6,4},{4,2},{2,0},{8,9},{9,11},{11,1... | collective-permute-start | bytes 786440 | tf_op jit(solution)/shard_map/ppermute | solution.py:79
  649.9 38.8 %collective-permute-start.73 = (bf16[512,1024]{1,0:T(8,128)(2,1)S(1)}, bf16[512,1024]{1,0:T(8,128)(2,1)}, u32[]{:S(2)}, u32[]{:S(2)}) collective-permute-start(bf16[512,1024]{1,0:T(8,128)(2,1)S(1)} %copy-done.75), channel_id=1, source_target_pairs={{0,16},{8,24},{16,0},{24,8},{1,17},{9,25},{17,1},{25,9},{2,18},{10... | collective-permute-start | bytes 3145736 | tf_op jit(solution)/shard_map/ppermute | solution.py:36
  734.1 26.1 %collective-permute-start.81 = (bf16[256,2048]{1,0:T(8,128)(2,1)S(1)}, bf16[256,2048]{1,0:T(8,128)(2,1)S(1)}, u32[]{:S(2)}, u32[]{:S(2)}) collective-permute-start(bf16[256,2048]{1,0:T(8,128)(2,1)S(1)} %get-tuple-element.191), channel_id=1, source_target_pairs={{0,1},{1,3},{3,5},{5,7},{7,6},{6,4},{4,2},{2,0},{8,9},{9,11},{11,1... | collective-permute-start | bytes 3145736 | tf_op jit(solution)/shard_map/ppermute | solution.py:79
  735.4 26.1 %collective-permute-start.82 = (bf16[256,2048]{1,0:T(8,128)(2,1)S(1)}, bf16[256,2048]{1,0:T(8,128)(2,1)S(1)}, u32[]{:S(2)}, u32[]{:S(2)}) collective-permute-start(bf16[256,2048]{1,0:T(8,128)(2,1)S(1)} %get-tuple-element.192), channel_id=1, source_target_pairs={{1,0},{3,1},{5,3},{7,5},{6,7},{4,6},{2,4},{0,2},{9,8},{11,9},{13,1... | collective-permute-start | bytes 3145736 | tf_op jit(solution)/shard_map/ppermute | solution.py:82
  745.6 24.8 %collective-permute-start.90 = (bf16[128,2048]{1,0:T(8,128)(2,1)S(1)}, bf16[128,2048]{1,0:T(8,128)(2,1)S(1)}, u32[]{:S(2)}, u32[]{:S(2)}) collective-permute-start(bf16[128,2048]{1,0:T(8,128)(2,1)S(1)} %fusion.56), channel_id=1, source_target_pairs={{0,1},{1,3},{3,5},{5,7},{7,6},{6,4},{4,2},{2,0},{8,9},{9,11},{11,1... | collective-permute-start | bytes 1572872 | tf_op jit(solution)/shard_map/ppermute | solution.py:79
  746.9 24.9 %collective-permute-start.91 = (bf16[128,2048]{1,0:T(8,128)(2,1)S(1)}, bf16[128,2048]{1,0:T(8,128)(2,1)S(1)}, u32[]{:S(2)}, u32[]{:S(2)}) collective-permute-start(bf16[128,2048]{1,0:T(8,128)(2,1)S(1)} %fusion.55), channel_id=1, source_target_pairs={{1,0},{3,1},{5,3},{7,5},{6,7},{4,6},{2,4},{0,2},{9,8},{11,9},{13,1... | collective-permute-start | bytes 1572872 | tf_op jit(solution)/shard_map/ppermute | solution.py:82
  765.9 26.1 %collective-permute-start.83 = (bf16[256,2048]{1,0:T(8,128)(2,1)S(1)}, bf16[256,2048]{1,0:T(8,128)(2,1)S(1)}, u32[]{:S(2)}, u32[]{:S(2)}) collective-permute-start(bf16[256,2048]{1,0:T(8,128)(2,1)S(1)} %get-tuple-element.194), channel_id=1, source_target_pairs={{0,1},{1,3},{3,5},{5,7},{7,6},{6,4},{4,2},{2,0},{8,9},{9,11},{11,1... | collective-permute-start | bytes 3145736 | tf_op jit(solution)/shard_map/ppermute | solution.py:79
  770.4 23.1 %collective-permute-start.84 = (bf16[256,2048]{1,0:T(8,128)(2,1)S(1)}, bf16[256,2048]{1,0:T(8,128)(2,1)S(1)}, u32[]{:S(2)}, u32[]{:S(2)}) collective-permute-start(bf16[256,2048]{1,0:T(8,128)(2,1)S(1)} %get-tuple-element.195), channel_id=1, source_target_pairs={{1,0},{3,1},{5,3},{7,5},{6,7},{4,6},{2,4},{0,2},{9,8},{11,9},{13,1... | collective-permute-start | bytes 3145736 | tf_op jit(solution)/shard_map/ppermute | solution.py:82
  772.5 23.2 %collective-permute-start.87 = (bf16[512,768]{1,0:T(8,128)(2,1)S(1)}, bf16[512,768]{1,0:T(8,128)(2,1)S(1)}, u32[]{:S(2)}, u32[]{:S(2)}) collective-permute-start(bf16[512,768]{1,0:T(8,128)(2,1)S(1)} %get-tuple-element.298), channel_id=1, source_target_pairs={{0,16},{8,24},{16,0},{24,8},{1,17},{9,25},{17,1},{25,9},{2,18},{10... | collective-permute-start | bytes 2359304 | tf_op jit(solution)/shard_map/ppermute | solution.py:36
  773.8 33.1 %collective-permute-start.92 = (f32[1,64,2048]{2,1,0:T(8,128)}, f32[1,64,2048]{2,1,0:T(8,128)}, u32[]{:S(2)}, u32[]{:S(2)}) collective-permute-start(f32[1,64,2048]{2,1,0:T(8,128)} %dynamic-slice_bitcast_fusion.1), channel_id=1, source_target_pairs={{0,16},{8,24},{16,0},{24,8},{1,17},{9,25},{17,1},{25,9},{2,18},{10... | collective-permute-start | bytes 1572872 | tf_op jit(solution)/shard_map/ppermute | solution.py:36
  795.6 27.0 %collective-permute-start.88 = (bf16[256,2048]{1,0:T(8,128)(2,1)}, bf16[256,2048]{1,0:T(8,128)(2,1)}, u32[]{:S(2)}, u32[]{:S(2)}) collective-permute-start(bf16[256,2048]{1,0:T(8,128)(2,1)} %get-tuple-element.197), channel_id=1, source_target_pairs={{0,1},{1,3},{3,5},{5,7},{7,6},{6,4},{4,2},{2,0},{8,9},{9,11},{11,1... | collective-permute-start | bytes 3145736 | tf_op jit(solution)/shard_map/ppermute | solution.py:79
  797.4 25.5 %collective-permute-start.89 = (bf16[256,2048]{1,0:T(8,128)(2,1)}, bf16[256,2048]{1,0:T(8,128)(2,1)}, u32[]{:S(2)}, u32[]{:S(2)}) collective-permute-start(bf16[256,2048]{1,0:T(8,128)(2,1)} %get-tuple-element.198), channel_id=1, source_target_pairs={{1,0},{3,1},{5,3},{7,5},{6,7},{4,6},{2,4},{0,2},{9,8},{11,9},{13,1... | collective-permute-start | bytes 3145736 | tf_op jit(solution)/shard_map/ppermute | solution.py:82
  798.8 37.1 %all-to-all-start.3 = ((bf16[8,64,768]{2,1,0:T(8,128)(2,1)}), bf16[8,64,768]{2,1,0:T(8,128)(2,1)}, u32[]{:S(2)}, u32[]{:S(2)}) async-start(bf16[8,64,768]{2,1,0:T(8,128)(2,1)} %bitcast.328), calls=%async_computation.3 | async-start | bytes 1572864 | tf_op jit(solution)/shard_map/all_to_all | solution.py:748
  (152 other events, 1839.5 us)
Sparse Core Ops, SparseCore 0:
  114.2 97.2 all-gather.1
